TPU v7x, 32 devices: a whole 2x2x4 slice. The times are simulated.
32 devices in a mesh: dp: 8 (over z, y), mp: 4 (over x, core).
Axes of the slice: x: 2, y: 2, z: 4, core: 2. Of those that a mesh axis runs over, the one named last changes fastest.
Arguments:
- tokens: bfloat16 [2, 12288, 384], P(None, ('dp', 'mp')), may hold values from -6 to 6
- crop_counts: int32 [2, 16], P(None, 'dp'), may hold values from 2 to 10, as said below
- slot_live: int32 [8], replicated, may hold values from 0 to 1, as said below
- block_w: float32 [2, 384, 4, 1280], P(None, None, 'mp', 'dp')
- block_m: float32 [2, 384, 4, 1280], P(None, None, 'mp', 'dp'), may hold values from -7.1525574e-07 to 7.1525574e-07
- block_v: float32 [2, 384, 4, 1280], P(None, None, 'mp', 'dp'), may hold values from 2.5268668e-14 to 4.042987e-13
- rotation_bases: float32 [2, 4, 384, 384], replicated, as said below
- precond_stats: float32 [2, 4, 384, 384], replicated, as said below
- head_w: float32 [2688, 2048], P('dp')
- head_m: float32 [2688, 2048], P('dp'), may hold values from -1.66893e-06 to 1.66893e-06
- head_v: float32 [2688, 2048], P('dp'), may hold values from 4.767673e-16 to 7.628277e-15
- proto_w: float32 [256, 65536], P('dp', 'mp'), may hold values from -2 to 2
- proto_m: float32 [256, 65536], P('dp', 'mp'), may hold values from -1.66893e-06 to 1.66893e-06
- proto_v: float32 [256, 65536], P('dp', 'mp'), may hold values from 4.767673e-16 to 7.628277e-15
- norm_params: float32 [10, 384], replicated
- norm_m: float32 [10, 384], replicated, may hold values from -1.5258789e-05 to 1.5258789e-05
- norm_v: float32 [10, 384], replicated, may hold values from 4.7676733e-14 to 7.6282774e-13
- teacher_block: float32 [2, 384, 4, 1280], P(None, None, 'mp', 'dp')
- teacher_head: float32 [2688, 2048], P('dp')
- teacher_proto: float32 [256, 65536], P('dp', 'mp'), may hold values from -2 to 2
- teacher_norm: float32 [10, 384], replicated
- center: float32 [65536], P('mp'), may hold values from -0.75 to 0.75
Outputs:
- distill_loss: float32 [], replicated
- grad_norm: float32 [], replicated
- new_block_w: float32 [2, 384, 4, 1280], P(None, None, 'mp', 'dp')
- new_block_m: float32 [2, 384, 4, 1280], P(None, None, 'mp', 'dp')
- new_block_v: float32 [2, 384, 4, 1280], P(None, None, 'mp', 'dp')
- new_bases: float32 [2, 4, 384, 384], replicated
- new_stats: float32 [2, 4, 384, 384], replicated
- new_head_w: float32 [2688, 2048], P('dp')
- new_head_m: float32 [2688, 2048], P('dp')
- new_head_v: float32 [2688, 2048], P('dp')
- new_proto_w: float32 [256, 65536], P('dp', 'mp')
- new_proto_m: float32 [256, 65536], P('dp', 'mp')
- new_proto_v: float32 [256, 65536], P('dp', 'mp')
- new_norm: float32 [10, 384], replicated
- new_norm_m: float32 [10, 384], replicated
- new_norm_v: float32 [10, 384], replicated
- new_teacher_block: float32 [2, 384, 4, 1280], P(None, None, 'mp', 'dp')
- new_teacher_head: float32 [2688, 2048], P('dp')
- new_teacher_proto: float32 [256, 65536], P('dp', 'mp')
- new_teacher_norm: float32 [10, 384], replicated
- new_center: float32 [65536], P('mp')
Inputs may be any that keep to these rules, and one draw needn't show every extreme that they name: `crop_counts`: local crops of each image; both 2 and 10 occur in every draw. `slot_live`: 1 marks a slot that holds a head; exactly 6 ones, each group of 2 slots of one index of mp holding one or two. `rotation_bases`: each of the matrices is orthonormal. `precond_stats`: each of the matrices is symmetric positive definite.
All inputs are finite; a program needn't handle non-finite values.
Results may differ from a plain program's by a relative error of at most 0.0085.
The roundings to bfloat16 on the way count: a program that leaves them out, or rounds other values in their place, can miss the bound.
Values may be sent and summed in bfloat16 or wider, within the bound.
No kernel may reach another device: no remote copies, remote signals or barrier semaphores. Data moves between devices by JAX's collectives and lax.ppermute only.
A program may use at most 384 MiB of HBM per device.

v0:
```python
import jax
import jax.numpy as jnp
from jax import lax
from jax.sharding import PartitionSpec as P

D = 384
HD = 64
HID = 2048
LAYERS = 2
SLOT_DEV = 2
GLOBAL_TOK = 197
LOCAL_TOK = 37
MAX_LOCAL = 10
IMG_ROWS = 768
STEP = 10
MICRO = 2
CROPS = 12


precise = lax.Precision.HIGHEST
TAU_S = 0.1
TAU_T = 0.07
CLIP_NORM = 0.005
BETA_ONE = 0.9
BETA_TWO = 0.999
ROT_ONE = 0.95
ROT_TWO = 0.95
SHAMPOO_BETA = 0.95
ADAM_EPS = 1e-08
WEIGHT_DECAY = 0.04
LR_BLOCK = 0.05
LR_HEAD = 0.03
LR_PROTO = 0.1
LR_NORM = 0.2
TEACHER_MOM = 0.7
CENTER_MOM = 0.9
CONTRACT_LAST = (((1,), (1,)), ((), ()))
CONTRACT_FIRST = (((0,), (0,)), ((), ()))


def norm_rows(inputs, gain_vec, bias_vec):
    row_mean = jnp.mean(inputs, axis=-1, keepdims=True)
    centred = inputs - row_mean
    spread = jnp.mean(centred * centred, axis=-1, keepdims=True)
    return centred * lax.rsqrt(spread + 1e-06) * gain_vec + bias_vec


def norm_back(inputs, gain_vec, bias_vec, grad_out):
    outputs, pullback = jax.vjp(norm_rows, inputs, gain_vec, bias_vec)
    return pullback(grad_out)


def gelu_exact(inputs):
    return jax.nn.gelu(inputs, approximate=False)


def gelu_back(inputs, grad_out):
    outputs, pullback = jax.vjp(gelu_exact, inputs)
    return pullback(grad_out)[0]


def unit_rows(inputs):
    return inputs * lax.rsqrt(jnp.sum(inputs * inputs, axis=-1, keepdims=True) + 1e-06)


def crop_mask(crop_count):
    row_ids = jnp.arange(IMG_ROWS)
    segment = jnp.where(
        row_ids < 2 * GLOBAL_TOK, row_ids // GLOBAL_TOK, 2 + (row_ids - 2 * GLOBAL_TOK) // LOCAL_TOK
    )
    segment = jnp.minimum(segment, 2 + MAX_LOCAL)
    alive_row = segment < 2 + crop_count
    same_crop = (segment[:, None] == segment[None, :]) & alive_row[:, None]
    return same_crop | jnp.eye(IMG_ROWS, dtype=bool)


def cls_positions(images):
    crop_ids = jnp.arange(CROPS)
    starts = jnp.where(
        crop_ids < 2, crop_ids * GLOBAL_TOK, 2 * GLOBAL_TOK + (crop_ids - 2) * LOCAL_TOK
    )
    return (jnp.arange(images)[:, None] * IMG_ROWS + starts[None, :]).reshape(-1)


def pick_rows(positions, first_row, row_count):
    return (positions[:, None] == first_row + jnp.arange(row_count)[None, :]).astype(jnp.float32)


def assemble(whole):
    groups = whole.shape[1]
    width = SLOT_DEV * HD
    ff_shard = (whole.shape[2] - 4 * width) // 2
    qkv_w = (
        whole[:, :, : 3 * width]
        .reshape(D, groups, 3, SLOT_DEV, HD)
        .transpose(0, 2, 1, 3, 4)
        .reshape(D, 3 * groups * width)
    )
    proj_t = whole[:, :, 3 * width : 4 * width].reshape(D, groups * width)
    up_w = whole[:, :, 4 * width : 4 * width + ff_shard].reshape(D, groups * ff_shard)
    down_t = whole[:, :, 4 * width + ff_shard :].reshape(D, groups * ff_shard)
    return (qkv_w, proj_t, up_w, down_t)


def disassemble(grads, groups):
    grad_qkv, grad_proj, grad_up, grad_down = grads
    width = SLOT_DEV * HD
    qkv_part = (
        grad_qkv.reshape(D, 3, groups, width).transpose(0, 2, 1, 3).reshape(D, groups, 3 * width)
    )
    return jnp.concatenate(
        [
            qkv_part,
            grad_proj.reshape(D, groups, width),
            grad_up.reshape(D, groups, -1),
            grad_down.reshape(D, groups, -1),
        ],
        axis=2,
    )


def group_heads(array, groups):
    images = array.shape[0]
    return (
        array.reshape(images, IMG_ROWS, groups, SLOT_DEV, HD)
        .transpose(0, 2, 1, 3, 4)
        .reshape(images * groups, IMG_ROWS, SLOT_DEV, HD)
    )


def ungroup_heads(array, groups):
    images = array.shape[0] // groups
    return (
        array.reshape(images, groups, IMG_ROWS, SLOT_DEV, HD)
        .transpose(0, 2, 1, 3, 4)
        .reshape(images, IMG_ROWS, groups * SLOT_DEV, HD)
    )


def gather_normed(rows):
    return lax.all_gather(rows, "mp", axis=0, tiled=True)


def gather_grads(rows):
    return lax.all_gather(rows, "mp", axis=0, tiled=True)


def attend_image(block_item):
    queries, keys_in, values, crop_count = block_item
    allowed = crop_mask(crop_count)
    scores = jnp.einsum(
        "qnh,knh->nqk", queries, keys_in, preferred_element_type=jnp.float32
    ) * HD ** (-0.5)
    expd_scores = jnp.where(allowed[None], jnp.exp(scores), 0.0)
    totals = jnp.sum(expd_scores, axis=-1)
    attn_probs = (expd_scores / totals[..., None]).astype(jnp.bfloat16)
    attn_mix = jnp.einsum("nqk,knh->qnh", attn_probs, values, preferred_element_type=jnp.float32)
    return (attn_mix, totals)


def attend_back(block_item):
    queries, keys_in, values, grad_mix, totals, crop_count = block_item
    allowed = crop_mask(crop_count)
    scores = jnp.einsum(
        "qnh,knh->nqk", queries, keys_in, preferred_element_type=jnp.float32
    ) * HD ** (-0.5)
    attn_probs = jnp.where(allowed[None], jnp.exp(scores), 0.0) / totals[..., None]
    grad_values = jnp.einsum(
        "nqk,qnh->knh",
        attn_probs.astype(jnp.bfloat16),
        grad_mix,
        preferred_element_type=jnp.float32,
    )
    grad_probs = jnp.einsum("qnh,knh->nqk", grad_mix, values, preferred_element_type=jnp.float32)
    grad_scores = attn_probs * (
        grad_probs - jnp.sum(attn_probs * grad_probs, axis=-1, keepdims=True)
    )
    grad_low = grad_scores.astype(jnp.bfloat16)
    grad_queries = jnp.einsum(
        "nqk,knh->qnh", grad_low, keys_in, preferred_element_type=jnp.float32
    ) * HD ** (-0.5)
    grad_keys = jnp.einsum(
        "nqk,qnh->knh", grad_low, queries, preferred_element_type=jnp.float32
    ) * HD ** (-0.5)
    return jnp.stack([grad_queries, grad_keys, grad_values], axis=1)


def block_forward(x_own, parts, gains, slot_alive, crop_counts):
    qkv_w, proj_t, up_w, down_t = parts
    images = crop_counts.shape[0]
    slots = slot_alive.shape[0]
    groups = slots // SLOT_DEV
    normed = norm_rows(x_own, gains[0], gains[1]).astype(jnp.bfloat16)
    normed_all = gather_normed(normed)
    qkv_all = jnp.dot(normed_all, qkv_w, preferred_element_type=jnp.float32).astype(jnp.bfloat16)
    qkv_all = qkv_all.reshape(images, IMG_ROWS, 3, slots, HD)
    grouped = (
        group_heads(qkv_all[:, :, 0], groups),
        group_heads(qkv_all[:, :, 1], groups),
        group_heads(qkv_all[:, :, 2], groups),
    )
    group_counts = jnp.repeat(crop_counts, groups)
    attn_mix, totals = lax.map(attend_image, (grouped[0], grouped[1], grouped[2], group_counts))
    attn_mix = ungroup_heads(attn_mix, groups)
    attn_mix = (
        (attn_mix * slot_alive[None, None, :, None])
        .astype(jnp.bfloat16)
        .reshape(images * IMG_ROWS, slots * HD)
    )
    portion = attn_mix
    middle = x_own + lax.psum_scatter(
        lax.dot_general(portion, proj_t, CONTRACT_LAST, preferred_element_type=jnp.float32).astype(
            jnp.bfloat16
        ),
        "mp",
        scatter_dimension=0,
        tiled=True,
    ).astype(jnp.float32)
    hidden_in = norm_rows(middle, gains[2], gains[3]).astype(jnp.bfloat16)
    hidden_all = gather_normed(hidden_in)
    up_proj = jnp.dot(hidden_all, up_w, preferred_element_type=jnp.float32)
    hidden = gelu_exact(up_proj).astype(jnp.bfloat16)
    portion = hidden
    output = middle + lax.psum_scatter(
        lax.dot_general(portion, down_t, CONTRACT_LAST, preferred_element_type=jnp.float32).astype(
            jnp.bfloat16
        ),
        "mp",
        scatter_dimension=0,
        tiled=True,
    ).astype(jnp.float32)
    kept = (
        normed_all,
        grouped,
        group_counts,
        totals,
        attn_mix,
        middle,
        hidden_all,
        up_proj,
        hidden,
    )
    return (output, kept)


def block_backward(x_own, parts, gains, slot_alive, crop_counts, kept, grad_out):
    qkv_w, proj_t, up_w, down_t = parts
    normed_all, grouped, group_counts, totals, attn_mix, middle, hidden_all, up_proj, hidden = kept
    images = crop_counts.shape[0]
    slots = slot_alive.shape[0]
    groups = slots // SLOT_DEV
    grad_down_in = gather_grads(grad_out.astype(jnp.bfloat16))
    grad_down = lax.dot_general(
        grad_down_in, hidden, CONTRACT_FIRST, preferred_element_type=jnp.float32
    )
    grad_hidden = jnp.dot(grad_down_in, down_t, preferred_element_type=jnp.float32)
    grad_upper = gelu_back(up_proj, grad_hidden).astype(jnp.bfloat16)
    grad_up = lax.dot_general(
        hidden_all, grad_upper, CONTRACT_FIRST, preferred_element_type=jnp.float32
    )
    portion = grad_upper
    grad_hidden_in = lax.psum_scatter(
        lax.dot_general(portion, up_w, CONTRACT_LAST, preferred_element_type=jnp.float32).astype(
            jnp.bfloat16
        ),
        "mp",
        scatter_dimension=0,
        tiled=True,
    ).astype(jnp.float32)
    grad_mid, grad_gain_two, grad_bias_two = norm_back(middle, gains[2], gains[3], grad_hidden_in)
    grad_mid = grad_mid + grad_out
    grad_mix_all = gather_grads(grad_mid.astype(jnp.bfloat16))
    grad_proj = lax.dot_general(
        grad_mix_all, attn_mix, CONTRACT_FIRST, preferred_element_type=jnp.float32
    )
    grad_mix = jnp.dot(grad_mix_all, proj_t, preferred_element_type=jnp.float32).astype(
        jnp.bfloat16
    )
    grad_mix = (
        grad_mix.reshape(images, IMG_ROWS, slots, HD)
        * slot_alive.astype(jnp.bfloat16)[None, None, :, None]
    )
    grad_qkv = lax.map(
        attend_back,
        (grouped[0], grouped[1], grouped[2], group_heads(grad_mix, groups), totals, group_counts),
    )
    grad_qkv = grad_qkv.reshape(images, groups, IMG_ROWS, 3, SLOT_DEV, HD).transpose(
        0, 2, 3, 1, 4, 5
    )
    grad_qkv = grad_qkv.reshape(images * IMG_ROWS, 3 * slots * HD).astype(jnp.bfloat16)
    grad_qkv_w = lax.dot_general(
        normed_all, grad_qkv, CONTRACT_FIRST, preferred_element_type=jnp.float32
    )
    portion = grad_qkv
    grad_normed = lax.psum_scatter(
        lax.dot_general(portion, qkv_w, CONTRACT_LAST, preferred_element_type=jnp.float32).astype(
            jnp.bfloat16
        ),
        "mp",
        scatter_dimension=0,
        tiled=True,
    ).astype(jnp.float32)
    grad_input, grad_gain_one, grad_bias_one = norm_back(x_own, gains[0], gains[1], grad_normed)
    block_grad = disassemble((grad_qkv_w, grad_proj, grad_up, grad_down), groups)
    return (
        grad_input + grad_mid,
        block_grad,
        jnp.stack([grad_gain_one, grad_bias_one, grad_gain_two, grad_bias_two]),
    )


def head_forward(cls_feats, head_full, head_norms):
    features = norm_rows(cls_feats, head_norms[0], head_norms[1]).astype(jnp.bfloat16)
    first_out = jnp.dot(features, head_full[:D], preferred_element_type=jnp.float32)
    act_one = gelu_exact(first_out).astype(jnp.bfloat16)
    second = jnp.dot(act_one, head_full[D : D + HID], preferred_element_type=jnp.float32)
    act_two = gelu_exact(second).astype(jnp.bfloat16)
    third_out = lax.dot_general(
        act_two, head_full[D + HID :], CONTRACT_LAST, preferred_element_type=jnp.float32
    )
    unit_out = unit_rows(third_out).astype(jnp.bfloat16)
    return (features, first_out, act_one, second, act_two, third_out, unit_out)


def head_backward(cls_feats, head_full, head_norms, saved, grad_unit):
    features, first_out, act_one, second, act_two, third_out, unit_out = saved
    outputs, unit_pull = jax.vjp(unit_rows, third_out)
    grad_third = unit_pull(grad_unit)[0].astype(jnp.bfloat16)
    grad_three = lax.dot_general(
        grad_third, act_two, CONTRACT_FIRST, preferred_element_type=jnp.float32
    )
    grad_act_two = jnp.dot(grad_third, head_full[D + HID :], preferred_element_type=jnp.float32)
    grad_second = gelu_back(second, grad_act_two).astype(jnp.bfloat16)
    grad_two = lax.dot_general(
        act_one, grad_second, CONTRACT_FIRST, preferred_element_type=jnp.float32
    )
    grad_act_one = lax.dot_general(
        grad_second, head_full[D : D + HID], CONTRACT_LAST, preferred_element_type=jnp.float32
    )
    grad_first = gelu_back(first_out, grad_act_one).astype(jnp.bfloat16)
    grad_one = lax.dot_general(
        features, grad_first, CONTRACT_FIRST, preferred_element_type=jnp.float32
    )
    grad_feats = lax.dot_general(
        grad_first, head_full[:D], CONTRACT_LAST, preferred_element_type=jnp.float32
    )
    grad_cls, grad_gain, grad_bias = norm_back(cls_feats, head_norms[0], head_norms[1], grad_feats)
    head_grad = jnp.concatenate([grad_one, grad_two, grad_three], axis=0)
    return (grad_cls, head_grad, jnp.stack([grad_gain, grad_bias]))


def adam_direction(first_mom, second_mom, beta_one, beta_two):
    return (
        first_mom / (1 - beta_one**STEP) / (jnp.sqrt(second_mom / (1 - beta_two**STEP)) + ADAM_EPS)
    )


def adamw(weight, grad_in, first_mom, second_mom, rate, decay):
    first_mom = BETA_ONE * first_mom + (1 - BETA_ONE) * grad_in
    second_mom = BETA_TWO * second_mom + (1 - BETA_TWO) * grad_in * grad_in
    weight = weight - rate * (
        adam_direction(first_mom, second_mom, BETA_ONE, BETA_TWO) + decay * weight
    )
    return (weight, first_mom, second_mom)


def renew_basis(stat_new, basis):
    turned = jnp.dot(stat_new, basis, precision=precise)
    gram = jnp.dot(turned.T, turned, precision=precise)
    lower = jnp.linalg.cholesky(gram)
    return jax.scipy.linalg.solve_triangular(lower, turned.T, lower=True).T


def add_up(total, fresh):
    if total is None:
        return fresh
    return jax.tree.map(jnp.add, total, fresh)


def shards(
    tokens,
    crop_counts,
    slot_live,
    block_w,
    block_m,
    block_v,
    rotation_bases,
    precond_stats,
    head_w,
    head_m,
    head_v,
    proto_w,
    proto_m,
    proto_v,
    norm_params,
    norm_m,
    norm_v,
    teacher_block,
    teacher_head,
    teacher_proto,
    teacher_norm,
    center,
):
    mp_index = lax.axis_index("mp")
    dp_index = lax.axis_index("dp")
    dp_count = lax.axis_size("dp")
    images_dev = crop_counts.shape[0] * crop_counts.shape[1]
    rows_piece = tokens.shape[1]
    gathered = (
        lax.all_gather(block_w.astype(jnp.bfloat16), "dp", axis=3, tiled=True),
        lax.all_gather(teacher_block.astype(jnp.bfloat16), "dp", axis=3, tiled=True),
        lax.all_gather(head_w.astype(jnp.bfloat16), "dp", axis=0, tiled=True),
        lax.all_gather(teacher_head.astype(jnp.bfloat16), "dp", axis=0, tiled=True),
        lax.all_gather(proto_w.astype(jnp.bfloat16), "dp", axis=0, tiled=True),
        lax.all_gather(teacher_proto.astype(jnp.bfloat16), "dp", axis=0, tiled=True),
    )
    student_layers = [assemble(gathered[0][layer]) for layer in range(LAYERS)]
    teacher_layers = [assemble(gathered[1][layer]) for layer in range(LAYERS)]
    head_student, head_teacher, proto_student, proto_teacher = gathered[2:]
    slot_vec = lax.dynamic_slice_in_dim(slot_live, mp_index * SLOT_DEV, SLOT_DEV)
    slot_alive = slot_vec.astype(jnp.float32)
    student_head_norms = norm_params[4 * LAYERS :]
    teacher_head_norms = teacher_norm[4 * LAYERS :]
    totals_acc = None
    for micro in range(MICRO):
        x_own = tokens[micro].astype(jnp.float32)
        counts = crop_counts[micro]
        teacher_y = x_own
        for layer in range(LAYERS):
            teacher_y, unused = block_forward(
                teacher_y,
                teacher_layers[layer],
                teacher_norm[4 * layer : 4 * layer + 4],
                slot_alive,
                counts,
            )
        inputs_kept, kept_all = ([], [])
        student_y = x_own
        for layer in range(LAYERS):
            inputs_kept.append(student_y)
            student_y, kept = block_forward(
                student_y,
                student_layers[layer],
                norm_params[4 * layer : 4 * layer + 4],
                slot_alive,
                counts,
            )
            kept_all.append(kept)
        positions = cls_positions(counts.shape[0])
        pick_own = pick_rows(positions, mp_index * rows_piece, rows_piece)
        cls_student, cls_teacher = (
            lax.psum(
                jnp.dot(pick_own, student_y, precision=precise).astype(jnp.bfloat16), "mp"
            ).astype(jnp.float32),
            lax.psum(
                jnp.dot(pick_own, teacher_y, precision=precise).astype(jnp.bfloat16), "mp"
            ).astype(jnp.float32),
        )
        images = counts.shape[0]
        student_saved = head_forward(cls_student, head_student, student_head_norms)
        teacher_saved = head_forward(cls_teacher, head_teacher, teacher_head_norms)
        student_scaled = (
            jnp.dot(student_saved[6], proto_student, preferred_element_type=jnp.float32).reshape(
                images, CROPS, -1
            )
            / TAU_S
        )
        teacher_glob = jnp.dot(
            teacher_saved[6], proto_teacher, preferred_element_type=jnp.float32
        ).reshape(images, CROPS, -1)[:, :2]
        teacher_exp = jnp.exp((teacher_glob - center) / TAU_T)
        student_exp = jnp.exp(student_scaled)
        cross_part = jnp.einsum("igk,ivk->igv", teacher_exp, student_scaled, precision=precise)
        teacher_total, student_total, cross = lax.psum(
            (jnp.sum(teacher_exp, axis=-1), jnp.sum(student_exp, axis=-1), cross_part), "mp"
        )
        crop_ids = jnp.arange(CROPS)
        pairs = (
            (crop_ids[None, None, :] != jnp.arange(2)[None, :, None])
            & (crop_ids[None, None, :] < 2 + counts[:, None, None])
        ).astype(jnp.float32)
        image_weight = 1.0 / (2.0 * counts.astype(jnp.float32) + 2.0)
        entropy = jnp.log(student_total)[:, None, :] - cross / teacher_total[:, :, None]
        loss_dev = jnp.sum(jnp.sum(entropy * pairs, axis=(1, 2)) * image_weight)
        center_part = jnp.sum(teacher_glob, axis=(0, 1))
        pair_weight = pairs * image_weight[:, None, None]
        target_mix = jnp.einsum(
            "igv,igk->ivk", pair_weight, teacher_exp / teacher_total[:, :, None], precision=precise
        )
        grad_scaled = (
            jnp.sum(pair_weight, axis=1)[:, :, None] * student_exp / student_total[:, :, None]
            - target_mix
        ) / TAU_S
        grad_logits = grad_scaled.reshape(images * CROPS, -1).astype(jnp.bfloat16)
        grad_unit = lax.psum(
            lax.dot_general(
                grad_logits, proto_student, CONTRACT_LAST, preferred_element_type=jnp.float32
            ),
            "mp",
        )
        grad_proto = lax.dot_general(
            student_saved[6], grad_logits, CONTRACT_FIRST, preferred_element_type=jnp.float32
        )
        grad_cls, head_grad, head_gains = head_backward(
            cls_student, head_student, student_head_norms, student_saved, grad_unit
        )
        grad_flow = jnp.dot(pick_own.T, grad_cls, precision=precise)
        layer_grads = [None] * LAYERS
        layer_gains = [None] * LAYERS
        for layer in reversed(range(LAYERS)):
            grad_flow, layer_grads[layer], layer_gains[layer] = block_backward(
                inputs_kept[layer],
                student_layers[layer],
                norm_params[4 * layer : 4 * layer + 4],
                slot_alive,
                counts,
                kept_all[layer],
                grad_flow,
            )
        block_grad = jnp.stack(layer_grads)
        block_gains = jnp.concatenate(layer_gains, axis=0)
        weight_grads = (block_grad, head_grad, grad_proto)
        totals_acc = add_up(
            totals_acc,
            (
                weight_grads[0],
                weight_grads[1],
                weight_grads[2],
                block_gains,
                head_gains,
                loss_dev,
                center_part,
            ),
        )
    block_acc, head_acc, proto_acc, block_gains, head_gains, loss_dev, center_part = totals_acc
    loss_total, center_total = lax.psum((loss_dev, center_part), "dp")
    block_red, head_g, proto_g = (
        lax.psum_scatter(block_acc, "dp", scatter_dimension=3, tiled=True),
        lax.psum_scatter(head_acc, "dp", scatter_dimension=0, tiled=True),
        lax.psum_scatter(proto_acc, "dp", scatter_dimension=0, tiled=True),
    )
    block_g = block_red[:, :, 0]
    head_first = (mp_index == 0).astype(jnp.float32)
    col_width = block_g.shape[2]
    width = SLOT_DEV * HD
    total_cols = col_width * dp_count
    ff_shard = (total_cols - 4 * width) // 2
    col_ids = dp_index * col_width + jnp.arange(col_width)
    bounds = [0, 3 * width, 4 * width, 4 * width + ff_shard, total_cols]
    col_masks = jnp.stack(
        [
            ((col_ids >= bounds[matrix_id]) & (col_ids < bounds[matrix_id + 1])).astype(jnp.float32)
            for matrix_id in range(4)
        ]
    )
    stat_part = jnp.einsum("ldc,kc,lec->lkde", block_g, col_masks, block_g, precision=precise)
    norm_part = jnp.concatenate([block_gains, head_first * head_gains], axis=0)
    square_part = (
        jnp.sum(block_g * block_g)
        + head_first * jnp.sum(head_g * head_g)
        + jnp.sum(proto_g * proto_g)
    )
    loss_carry = jnp.zeros((), jnp.float32)
    center_carry = jnp.zeros((1, 1), jnp.float32)
    summed = lax.psum((stat_part, norm_part, square_part, loss_carry, center_carry), ("dp", "mp"))
    norm_total = summed[1]
    grad_norm = jnp.sqrt(summed[2] + jnp.sum(norm_total * norm_total))
    clip_factor = jnp.minimum(1.0, CLIP_NORM / (grad_norm + 1e-06))
    new_stats = (
        SHAMPOO_BETA * precond_stats + (1 - SHAMPOO_BETA) * (clip_factor * clip_factor) * summed[0]
    )
    new_bases = jnp.stack(
        [
            jnp.stack(
                [
                    renew_basis(new_stats[layer, matrix_id], rotation_bases[layer, matrix_id])
                    for matrix_id in range(4)
                ]
            )
            for layer in range(LAYERS)
        ]
    )
    grad_cols = clip_factor * block_g
    rotated = jnp.einsum("lkde,ldc,kc->lec", new_bases, grad_cols, col_masks, precision=precise)
    first_mom = ROT_ONE * block_m[:, :, 0] + (1 - ROT_ONE) * rotated
    second_mom = ROT_TWO * block_v[:, :, 0] + (1 - ROT_TWO) * rotated * rotated
    direction = adam_direction(first_mom, second_mom, ROT_ONE, ROT_TWO)
    turned_back = jnp.einsum("lkde,lec,kc->ldc", new_bases, direction, col_masks, precision=precise)
    master = block_w[:, :, 0]
    new_block_w = (master - LR_BLOCK * (turned_back + WEIGHT_DECAY * master))[:, :, None]
    new_head_w, new_head_m, new_head_v = adamw(
        head_w, clip_factor * head_g, head_m, head_v, LR_HEAD, WEIGHT_DECAY
    )
    new_proto_w, new_proto_m, new_proto_v = adamw(
        proto_w, clip_factor * proto_g, proto_m, proto_v, LR_PROTO, WEIGHT_DECAY
    )
    new_norm, new_norm_m, new_norm_v = adamw(
        norm_params, clip_factor * norm_total, norm_m, norm_v, LR_NORM, 0.0
    )
    new_teacher_block = TEACHER_MOM * teacher_block + (1 - TEACHER_MOM) * new_block_w
    new_teacher_head = TEACHER_MOM * teacher_head + (1 - TEACHER_MOM) * new_head_w
    new_teacher_proto = TEACHER_MOM * teacher_proto + (1 - TEACHER_MOM) * new_proto_w
    new_teacher_norm = TEACHER_MOM * teacher_norm + (1 - TEACHER_MOM) * new_norm
    new_center = CENTER_MOM * center + (1 - CENTER_MOM) * center_total / (
        2.0 * images_dev * dp_count
    )
    return (
        loss_total,
        grad_norm,
        new_block_w,
        first_mom[:, :, None],
        second_mom[:, :, None],
        new_bases,
        new_stats,
        new_head_w,
        new_head_m,
        new_head_v,
        new_proto_w,
        new_proto_m,
        new_proto_v,
        new_norm,
        new_norm_m,
        new_norm_v,
        new_teacher_block,
        new_teacher_head,
        new_teacher_proto,
        new_teacher_norm,
        new_center,
    )


def solution(mesh):
    in_specs = (
        P(None, ("dp", "mp"), None),
        P(None, "dp"),
        P(),
        P(None, None, "mp", "dp"),
        P(None, None, "mp", "dp"),
        P(None, None, "mp", "dp"),
        P(),
        P(),
        P("dp", None),
        P("dp", None),
        P("dp", None),
        P("dp", "mp"),
        P("dp", "mp"),
        P("dp", "mp"),
        P(),
        P(),
        P(),
        P(None, None, "mp", "dp"),
        P("dp", None),
        P("dp", "mp"),
        P(),
        P("mp"),
    )
    out_specs = (
        P(),
        P(),
        P(None, None, "mp", "dp"),
        P(None, None, "mp", "dp"),
        P(None, None, "mp", "dp"),
        P(),
        P(),
        P("dp", None),
        P("dp", None),
        P("dp", None),
        P("dp", "mp"),
        P("dp", "mp"),
        P("dp", "mp"),
        P(),
        P(),
        P(),
        P(None, None, "mp", "dp"),
        P("dp", None),
        P("dp", "mp"),
        P(),
        P("mp"),
    )
    return jax.shard_map(shards, mesh=mesh, in_specs=in_specs, out_specs=out_specs, check_vma=False)
```

profile of v0, /device:TPU:0, one launch (start us, length us, event | category | flops | bytes accessed | tf_op | source)
XLA Modules:
  0.0 4185.7 jit_solution(4513007383367677078)
XLA Ops:
  16.3 44.8 %all-gather.47.cloned.1.call-done = bf16[2,384,1,1280]{1,3,2,0:T(8,128)(2,1)} async-done(((bf16[2,384,1,160]{1,3,2,0:T(8,128)(2,1)}), bf16[2,384,1,1280]{1,3,2,0:T(8,128)(2,1)}) %all-gather.47.cloned.1.call-update) | async-done | bytes 1966096 | tf_op jit(solution)/shard_map/all_gather | solution.py:411
  100.8 24.4 reduce-scatter.52.cloned.1.call-done
  128.4 47.2 %all-gather.33.cloned.1.call-done = bf16[2,384,1,1280]{1,3,2,0:T(8,128)(2,1)} async-done(((bf16[2,384,1,160]{1,3,2,0:T(8,128)(2,1)}), bf16[2,384,1,1280]{1,3,2,0:T(8,128)(2,1)}) %all-gather.33.cloned.1.call-update) | async-done | bytes 1966096 | tf_op jit(solution)/shard_map/all_gather | solution.py:410
  272.6 20.9 reduce-scatter.36.cloned.1.call-done
  293.6 28.9 reduce-scatter.44.cloned.1.call-done
  322.4 28.9 reduce-scatter.28.cloned.1.call-done
  356.7 16.8 all-gather.49.cloned.1.call-done
  402.0 19.9 reduce-scatter.38.cloned.1.call-done
  421.9 28.9 reduce-scatter.54.cloned.1.call-done
  560.1 28.9 reduce-scatter.46.cloned.1.call-done
  673.8 17.0 reduce-scatter.32.cloned.1.call-done
  692.2 27.5 reduce-scatter.48.cloned.1.call-done
  723.1 25.5 reduce-scatter.40.cloned.1.call-done
  749.8 27.7 reduce-scatter.56.cloned.1.call-done
  864.8 19.8 reduce-scatter.50.cloned.1.call-done
  886.6 27.1 reduce-scatter.34.cloned.1.call-done
  915.7 26.8 reduce-scatter.58.cloned.1.call-done
  944.4 27.1 reduce-scatter.42.cloned.1.call-done
  985.7 19.2 all-reduce.13.cloned.1.call-done
  1006.7 160.2 %all-gather.41.cloned.1.call-done = bf16[2688,2048]{1,0:T(8,128)(2,1)} async-done(((bf16[336,2048]{1,0:T(8,128)(2,1)}), bf16[2688,2048]{1,0:T(8,128)(2,1)}) %all-gather.41.cloned.1.call-update) | async-done | bytes 11010064 | tf_op jit(solution)/shard_map/all_gather | solution.py:412
  1176.0 116.8 %all-gather.43.cloned.1.call-done = bf16[256,16384]{1,0:T(8,128)(2,1)} async-done(((bf16[32,16384]{1,0:T(8,128)(2,1)}), bf16[256,16384]{1,0:T(8,128)(2,1)}) %all-gather.43.cloned.1.call-update) | async-done | bytes 8388624 | tf_op jit(solution)/shard_map/all_gather | solution.py:414
  1299.3 151.8 %all-gather.55.cloned.1.call-done = bf16[2688,2048]{1,0:T(8,128)(2,1)} async-done(((bf16[336,2048]{1,0:T(8,128)(2,1)}), bf16[2688,2048]{1,0:T(8,128)(2,1)}) %all-gather.55.cloned.1.call-update) | async-done | bytes 11010064 | tf_op jit(solution)/shard_map/all_gather | solution.py:413
  1458.8 118.3 %all-gather.57.cloned.1.call-done = bf16[256,16384]{1,0:T(8,128)(2,1)} async-done(((bf16[32,16384]{1,0:T(8,128)(2,1)}), bf16[256,16384]{1,0:T(8,128)(2,1)}) %all-gather.57.cloned.1.call-update) | async-done | bytes 8388624 | tf_op jit(solution)/shard_map/all_gather | solution.py:415
  1725.3 21.6 reduce-scatter.66.cloned.1.call-done
  1746.9 28.7 reduce-scatter.60.cloned.1.call-done
  1800.8 17.5 all-gather.77.cloned.1.call-done
  1846.4 16.8 while.188
  1870.7 28.8 reduce-scatter.62.cloned.1.call-done
  1907.4 17.0 all-gather.79.cloned.1.call-done
  1951.3 21.8 reduce-scatter.64.cloned.1.call-done
  1973.1 28.7 reduce-scatter.70.cloned.1.call-done
  2134.4 21.4 maximum_add_fusion
  2157.5 19.4 reduce-scatter.72.cloned.1.call-done
  2188.4 20.6 psum.129
  2209.3 25.2 reduce-scatter.78.cloned.1.call-done
  2236.9 284.1 %reduce-scatter.76.cloned.1.call-done = f32[32,16384]{1,0:T(8,128)} async-done(((f32[256,16384]{1,0:T(8,128)}), f32[32,16384]{1,0:T(8,128)}) %reduce-scatter.76.cloned.1.call-update) | async-done | bytes 2097168 | tf_op jit(solution)/shard_map/reduce_scatter | solution.py:540
  2523.7 359.1 %reduce-scatter.74.cloned.1.call-done = f32[336,2048]{1,0:T(8,128)} async-done(((f32[2688,2048]{1,0:T(8,128)}), f32[336,2048]{1,0:T(8,128)}) %reduce-scatter.74.cloned.1.call-update) | async-done | bytes 2752528 | tf_op jit(solution)/shard_map/reduce_scatter | solution.py:539
  2887.8 66.5 %all-reduce.11.cloned.1.call-done = f32[16384]{0:T(1024)} async-done(((f32[16384]{0:T(1024)}), f32[16384]{0:T(1024)}) %all-reduce.11.cloned.1.call-update) | async-done | bytes 65552 | tf_op jit(solution)/shard_map/psum | solution.py:536
  2955.7 41.6 all-reduce.1
  2999.4 106.1 %all-reduce.9.cloned.1.call-done = f32[2,4,384,384]{3,2,1,0:T(8,128)} async-done(((f32[2,4,384,384]{3,2,1,0:T(8,128)}), f32[2,4,384,384]{3,2,1,0:T(8,128)}) %all-reduce.9.cloned.1.call-update) | async-done | bytes 4718608 | tf_op jit(solution)/shard_map/psum | solution.py:565
  3230.6 31.3 custom-call.61
  3370.2 31.1 custom-call.58
  3509.8 31.1 custom-call.55
  3638.1 29.9 custom-call.52
  3761.9 29.7 custom-call.49
  3885.6 29.7 custom-call.46
  3992.5 29.9 custom-call.43
  4099.5 31.1 custom-call.40
  (1819 shorter events, 1930.5 us)
Async XLA Ops:
  9.0 70.7 %all-gather.67.cloned.1.call-start = ((), (), s32[]{:S(2)}) async-start(), calls=%async_computation.57 | async-start | bytes 1474560 | tf_op jit(solution)/shard_map/all_gather | solution.py:141
  15.1 110.1 %reduce-scatter.52.cloned.1.call-start = ((), (), s32[]{:S(2)}) async-start(), calls=%async_computation.58 | async-start | bytes 1474560 | tf_op jit(solution)/shard_map/reduce_scatter | solution.py:211
  99.3 76.3 %all-gather.33.cloned.1.call-start = ((), (), s32[]{:S(2)}) async-start(), calls=%async_computation.28 | async-start | bytes 2211840 | tf_op jit(solution)/shard_map/all_gather | solution.py:410
  100.1 94.1 %all-gather.31.cloned.1.call-start = ((), (), s32[]{:S(2)}) async-start(), calls=%async_computation.27 | async-start | bytes 1474560 | tf_op jit(solution)/shard_map/all_gather | solution.py:141
  127.7 86.0 %all-gather.45.cloned.1.call-start = ((), (), s32[]{:S(2)}) async-start(), calls=%async_computation.38 | async-start | bytes 1474560 | tf_op jit(solution)/shard_map/all_gather | solution.py:141
  128.3 112.0 %all-gather.59.cloned.1.call-start = ((), (), s32[]{:S(2)}) async-start(), calls=%async_computation.49 | async-start | bytes 1474560 | tf_op jit(solution)/shard_map/all_gather | solution.py:141
  178.3 115.2 %reduce-scatter.36.cloned.1.call-start = ((), (), s32[]{:S(2)}) async-start(), calls=%async_computation.40 | async-start | bytes 1474560 | tf_op jit(solution)/shard_map/reduce_scatter | solution.py:211
  270.5 80.9 %reduce-scatter.28.cloned.1.call-start = ((), (), s32[]{:S(2)}) async-start(), calls=%async_computation.29 | async-start | bytes 1474560 | tf_op jit(solution)/shard_map/reduce_scatter | solution.py:211
  272.6 101.0 %all-gather.49.cloned.1.call-start = ((), (), s32[]{:S(2)}) async-start(), calls=%async_computation.41 | async-start | bytes 1474560 | tf_op jit(solution)/shard_map/all_gather | solution.py:141
  356.5 65.4 %reduce-scatter.38.cloned.1.call-start = ((), (), s32[]{:S(2)}) async-start(), calls=%async_computation.42 | async-start | bytes 1474560 | tf_op jit(solution)/shard_map/reduce_scatter | solution.py:224
  382.4 68.4 %reduce-scatter.54.cloned.1.call-start = ((), (), s32[]{:S(2)}) async-start(), calls=%async_computation.60 | async-start | bytes 1474560 | tf_op jit(solution)/shard_map/reduce_scatter | solution.py:224
  401.9 70.9 %all-gather.51.cloned.1.call-start = ((), (), s32[]{:S(2)}) async-start(), calls=%async_computation.43 | async-start | bytes 1474560 | tf_op jit(solution)/shard_map/all_gather | solution.py:141
  455.8 56.0 %all-gather.71.cloned.1.call-start = ((), (), s32[]{:S(2)}) async-start(), calls=%async_computation.61 | async-start | bytes 1474560 | tf_op jit(solution)/shard_map/all_gather | solution.py:141
  456.3 74.9 %all-gather.61.cloned.1.call-start = ((), (), s32[]{:S(2)}) async-start(), calls=%async_computation.51 | async-start | bytes 1474560 | tf_op jit(solution)/shard_map/all_gather | solution.py:141
  456.9 103.2 %reduce-scatter.30.cloned.1.call-start = ((), (), s32[]{:S(2)}) async-start(), calls=%async_computation.31 | async-start | bytes 1474560 | tf_op jit(solution)/shard_map/reduce_scatter | solution.py:224
  503.6 85.5 %reduce-scatter.46.cloned.1.call-start = ((), (), s32[]{:S(2)}) async-start(), calls=%async_computation.52 | async-start | bytes 1474560 | tf_op jit(solution)/shard_map/reduce_scatter | solution.py:224
  542.5 67.8 %all-gather.63.cloned.1.call-start = ((), (), s32[]{:S(2)}) async-start(), calls=%async_computation.53 | async-start | bytes 1474560 | tf_op jit(solution)/shard_map/all_gather | solution.py:141
  604.6 86.2 %reduce-scatter.32.cloned.1.call-start = ((), (), s32[]{:S(2)}) async-start(), calls=%async_computation.33 | async-start | bytes 1474560 | tf_op jit(solution)/shard_map/reduce_scatter | solution.py:211
  667.8 80.8 %reduce-scatter.40.cloned.1.call-start = ((), (), s32[]{:S(2)}) async-start(), calls=%async_computation.44 | async-start | bytes 1474560 | tf_op jit(solution)/shard_map/reduce_scatter | solution.py:211
  670.8 106.7 %reduce-scatter.56.cloned.1.call-start = ((), (), s32[]{:S(2)}) async-start(), calls=%async_computation.62 | async-start | bytes 1474560 | tf_op jit(solution)/shard_map/reduce_scatter | solution.py:211
  673.7 123.3 %all-gather.65.cloned.1.call-start = ((), (), s32[]{:S(2)}) async-start(), calls=%async_computation.55 | async-start | bytes 1474560 | tf_op jit(solution)/shard_map/all_gather | solution.py:141
  722.3 94.4 %all-gather.39.cloned.1.call-start = ((), (), s32[]{:S(2)}) async-start(), calls=%async_computation.34 | async-start | bytes 1474560 | tf_op jit(solution)/shard_map/all_gather | solution.py:141
  723.0 113.2 %all-gather.73.cloned.1.call-start = ((), (), s32[]{:S(2)}) async-start(), calls=%async_computation.63 | async-start | bytes 1474560 | tf_op jit(solution)/shard_map/all_gather | solution.py:141
  782.3 73.5 %all-gather.53.cloned.1.call-start = ((), (), s32[]{:S(2)}) async-start(), calls=%async_computation.45 | async-start | bytes 1474560 | tf_op jit(solution)/shard_map/all_gather | solution.py:141
  782.9 101.8 %reduce-scatter.50.cloned.1.call-start = ((), (), s32[]{:S(2)}) async-start(), calls=%async_computation.56 | async-start | bytes 1474560 | tf_op jit(solution)/shard_map/reduce_scatter | solution.py:224
  809.2 104.5 %reduce-scatter.34.cloned.1.call-start = ((), (), s32[]{:S(2)}) async-start(), calls=%async_computation.35 | async-start | bytes 1474560 | tf_op jit(solution)/shard_map/reduce_scatter | solution.py:224
  828.8 113.6 %reduce-scatter.58.cloned.1.call-start = ((), (), s32[]{:S(2)}) async-start(), calls=%async_computation.64 | async-start | bytes 1474560 | tf_op jit(solution)/shard_map/reduce_scatter | solution.py:224
  845.1 126.4 %reduce-scatter.42.cloned.1.call-start = ((), (), s32[]{:S(2)}) async-start(), calls=%async_computation.46 | async-start | bytes 1474560 | tf_op jit(solution)/shard_map/reduce_scatter | solution.py:224
  864.6 140.3 %all-reduce.13.cloned.1.call-start = ((), (), s32[]{:S(2)}) async-start(), calls=%async_computation.86 | async-start | bytes 147456 | tf_op jit(solution)/shard_map/psum | solution.py:452
  973.5 193.3 %all-gather.41.cloned.1.call-start = ((), (), s32[]{:S(2)}) async-start(), calls=%async_computation.36 | async-start | bytes 12386304 | tf_op jit(solution)/shard_map/all_gather | solution.py:412
  976.7 316.1 %all-gather.43.cloned.1.call-start = ((), (), s32[]{:S(2)}) async-start(), calls=%async_computation.37 | async-start | bytes 9437184 | tf_op jit(solution)/shard_map/all_gather | solution.py:414
  979.4 471.8 %all-gather.55.cloned.1.call-start = ((), (), s32[]{:S(2)}) async-start(), calls=%async_computation.47 | async-start | bytes 12386304 | tf_op jit(solution)/shard_map/all_gather | solution.py:413
  982.6 594.5 %all-gather.57.cloned.1.call-start = ((), (), s32[]{:S(2)}) async-start(), calls=%async_computation.48 | async-start | bytes 9437184 | tf_op jit(solution)/shard_map/all_gather | solution.py:415
  985.3 712.8 %all-gather.83.cloned.1.call-start = ((), (), s32[]{:S(2)}) async-start(), calls=%async_computation.72 | async-start | bytes 1474560 | tf_op jit(solution)/shard_map/all_gather | solution.py:145
  1684.1 62.8 %reduce-scatter.66.cloned.1.call-start = ((), (), s32[]{:S(2)}) async-start(), calls=%async_computation.73 | async-start | bytes 1474560 | tf_op jit(solution)/shard_map/reduce_scatter | solution.py:262
  1705.3 70.3 %reduce-scatter.60.cloned.1.call-start = ((), (), s32[]{:S(2)}) async-start(), calls=%async_computation.66 | async-start | bytes 1474560 | tf_op jit(solution)/shard_map/reduce_scatter | solution.py:262
  1725.0 73.8 %all-gather.85.cloned.1.call-start = ((), (), s32[]{:S(2)}) async-start(), calls=%async_computation.74 | async-start | bytes 1474560 | tf_op jit(solution)/shard_map/all_gather | solution.py:145
  1783.1 87.5 %reduce-scatter.68.cloned.1.call-start = ((), (), s32[]{:S(2)}) async-start(), calls=%async_computation.75 | async-start | bytes 1474560 | tf_op jit(solution)/shard_map/reduce_scatter | solution.py:295
  1907.4 65.7 %reduce-scatter.64.cloned.1.call-start = ((), (), s32[]{:S(2)}) async-start(), calls=%async_computation.70 | async-start | bytes 1474560 | tf_op jit(solution)/shard_map/reduce_scatter | solution.py:262
  1931.6 70.2 %reduce-scatter.70.cloned.1.call-start = ((), (), s32[]{:S(2)}) async-start(), calls=%async_computation.77 | async-start | bytes 1474560 | tf_op jit(solution)/shard_map/reduce_scatter | solution.py:262
  1951.2 79.4 %all-gather.89.cloned.1.call-start = ((), (), s32[]{:S(2)}) async-start(), calls=%async_computation.78 | async-start | bytes 1474560 | tf_op jit(solution)/shard_map/all_gather | solution.py:145
  2018.6 158.3 %reduce-scatter.72.cloned.1.call-start = ((), (), s32[]{:S(2)}) async-start(), calls=%async_computation.79 | async-start | bytes 4423680 | tf_op jit(solution)/shard_map/reduce_scatter | solution.py:538
  2092.4 116.9 %reduce-scatter.80.cloned.1.call-start = ((), (), s32[]{:S(2)}) async-start(), calls=%async_computation.83 | async-start | bytes 1474560 | tf_op jit(solution)/shard_map/reduce_scatter | solution.py:295
  2096.8 137.7 %reduce-scatter.78.cloned.1.call-start = ((), (), s32[]{:S(2)}) async-start(), calls=%async_computation.82 | async-start | bytes 1474560 | tf_op jit(solution)/shard_map/reduce_scatter | solution.py:295
  2098.9 422.1 %reduce-scatter.76.cloned.1.call-start = ((), (), s32[]{:S(2)}) async-start(), calls=%async_computation.81 | async-start | bytes 18874368 | tf_op jit(solution)/shard_map/reduce_scatter | solution.py:540
  2109.7 773.0 %reduce-scatter.74.cloned.1.call-start = ((), (), s32[]{:S(2)}) async-start(), calls=%async_computation.80 | async-start | bytes 24772608 | tf_op jit(solution)/shard_map/reduce_scatter | solution.py:539
  2155.9 798.3 %all-reduce.11.cloned.1.call-start = ((), (), s32[]{:S(2)}) async-start(), calls=%async_computation.85 | async-start | bytes 131072 | tf_op jit(solution)/shard_map/psum | solution.py:536
  2157.4 948.1 %all-reduce.9.cloned.1.call-start = ((), (), s32[]{:S(2)}) async-start(), calls=%async_computation.84 | async-start | bytes 9437184 | tf_op jit(solution)/shard_map/psum | solution.py:565
  (382 other events, 11574.6 us)
Sparse Core Ops, SparseCore 0:
  10.8 50.2 all-gather.46
  99.4 25.7 reduce-scatter.51
  128.0 47.5 all-gather.32
  216.0 17.4 all-gather.58
  267.8 25.7 reduce-scatter.35
  296.7 25.7 reduce-scatter.43
  325.6 25.7 reduce-scatter.27
  375.5 17.4 all-gather.68
  396.2 25.6 reduce-scatter.37
  425.1 25.6 reduce-scatter.53
  455.3 17.4 all-gather.50
  494.3 17.4 all-gather.70
  513.7 17.4 all-gather.60
  534.4 25.7 reduce-scatter.29
  563.3 25.7 reduce-scatter.45
  664.9 25.8 reduce-scatter.31
  694.0 25.7 reduce-scatter.47
  722.8 25.7 reduce-scatter.39
  751.8 25.7 reduce-scatter.55
  779.5 17.4 all-gather.64
  818.8 17.4 all-gather.72
  838.3 17.4 all-gather.52
  858.9 25.7 reduce-scatter.49
  888.0 25.7 reduce-scatter.33
  916.7 25.7 reduce-scatter.57
  945.8 25.7 reduce-scatter.41
  975.2 29.6 all-reduce.12
  1007.7 159.0 all-gather.40
  1169.6 123.0 all-gather.42
  1295.7 155.4 all-gather.54
  1454.0 123.1 all-gather.56
  1700.3 17.4 all-gather.74
  1721.1 25.7 reduce-scatter.65
  1749.9 25.7 reduce-scatter.59
  1844.9 25.6 reduce-scatter.67
  1873.6 25.7 reduce-scatter.61
  1906.9 17.4 all-gather.78
  1947.3 25.7 reduce-scatter.63
  1976.1 25.7 reduce-scatter.69
  2008.0 17.4 all-gather.88
  2027.6 17.5 all-gather.80
  2092.5 84.3 reduce-scatter.71
  2180.0 25.3 reduce-scatter.79
  2208.7 25.6 reduce-scatter.77
  2238.3 282.6 reduce-scatter.75
  2525.2 357.4 reduce-scatter.73
  2886.6 67.6 all-reduce.10
  2960.5 144.9 all-reduce.8
  (12 shorter events, 204.9 us)
where the time goes:
time: 4200 us; the launch traced here: 4190 us
  waiting for transfers between devices  2290 us (55%)
  other arithmetic  942 us (22%)
  matrix products  540 us (13%)
  local copies, waits for them, and re-layouts  269 us (6%)
  blocking collectives  79.6 us (2%)
  between operations  42.5 us (1%)
    another operation x88, other arithmetic, renew_basis(): lower = jnp.linalg.cholesky(gram)  518 us
    reduce_scatter x1, waiting for transfers between devices, shards(): lax.psum_scatter(head_acc, 'dp', scatter_dimension=0, tiled=True)  359 us
    reduce_scatter x1, waiting for transfers between devices, shards(): lax.psum_scatter(proto_acc, 'dp', scatter_dimension=0, tiled=True)  284 us
    another operation x17, other arithmetic, renew_basis(): return jax.scipy.linalg.solve_triangular(lower, turned.T, lower=True).T  253 us
    reduce_scatter x8, waiting for transfers between devices, block_forward(): lax.psum_scatter(lax.dot_general(portion, proj_t, CONTRACT_LAST, preferre...  201 us
    reduce_scatter x8, waiting for transfers between devices, block_forward(): lax.psum_scatter(lax.dot_general(portion, down_t, CONTRACT_LAST, preferre...  186 us
    all_gather x1, waiting for transfers between devices, shards(): lax.all_gather(head_w.astype(jnp.bfloat16), 'dp', axis=0, tiled=True)  160 us
    all_gather x1, waiting for transfers between devices, shards(): lax.all_gather(teacher_head.astype(jnp.bfloat16), 'dp', axis=0, tiled=True)  152 us
  transfers between devices with their start and end apart: 60, of which 56 were waited for; matrix products, arithmetic and copies ran while one was open for 10% of the time, Pallas kernels for 0%

commit v1 on v0

v1 whole, which is shorter than its diff:
```python
import functools

import jax
import jax.numpy as jnp
from jax import lax
from jax.experimental import pallas as pl
from jax.experimental.pallas import tpu as pltpu
from jax.sharding import PartitionSpec as P

D = 384
HD = 64
HID = 2048
LAYERS = 2
SLOT_DEV = 2
GLOBAL_TOK = 197
LOCAL_TOK = 37
MAX_LOCAL = 10
IMG_ROWS = 768
STEP = 10
MICRO = 2
CROPS = 12
GLOBAL_PAD = 200
LOCAL_PAD = 40
CHUNK = 400
CLS = 16

precise = lax.Precision.HIGHEST
TAU_S = 0.1
TAU_T = 0.07
CLIP_NORM = 0.005
BETA_ONE = 0.9
BETA_TWO = 0.999
ROT_ONE = 0.95
ROT_TWO = 0.95
SHAMPOO_BETA = 0.95
ADAM_EPS = 1e-08
WEIGHT_DECAY = 0.04
LR_BLOCK = 0.05
LR_HEAD = 0.03
LR_PROTO = 0.1
LR_NORM = 0.2
TEACHER_MOM = 0.7
CENTER_MOM = 0.9
NN = (((1,), (0,)), ((), ()))
NT = (((1,), (1,)), ((), ()))
TN = (((0,), (0,)), ((), ()))
bf16 = jnp.bfloat16
f32 = jnp.float32
VMEM_LIMIT = 58 * 1024 * 1024


def mm(lhs, rhs, dims=NN, precision=None):
    return lax.dot_general(lhs, rhs, dims, precision=precision, preferred_element_type=f32)


def normalize(inputs):
    centred = inputs - jnp.mean(inputs, axis=-1, keepdims=True)
    spread = jnp.mean(centred * centred, axis=-1, keepdims=True)
    inv = lax.rsqrt(spread + 1e-06)
    return centred * inv, inv


def norm_rows(inputs, gain, bias):
    return normalize(inputs)[0] * gain + bias


def norm_back(inputs, gain, grad_out):
    unit, inv = normalize(inputs)
    scaled = grad_out * gain
    grad = inv * (
        scaled
        - jnp.mean(scaled, axis=-1, keepdims=True)
        - unit * jnp.mean(scaled * unit, axis=-1, keepdims=True)
    )
    return (
        grad,
        jnp.sum(grad_out * unit, axis=0, keepdims=True),
        jnp.sum(grad_out, axis=0, keepdims=True),
    )


def gelu_cdf(inputs):
    return 0.5 + 0.5 * lax.erf(inputs * (0.5**0.5))


def gelu_exact(inputs):
    return inputs * gelu_cdf(inputs)


def gelu_slope(inputs):
    return gelu_cdf(inputs) + inputs * (jnp.exp(-0.5 * inputs * inputs) * 0.3989422804014327)


def low_half(shape):
    return lax.broadcasted_iota(jnp.int32, shape, 1) < HD


def halves(array):
    low = low_half(array.shape)
    zero = jnp.zeros_like(array)
    return jnp.where(low, array, zero), jnp.where(low, zero, array)


def block_fwd_kernel(
    x_ref, wt_ref, gains_ref, seg_col_ref, seg_row_ref, slot_ref,
    out_ref, h1_ref, qkv_ref, o_ref, x2_ref,
):
    x = x_ref[...]
    h1 = norm_rows(x, gains_ref[0:1], gains_ref[1:2]).astype(bf16)
    h1_ref[...] = h1
    allowed = seg_col_ref[0] == seg_row_ref[0]

    def heads(group, att):
        qkv = mm(h1, wt_ref[group, 0:384], NT).astype(bf16)
        qkv_ref[group] = qkv
        keys, values = qkv[:, 128:256], qkv[:, 256:384]
        mixes = []
        for query in halves(qkv[:, 0:128]):
            expd = jnp.where(allowed, jnp.exp(mm(query, keys, NT) * HD ** (-0.5)), 0.0)
            prob = expd / jnp.sum(expd, axis=-1, keepdims=True)
            mixes.append(mm(prob.astype(bf16), values))
        mix = jnp.where(low_half(mixes[0].shape), mixes[0], mixes[1])
        mix = (mix * slot_ref[group]).astype(bf16)
        o_ref[group] = mix
        return att + mm(mix, wt_ref[group, 384:512])

    att = lax.fori_loop(0, wt_ref.shape[0], heads, jnp.zeros(x.shape, f32))
    x2 = x + att
    x2_ref[...] = x2
    h2 = norm_rows(x2, gains_ref[2:3], gains_ref[3:4]).astype(bf16)

    def units(group, total):
        hidden = gelu_exact(mm(h2, wt_ref[group, 512:896], NT)).astype(bf16)
        return total + mm(hidden, wt_ref[group, 896:1280])

    out_ref[...] = x2 + lax.fori_loop(0, wt_ref.shape[0], units, jnp.zeros(x.shape, f32))


def block_bwd_kernel(
    x_ref, wt_ref, gains_ref, seg_col_ref, seg_row_ref, slot_ref,
    h1_ref, qkv_ref, o_ref, x2_ref, grad_ref,
    dwt_ref, dgains_ref,
):
    @pl.when(pl.program_id(0) == 0)
    def _():
        dwt_ref[...] = jnp.zeros_like(dwt_ref)
        dgains_ref[...] = jnp.zeros_like(dgains_ref)

    grad = grad_ref[...]
    grad_low = grad.astype(bf16)
    x2 = x2_ref[...]
    h2 = norm_rows(x2, gains_ref[2:3], gains_ref[3:4]).astype(bf16)

    def units(group, total):
        up = mm(h2, wt_ref[group, 512:896], NT)
        hidden = gelu_exact(up).astype(bf16)
        grad_up = (mm(grad_low, wt_ref[group, 896:1280], NT) * gelu_slope(up)).astype(bf16)
        dwt_ref[group, 512:896] += mm(grad_up, h2, TN)
        dwt_ref[group, 896:1280] += mm(hidden, grad_low, TN)
        return total + mm(grad_up, wt_ref[group, 512:896])

    groups = wt_ref.shape[0]
    grad_h2 = lax.fori_loop(0, groups, units, jnp.zeros(grad.shape, f32))
    grad_x2, gain_two, bias_two = norm_back(x2, gains_ref[2:3], grad_h2)
    grad_att = (grad + grad_x2).astype(bf16)
    allowed = seg_col_ref[0] == seg_row_ref[0]
    h1 = h1_ref[...]

    def heads(group, total):
        grad_mix = mm(grad_att, wt_ref[group, 384:512], NT).astype(bf16)
        grad_mix = grad_mix * slot_ref[group].astype(bf16)
        dwt_ref[group, 384:512] += mm(o_ref[group], grad_att, TN)
        qkv = qkv_ref[group]
        keys, values = qkv[:, 128:256], qkv[:, 256:384]
        grad_values = jnp.zeros(values.shape, f32)
        grad_keys = jnp.zeros(values.shape, f32)
        grad_queries = []
        for query, gmix in zip(halves(qkv[:, 0:128]), halves(grad_mix)):
            expd = jnp.where(allowed, jnp.exp(mm(query, keys, NT) * HD ** (-0.5)), 0.0)
            prob = expd / jnp.sum(expd, axis=-1, keepdims=True)
            grad_values = grad_values + mm(prob.astype(bf16), gmix, TN)
            grad_prob = mm(gmix, values, NT)
            scored = prob * (grad_prob - jnp.sum(prob * grad_prob, axis=-1, keepdims=True))
            scored = scored.astype(bf16)
            grad_queries.append(mm(scored, keys))
            grad_keys = grad_keys + mm(scored, query, TN)
        low = low_half(grad_queries[0].shape)
        grad_query = jnp.where(low, grad_queries[0], grad_queries[1]) * HD ** (-0.5)
        grad_qkv = jnp.concatenate(
            [grad_query.astype(bf16), (grad_keys * HD ** (-0.5)).astype(bf16), grad_values.astype(bf16)],
            axis=1,
        )
        dwt_ref[group, 0:384] += mm(grad_qkv, h1, TN)
        return total + mm(grad_qkv, wt_ref[group, 0:384])

    grad_h1 = lax.fori_loop(0, groups, heads, jnp.zeros(grad.shape, f32))
    _, gain_one, bias_one = norm_back(x_ref[...], gains_ref[0:1], grad_h1)
    dgains_ref[...] += jnp.concatenate([gain_one, bias_one, gain_two, bias_two], axis=0)


def whole_spec(shape):
    return pl.BlockSpec(shape, lambda *_: (0,) * len(shape))


def block_specs(groups, layer):
    row = pl.BlockSpec((CHUNK, D), lambda c: (c, 0))
    return dict(
        row=row,
        wt=pl.BlockSpec((groups, 1280, D), lambda c: (0, 0, layer)),
        gains=whole_spec((4, D)),
        seg_col=pl.BlockSpec((1, CHUNK, 1), lambda c: (c, 0, 0)),
        seg_row=pl.BlockSpec((1, 1, CHUNK), lambda c: (c, 0, 0)),
        slot=whole_spec((groups, 1, 128)),
        qkv=pl.BlockSpec((groups, CHUNK, 384), lambda c: (0, c, 0)),
        mix=pl.BlockSpec((groups, CHUNK, 128), lambda c: (0, c, 0)),
    )


def block_fwd(x, weights, layer, gains, seg_col, seg_row, slot):
    rows, groups = x.shape[0], weights.shape[0]
    s = block_specs(groups, layer)
    return pl.pallas_call(
        block_fwd_kernel,
        grid=(rows // CHUNK,),
        in_specs=[s["row"], s["wt"], s["gains"], s["seg_col"], s["seg_row"], s["slot"]],
        out_specs=[s["row"], s["row"], s["qkv"], s["mix"], s["row"]],
        out_shape=[
            jax.ShapeDtypeStruct((rows, D), f32),
            jax.ShapeDtypeStruct((rows, D), bf16),
            jax.ShapeDtypeStruct((groups, rows, 384), bf16),
            jax.ShapeDtypeStruct((groups, rows, 128), bf16),
            jax.ShapeDtypeStruct((rows, D), f32),
        ],
        compiler_params=pltpu.CompilerParams(vmem_limit_bytes=VMEM_LIMIT),
        cost_estimate=pl.CostEstimate(
            flops=rows * 9_000_000, bytes_accessed=8_000_000, transcendentals=rows * 4000
        ),
    )(x, weights, gains, seg_col, seg_row, slot)


def block_bwd(x, weights, layer, gains, seg_col, seg_row, slot, saved, grad):
    rows, groups = x.shape[0], weights.shape[0]
    s = block_specs(groups, layer)
    h1, qkv, mix, x2 = saved
    return pl.pallas_call(
        block_bwd_kernel,
        grid=(rows // CHUNK,),
        in_specs=[
            s["row"], s["wt"], s["gains"], s["seg_col"], s["seg_row"], s["slot"],
            s["row"], s["qkv"], s["mix"], s["row"], s["row"],
        ],
        out_specs=[whole_spec((groups, 1280, D)), whole_spec((4, D))],
        out_shape=[
            jax.ShapeDtypeStruct((groups, 1280, D), f32),
            jax.ShapeDtypeStruct((4, D), f32),
        ],
        compiler_params=pltpu.CompilerParams(vmem_limit_bytes=VMEM_LIMIT),
        cost_estimate=pl.CostEstimate(
            flops=rows * 22_000_000, bytes_accessed=16_000_000, transcendentals=rows * 6000
        ),
    )(x, weights, gains, seg_col, seg_row, slot, h1, qkv, mix, x2, grad)


def crop_starts(crops):
    return [
        crop * GLOBAL_PAD if crop < 2 else 2 * GLOBAL_PAD + (crop - 2) * LOCAL_PAD
        for crop in range(crops)
    ]


def take_cls(ref, crops):
    rows = [ref[start : start + 1, :] for start in crop_starts(crops)]
    return jnp.concatenate(rows + [jnp.zeros((CLS - crops, ref.shape[1]), f32)], axis=0)


def last_fwd_kernel(
    crops, x_ref, wt_ref, gains_ref, seg_cls_ref, seg_row_ref, slot_ref,
    out_ref, h1_ref, kv_ref, q_ref, o_ref, x2_ref,
):
    gain, bias = gains_ref[0:1], gains_ref[1:2]
    h1 = norm_rows(x_ref[...], gain, bias).astype(bf16)
    h1_ref[...] = h1
    x_cls = take_cls(x_ref, crops)
    h1_cls = norm_rows(x_cls, gain, bias).astype(bf16)
    allowed = seg_cls_ref[...] == seg_row_ref[...]

    def heads(group, att):
        kv = mm(h1, wt_ref[group, 128:384], NT).astype(bf16)
        kv_ref[group] = kv
        query = mm(h1_cls, wt_ref[group, 0:128], NT).astype(bf16)
        q_ref[group] = query
        both = jnp.concatenate(halves(query), axis=0)
        scores = mm(both, kv[:, 0:128], NT) * HD ** (-0.5)
        expd = jnp.where(allowed, jnp.exp(scores), 0.0)
        prob = expd / jnp.sum(expd, axis=-1, keepdims=True)
        mix = mm(prob.astype(bf16), kv[:, 128:256])
        mix = jnp.where(low_half((CLS, 128)), mix[0:CLS], mix[CLS:])
        mix = (mix * slot_ref[group]).astype(bf16)
        o_ref[group] = mix
        return att + mm(mix, wt_ref[group, 384:512])

    att = lax.fori_loop(0, wt_ref.shape[0], heads, jnp.zeros((CLS, D), f32))
    x2 = x_cls + att
    x2_ref[...] = x2
    h2 = norm_rows(x2, gains_ref[2:3], gains_ref[3:4]).astype(bf16)

    def units(group, total):
        hidden = gelu_exact(mm(h2, wt_ref[group, 512:896], NT)).astype(bf16)
        return total + mm(hidden, wt_ref[group, 896:1280])

    out_ref[...] = x2 + lax.fori_loop(0, wt_ref.shape[0], units, jnp.zeros((CLS, D), f32))


def last_bwd_kernel(
    crops, x_ref, wt_ref, gains_ref, seg_cls_ref, seg_row_ref, slot_ref,
    h1_ref, kv_ref, q_ref, o_ref, x2_ref, grad_ref,
    dwt_ref, dgains_ref, dx_ref,
):
    grad = grad_ref[...]
    grad_low = grad.astype(bf16)
    x2 = x2_ref[...]
    h2 = norm_rows(x2, gains_ref[2:3], gains_ref[3:4]).astype(bf16)
    groups = wt_ref.shape[0]

    def units(group, total):
        up = mm(h2, wt_ref[group, 512:896], NT)
        hidden = gelu_exact(up).astype(bf16)
        grad_up = (mm(grad_low, wt_ref[group, 896:1280], NT) * gelu_slope(up)).astype(bf16)
        dwt_ref[group, 512:896] = mm(grad_up, h2, TN)
        dwt_ref[group, 896:1280] = mm(hidden, grad_low, TN)
        return total + mm(grad_up, wt_ref[group, 512:896])

    grad_h2 = lax.fori_loop(0, groups, units, jnp.zeros((CLS, D), f32))
    grad_x2, gain_two, bias_two = norm_back(x2, gains_ref[2:3], grad_h2)
    grad_x2 = grad + grad_x2
    grad_att = grad_x2.astype(bf16)
    allowed = seg_cls_ref[...] == seg_row_ref[...]
    h1 = h1_ref[...]
    h1_cls = norm_rows(take_cls(x_ref, crops), gains_ref[0:1], gains_ref[1:2]).astype(bf16)

    def heads(group, carry):
        total, total_cls = carry
        grad_mix = mm(grad_att, wt_ref[group, 384:512], NT).astype(bf16)
        grad_mix = grad_mix * slot_ref[group].astype(bf16)
        dwt_ref[group, 384:512] = mm(o_ref[group], grad_att, TN)
        kv = kv_ref[group]
        keys, values = kv[:, 0:128], kv[:, 128:256]
        both = jnp.concatenate(halves(q_ref[group]), axis=0)
        gboth = jnp.concatenate(halves(grad_mix), axis=0)
        expd = jnp.where(allowed, jnp.exp(mm(both, keys, NT) * HD ** (-0.5)), 0.0)
        prob = expd / jnp.sum(expd, axis=-1, keepdims=True)
        grad_prob = mm(gboth, values, NT)
        scored = prob * (grad_prob - jnp.sum(prob * grad_prob, axis=-1, keepdims=True))
        scored = scored.astype(bf16)
        grad_values = mm(prob.astype(bf16), gboth, TN)
        grad_keys = mm(scored, both, TN) * HD ** (-0.5)
        grad_query = mm(scored, keys)
        low = low_half((CLS, 128))
        grad_query = jnp.where(low, grad_query[0:CLS], grad_query[CLS:]) * HD ** (-0.5)
        grad_query = grad_query.astype(bf16)
        grad_kv = jnp.concatenate([grad_keys.astype(bf16), grad_values.astype(bf16)], axis=1)
        dwt_ref[group, 0:128] = mm(grad_query, h1_cls, TN)
        dwt_ref[group, 128:384] = mm(grad_kv, h1, TN)
        return (
            total + mm(grad_kv, wt_ref[group, 128:384]),
            total_cls + mm(grad_query, wt_ref[group, 0:128]),
        )

    grad_h1, grad_cls = lax.fori_loop(
        0, groups, heads, (jnp.zeros(h1.shape, f32), jnp.zeros((CLS, D), f32))
    )
    dx_ref[...] = grad_h1
    starts = crop_starts(crops)
    for crop, start in enumerate(starts):
        dx_ref[start : start + 1, :] += grad_cls[crop : crop + 1, :]
    grad_x, gain_one, bias_one = norm_back(x_ref[...], gains_ref[0:1], dx_ref[...])
    dx_ref[...] = grad_x
    for crop, start in enumerate(starts):
        dx_ref[start : start + 1, :] += grad_x2[crop : crop + 1, :]
    dgains_ref[...] = jnp.concatenate([gain_one, bias_one, gain_two, bias_two], axis=0)


def last_in_specs(rows, groups, layer):
    return [
        whole_spec((rows, D)),
        pl.BlockSpec((groups, 1280, D), lambda i: (0, 0, layer)),
        whole_spec((4, D)),
        whole_spec((2 * CLS, 1)),
        whole_spec((1, rows)),
        whole_spec((groups, 1, 128)),
    ]


def last_saved(rows, groups):
    return [
        jax.ShapeDtypeStruct((rows, D), bf16),
        jax.ShapeDtypeStruct((groups, rows, 256), bf16),
        jax.ShapeDtypeStruct((groups, CLS, 128), bf16),
        jax.ShapeDtypeStruct((groups, CLS, 128), bf16),
        jax.ShapeDtypeStruct((CLS, D), f32),
    ]


def last_fwd(crops, x, weights, layer, gains, seg_cls, seg_row, slot):
    rows, groups = x.shape[0], weights.shape[0]
    out_shape = [jax.ShapeDtypeStruct((CLS, D), f32)] + last_saved(rows, groups)
    return pl.pallas_call(
        functools.partial(last_fwd_kernel, crops),
        grid=(1,),
        in_specs=last_in_specs(rows, groups, layer),
        out_specs=[whole_spec(a.shape) for a in out_shape],
        out_shape=out_shape,
        compiler_params=pltpu.CompilerParams(vmem_limit_bytes=VMEM_LIMIT),
        cost_estimate=pl.CostEstimate(
            flops=rows * 1_600_000, bytes_accessed=8_000_000, transcendentals=rows * 200
        ),
    )(x, weights, gains, seg_cls, seg_row, slot)


def last_bwd(crops, x, weights, layer, gains, seg_cls, seg_row, slot, saved, grad):
    rows, groups = x.shape[0], weights.shape[0]
    out_shape = [
        jax.ShapeDtypeStruct((groups, 1280, D), f32),
        jax.ShapeDtypeStruct((4, D), f32),
        jax.ShapeDtypeStruct((rows, D), f32),
    ]
    return pl.pallas_call(
        functools.partial(last_bwd_kernel, crops),
        grid=(1,),
        in_specs=last_in_specs(rows, groups, layer)
        + [whole_spec(a.shape) for a in last_saved(rows, groups)]
        + [whole_spec((CLS, D))],
        out_specs=[whole_spec(a.shape) for a in out_shape],
        out_shape=out_shape,
        compiler_params=pltpu.CompilerParams(vmem_limit_bytes=VMEM_LIMIT),
        cost_estimate=pl.CostEstimate(
            flops=rows * 4_000_000, bytes_accessed=16_000_000, transcendentals=rows * 400
        ),
    )(x, weights, gains, seg_cls, seg_row, slot, *saved, grad)


def basis_kernel(clip_ref, grads_ref, stats_ref, bases_ref, new_stats_ref, new_bases_ref, s_ref):
    layers, kinds = stats_ref.shape[0] // 4, 4
    mats = layers * kinds
    groups = grads_ref.shape[0]
    clip = clip_ref[0]
    bounds = (0, 384, 512, 896, 1280)
    for layer in range(layers):
        for kind in range(kinds):
            mat = layer * kinds + kind

            def outer(group, total, layer=layer, kind=kind):
                part = grads_ref[group, bounds[kind] : bounds[kind + 1], layer * D : layer * D + D]
                return total + mm(part, part, TN)

            stat = lax.fori_loop(0, groups, outer, jnp.zeros((D, D), f32))
            new_stats_ref[mat] = (
                SHAMPOO_BETA * stats_ref[mat] + (1 - SHAMPOO_BETA) * (clip * clip) * stat
            )

    def turn(mat, carry):
        new_bases_ref[mat] = mm(new_stats_ref[mat], bases_ref[mat], precision=precise)
        return carry

    lax.fori_loop(0, mats, turn, 0)
    lanes = lax.broadcasted_iota(jnp.int32, (mats, 128), 1)
    for block in range(D // 128):
        low, high = block * 128, block * 128 + 128
        for mat in range(mats):
            part = new_bases_ref[mat, :, low:high]
            s_ref[:, mat, :] = mm(part, part, TN, precise)
        pivots = jnp.zeros((mats, 128), f32)
        for first in range(0, 128, 32):

            def eliminate(step, pivots, first=first):
                row = s_ref[step]
                here = lanes == step
                pivot = jnp.sum(jnp.where(here, row, 0.0), axis=-1, keepdims=True)
                factors = jnp.where(lanes > step, row / pivot, 0.0)
                source = jnp.where(here, 1.0, row)
                for other in range(first, 128):
                    s_ref[other] = (
                        jnp.where(here, 0.0, s_ref[other]) - factors[:, other : other + 1] * source
                    )
                return jnp.where(here, pivot, pivots)

            pivots = lax.fori_loop(first, first + 32, eliminate, pivots)
        scale = lax.rsqrt(pivots)
        for other in range(128):
            row = jnp.where(lanes < other, s_ref[other], jnp.where(lanes == other, 1.0, 0.0))
            s_ref[other] = row * scale[:, other : other + 1]
        for mat in range(mats):
            part = mm(new_bases_ref[mat, :, low:high], s_ref[:, mat, :], NT, precise)
            new_bases_ref[mat, :, low:high] = part
            if high < D:
                rest = new_bases_ref[mat, :, high:]
                cross = mm(part, rest, TN, precise)
                new_bases_ref[mat, :, high:] = rest - mm(part, cross, NN, precise)


def renew_bases(clip_factor, grads, stats, bases):
    shape = stats.shape
    mats = shape[0] * shape[1]
    new_stats, new_bases = pl.pallas_call(
        basis_kernel,
        in_specs=[pl.BlockSpec(memory_space=pltpu.SMEM)]
        + [pl.BlockSpec(memory_space=pltpu.VMEM)] * 3,
        out_specs=[pl.BlockSpec(memory_space=pltpu.VMEM)] * 2,
        out_shape=[jax.ShapeDtypeStruct((mats, D, D), f32)] * 2,
        scratch_shapes=[pltpu.VMEM((128, mats, 128), f32)],
        compiler_params=pltpu.CompilerParams(vmem_limit_bytes=VMEM_LIMIT),
    )(clip_factor.reshape(1), grads, stats.reshape(mats, D, D), bases.reshape(mats, D, D))
    return new_stats.reshape(shape), new_bases.reshape(shape)


def flip_perm(count, bit):
    return [(i, i ^ bit) for i in range(count)]


def flips(axis):
    count = lax.axis_size(axis)
    bits, bit = [], 1
    while bit < count:
        bits.append(bit)
        bit *= 2
    return count, bits


def sum_over(array, axes):
    for axis in axes:
        count, bits = flips(axis)
        for bit in bits:
            array = array + lax.ppermute(array, axis, flip_perm(count, bit))
    return array


def shift_perm(count, step):
    return [(i, (i + step) % count) for i in range(count)]


def gather_over(array, axis):
    count = lax.axis_size(axis)
    if count > 8:
        return lax.all_gather(array, axis, axis=0)
    me = lax.axis_index(axis)
    out = jnp.zeros((count, *array.shape), array.dtype)
    out = lax.dynamic_update_index_in_dim(out, array, me, 0)
    for step in range(1, count):
        got = lax.ppermute(array, axis, shift_perm(count, step))
        out = lax.dynamic_update_index_in_dim(out, got, (me - step) % count, 0)
    return out


def swap_over(pick, axis):
    count = lax.axis_size(axis)
    me = lax.axis_index(axis)
    if count > 8:
        return lax.all_to_all(jnp.stack([pick(i) for i in range(count)]), axis, 0, 0)
    own = pick(me)
    out = jnp.zeros((count, *own.shape), own.dtype)
    out = lax.dynamic_update_index_in_dim(out, own, me, 0)
    for step in range(1, count):
        got = lax.ppermute(pick((me + step) % count), axis, shift_perm(count, step))
        out = lax.dynamic_update_index_in_dim(out, got, (me - step) % count, 0)
    return out


def adam_direction(first_mom, second_mom, beta_one, beta_two):
    return (
        first_mom / (1 - beta_one**STEP) / (jnp.sqrt(second_mom / (1 - beta_two**STEP)) + ADAM_EPS)
    )


def adamw(weight, grad_in, first_mom, second_mom, rate, decay):
    first_mom = BETA_ONE * first_mom + (1 - BETA_ONE) * grad_in
    second_mom = BETA_TWO * second_mom + (1 - BETA_TWO) * grad_in * grad_in
    weight = weight - rate * (
        adam_direction(first_mom, second_mom, BETA_ONE, BETA_TWO) + decay * weight
    )
    return (weight, first_mom, second_mom)


def row_layout(crop_count):
    rows = jnp.arange(2 * CHUNK)
    is_global = rows < 2 * GLOBAL_PAD
    local = rows - 2 * GLOBAL_PAD
    crop = jnp.where(is_global, rows // GLOBAL_PAD, 2 + local // LOCAL_PAD)
    offset = jnp.where(is_global, rows % GLOBAL_PAD, local % LOCAL_PAD)
    real = offset < jnp.where(is_global, GLOBAL_TOK, LOCAL_TOK)
    source = jnp.where(
        is_global, crop * GLOBAL_TOK + offset, 2 * GLOBAL_TOK + (crop - 2) * LOCAL_TOK + offset
    )
    source = jnp.where(real, source, -1)
    segment = jnp.where(real & (crop < 2 + crop_count), crop, 1000 + rows)
    return source, segment.astype(jnp.int32)


def shards(
    tokens, crop_counts, slot_live, block_w, block_m, block_v, rotation_bases, precond_stats,
    head_w, head_m, head_v, proto_w, proto_m, proto_v, norm_params, norm_m, norm_v,
    teacher_block, teacher_head, teacher_proto, teacher_norm, center,
):
    mp_index = lax.axis_index("mp")
    dp_index = lax.axis_index("dp")
    mp_count = lax.axis_size("mp")
    dp_count = lax.axis_size("dp")
    col_width = block_w.shape[3]
    micro, place = mp_index % MICRO, mp_index // MICRO
    crop_count = crop_counts[micro, place]
    own_t = jnp.concatenate(
        [
            part[layer, :, 0].astype(bf16).T
            for part in (teacher_block, block_w)
            for layer in range(LAYERS)
        ],
        axis=1,
    )
    weights = lax.all_gather(own_t, ("mp", "dp"), axis=0, tiled=True)
    weights = weights.reshape(mp_count, dp_count * col_width, 2 * LAYERS * D)
    head_cols = head_w.shape[1] // mp_count
    proto_cols = proto_w.shape[1] // dp_count

    def take_head(part):
        part = lax.dynamic_slice_in_dim(part, mp_index * head_cols, head_cols, 1).astype(bf16)
        return lax.all_gather(part, "dp", axis=0, tiled=True)

    def take_proto(part):
        def pick(i):
            return lax.dynamic_slice_in_dim(part, i * proto_cols, proto_cols, 1).astype(bf16)

        return swap_over(pick, "dp").reshape(-1, proto_cols)

    head_t, head_s = take_head(teacher_head), take_head(head_w)
    proto_t, proto_s = take_proto(teacher_proto), take_proto(proto_w)
    counts_own = jnp.stack([crop_counts[i % MICRO, i // MICRO] for i in range(mp_count)])
    counts = gather_over(counts_own[None], "dp").reshape(-1)
    other = lax.ppermute(
        lax.dynamic_index_in_dim(tokens, 1 - micro, 0, keepdims=False), "mp", flip_perm(mp_count, 1)
    )
    mine = lax.dynamic_index_in_dim(tokens, micro, 0, keepdims=False)
    first = micro == 0
    image = jnp.concatenate([jnp.where(first, mine, other), jnp.where(first, other, mine)], axis=0)
    source, segment = row_layout(crop_count)
    spread = (source[:, None] == jnp.arange(IMG_ROWS)[None, :]).astype(bf16)
    x0 = mm(spread, image)
    seg_col, seg_row = segment.reshape(2, CHUNK, 1), segment.reshape(2, 1, CHUNK)
    starts = crop_starts(CROPS)
    seg_cls = jnp.concatenate([segment[jnp.array(starts)], jnp.zeros((CLS - CROPS,), jnp.int32)])
    seg_cls = jnp.concatenate([seg_cls, seg_cls])[:, None]
    slot = jnp.repeat(slot_live.astype(f32).reshape(mp_count, SLOT_DEV), HD, axis=1)[:, None, :]
    x0_t = x0[:CHUNK]
    x1_t = block_fwd(x0_t, weights, 0, teacher_norm[0:4], seg_col, seg_row, slot)[0]
    y_t = last_fwd(
        2, x1_t, weights, 1, teacher_norm[4:8], seg_cls, segment[None, :CHUNK], slot
    )[0]
    x1, *saved0 = block_fwd(x0, weights, 2, norm_params[0:4], seg_col, seg_row, slot)
    y_s, *saved1 = last_fwd(
        CROPS, x1, weights, 3, norm_params[4:8], seg_cls, segment[None], slot
    )
    y_all = lax.all_gather(jnp.concatenate([y_s[:CROPS], y_t[:4]], axis=0), "mp", axis=0)
    cls_s = y_all[:, :CROPS].reshape(mp_count * CROPS, D)
    cls_t = y_all[:, CROPS : CROPS + 2].reshape(mp_count * 2, D)
    n_s, n_t = cls_s.shape[0], cls_t.shape[0]
    h1_s, h2_s, h3_s = head_s[:D], head_s[D : D + HID], head_s[D + HID :]
    h1_t, h2_t, h3_t = head_t[:D], head_t[D : D + HID], head_t[D + HID :]
    gain_s, bias_s = norm_params[8:9], norm_params[9:10]
    feats_s = norm_rows(cls_s, gain_s, bias_s).astype(bf16)
    feats_t = norm_rows(cls_t, teacher_norm[8:9], teacher_norm[9:10]).astype(bf16)
    a1_s, a1_t = mm(feats_s, h1_s), mm(feats_t, h1_t)
    b1_own = jnp.concatenate([gelu_exact(a1_s), gelu_exact(a1_t)], axis=0).astype(bf16)
    b1 = lax.all_gather(b1_own, "mp", axis=1, tiled=True)
    a2_s, a2_t = mm(b1[:n_s], h2_s), mm(b1[n_s:], h2_t)
    b2_s = gelu_exact(a2_s).astype(bf16)
    b2_t = gelu_exact(a2_t).astype(bf16)
    third = sum_over(jnp.concatenate([mm(b2_s, h3_s, NT), mm(b2_t, h3_t, NT)], axis=0), ("mp",))
    inv = lax.rsqrt(jnp.sum(third * third, axis=-1, keepdims=True) + 1e-06)
    unit = (third * inv).astype(bf16)
    unit_all = gather_over(unit, "dp")
    z_s = unit_all[:, :n_s].reshape(dp_count * n_s, -1)
    z_t = unit_all[:, n_s:].reshape(dp_count * n_t, -1)
    images = dp_count * mp_count
    scaled_s = mm(z_s, proto_s) / TAU_S
    glob = mm(z_t, proto_t)
    center_own = lax.dynamic_slice_in_dim(center, dp_index * proto_cols, proto_cols)
    scaled_t = (glob - center_own) / TAU_T
    center_part = jnp.sum(glob, axis=0)
    max_s = jnp.max(scaled_s, axis=-1, keepdims=True)
    max_t = jnp.max(scaled_t, axis=-1, keepdims=True)
    exp_s, exp_t = jnp.exp(scaled_s - max_s), jnp.exp(scaled_t - max_t)
    cross = mm(exp_t, scaled_s, NT, precise)
    same = jnp.arange(images * 2)[:, None] // 2 == jnp.arange(images * CROPS)[None, :] // CROPS
    cross = jnp.sum(
        jnp.where(same, cross, 0.0).reshape(images * 2, images, CROPS), axis=1
    )
    stats = jnp.concatenate(
        [
            max_s.reshape(-1),
            jnp.sum(exp_s, axis=-1),
            max_t.reshape(-1),
            jnp.sum(exp_t, axis=-1),
            cross.reshape(-1),
        ]
    )
    stats = gather_over(lax.all_gather(stats[None], "mp", axis=0, tiled=True), "dp")
    stats = stats.reshape(images, -1)
    r_s, r_t = images * CROPS, images * 2
    maxes_s, sums_s = stats[:, :r_s], stats[:, r_s : 2 * r_s]
    maxes_t, sums_t = stats[:, 2 * r_s : 2 * r_s + r_t], stats[:, 2 * r_s + r_t : 2 * (r_s + r_t)]
    crosses = stats[:, 2 * (r_s + r_t) :].reshape(images, r_t, CROPS)
    top_s, top_t = jnp.max(maxes_s, axis=0), jnp.max(maxes_t, axis=0)
    total_s = jnp.sum(sums_s * jnp.exp(maxes_s - top_s), axis=0)
    shrink_t = jnp.exp(maxes_t - top_t)
    total_t = jnp.sum(sums_t * shrink_t, axis=0)
    cross_total = jnp.sum(crosses * shrink_t[:, :, None], axis=0) / total_t[:, None]
    log_norm = (jnp.log(total_s) + top_s).reshape(images, 1, CROPS)
    crop_ids = jnp.arange(CROPS)
    pairs = (
        (crop_ids[None, None, :] != jnp.arange(2)[None, :, None])
        & (crop_ids[None, None, :] < 2 + counts[:, None, None])
    ).astype(f32)
    image_weight = 1.0 / (2.0 * counts.astype(f32) + 2.0)
    pair_weight = pairs * image_weight[:, None, None]
    entropy = log_norm - cross_total.reshape(images, 2, CROPS)
    loss_total = jnp.sum(entropy * pair_weight)
    coef_s = jnp.sum(pair_weight, axis=1).reshape(-1, 1) / total_s[:, None]
    coef_s = coef_s * jnp.exp(max_s - top_s[:, None])
    coef_t = jnp.exp(max_t[:, 0] - top_t) / total_t
    coef_t = pair_weight.reshape(r_t, CROPS) * coef_t[:, None]
    mix = jnp.where(same, jnp.tile(coef_t, (1, images)), 0.0)
    grad_scaled = (coef_s * exp_s - mm(mix, exp_t, TN, precise)) / TAU_S
    grad_logits = grad_scaled.astype(bf16)
    grad_unit_part = mm(grad_logits, proto_s, NT)
    grad_proto = mm(z_s, grad_logits, TN)

    def pick_unit(i):
        return lax.dynamic_slice_in_dim(grad_unit_part, i * n_s, n_s, 0)

    grad_unit = sum_over(jnp.sum(swap_over(pick_unit, "dp"), axis=0), ("mp",))
    third_s, inv_s = third[:n_s], inv[:n_s]
    along = jnp.sum(grad_unit * third_s, axis=-1, keepdims=True)
    grad_third = (inv_s * grad_unit - third_s * (inv_s * inv_s * inv_s * along)).astype(bf16)
    grad_a2 = (mm(grad_third, h3_s) * gelu_slope(a2_s)).astype(bf16)
    grad_b1 = lax.psum_scatter(mm(grad_a2, h2_s, NT), "mp", scatter_dimension=1, tiled=True)
    grad_a1 = (grad_b1 * gelu_slope(a1_s)).astype(bf16)
    grad_feats = sum_over(mm(grad_a1, h1_s, NT), ("mp",))
    grad_cls, head_gain, head_bias = norm_back(cls_s, gain_s, grad_feats)
    grad_y = lax.dynamic_slice_in_dim(grad_cls, mp_index * CROPS, CROPS, 0)
    grad_y = jnp.concatenate([grad_y, jnp.zeros((CLS - CROPS, D), f32)], axis=0)
    dwt1, dgains1, grad_x1 = last_bwd(
        CROPS, x1, weights, 3, norm_params[4:8], seg_cls, segment[None], slot, saved1, grad_y
    )
    dwt0, dgains0 = block_bwd(
        x0, weights, 2, norm_params[0:4], seg_col, seg_row, slot, saved0, grad_x1
    )
    block_g = jnp.concatenate(
        [
            lax.psum_scatter(
                dwt.reshape(-1, D), ("mp", "dp"), scatter_dimension=0, tiled=True
            )
            for dwt in (dwt0, dwt1)
        ],
        axis=1,
    )
    rows_left = jnp.concatenate([feats_s, b1[:n_s], grad_third], axis=1)
    head_rows = head_w.shape[0]

    def pick_left(i):
        return lax.dynamic_slice_in_dim(rows_left, i * head_rows, head_rows, 1)

    left = swap_over(pick_left, "dp").reshape(dp_count * n_s, head_rows)
    right = gather_over(jnp.concatenate([grad_a1, grad_a2, b2_s], axis=1), "dp")
    right = right.reshape(dp_count * n_s, 3 * head_cols)
    stack_ids = dp_index * head_rows + jnp.arange(head_rows)[None, :]
    edges = (0, D, D + HID, D + HID + third.shape[1])
    head_g = sum(
        mm(
            jnp.where((stack_ids >= edges[i]) & (stack_ids < edges[i + 1]), left, 0).astype(bf16),
            right[:, i * head_cols : (i + 1) * head_cols],
            TN,
        )
        for i in range(3)
    )
    head_square = jnp.sum(head_g * head_g)
    head_g = lax.all_gather(head_g, "mp", axis=1, tiled=True)
    proto_square = jnp.sum(grad_proto * grad_proto)
    proto_rows = proto_w.shape[0]

    def pick_proto(i):
        return lax.dynamic_slice_in_dim(grad_proto, i * proto_rows, proto_rows, 0)

    proto_g = swap_over(pick_proto, "dp")
    proto_g = proto_g.transpose(1, 0, 2).reshape(proto_rows, -1)
    center_total = gather_over(center_part, "dp").reshape(-1)
    head_first = (mp_index == 0).astype(f32)
    square = jnp.sum(block_g * block_g) + head_square + proto_square
    norm_part = jnp.concatenate(
        [
            dgains0,
            dgains1,
            head_first * head_gain,
            head_first * head_bias,
            jnp.full((1, D), square),
        ],
        axis=0,
    )
    norm_sum = sum_over(norm_part, ("mp", "dp"))
    norm_total = norm_sum[:10]
    grad_norm = jnp.sqrt(norm_sum[10, 0] + jnp.sum(norm_total * norm_total))
    clip_factor = jnp.minimum(1.0, CLIP_NORM / (grad_norm + 1e-06))
    grads_all = lax.all_gather(block_g.astype(bf16), ("mp", "dp"), axis=0, tiled=True)
    grads_all = grads_all.reshape(mp_count, dp_count * col_width, LAYERS * D)
    new_stats, new_bases = renew_bases(clip_factor, grads_all, precond_stats, rotation_bases)
    col_ids = dp_index * col_width + jnp.arange(col_width)
    bounds = (0, 384, 512, 896, 1280)
    col_masks = jnp.stack(
        [((col_ids >= bounds[k]) & (col_ids < bounds[k + 1])).astype(f32) for k in range(4)]
    )
    grad_cols = (clip_factor * block_g).reshape(col_width, LAYERS, D)
    rotated = jnp.einsum("lkde,cld,kc->lec", new_bases, grad_cols, col_masks, precision=precise)
    first_mom = ROT_ONE * block_m[:, :, 0] + (1 - ROT_ONE) * rotated
    second_mom = ROT_TWO * block_v[:, :, 0] + (1 - ROT_TWO) * rotated * rotated
    direction = adam_direction(first_mom, second_mom, ROT_ONE, ROT_TWO)
    turned_back = jnp.einsum("lkde,lec,kc->ldc", new_bases, direction, col_masks, precision=precise)
    master = block_w[:, :, 0]
    new_block_w = (master - LR_BLOCK * (turned_back + WEIGHT_DECAY * master))[:, :, None]
    new_head_w, new_head_m, new_head_v = adamw(
        head_w, clip_factor * head_g, head_m, head_v, LR_HEAD, WEIGHT_DECAY
    )
    new_proto_w, new_proto_m, new_proto_v = adamw(
        proto_w, clip_factor * proto_g, proto_m, proto_v, LR_PROTO, WEIGHT_DECAY
    )
    new_norm, new_norm_m, new_norm_v = adamw(
        norm_params, clip_factor * norm_total, norm_m, norm_v, LR_NORM, 0.0
    )
    new_teacher_block = TEACHER_MOM * teacher_block + (1 - TEACHER_MOM) * new_block_w
    new_teacher_head = TEACHER_MOM * teacher_head + (1 - TEACHER_MOM) * new_head_w
    new_teacher_proto = TEACHER_MOM * teacher_proto + (1 - TEACHER_MOM) * new_proto_w
    new_teacher_norm = TEACHER_MOM * teacher_norm + (1 - TEACHER_MOM) * new_norm
    new_center = CENTER_MOM * center + (1 - CENTER_MOM) * center_total / (2.0 * images)
    return (
        loss_total, grad_norm, new_block_w, first_mom[:, :, None], second_mom[:, :, None],
        new_bases, new_stats, new_head_w, new_head_m, new_head_v,
        new_proto_w, new_proto_m, new_proto_v, new_norm, new_norm_m, new_norm_v,
        new_teacher_block, new_teacher_head, new_teacher_proto, new_teacher_norm, new_center,
    )


def solution(mesh):
    block, head, proto, rep = P(None, None, "mp", "dp"), P("dp", None), P("dp", "mp"), P()
    in_specs = (
        P(None, ("dp", "mp"), None), P(None, "dp"), rep, block, block, block, rep, rep,
        head, head, head, proto, proto, proto, rep, rep, rep, block, head, proto, rep, P("mp"),
    )
    out_specs = (
        rep, rep, block, block, block, rep, rep, head, head, head, proto, proto, proto,
        rep, rep, rep, block, head, proto, rep, P("mp"),
    )
    return jax.shard_map(shards, mesh=mesh, in_specs=in_specs, out_specs=out_specs, check_vma=False)
```

time: 4200 us -> 1050 us (0.25)
  waiting for transfers between devices: 2290 us -> 413 us
  other arithmetic: 942 us -> 44.4 us
  matrix products: 540 us -> 39.2 us
  Pallas kernels: 0 us -> 290 us
  local copies, waits for them, and re-layouts: 269 us -> 68.8 us
  starting transfers between devices: 5.61 us -> 151 us
  blocking collectives: 79.6 us -> 16.2 us
    reduce_scatter x27 -> x3, waiting for transfers between devices: 1200 us -> 234 us  [the longest x2 212 us: shards(): lax.psum_scatter(dwt.reshape(-1, D), ('mp', 'dp'), scatter_dimension=0, t...]
    all_gather x30 -> x5, waiting for transfers between devices: 888 us -> 103 us  [the longest x2 48.4 us: take_head(): return lax.all_gather(part, 'dp', axis=0, tiled=True)]
    another operation x121 -> x3, other arithmetic: 781 us -> 2.14 us  [the longest x88 518 us: renew_basis(): lower = jnp.linalg.cholesky(gram)]
    dot_general x190 -> x19, matrix products: 451 us -> 34.3 us  [the longest x18 26.7 us: mm(): lax.dot_general(lhs, rhs, dims, precision=precision, preferred_element_ty...]
    pallas_call x0 -> x7, Pallas kernels: none -> 290 us  [the longest x1 176 us: renew_bases(): pl.pallas_call(basis_kernel, in_specs=[pl.BlockSpec(memory_space=pltpu.SM...]
    psum x3 -> x0, waiting for transfers between devices: 192 us -> none  [the longest x1 106 us: shards(): lax.psum((stat_part, norm_part, square_part, loss_carry, center_carry), (...]
    ppermute x0 -> x82, starting transfers between devices: none -> 150 us  [the longest x35 65.7 us: swap_over(): got = lax.ppermute(pick((me + step) % count), axis, shift_perm(count, step))]
    another operation x130 -> x7, local copies, waits for them, and re-layouts: 106 us -> 3.35 us  [the longest x3 2.45 us: shards(): mix = jnp.where(same, jnp.tile(coef_t, (1, images)), 0.0)]
  transfers between devices with their start and end apart: 60 -> 90, of which waited for: 56 -> 33; matrix products, arithmetic and copies ran while one was open for 10% -> 9% of each run, Pallas kernels for 0% -> 5%
where the time goes in v1:
time: 1050 us; the launch traced here: 1040 us
  waiting for transfers between devices  413 us (39%)
  Pallas kernels  290 us (28%)
  starting transfers between devices  151 us (14%)
  local copies, waits for them, and re-layouts  68.8 us (7%)
  other arithmetic  44.4 us (4%)
  matrix products  39.2 us (4%)
  between operations  21.7 us (2%)
  blocking collectives  16.2 us (2%)
    reduce_scatter x2, waiting for transfers between devices, shards(): lax.psum_scatter(dwt.reshape(-1, D), ('mp', 'dp'), scatter_dimension=0, t...  212 us
    pallas_call x1, Pallas kernels, renew_bases(): pl.pallas_call(basis_kernel, in_specs=[pl.BlockSpec(memory_space=pltpu.SM...  176 us
    ppermute x35, starting transfers between devices, swap_over(): got = lax.ppermute(pick((me + step) % count), axis, shift_perm(count, step))  65.7 us
    ppermute x35, starting transfers between devices, gather_over(): got = lax.ppermute(array, axis, shift_perm(count, step))  60.3 us
    ppermute x35, waiting for transfers between devices, swap_over(): got = lax.ppermute(pick((me + step) % count), axis, shift_perm(count, step))  48.9 us
    all_gather x2, waiting for transfers between devices, take_head(): return lax.all_gather(part, 'dp', axis=0, tiled=True)  48.4 us
    pallas_call x1, Pallas kernels, block_bwd(): pl.pallas_call(block_bwd_kernel, grid=(rows // CHUNK,), in_specs=[s['row'...  43 us
    all_gather x1, waiting for transfers between devices, shards(): weights = lax.all_gather(own_t, ('mp', 'dp'), axis=0, tiled=True)  42.6 us
  transfers between devices with their start and end apart: 90, of which 33 were waited for; matrix products, arithmetic and copies ran while one was open for 9% of the time, Pallas kernels for 5%

profile of v1, /device:TPU:0, one launch (start us, length us, event | category | flops | bytes accessed | tf_op | source)
XLA Modules:
  0.0 1044.2 jit_solution(4083215817148068570)
XLA Ops:
  13.1 2.7 fusion.213
  15.8 3.0 collective-permute-start.31
  24.1 2.6 collective-permute-start.35
  28.7 2.7 fusion.214
  50.9 3.6 collective-permute-start.13
  56.2 4.2 collective-permute-done.10
  64.3 12.9 %collective-permute-done.12 = bf16[32,2048]{1,0:T(8,128)(2,1)} collective-permute-done((bf16[32,2048]{1,0:T(8,128)(2,1)}, bf16[32,2048]{1,0:T(8,128)(2,1)}, u32[]{:S(2)}, u32[]{:S(2)}) %collective-permute-start.12) | collective-permute-done | bytes 131104 | tf_op jit(solution)/shard_map/ppermute | solution.py:563
  78.6 6.3 collective-permute-start.17
  85.8 5.0 collective-permute-start.18
  94.4 2.7 collective-permute-done.17
  100.9 5.0 collective-permute-start.22
  106.0 9.5 collective-permute-done.19
  119.0 42.6 %all-gather.9.cloned.1.call-done = bf16[5120,1536]{1,0:T(8,128)(2,1)} async-done(((bf16[160,1536]{1,0:T(8,128)(2,1)}), bf16[5120,1536]{1,0:T(8,128)(2,1)}) %all-gather.9.cloned.1.call-update) | async-done | bytes 15728656 | tf_op jit(solution)/shard_map/all_gather | solution.py:618
  161.6 12.9 %shard_map.384 = (f32[400,384]{1,0:T(8,128)}, bf16[400,384]{1,0:T(8,128)(2,1)}, bf16[4,400,384]{2,1,0:T(8,128)(2,1)}, bf16[4,400,128]{2,1,0:T(8,128)(2,1)}, f32[400,384]{1,0:T(8,128)}) custom-call(f32[400,384]{1,0:T(8,128)} %slice.193.x_ref, bf16[4,1280,1536]{2,1,0:T(8,128)(2,1)} %bitcast.359, f32[4,384]{1,0:T(4,128)} %get-tuple-element.255.gains_ref, ...), custom_call_target="tpu_custom_call" | custom-call | flops 3600000000 | bytes 8000000 | tf_op jit(solution)/shard_map/pallas_call | solution.py:222
  174.5 8.4 shard_map.385
  183.6 23.5 %shard_map.382 = (f32[800,384]{1,0:T(8,128)}, bf16[800,384]{1,0:T(8,128)(2,1)}, bf16[4,800,384]{2,1,0:T(8,128)(2,1)}, bf16[4,800,128]{2,1,0:T(8,128)(2,1)}, f32[800,384]{1,0:T(8,128)}) custom-call(f32[800,384]{1,0:T(8,128)} %copy-done.32, bf16[4,1280,1536]{2,1,0:T(8,128)(2,1)} %bitcast.361, f32[4,384]{1,0:T(4,128)} %get-tuple-element.253.gains_ref, ...), custom_call_target="tpu_custom_call" | custom-call | flops 7200000000 | bytes 8000000 | tf_op jit(solution)/shard_map/pallas_call | solution.py:222
  207.1 10.0 shard_map.383
  217.9 5.3 all-gather
  226.8 48.4 %all-gather.13.cloned.1.call-done = bf16[2688,512]{1,0:T(8,128)(2,1)} async-done(((bf16[336,512]{1,0:T(8,128)(2,1)}), bf16[2688,512]{1,0:T(8,128)(2,1)}) %all-gather.13.cloned.1.call-update) | async-done | bytes 2752528 | tf_op jit(solution)/shard_map/all_gather | solution.py:625
  276.4 5.7 all_gather.32
  284.2 2.8 multiply_convert_fusion.1
  299.0 2.8 collective-permute-start.6
  311.7 3.7 convolution_select_fusion
  318.4 5.2 all-gather.2
  329.7 3.8 collective-permute-start.28
  363.0 4.5 multiply_convert_fusion
  371.7 3.1 collective-permute-start.41
  384.4 2.6 collective-permute-done.46
  390.3 22.1 %reduce-scatter.4.cloned.1.call-done = f32[48,512]{1,0:T(8,128)} async-done(((f32[48,2048]{1,0:T(8,128)}), f32[48,512]{1,0:T(8,128)}) %reduce-scatter.4.cloned.1.call-update) | async-done | bytes 98320 | tf_op jit(solution)/shard_map/reduce_scatter | solution.py:743
  415.4 4.0 collective-permute-done.48
  420.3 16.0 %shard_map.386 = (f32[4,1280,384]{2,1,0:T(8,128)}, f32[4,384]{1,0:T(4,128)}, f32[800,384]{1,0:T(8,128)}) custom-call(f32[800,384]{1,0:T(8,128)} %get-tuple-element.41.x_ref, bf16[4,1280,1536]{2,1,0:T(8,128)(2,1)} %bitcast.363, f32[4,384]{1,0:T(4,128)} %get-tuple-element.252.gains_ref, s32[32,1]{1,0:T(8,128)} %copy.147.seg_cls_ref, ...), custom_call_target="tpu_custom_call" | custom-call | flops 3200000000 | bytes 16000000 | tf_op jit(solution)/shard_map/pallas_call | solution.py:427
  436.3 43.0 %shard_map.387 = (f32[4,1280,384]{2,1,0:T(8,128)}, f32[4,384]{1,0:T(4,128)}) custom-call(f32[800,384]{1,0:T(8,128)} %copy-done.32, bf16[4,1280,1536]{2,1,0:T(8,128)(2,1)} %bitcast.364, f32[4,384]{1,0:T(4,128)} %get-tuple-element.253.gains_ref, s32[2,400,1]{2,1,0:T(8,128)} %add_select_fusion.4.seg_col_ref, s32[2,1,400]{2,1,0:T(1,128)} %and_select_fusion.seg_row_ref, ...), custom_call_target="tpu_custom_call" | custom-call | flops 17600000000 | bytes 16000000 | tf_op jit(solution)/shard_map/pallas_call | solution.py:245
  501.6 3.6 collective-permute-start.60
  508.1 5.4 collective-permute-done.58
  516.7 85.2 %reduce-scatter.6.cloned.1.call-done = f32[160,384]{1,0:T(8,128)} async-done(((f32[5120,384]{1,0:T(8,128)}), f32[160,384]{1,0:T(8,128)}) %reduce-scatter.6.cloned.1.call-update) | async-done | bytes 245776 | tf_op jit(solution)/shard_map/reduce_scatter | solution.py:757
  602.9 127.2 %reduce-scatter.8.cloned.1.call-done = f32[160,384]{1,0:T(8,128)} async-done(((f32[5120,384]{1,0:T(8,128)}), f32[160,384]{1,0:T(8,128)}) %reduce-scatter.8.cloned.1.call-update) | async-done | bytes 245776 | tf_op jit(solution)/shard_map/reduce_scatter | solution.py:757
  754.7 3.3 collective-permute-start.72
  766.6 13.1 %collective-permute-done.70 = f32[32,2048]{1,0:T(8,128)S(1)} collective-permute-done((f32[32,2048]{1,0:T(8,128)S(1)}, f32[32,2048]{1,0:T(8,128)S(1)}, u32[]{:S(2)}, u32[]{:S(2)}) %collective-permute-start.70) | collective-permute-done | bytes 262176 | tf_op jit(solution)/shard_map/ppermute | solution.py:563
  784.3 3.1 collective-permute-done.65
  787.4 14.1 %collective-permute-start.66 = (f32[11,384]{1,0:T(8,128)S(1)}, f32[11,384]{1,0:T(8,128)S(1)}, u32[]{:S(2)}, u32[]{:S(2)}) collective-permute-start(f32[11,384]{1,0:T(8,128)S(1)} %add.1148), channel_id=1, source_target_pairs={{0,8},{4,12},{8,0},{12,4},{16,24},{20,28},{24,16},{28,20},{1,9},{5... | collective-permute-start | bytes 50696 | tf_op jit(solution)/shard_map/ppermute | solution.py:533
  803.3 4.6 collective-permute-start.67
  808.6 2.8 copy.167
  818.0 9.6 multiply_add_fusion
  829.7 4.6 multiply_add_fusion.2
  834.3 12.1 %all-gather.15.cloned.1.call-done = bf16[5120,768]{1,0:T(8,128)(2,1)} async-done(((bf16[160,768]{1,0:T(8,128)(2,1)}), bf16[5120,768]{1,0:T(8,128)(2,1)}) %all-gather.15.cloned.1.call-update) | async-done | bytes 7864336 | tf_op jit(solution)/shard_map/all_gather | solution.py:810
  846.4 176.2 %shard_map.388 = (f32[8,384,384]{2,1,0:T(8,128)}, f32[8,384,384]{2,1,0:T(8,128)}) custom-call(f32[1]{0:T(128)} %bitcast.105.clip_ref, bf16[4,1280,768]{2,1,0:T(8,128)(2,1)} %bitcast.372, f32[8,384,384]{2,1,0:T(8,128)} %bitcast.375, f32[8,384,384]{2,1,0:T(8,128)} %bitcast.376), custom_call_target="tpu_custom_call" | custom-call | tf_op jit(solution)/shard_map/pallas_call | solution.py:504
  1022.6 7.6 fusion.86
  1030.2 4.9 fusion.29
  (544 shorter events, 214.6 us)
Async XLA Ops:
  7.2 154.4 %all-gather.9.cloned.1.call-start = ((), (), s32[]{:S(2)}) async-start(), calls=%async_computation.3 | async-start | bytes 16220160 | tf_op jit(solution)/shard_map/all_gather | solution.py:618
  10.3 214.6 %all-gather.11.cloned.1.call-start = ((), (), s32[]{:S(2)}) async-start(), calls=%async_computation.4 | async-start | bytes 3096576 | tf_op jit(solution)/shard_map/all_gather | solution.py:625
  12.4 262.7 %all-gather.13.cloned.1.call-start = ((), (), s32[]{:S(2)}) async-start(), calls=%async_computation.5 | async-start | bytes 3096576 | tf_op jit(solution)/shard_map/all_gather | solution.py:625
  15.8 29.4 %collective-permute-start.31 = (s32[1,4]{1,0:T(1,128)S(1)}, s32[1,4]{1,0:T(1,128)S(1)}, u32[]{:S(2)}, u32[]{:S(2)}) collective-permute-start(s32[1,4]{1,0:T(1,128)S(1)} %fusion.213), channel_id=1, source_target_pairs={{0,4},{4,8},{8,12},{12,16},{16,20},{20,24},{24,28},{28,0},{1,5},{5... | collective-permute-start | bytes 56 | tf_op jit(solution)/shard_map/ppermute | solution.py:549
  18.7 27.8 %collective-permute-start.32 = (s32[1,4]{1,0:T(1,128)S(1)}, s32[1,4]{1,0:T(1,128)S(1)}, u32[]{:S(2)}, u32[]{:S(2)}) collective-permute-start(s32[1,4]{1,0:T(1,128)S(1)} %fusion.213), channel_id=1, source_target_pairs={{0,8},{4,12},{8,16},{12,20},{16,24},{20,28},{24,0},{28,4},{1,9},{5... | collective-permute-start | bytes 56 | tf_op jit(solution)/shard_map/ppermute | solution.py:549
  20.3 27.7 %collective-permute-start.33 = (s32[1,4]{1,0:T(1,128)S(1)}, s32[1,4]{1,0:T(1,128)S(1)}, u32[]{:S(2)}, u32[]{:S(2)}) collective-permute-start(s32[1,4]{1,0:T(1,128)S(1)} %fusion.213), channel_id=1, source_target_pairs={{0,12},{4,16},{8,20},{12,24},{16,28},{20,0},{24,4},{28,8},{1,13},{... | collective-permute-start | bytes 56 | tf_op jit(solution)/shard_map/ppermute | solution.py:549
  22.9 25.3 %collective-permute-start.34 = (s32[1,4]{1,0:T(1,128)S(1)}, s32[1,4]{1,0:T(1,128)S(1)}, u32[]{:S(2)}, u32[]{:S(2)}) collective-permute-start(s32[1,4]{1,0:T(1,128)S(1)} %fusion.213), channel_id=1, source_target_pairs={{0,16},{4,20},{8,24},{12,28},{16,0},{20,4},{24,8},{28,12},{1,17},{... | collective-permute-start | bytes 56 | tf_op jit(solution)/shard_map/ppermute | solution.py:549
  24.1 24.8 %collective-permute-start.35 = (s32[1,4]{1,0:T(1,128)S(1)}, s32[1,4]{1,0:T(1,128)S(1)}, u32[]{:S(2)}, u32[]{:S(2)}) collective-permute-start(s32[1,4]{1,0:T(1,128)S(1)} %fusion.213), channel_id=1, source_target_pairs={{0,20},{4,24},{8,28},{12,0},{16,4},{20,8},{24,12},{28,16},{1,21},{... | collective-permute-start | bytes 56 | tf_op jit(solution)/shard_map/ppermute | solution.py:549
  28.6 383.8 %reduce-scatter.4.cloned.1.call-start = ((), (), s32[]{:S(2)}) async-start(), calls=%async_computation.6 | async-start | bytes 491520 | tf_op jit(solution)/shard_map/reduce_scatter | solution.py:743
  48.0 68.1 %collective-permute-start = (bf16[384,384]{1,0:T(8,128)(2,1)S(1)}, bf16[384,384]{1,0:T(8,128)(2,1)S(1)}, u32[]{:S(2)}, u32[]{:S(2)}) collective-permute-start(bf16[384,384]{1,0:T(8,128)(2,1)S(1)} %dynamic-slice_bitcast_fusion), channel_id=1, source_target_pairs={{0,1},{1,0},{2,3},{3,2},{4,5},{5,4},{6,7},{7,6},{8,9},{9,8},{10,11... | collective-permute-start | bytes 884744 | tf_op jit(solution)/shard_map/ppermute | solution.py:637
  48.2 12.2 %collective-permute-start.10 = (bf16[32,2048]{1,0:T(8,128)(2,1)}, bf16[32,2048]{1,0:T(8,128)(2,1)}, u32[]{:S(2)}, u32[]{:S(2)}) collective-permute-start(bf16[32,2048]{1,0:T(8,128)(2,1)} %get-tuple-element.219), channel_id=1, source_target_pairs={{0,4},{4,8},{8,12},{12,16},{16,20},{20,24},{24,28},{28,0},{1,5},{5... | collective-permute-start | bytes 393224 | tf_op jit(solution)/shard_map/ppermute | solution.py:563
  48.9 12.4 %collective-permute-start.11 = (bf16[32,2048]{1,0:T(8,128)(2,1)}, bf16[32,2048]{1,0:T(8,128)(2,1)}, u32[]{:S(2)}, u32[]{:S(2)}) collective-permute-start(bf16[32,2048]{1,0:T(8,128)(2,1)} %get-tuple-element.218), channel_id=1, source_target_pairs={{0,8},{4,12},{8,16},{12,20},{16,24},{20,28},{24,0},{28,4},{1,9},{5... | collective-permute-start | bytes 393224 | tf_op jit(solution)/shard_map/ppermute | solution.py:563
  49.7 27.5 %collective-permute-start.12 = (bf16[32,2048]{1,0:T(8,128)(2,1)}, bf16[32,2048]{1,0:T(8,128)(2,1)}, u32[]{:S(2)}, u32[]{:S(2)}) collective-permute-start(bf16[32,2048]{1,0:T(8,128)(2,1)} %get-tuple-element.217), channel_id=1, source_target_pairs={{0,12},{4,16},{8,20},{12,24},{16,28},{20,0},{24,4},{28,8},{1,13},{... | collective-permute-start | bytes 393224 | tf_op jit(solution)/shard_map/ppermute | solution.py:563
  50.9 27.7 %collective-permute-start.13 = (bf16[32,2048]{1,0:T(8,128)(2,1)}, bf16[32,2048]{1,0:T(8,128)(2,1)}, u32[]{:S(2)}, u32[]{:S(2)}) collective-permute-start(bf16[32,2048]{1,0:T(8,128)(2,1)} %get-tuple-element.216), channel_id=1, source_target_pairs={{0,16},{4,20},{8,24},{12,28},{16,0},{20,4},{24,8},{28,12},{1,17},{... | collective-permute-start | bytes 393224 | tf_op jit(solution)/shard_map/ppermute | solution.py:563
  60.4 25.5 %collective-permute-start.14 = (bf16[32,2048]{1,0:T(8,128)(2,1)}, bf16[32,2048]{1,0:T(8,128)(2,1)S(1)}, u32[]{:S(2)}, u32[]{:S(2)}) collective-permute-start(bf16[32,2048]{1,0:T(8,128)(2,1)} %get-tuple-element.215), channel_id=1, source_target_pairs={{0,20},{4,24},{8,28},{12,0},{16,4},{20,8},{24,12},{28,16},{1,21},{... | collective-permute-start | bytes 393224 | tf_op jit(solution)/shard_map/ppermute | solution.py:563
  61.3 29.5 %collective-permute-start.15 = (bf16[32,2048]{1,0:T(8,128)(2,1)}, bf16[32,2048]{1,0:T(8,128)(2,1)S(1)}, u32[]{:S(2)}, u32[]{:S(2)}) collective-permute-start(bf16[32,2048]{1,0:T(8,128)(2,1)} %get-tuple-element.214), channel_id=1, source_target_pairs={{0,24},{4,28},{8,0},{12,4},{16,8},{20,12},{24,16},{28,20},{1,25},{... | collective-permute-start | bytes 393224 | tf_op jit(solution)/shard_map/ppermute | solution.py:563
  77.2 16.3 %collective-permute-start.16 = (bf16[32,2048]{1,0:T(8,128)(2,1)}, bf16[32,2048]{1,0:T(8,128)(2,1)S(1)}, u32[]{:S(2)}, u32[]{:S(2)}) collective-permute-start(bf16[32,2048]{1,0:T(8,128)(2,1)} %get-tuple-element.213), channel_id=1, source_target_pairs={{0,28},{4,0},{8,4},{12,8},{16,12},{20,16},{24,20},{28,24},{1,29},{... | collective-permute-start | bytes 393224 | tf_op jit(solution)/shard_map/ppermute | solution.py:563
  78.6 18.5 %collective-permute-start.17 = (bf16[32,2048]{1,0:T(8,128)(2,1)}, bf16[32,2048]{1,0:T(8,128)(2,1)S(1)}, u32[]{:S(2)}, u32[]{:S(2)}) collective-permute-start(bf16[32,2048]{1,0:T(8,128)(2,1)} %get-tuple-element.212), channel_id=1, source_target_pairs={{0,4},{4,8},{8,12},{12,16},{16,20},{20,24},{24,28},{28,0},{1,5},{5... | collective-permute-start | bytes 393224 | tf_op jit(solution)/shard_map/ppermute | solution.py:563
  85.8 15.1 %collective-permute-start.18 = (bf16[32,2048]{1,0:T(8,128)(2,1)}, bf16[32,2048]{1,0:T(8,128)(2,1)S(1)}, u32[]{:S(2)}, u32[]{:S(2)}) collective-permute-start(bf16[32,2048]{1,0:T(8,128)(2,1)} %get-tuple-element.211), channel_id=1, source_target_pairs={{0,8},{4,12},{8,16},{12,20},{16,24},{20,28},{24,0},{28,4},{1,9},{5... | collective-permute-start | bytes 393224 | tf_op jit(solution)/shard_map/ppermute | solution.py:563
  90.8 24.6 %collective-permute-start.19 = (bf16[32,2048]{1,0:T(8,128)(2,1)}, bf16[32,2048]{1,0:T(8,128)(2,1)S(1)}, u32[]{:S(2)}, u32[]{:S(2)}) collective-permute-start(bf16[32,2048]{1,0:T(8,128)(2,1)} %get-tuple-element.210), channel_id=1, source_target_pairs={{0,12},{4,16},{8,20},{12,24},{16,28},{20,0},{24,4},{28,8},{1,13},{... | collective-permute-start | bytes 393224 | tf_op jit(solution)/shard_map/ppermute | solution.py:563
  93.5 22.6 %collective-permute-start.20 = (bf16[32,2048]{1,0:T(8,128)(2,1)}, bf16[32,2048]{1,0:T(8,128)(2,1)S(1)}, u32[]{:S(2)}, u32[]{:S(2)}) collective-permute-start(bf16[32,2048]{1,0:T(8,128)(2,1)} %get-tuple-element.209), channel_id=1, source_target_pairs={{0,16},{4,20},{8,24},{12,28},{16,0},{20,4},{24,8},{28,12},{1,17},{... | collective-permute-start | bytes 393224 | tf_op jit(solution)/shard_map/ppermute | solution.py:563
  97.1 191.6 %collective-permute-start.21 = (bf16[32,2048]{1,0:T(8,128)(2,1)}, bf16[32,2048]{1,0:T(8,128)(2,1)}, u32[]{:S(2)}, u32[]{:S(2)}) collective-permute-start(bf16[32,2048]{1,0:T(8,128)(2,1)} %get-tuple-element.208), channel_id=1, source_target_pairs={{0,20},{4,24},{8,28},{12,0},{16,4},{20,8},{24,12},{28,16},{1,21},{... | collective-permute-start | bytes 393224 | tf_op jit(solution)/shard_map/ppermute | solution.py:563
  100.9 190.2 %collective-permute-start.22 = (bf16[32,2048]{1,0:T(8,128)(2,1)}, bf16[32,2048]{1,0:T(8,128)(2,1)}, u32[]{:S(2)}, u32[]{:S(2)}) collective-permute-start(bf16[32,2048]{1,0:T(8,128)(2,1)} %get-tuple-element.207), channel_id=1, source_target_pairs={{0,24},{4,28},{8,0},{12,4},{16,8},{20,12},{24,16},{28,20},{1,25},{... | collective-permute-start | bytes 393224 | tf_op jit(solution)/shard_map/ppermute | solution.py:563
  115.5 179.2 %collective-permute-start.23 = (bf16[32,2048]{1,0:T(8,128)(2,1)S(1)}, bf16[32,2048]{1,0:T(8,128)(2,1)}, u32[]{:S(2)}, u32[]{:S(2)}) collective-permute-start(bf16[32,2048]{1,0:T(8,128)(2,1)S(1)} %copy-done.34), channel_id=1, source_target_pairs={{0,28},{4,0},{8,4},{12,8},{16,12},{20,16},{24,20},{28,24},{1,29},{... | collective-permute-start | bytes 393224 | tf_op jit(solution)/shard_map/ppermute | solution.py:563
  297.1 9.8 collective-permute-start.5
  323.6 11.3 %collective-permute-start.24 = (f32[4,1664]{1,0:T(4,128)S(1)}, f32[4,1664]{1,0:T(4,128)S(1)}, u32[]{:S(2)}, u32[]{:S(2)}) collective-permute-start(f32[4,1664]{1,0:T(4,128)S(1)} %bitcast.394), channel_id=1, source_target_pairs={{0,4},{4,8},{8,12},{12,16},{16,20},{20,24},{24,28},{28,0},{1,5},{5... | collective-permute-start | bytes 79880 | tf_op jit(solution)/shard_map/ppermute | solution.py:549
  325.0 10.6 %collective-permute-start.25 = (f32[4,1664]{1,0:T(4,128)S(1)}, f32[4,1664]{1,0:T(4,128)S(1)}, u32[]{:S(2)}, u32[]{:S(2)}) collective-permute-start(f32[4,1664]{1,0:T(4,128)S(1)} %bitcast.395), channel_id=1, source_target_pairs={{0,8},{4,12},{8,16},{12,20},{16,24},{20,28},{24,0},{28,4},{1,9},{5... | collective-permute-start | bytes 79880 | tf_op jit(solution)/shard_map/ppermute | solution.py:549
  326.9 10.7 %collective-permute-start.26 = (f32[4,1664]{1,0:T(4,128)S(1)}, f32[4,1664]{1,0:T(4,128)S(1)}, u32[]{:S(2)}, u32[]{:S(2)}) collective-permute-start(f32[4,1664]{1,0:T(4,128)S(1)} %bitcast.396), channel_id=1, source_target_pairs={{0,12},{4,16},{8,20},{12,24},{16,28},{20,0},{24,4},{28,8},{1,13},{... | collective-permute-start | bytes 79880 | tf_op jit(solution)/shard_map/ppermute | solution.py:549
  327.1 11.0 %collective-permute-start.27 = (f32[4,1664]{1,0:T(4,128)S(1)}, f32[4,1664]{1,0:T(4,128)S(1)}, u32[]{:S(2)}, u32[]{:S(2)}) collective-permute-start(f32[4,1664]{1,0:T(4,128)S(1)} %bitcast.397), channel_id=1, source_target_pairs={{0,16},{4,20},{8,24},{12,28},{16,0},{20,4},{24,8},{28,12},{1,17},{... | collective-permute-start | bytes 79880 | tf_op jit(solution)/shard_map/ppermute | solution.py:549
  389.9 212.0 %reduce-scatter.6.cloned.1.call-start = ((), (), s32[]{:S(2)}) async-start(), calls=%async_computation.7 | async-start | bytes 8110080 | tf_op jit(solution)/shard_map/reduce_scatter | solution.py:757
  479.4 250.7 %reduce-scatter.8.cloned.1.call-start = ((), (), s32[]{:S(2)}) async-start(), calls=%async_computation.8 | async-start | bytes 8110080 | tf_op jit(solution)/shard_map/reduce_scatter | solution.py:757
  480.0 338.0 %all-gather.17.cloned.1.call-start = ((), (), s32[]{:S(2)}) async-start(), calls=%async_computation.10 | async-start | bytes 3440640 | tf_op jit(solution)/shard_map/all_gather | solution.py:784
  480.6 9.4 collective-permute-start.49
  483.6 9.4 collective-permute-start.51
  495.6 9.8 collective-permute-start.56
  497.8 15.7 %collective-permute-start.58 = (bf16[48,1536]{1,0:T(8,128)(2,1)S(1)}, bf16[48,1536]{1,0:T(8,128)(2,1)S(1)}, u32[]{:S(2)}, u32[]{:S(2)}) collective-permute-start(bf16[48,1536]{1,0:T(8,128)(2,1)S(1)} %pad_maximum_fusion.2), channel_id=1, source_target_pairs={{0,12},{4,16},{8,20},{12,24},{16,28},{20,0},{24,4},{28,8},{1,13},{... | collective-permute-start | bytes 442376 | tf_op jit(solution)/shard_map/ppermute | solution.py:549
  499.5 14.5 %collective-permute-start.59 = (bf16[48,1536]{1,0:T(8,128)(2,1)S(1)}, bf16[48,1536]{1,0:T(8,128)(2,1)S(1)}, u32[]{:S(2)}, u32[]{:S(2)}) collective-permute-start(bf16[48,1536]{1,0:T(8,128)(2,1)S(1)} %pad_maximum_fusion.2), channel_id=1, source_target_pairs={{0,16},{4,20},{8,24},{12,28},{16,0},{20,4},{24,8},{28,12},{1,17},{... | collective-permute-start | bytes 442376 | tf_op jit(solution)/shard_map/ppermute | solution.py:549
  501.6 12.4 %collective-permute-start.60 = (bf16[48,1536]{1,0:T(8,128)(2,1)S(1)}, bf16[48,1536]{1,0:T(8,128)(2,1)S(1)}, u32[]{:S(2)}, u32[]{:S(2)}) collective-permute-start(bf16[48,1536]{1,0:T(8,128)(2,1)S(1)} %pad_maximum_fusion.2), channel_id=1, source_target_pairs={{0,20},{4,24},{8,28},{12,0},{16,4},{20,8},{24,12},{28,16},{1,21},{... | collective-permute-start | bytes 442376 | tf_op jit(solution)/shard_map/ppermute | solution.py:549
  516.7 329.8 %all-gather.15.cloned.1.call-start = ((), (), s32[]{:S(2)}) async-start(), calls=%async_computation.9 | async-start | bytes 8110080 | tf_op jit(solution)/shard_map/all_gather | solution.py:810
  748.2 12.1 %collective-permute-start.68 = (f32[32,2048]{1,0:T(8,128)S(1)}, f32[32,2048]{1,0:T(8,128)S(1)}, u32[]{:S(2)}, u32[]{:S(2)}) collective-permute-start(f32[32,2048]{1,0:T(8,128)S(1)} %get-tuple-element.205), channel_id=1, source_target_pairs={{0,4},{4,8},{8,12},{12,16},{16,20},{20,24},{24,28},{28,0},{1,5},{5... | collective-permute-start | bytes 786440 | tf_op jit(solution)/shard_map/ppermute | solution.py:563
  750.3 13.2 %collective-permute-start.69 = (f32[32,2048]{1,0:T(8,128)S(1)}, f32[32,2048]{1,0:T(8,128)S(1)}, u32[]{:S(2)}, u32[]{:S(2)}) collective-permute-start(f32[32,2048]{1,0:T(8,128)S(1)} %get-tuple-element.204), channel_id=1, source_target_pairs={{0,8},{4,12},{8,16},{12,20},{16,24},{20,28},{24,0},{28,4},{1,9},{5... | collective-permute-start | bytes 786440 | tf_op jit(solution)/shard_map/ppermute | solution.py:563
  751.6 28.1 %collective-permute-start.70 = (f32[32,2048]{1,0:T(8,128)S(1)}, f32[32,2048]{1,0:T(8,128)S(1)}, u32[]{:S(2)}, u32[]{:S(2)}) collective-permute-start(f32[32,2048]{1,0:T(8,128)S(1)} %get-tuple-element.203), channel_id=1, source_target_pairs={{0,12},{4,16},{8,20},{12,24},{16,28},{20,0},{24,4},{28,8},{1,13},{... | collective-permute-start | bytes 786440 | tf_op jit(solution)/shard_map/ppermute | solution.py:563
  753.0 30.6 %collective-permute-start.71 = (f32[32,2048]{1,0:T(8,128)S(1)}, f32[32,2048]{1,0:T(8,128)S(1)}, u32[]{:S(2)}, u32[]{:S(2)}) collective-permute-start(f32[32,2048]{1,0:T(8,128)S(1)} %get-tuple-element.202), channel_id=1, source_target_pairs={{0,16},{4,20},{8,24},{12,28},{16,0},{20,4},{24,8},{28,12},{1,17},{... | collective-permute-start | bytes 786440 | tf_op jit(solution)/shard_map/ppermute | solution.py:563
  754.7 46.8 %collective-permute-start.72 = (f32[32,2048]{1,0:T(8,128)S(1)}, f32[32,2048]{1,0:T(8,128)S(1)}, u32[]{:S(2)}, u32[]{:S(2)}) collective-permute-start(f32[32,2048]{1,0:T(8,128)S(1)} %get-tuple-element.201), channel_id=1, source_target_pairs={{0,20},{4,24},{8,28},{12,0},{16,4},{20,8},{24,12},{28,16},{1,21},{... | collective-permute-start | bytes 786440 | tf_op jit(solution)/shard_map/ppermute | solution.py:563
  760.3 47.6 %collective-permute-start.73 = (f32[32,2048]{1,0:T(8,128)S(1)}, f32[32,2048]{1,0:T(8,128)S(1)}, u32[]{:S(2)}, u32[]{:S(2)}) collective-permute-start(f32[32,2048]{1,0:T(8,128)S(1)} %get-tuple-element.200), channel_id=1, source_target_pairs={{0,24},{4,28},{8,0},{12,4},{16,8},{20,12},{24,16},{28,20},{1,25},{... | collective-permute-start | bytes 786440 | tf_op jit(solution)/shard_map/ppermute | solution.py:563
  764.7 46.7 %collective-permute-start.74 = (f32[32,2048]{1,0:T(8,128)S(1)}, f32[32,2048]{1,0:T(8,128)S(1)}, u32[]{:S(2)}, u32[]{:S(2)}) collective-permute-start(f32[32,2048]{1,0:T(8,128)S(1)} %get-tuple-element.199), channel_id=1, source_target_pairs={{0,28},{4,0},{8,4},{12,8},{16,12},{20,16},{24,20},{28,24},{1,29},{... | collective-permute-start | bytes 786440 | tf_op jit(solution)/shard_map/ppermute | solution.py:563
  787.4 15.9 %collective-permute-start.66 = (f32[11,384]{1,0:T(8,128)S(1)}, f32[11,384]{1,0:T(8,128)S(1)}, u32[]{:S(2)}, u32[]{:S(2)}) collective-permute-start(f32[11,384]{1,0:T(8,128)S(1)} %add.1148), channel_id=1, source_target_pairs={{0,8},{4,12},{8,0},{12,4},{16,24},{20,28},{24,16},{28,20},{1,9},{5... | collective-permute-start | bytes 50696 | tf_op jit(solution)/shard_map/ppermute | solution.py:533
  803.3 9.8 collective-permute-start.67
  (106 other events, 2984.6 us)
Sparse Core Ops, SparseCore 0:
  11.5 150.0 all-gather.8
  164.3 53.2 all-gather.10
  220.4 54.6 all-gather.12
  390.0 22.3 reduce-scatter.3
  479.5 122.3 reduce-scatter.5
  608.4 121.6 reduce-scatter.7
  732.2 25.4 all-gather.16
  761.2 85.2 all-gather.14

commit v2 on v1

--- a/solution.py
+++ b/solution.py
@@ -136,11 +136,7 @@
     out_ref[...] = x2 + lax.fori_loop(0, wt_ref.shape[0], units, jnp.zeros(x.shape, f32))
 
 
-def block_bwd_kernel(
-    x_ref, wt_ref, gains_ref, seg_col_ref, seg_row_ref, slot_ref,
-    h1_ref, qkv_ref, o_ref, x2_ref, grad_ref,
-    dwt_ref, dgains_ref,
-):
+def mlp_bwd_kernel(wt_ref, gains_ref, x2_ref, grad_ref, dwt_ref, dgains_ref, dx2_ref):
     @pl.when(pl.program_id(0) == 0)
     def _():
         dwt_ref[...] = jnp.zeros_like(dwt_ref)
@@ -153,16 +149,36 @@
 
     def units(group, total):
         up = mm(h2, wt_ref[group, 512:896], NT)
-        hidden = gelu_exact(up).astype(bf16)
-        grad_up = (mm(grad_low, wt_ref[group, 896:1280], NT) * gelu_slope(up)).astype(bf16)
+        cdf = gelu_cdf(up)
+        hidden = (up * cdf).astype(bf16)
+        slope = cdf + up * (jnp.exp(-0.5 * up * up) * 0.3989422804014327)
+        grad_up = (mm(grad_low, wt_ref[group, 896:1280], NT) * slope).astype(bf16)
         dwt_ref[group, 512:896] += mm(grad_up, h2, TN)
         dwt_ref[group, 896:1280] += mm(hidden, grad_low, TN)
         return total + mm(grad_up, wt_ref[group, 512:896])
 
-    groups = wt_ref.shape[0]
-    grad_h2 = lax.fori_loop(0, groups, units, jnp.zeros(grad.shape, f32))
+    grad_h2 = lax.fori_loop(0, wt_ref.shape[0], units, jnp.zeros(grad.shape, f32))
     grad_x2, gain_two, bias_two = norm_back(x2, gains_ref[2:3], grad_h2)
-    grad_att = (grad + grad_x2).astype(bf16)
+    dx2_ref[...] = grad + grad_x2
+    dgains_ref[...] += jnp.concatenate([gain_two, bias_two], axis=0)
+
+
+def attention_bwd_kernel(
+    last, wt_ref, gains_ref, seg_col_ref, seg_row_ref, slot_ref, h1_ref, qkv_ref, o_ref, dx2_ref,
+    *refs,
+):
+    if last:
+        x_ref, partial_ref, _, dwt_ref, dgains_ref = refs
+    else:
+        _, dwt_ref, dh1_ref = refs
+
+    @pl.when(pl.program_id(0) == 0)
+    def _():
+        dwt_ref[...] = jnp.zeros_like(dwt_ref)
+        if last:
+            dgains_ref[...] = jnp.zeros_like(dgains_ref)
+
+    grad_att = dx2_ref[...].astype(bf16)
     allowed = seg_col_ref[0] == seg_row_ref[0]
     h1 = h1_ref[...]
 
@@ -177,7 +193,7 @@
         grad_queries = []
         for query, gmix in zip(halves(qkv[:, 0:128]), halves(grad_mix)):
             expd = jnp.where(allowed, jnp.exp(mm(query, keys, NT) * HD ** (-0.5)), 0.0)
-            prob = expd / jnp.sum(expd, axis=-1, keepdims=True)
+            prob = expd * (1.0 / jnp.sum(expd, axis=-1, keepdims=True))
             grad_values = grad_values + mm(prob.astype(bf16), gmix, TN)
             grad_prob = mm(gmix, values, NT)
             scored = prob * (grad_prob - jnp.sum(prob * grad_prob, axis=-1, keepdims=True))
@@ -193,9 +209,13 @@
         dwt_ref[group, 0:384] += mm(grad_qkv, h1, TN)
         return total + mm(grad_qkv, wt_ref[group, 0:384])
 
-    grad_h1 = lax.fori_loop(0, groups, heads, jnp.zeros(grad.shape, f32))
-    _, gain_one, bias_one = norm_back(x_ref[...], gains_ref[0:1], grad_h1)
-    dgains_ref[...] += jnp.concatenate([gain_one, bias_one, gain_two, bias_two], axis=0)
+    start = partial_ref[...] if last else jnp.zeros(h1.shape, f32)
+    grad_h1 = lax.fori_loop(0, wt_ref.shape[0], heads, start)
+    if last:
+        _, gain_one, bias_one = norm_back(x_ref[...], gains_ref[0:1], grad_h1)
+        dgains_ref[...] += jnp.concatenate([gain_one, bias_one], axis=0)
+    else:
+        dh1_ref[...] = grad_h1
 
 
 def whole_spec(shape):
@@ -233,32 +253,61 @@
         ],
         compiler_params=pltpu.CompilerParams(vmem_limit_bytes=VMEM_LIMIT),
         cost_estimate=pl.CostEstimate(
-            flops=rows * 9_000_000, bytes_accessed=8_000_000, transcendentals=rows * 4000
+            flops=rows * 30_000_000, bytes_accessed=8_000_000, transcendentals=rows * 4000
         ),
     )(x, weights, gains, seg_col, seg_row, slot)
 
 
-def block_bwd(x, weights, layer, gains, seg_col, seg_row, slot, saved, grad):
-    rows, groups = x.shape[0], weights.shape[0]
+def mlp_bwd(weights, layer, gains, x2, grad):
+    rows, groups = x2.shape[0], weights.shape[0]
     s = block_specs(groups, layer)
-    h1, qkv, mix, x2 = saved
     return pl.pallas_call(
-        block_bwd_kernel,
+        mlp_bwd_kernel,
         grid=(rows // CHUNK,),
-        in_specs=[
-            s["row"], s["wt"], s["gains"], s["seg_col"], s["seg_row"], s["slot"],
-            s["row"], s["qkv"], s["mix"], s["row"], s["row"],
-        ],
-        out_specs=[whole_spec((groups, 1280, D)), whole_spec((4, D))],
+        in_specs=[s["wt"], s["gains"], s["row"], s["row"]],
+        out_specs=[whole_spec((groups, 1280, D)), whole_spec((2, D)), s["row"]],
         out_shape=[
             jax.ShapeDtypeStruct((groups, 1280, D), f32),
-            jax.ShapeDtypeStruct((4, D), f32),
+            jax.ShapeDtypeStruct((2, D), f32),
+            jax.ShapeDtypeStruct((rows, D), f32),
         ],
         compiler_params=pltpu.CompilerParams(vmem_limit_bytes=VMEM_LIMIT),
         cost_estimate=pl.CostEstimate(
-            flops=rows * 22_000_000, bytes_accessed=16_000_000, transcendentals=rows * 6000
+            flops=rows * 24_000_000, bytes_accessed=16_000_000, transcendentals=rows * 6000
         ),
-    )(x, weights, gains, seg_col, seg_row, slot, h1, qkv, mix, x2, grad)
+    )(weights, gains, x2, grad)
+
+
+def attention_bwd(part, weights, layer, gains, seg_col, seg_row, slot, saved, grad_x2, dwt, last=()):
+    h1, qkv, mix, _ = saved
+    rows, groups = h1.shape[0], weights.shape[0] // 2
+    s = block_specs(groups, layer)
+    heads = pl.BlockSpec((groups, 512, D), lambda c: (part, 0, 0))
+    in_specs = [
+        pl.BlockSpec((groups, 512, D), lambda c: (part, 0, layer)),
+        s["gains"], s["seg_col"], s["seg_row"],
+        pl.BlockSpec((groups, 1, 128), lambda c: (part, 0, 0)),
+        s["row"],
+        pl.BlockSpec((groups, CHUNK, 384), lambda c: (part, c, 0)),
+        pl.BlockSpec((groups, CHUNK, 128), lambda c: (part, c, 0)),
+        s["row"],
+    ] + [s["row"]] * len(last)
+    args = (weights, gains, seg_col, seg_row, slot, h1, qkv, mix, grad_x2, *last, dwt)
+    return pl.pallas_call(
+        functools.partial(attention_bwd_kernel, bool(last)),
+        grid=(rows // CHUNK,),
+        in_specs=in_specs + [pl.BlockSpec(memory_space=pl.ANY)],
+        out_specs=[heads, whole_spec((2, D)) if last else s["row"]],
+        out_shape=[
+            jax.ShapeDtypeStruct(dwt.shape, f32),
+            jax.ShapeDtypeStruct((2, D) if last else (rows, D), f32),
+        ],
+        input_output_aliases={len(args) - 1: 0},
+        compiler_params=pltpu.CompilerParams(vmem_limit_bytes=VMEM_LIMIT),
+        cost_estimate=pl.CostEstimate(
+            flops=rows * 19_000_000, bytes_accessed=8_000_000, transcendentals=rows * 3000
+        ),
+    )(*args)
 
 
 def crop_starts(crops):
@@ -412,7 +461,7 @@
         out_shape=out_shape,
         compiler_params=pltpu.CompilerParams(vmem_limit_bytes=VMEM_LIMIT),
         cost_estimate=pl.CostEstimate(
-            flops=rows * 1_600_000, bytes_accessed=8_000_000, transcendentals=rows * 200
+            flops=rows * 15_000_000, bytes_accessed=8_000_000, transcendentals=rows * 200
         ),
     )(x, weights, gains, seg_cls, seg_row, slot)
 
@@ -434,83 +483,87 @@
         out_shape=out_shape,
         compiler_params=pltpu.CompilerParams(vmem_limit_bytes=VMEM_LIMIT),
         cost_estimate=pl.CostEstimate(
-            flops=rows * 4_000_000, bytes_accessed=16_000_000, transcendentals=rows * 400
+            flops=rows * 20_000_000, bytes_accessed=16_000_000, transcendentals=rows * 400
         ),
     )(x, weights, gains, seg_cls, seg_row, slot, *saved, grad)
 
 
-def basis_kernel(clip_ref, grads_ref, stats_ref, bases_ref, new_stats_ref, new_bases_ref, s_ref):
-    layers, kinds = stats_ref.shape[0] // 4, 4
-    mats = layers * kinds
-    groups = grads_ref.shape[0]
-    clip = clip_ref[0]
-    bounds = (0, 384, 512, 896, 1280)
-    for layer in range(layers):
-        for kind in range(kinds):
-            mat = layer * kinds + kind
-
-            def outer(group, total, layer=layer, kind=kind):
-                part = grads_ref[group, bounds[kind] : bounds[kind + 1], layer * D : layer * D + D]
-                return total + mm(part, part, TN)
-
-            stat = lax.fori_loop(0, groups, outer, jnp.zeros((D, D), f32))
-            new_stats_ref[mat] = (
-                SHAMPOO_BETA * stats_ref[mat] + (1 - SHAMPOO_BETA) * (clip * clip) * stat
-            )
-
-    def turn(mat, carry):
-        new_bases_ref[mat] = mm(new_stats_ref[mat], bases_ref[mat], precision=precise)
-        return carry
-
-    lax.fori_loop(0, mats, turn, 0)
-    lanes = lax.broadcasted_iota(jnp.int32, (mats, 128), 1)
+PANEL = 32
+
+
+def panel_steps(panels):
+    lanes = lax.broadcasted_iota(jnp.int32, (PANEL, 128), 1)
+    ids = lax.broadcasted_iota(jnp.int32, (PANEL, 1), 0)
+    panels = list(panels)
+    pivots = [jnp.zeros((PANEL, 1), f32) for _ in panels]
+    for step in range(PANEL):
+        here = lanes == step
+        for i, panel in enumerate(panels):
+            row = panel[step : step + 1]
+            pivot = row[:, step : step + 1]
+            column = jnp.where(ids > step, panel[:, step : step + 1], 0.0)
+            source = jnp.where(here[0:1], 1.0, row) * (1.0 / pivot)
+            cleared = jnp.where(here & (ids > step), 0.0, panel)
+            panels[i] = cleared - column * source
+            pivots[i] = jnp.where(ids == step, pivot, pivots[i])
+    return panels, pivots
+
+
+def basis_kernel(stats_ref, bases_ref, out_ref, gram_ref, inverse_ref):
+    mats = stats_ref.shape[0]
+    lanes = lax.broadcasted_iota(jnp.int32, (128, 128), 1)
+    rows = lax.broadcasted_iota(jnp.int32, (128, 128), 0)
+    near_lanes, near_rows = lanes[:PANEL], rows[:PANEL]
+    for mat in range(mats):
+        out_ref[mat] = mm(stats_ref[mat], bases_ref[mat], precision=precise)
     for block in range(D // 128):
         low, high = block * 128, block * 128 + 128
         for mat in range(mats):
-            part = new_bases_ref[mat, :, low:high]
-            s_ref[:, mat, :] = mm(part, part, TN, precise)
-        pivots = jnp.zeros((mats, 128), f32)
-        for first in range(0, 128, 32):
-
-            def eliminate(step, pivots, first=first):
-                row = s_ref[step]
-                here = lanes == step
-                pivot = jnp.sum(jnp.where(here, row, 0.0), axis=-1, keepdims=True)
-                factors = jnp.where(lanes > step, row / pivot, 0.0)
-                source = jnp.where(here, 1.0, row)
-                for other in range(first, 128):
-                    s_ref[other] = (
-                        jnp.where(here, 0.0, s_ref[other]) - factors[:, other : other + 1] * source
-                    )
-                return jnp.where(here, pivot, pivots)
-
-            pivots = lax.fori_loop(first, first + 32, eliminate, pivots)
-        scale = lax.rsqrt(pivots)
-        for other in range(128):
-            row = jnp.where(lanes < other, s_ref[other], jnp.where(lanes == other, 1.0, 0.0))
-            s_ref[other] = row * scale[:, other : other + 1]
+            part = out_ref[mat, :, low:high]
+            gram_ref[mat] = mm(part, part, TN, precise)
+
+        def panels(index, carry):
+            first = pl.multiple_of(index * PANEL, PANEL)
+            last = first + PANEL
+            started = [
+                pltpu.roll(gram_ref[mat, pl.ds(first, PANEL), :], 128 - first, 1)
+                for mat in range(mats)
+            ]
+            for mat, (panel, pivots) in enumerate(zip(*panel_steps(started))):
+                panel = pltpu.roll(panel, first, 1)
+                own = near_lanes - first
+                unit = jnp.where(own < near_rows, panel, jnp.where(own == near_rows, 1.0, 0.0))
+                inverse_ref[mat, pl.ds(first, PANEL), :] = unit * lax.rsqrt(pivots)
+                source = jnp.where(near_lanes < last, unit, panel)
+                factors = jnp.where(near_lanes < last, 0.0, panel / pivots)
+                gram = gram_ref[mat]
+                gram = jnp.where((lanes >= first) & (lanes < last) & (rows >= last), 0.0, gram)
+                gram_ref[mat] = gram - mm(factors, source, TN, precise)
+            return carry
+
+        lax.fori_loop(0, 128 // PANEL, panels, 0)
         for mat in range(mats):
-            part = mm(new_bases_ref[mat, :, low:high], s_ref[:, mat, :], NT, precise)
-            new_bases_ref[mat, :, low:high] = part
+            part = mm(out_ref[mat, :, low:high], inverse_ref[mat], NT, precise)
+            out_ref[mat, :, low:high] = part
             if high < D:
-                rest = new_bases_ref[mat, :, high:]
+                rest = out_ref[mat, :, high:]
                 cross = mm(part, rest, TN, precise)
-                new_bases_ref[mat, :, high:] = rest - mm(part, cross, NN, precise)
-
-
-def renew_bases(clip_factor, grads, stats, bases):
-    shape = stats.shape
-    mats = shape[0] * shape[1]
-    new_stats, new_bases = pl.pallas_call(
+                out_ref[mat, :, high:] = rest - mm(part, cross, NN, precise)
+
+
+def renew_bases(new_stats, bases):
+    mats = new_stats.shape[0]
+    return pl.pallas_call(
         basis_kernel,
-        in_specs=[pl.BlockSpec(memory_space=pltpu.SMEM)]
-        + [pl.BlockSpec(memory_space=pltpu.VMEM)] * 3,
-        out_specs=[pl.BlockSpec(memory_space=pltpu.VMEM)] * 2,
-        out_shape=[jax.ShapeDtypeStruct((mats, D, D), f32)] * 2,
-        scratch_shapes=[pltpu.VMEM((128, mats, 128), f32)],
+        in_specs=[pl.BlockSpec(memory_space=pltpu.VMEM)] * 2,
+        out_specs=pl.BlockSpec(memory_space=pltpu.VMEM),
+        out_shape=jax.ShapeDtypeStruct((mats, D, D), f32),
+        scratch_shapes=[pltpu.VMEM((mats, 128, 128), f32), pltpu.VMEM((mats, 128, 128), f32)],
         compiler_params=pltpu.CompilerParams(vmem_limit_bytes=VMEM_LIMIT),
-    )(clip_factor.reshape(1), grads, stats.reshape(mats, D, D), bases.reshape(mats, D, D))
-    return new_stats.reshape(shape), new_bases.reshape(shape)
+        cost_estimate=pl.CostEstimate(
+            flops=60_000_000_000, bytes_accessed=6_000_000, transcendentals=1000
+        ),
+    )(new_stats, bases)
 
 
 def flip_perm(count, bit):
@@ -526,6 +579,19 @@
     return count, bits
 
 
+def thirds(array):
+    high = lax.optimization_barrier(array.astype(bf16))
+    rest = array - high.astype(f32)
+    middle = lax.optimization_barrier(rest.astype(bf16))
+    return jnp.stack([high, middle, (rest - middle.astype(f32)).astype(bf16)])
+
+
+def whole_of(parts):
+    layers, count = parts.shape[:2]
+    parts = parts.transpose(1, 0, 2, 3).reshape(count, 3, -1, parts.shape[-1]).astype(f32)
+    return jnp.sum(parts[:, 0] + (parts[:, 1] + parts[:, 2]), axis=0)
+
+
 def sum_over(array, axes):
     for axis in axes:
         count, bits = flips(axis)
@@ -540,29 +606,127 @@
 
 def gather_over(array, axis):
     count = lax.axis_size(axis)
-    if count > 8:
+    if lax.axis_size("dp") > 8:
         return lax.all_gather(array, axis, axis=0)
-    me = lax.axis_index(axis)
-    out = jnp.zeros((count, *array.shape), array.dtype)
-    out = lax.dynamic_update_index_in_dim(out, array, me, 0)
-    for step in range(1, count):
-        got = lax.ppermute(array, axis, shift_perm(count, step))
-        out = lax.dynamic_update_index_in_dim(out, got, (me - step) % count, 0)
-    return out
-
-
-def swap_over(pick, axis):
+    return lax.all_to_all(jnp.broadcast_to(array[None], (count, *array.shape)), axis, 0, 0)
+
+
+def swap_over(pick, axis, after=None):
     count = lax.axis_size(axis)
     me = lax.axis_index(axis)
     if count > 8:
         return lax.all_to_all(jnp.stack([pick(i) for i in range(count)]), axis, 0, 0)
     own = pick(me)
+    picks = [pick(lax.rem(me + step, count)) for step in range(1, count)]
+    if after is not None:
+        picks, _ = lax.optimization_barrier((picks, after))
     out = jnp.zeros((count, *own.shape), own.dtype)
-    out = lax.dynamic_update_index_in_dim(out, own, me, 0)
+    out = put(out, own, me)
     for step in range(1, count):
-        got = lax.ppermute(pick((me + step) % count), axis, shift_perm(count, step))
-        out = lax.dynamic_update_index_in_dim(out, got, (me - step) % count, 0)
+        got = lax.ppermute(picks[step - 1], axis, shift_perm(count, step))
+        out = put(out, got, lax.rem(me + (count - step), count))
     return out
+
+
+RING = (0, 2, 4, 6, 7, 5, 3, 1)
+
+
+def unsigned(index):
+    return lax.convert_element_type(index, jnp.uint32)
+
+
+def put(out, piece, index):
+    return lax.dynamic_update_index_in_dim(out, piece, unsigned(index), 0)
+
+
+def ring_at(offset):
+    count = len(RING)
+    table = [RING[(RING.index(i) + offset) % count] for i in range(count)]
+    return lax.dynamic_slice(
+        jnp.array(table, jnp.uint32), (lax.axis_index("dp").astype(jnp.uint32),), (1,)
+    )[0]
+
+
+def ring_perm(step):
+    count = len(RING)
+    return [(RING[i], RING[(i + step) % count]) for i in range(count)]
+
+
+def ring_gather(piece):
+    count = lax.axis_size("dp")
+    if count != len(RING):
+        return lax.all_gather(piece, "dp", axis=0)
+    out = put(jnp.zeros((count, *piece.shape), piece.dtype), piece, lax.axis_index("dp"))
+    right = left = piece
+    for step in range(1, count // 2):
+        right = lax.ppermute(right, "dp", ring_perm(1))
+        left = lax.ppermute(left, "dp", ring_perm(-1))
+        out = put(out, right, ring_at(-step))
+        out = put(out, left, ring_at(step))
+    half = piece.shape[-2] // 2
+    right = lax.ppermute(right[..., :half, :], "dp", ring_perm(1))
+    left = lax.ppermute(left[..., half:, :], "dp", ring_perm(-1))
+    return put(out, jnp.concatenate([right, left], axis=-2), ring_at(count // 2))
+
+
+class RingScatter:
+    steps = len(RING) // 2
+
+    def __init__(self, parts):
+        self.parts = parts
+        self.ringed = lax.axis_size("dp") == len(RING)
+        self.right = self.left = None
+        if self.ringed:
+            far = self.own(self.steps)
+            self.send_right, self.send_left = far[0:1], far[1:2]
+
+    def own(self, offset):
+        return lax.dynamic_index_in_dim(self.parts, ring_at(offset), 1, keepdims=False)
+
+    def step(self, index):
+        if not self.ringed:
+            return
+        if index > 0:
+            right, left = self.own(self.steps - index), self.own(index - self.steps)
+            if index == 1:
+                right = jnp.concatenate([right[0:1] + self.right, right[1:2]])
+                left = jnp.concatenate([left[0:1], left[1:2] + self.left])
+            else:
+                right, left = right + self.right, left + self.left
+            self.send_right, self.send_left = right, left
+        self.right = lax.ppermute(self.send_right, "dp", ring_perm(1))
+        self.left = lax.ppermute(self.send_left, "dp", ring_perm(-1))
+
+    def tie(self, other):
+        if self.ringed:
+            other, self.right, self.left = lax.optimization_barrier((other, self.right, self.left))
+        return other
+
+    def total(self):
+        if not self.ringed:
+            return lax.psum_scatter(self.parts, "dp", scatter_dimension=1, tiled=True)[:, 0]
+        return self.own(0) + self.right + self.left
+
+
+def core_halves(grad, dp_count, core):
+    parts = grad.reshape(2, 2, dp_count, -1, D)
+    send = lax.dynamic_index_in_dim(parts, unsigned(1 - core), 1, keepdims=False)
+    return send, lax.dynamic_index_in_dim(parts, unsigned(core), 1, keepdims=False)
+
+
+def across_sum(parts, across):
+    send = lax.dynamic_index_in_dim(parts, unsigned(1 - across), 0, keepdims=False)
+    own = lax.dynamic_index_in_dim(parts, unsigned(across), 0, keepdims=False)
+    return own + lax.ppermute(send, "mp", flip_perm(4, 2))
+
+
+def gather_mats(own, far, across, core):
+    pair = put(jnp.stack([own, own]), far, 1 - across)
+    other = lax.ppermute(pair, "mp", flip_perm(4, 1))
+    whole = jnp.zeros((2, 2, *own.shape), own.dtype)
+    whole = lax.dynamic_update_index_in_dim(whole, pair, unsigned(core), 1)
+    whole = lax.dynamic_update_index_in_dim(whole, other, unsigned(1 - core), 1)
+    return whole.reshape(4, *own.shape)
 
 
 def adam_direction(first_mom, second_mom, beta_one, beta_two):
@@ -607,31 +771,30 @@
     col_width = block_w.shape[3]
     micro, place = mp_index % MICRO, mp_index // MICRO
     crop_count = crop_counts[micro, place]
-    own_t = jnp.concatenate(
+    across, core = mp_index // 2, mp_index % 2
+    own_t = [teacher_block[layer, :, 0].astype(bf16).T for layer in range(LAYERS)]
+    own_s = [block_w[layer, :, 0].astype(bf16).T for layer in range(LAYERS)]
+    weights = lax.all_gather(
+        jnp.concatenate([*own_t, *own_s], axis=1), ("mp", "dp"), axis=0, tiled=True
+    ).reshape(mp_count, -1, 2 * LAYERS * D)
+    head_cols = head_w.shape[1] // mp_count
+    proto_cols = proto_w.shape[1] // dp_count
+    heads = jnp.concatenate(
         [
-            part[layer, :, 0].astype(bf16).T
-            for part in (teacher_block, block_w)
-            for layer in range(LAYERS)
+            lax.dynamic_slice_in_dim(part, unsigned(mp_index * head_cols), head_cols, 1)
+            for part in (teacher_head, head_w)
         ],
         axis=1,
-    )
-    weights = lax.all_gather(own_t, ("mp", "dp"), axis=0, tiled=True)
-    weights = weights.reshape(mp_count, dp_count * col_width, 2 * LAYERS * D)
-    head_cols = head_w.shape[1] // mp_count
-    proto_cols = proto_w.shape[1] // dp_count
-
-    def take_head(part):
-        part = lax.dynamic_slice_in_dim(part, mp_index * head_cols, head_cols, 1).astype(bf16)
-        return lax.all_gather(part, "dp", axis=0, tiled=True)
-
-    def take_proto(part):
-        def pick(i):
-            return lax.dynamic_slice_in_dim(part, i * proto_cols, proto_cols, 1).astype(bf16)
-
-        return swap_over(pick, "dp").reshape(-1, proto_cols)
-
-    head_t, head_s = take_head(teacher_head), take_head(head_w)
-    proto_t, proto_s = take_proto(teacher_proto), take_proto(proto_w)
+    ).astype(bf16)
+
+    def pick_cols(i):
+        return jnp.stack(
+            [
+                lax.dynamic_slice_in_dim(part, unsigned(i * proto_cols), proto_cols, 1).astype(bf16)
+                for part in (teacher_proto, proto_w)
+            ]
+        )
+
     counts_own = jnp.stack([crop_counts[i % MICRO, i // MICRO] for i in range(mp_count)])
     counts = gather_over(counts_own[None], "dp").reshape(-1)
     other = lax.ppermute(
@@ -648,12 +811,20 @@
     seg_cls = jnp.concatenate([segment[jnp.array(starts)], jnp.zeros((CLS - CROPS,), jnp.int32)])
     seg_cls = jnp.concatenate([seg_cls, seg_cls])[:, None]
     slot = jnp.repeat(slot_live.astype(f32).reshape(mp_count, SLOT_DEV), HD, axis=1)[:, None, :]
+    protos = swap_over(pick_cols, "dp")
+    x0, weights, heads, protos, counts, seg_col, seg_row, seg_cls, slot = lax.optimization_barrier(
+        (x0, weights, heads, protos, counts, seg_col, seg_row, seg_cls, slot)
+    )
+    heads = lax.all_gather(heads, "dp", axis=0, tiled=True)
+    head_t, head_s = heads[:, :head_cols], heads[:, head_cols:]
+    protos = protos.transpose(1, 0, 2, 3).reshape(2, -1, proto_cols)
+    proto_t, proto_s = protos[0], protos[1]
     x0_t = x0[:CHUNK]
     x1_t = block_fwd(x0_t, weights, 0, teacher_norm[0:4], seg_col, seg_row, slot)[0]
+    x1, *saved0 = block_fwd(x0, weights, 2, norm_params[0:4], seg_col, seg_row, slot)
     y_t = last_fwd(
         2, x1_t, weights, 1, teacher_norm[4:8], seg_cls, segment[None, :CHUNK], slot
     )[0]
-    x1, *saved0 = block_fwd(x0, weights, 2, norm_params[0:4], seg_col, seg_row, slot)
     y_s, *saved1 = last_fwd(
         CROPS, x1, weights, 3, norm_params[4:8], seg_cls, segment[None], slot
     )
@@ -701,8 +872,7 @@
             cross.reshape(-1),
         ]
     )
-    stats = gather_over(lax.all_gather(stats[None], "mp", axis=0, tiled=True), "dp")
-    stats = stats.reshape(images, -1)
+    stats = gather_over(stats, ("dp", "mp"))
     r_s, r_t = images * CROPS, images * 2
     maxes_s, sums_s = stats[:, :r_s], stats[:, r_s : 2 * r_s]
     maxes_t, sums_t = stats[:, 2 * r_s : 2 * r_s + r_t], stats[:, 2 * r_s + r_t : 2 * (r_s + r_t)]
@@ -732,47 +902,56 @@
     grad_unit_part = mm(grad_logits, proto_s, NT)
     grad_proto = mm(z_s, grad_logits, TN)
 
-    def pick_unit(i):
-        return lax.dynamic_slice_in_dim(grad_unit_part, i * n_s, n_s, 0)
-
-    grad_unit = sum_over(jnp.sum(swap_over(pick_unit, "dp"), axis=0), ("mp",))
+    grad_unit = lax.all_to_all(grad_unit_part.reshape(dp_count, n_s, -1), "dp", 0, 0)
+    grad_unit = sum_over(jnp.sum(grad_unit, axis=0), ("mp",))
     third_s, inv_s = third[:n_s], inv[:n_s]
     along = jnp.sum(grad_unit * third_s, axis=-1, keepdims=True)
     grad_third = (inv_s * grad_unit - third_s * (inv_s * inv_s * inv_s * along)).astype(bf16)
     grad_a2 = (mm(grad_third, h3_s) * gelu_slope(a2_s)).astype(bf16)
-    grad_b1 = lax.psum_scatter(mm(grad_a2, h2_s, NT), "mp", scatter_dimension=1, tiled=True)
+    grad_b1 = mm(grad_a2, h2_s, NT).reshape(n_s, mp_count, head_cols).transpose(1, 0, 2)
+    grad_b1 = jnp.sum(lax.all_to_all(grad_b1, "mp", 0, 0), axis=0)
     grad_a1 = (grad_b1 * gelu_slope(a1_s)).astype(bf16)
     grad_feats = sum_over(mm(grad_a1, h1_s, NT), ("mp",))
     grad_cls, head_gain, head_bias = norm_back(cls_s, gain_s, grad_feats)
     grad_y = lax.dynamic_slice_in_dim(grad_cls, mp_index * CROPS, CROPS, 0)
     grad_y = jnp.concatenate([grad_y, jnp.zeros((CLS - CROPS, D), f32)], axis=0)
+    proto_square = jnp.sum(grad_proto * grad_proto)
+    proto_rows = proto_w.shape[0]
+
+    def pick_proto(i):
+        return lax.dynamic_slice_in_dim(grad_proto, unsigned(i * proto_rows), proto_rows, 0)
+
+    proto_g = swap_over(pick_proto, "dp", grad_unit)
+    proto_g = proto_g.transpose(1, 0, 2).reshape(proto_rows, -1)
+    rows_left = jnp.concatenate([feats_s, b1[:n_s], grad_third], axis=1)
+    head_rows = head_w.shape[0]
+
+    left = rows_left.reshape(n_s, dp_count, head_rows).transpose(1, 0, 2)
+    left = lax.all_to_all(left, "dp", 0, 0).reshape(dp_count * n_s, head_rows)
+    right = lax.all_gather(jnp.concatenate([grad_a1, grad_a2, b2_s], axis=1), "dp", axis=0)
+    right = right.reshape(dp_count * n_s, 3 * head_cols)
     dwt1, dgains1, grad_x1 = last_bwd(
         CROPS, x1, weights, 3, norm_params[4:8], seg_cls, segment[None], slot, saved1, grad_y
     )
-    dwt0, dgains0 = block_bwd(
-        x0, weights, 2, norm_params[0:4], seg_col, seg_row, slot, saved0, grad_x1
-    )
-    block_g = jnp.concatenate(
-        [
-            lax.psum_scatter(
-                dwt.reshape(-1, D), ("mp", "dp"), scatter_dimension=0, tiled=True
-            )
-            for dwt in (dwt0, dwt1)
-        ],
-        axis=1,
-    )
-    rows_left = jnp.concatenate([feats_s, b1[:n_s], grad_third], axis=1)
-    head_rows = head_w.shape[0]
-
-    def pick_left(i):
-        return lax.dynamic_slice_in_dim(rows_left, i * head_rows, head_rows, 1)
-
-    left = swap_over(pick_left, "dp").reshape(dp_count * n_s, head_rows)
-    right = gather_over(jnp.concatenate([grad_a1, grad_a2, b2_s], axis=1), "dp")
-    right = right.reshape(dp_count * n_s, 3 * head_cols)
+    send1, own1 = core_halves(dwt1, dp_count, core)
+    grad_x1, send1 = lax.optimization_barrier((grad_x1, send1))
+    got1 = lax.ppermute(send1, "mp", flip_perm(4, 1))
+    dwt0, dgains0b, grad_x2 = mlp_bwd(weights, 2, norm_params[0:4], saved0[3], grad_x1)
+    grad_x2, got1 = lax.optimization_barrier((grad_x2, got1))
+    ring1 = RingScatter(own1 + got1)
+    ring1.step(0)
+    block_args = (weights, 2, norm_params[0:4], seg_col, seg_row, slot, saved0)
+    dwt0, grad_h1 = attention_bwd(0, *block_args, grad_x2, dwt0)
+    grad_h1 = ring1.tie(grad_h1)
+    ring1.step(1)
+    dwt0, dgains0a = attention_bwd(1, *block_args, grad_x2, dwt0, (x0, grad_h1))
+    send0, own0 = core_halves(dwt0, dp_count, core)
+    send0, proto_g, left, right = lax.optimization_barrier(
+        (ring1.tie(send0), proto_g, left, right)
+    )
     stack_ids = dp_index * head_rows + jnp.arange(head_rows)[None, :]
     edges = (0, D, D + HID, D + HID + third.shape[1])
-    head_g = sum(
+    head_own = sum(
         mm(
             jnp.where((stack_ids >= edges[i]) & (stack_ids < edges[i + 1]), left, 0).astype(bf16),
             right[:, i * head_cols : (i + 1) * head_cols],
@@ -780,61 +959,106 @@
         )
         for i in range(3)
     )
-    head_square = jnp.sum(head_g * head_g)
-    head_g = lax.all_gather(head_g, "mp", axis=1, tiled=True)
-    proto_square = jnp.sum(grad_proto * grad_proto)
-    proto_rows = proto_w.shape[0]
-
-    def pick_proto(i):
-        return lax.dynamic_slice_in_dim(grad_proto, i * proto_rows, proto_rows, 0)
-
-    proto_g = swap_over(pick_proto, "dp")
-    proto_g = proto_g.transpose(1, 0, 2).reshape(proto_rows, -1)
+    ring1.step(2)
+    ring0 = RingScatter(own0 + lax.ppermute(send0, "mp", flip_perm(4, 1)))
+    ring0.step(0)
+    ring1.step(3)
+    block_g1 = across_sum(ring1.total(), across)
+    for index in range(1, RingScatter.steps):
+        ring0.step(index)
+    block_g = jnp.stack([across_sum(ring0.total(), across), block_g1])
+    head_square = jnp.sum(head_own * head_own)
     center_total = gather_over(center_part, "dp").reshape(-1)
     head_first = (mp_index == 0).astype(f32)
-    square = jnp.sum(block_g * block_g) + head_square + proto_square
+    square = head_square + proto_square
     norm_part = jnp.concatenate(
         [
-            dgains0,
+            dgains0a,
+            dgains0b,
             dgains1,
             head_first * head_gain,
             head_first * head_bias,
             jnp.full((1, D), square),
+            jnp.zeros((5, D), f32),
         ],
         axis=0,
     )
-    norm_sum = sum_over(norm_part, ("mp", "dp"))
+    norm_part = sum_over(norm_part, ("mp",))
+    norm_rows_sent = thirds(norm_part).reshape(LAYERS, -1, D)
+    columns = jnp.concatenate([block_g.astype(bf16), norm_rows_sent], axis=1)
+    columns = ring_gather(columns).transpose(1, 0, 2, 3)
+    norm_sum = whole_of(columns[:, :, col_width:])
     norm_total = norm_sum[:10]
-    grad_norm = jnp.sqrt(norm_sum[10, 0] + jnp.sum(norm_total * norm_total))
+    columns = columns[:, :, :col_width].reshape(LAYERS, dp_count * col_width, D)
+    wide = columns.astype(f32)
+    block_square = sum_over(jnp.full((1, 128), jnp.sum(wide * wide)), ("mp",))[0, 0]
+    grad_norm = jnp.sqrt(norm_sum[10, 0] + block_square + jnp.sum(norm_total * norm_total))
     clip_factor = jnp.minimum(1.0, CLIP_NORM / (grad_norm + 1e-06))
-    grads_all = lax.all_gather(block_g.astype(bf16), ("mp", "dp"), axis=0, tiled=True)
-    grads_all = grads_all.reshape(mp_count, dp_count * col_width, LAYERS * D)
-    new_stats, new_bases = renew_bases(clip_factor, grads_all, precond_stats, rotation_bases)
+    bounds = (0, 384, 512, 896, 1280)
+    longest = 384
+
+    def kind_rows(kind):
+        start = jnp.array(bounds[:4])[kind]
+        rows = lax.dynamic_slice_in_dim(columns, start, longest, 1)
+        inside = start + jnp.arange(longest) < jnp.array(bounds[1:])[kind]
+        return jnp.where(inside[None, :, None], rows, 0).astype(bf16)
+
+    kinds = [kind_rows(mp_index)] + [
+        lax.ppermute(kind_rows(mp_index ^ flip), "mp", flip_perm(mp_count, flip))
+        for flip in (1, 2, 3)
+    ]
+    kinds = jnp.concatenate(kinds, axis=1)
+    stat = lax.dot_general(
+        kinds, kinds, (((1,), (1,)), ((0,), (0,))), preferred_element_type=f32
+    )
+    stats_own = lax.dynamic_index_in_dim(precond_stats, mp_index, 1, keepdims=False)
+    bases_own = lax.dynamic_index_in_dim(rotation_bases, mp_index, 1, keepdims=False)
+    stats_own = SHAMPOO_BETA * stats_own + (1 - SHAMPOO_BETA) * (clip_factor * clip_factor) * stat
+    far_stats = lax.ppermute(stats_own, "mp", flip_perm(4, 2))
+    stats_own, head_own = lax.optimization_barrier((stats_own, head_own))
+    far_head = lax.ppermute(head_own, "mp", flip_perm(4, 2))
+    basis_own, late_clip, far_head = lax.optimization_barrier(
+        (renew_bases(stats_own, bases_own), clip_factor, far_head)
+    )
+    head_g = gather_mats(head_own, far_head, across, core).transpose(1, 0, 2)
+    head_g = head_g.reshape(head_rows, -1)
+    new_head_w, new_head_m, new_head_v = adamw(
+        head_w, late_clip * head_g, head_m, head_v, LR_HEAD, WEIGHT_DECAY
+    )
+    new_proto_w, new_proto_m, new_proto_v = adamw(
+        proto_w, late_clip * proto_g, proto_m, proto_v, LR_PROTO, WEIGHT_DECAY
+    )
+    new_teacher_head = TEACHER_MOM * teacher_head + (1 - TEACHER_MOM) * new_head_w
+    new_teacher_proto = TEACHER_MOM * teacher_proto + (1 - TEACHER_MOM) * new_proto_w
+    beside = (
+        new_head_w, new_head_m, new_head_v, new_proto_w, new_proto_m, new_proto_v,
+        new_teacher_head, new_teacher_proto,
+    )
+    far_bases = lax.ppermute(basis_own, "mp", flip_perm(4, 2))
+    far_stats, far_bases, beside = lax.optimization_barrier((far_stats, far_bases, beside))
+    new_bases = gather_mats(basis_own, far_bases, across, core)
+    new_stats = gather_mats(stats_own, far_stats, across, core).transpose(1, 0, 2, 3)
+    (
+        new_head_w, new_head_m, new_head_v, new_proto_w, new_proto_m, new_proto_v,
+        new_teacher_head, new_teacher_proto,
+    ) = beside
+    new_bases = new_bases.transpose(1, 0, 2, 3)
     col_ids = dp_index * col_width + jnp.arange(col_width)
-    bounds = (0, 384, 512, 896, 1280)
     col_masks = jnp.stack(
         [((col_ids >= bounds[k]) & (col_ids < bounds[k + 1])).astype(f32) for k in range(4)]
     )
-    grad_cols = (clip_factor * block_g).reshape(col_width, LAYERS, D)
-    rotated = jnp.einsum("lkde,cld,kc->lec", new_bases, grad_cols, col_masks, precision=precise)
+    grad_cols = clip_factor * block_g
+    rotated = jnp.einsum("lkde,lcd,kc->lec", new_bases, grad_cols, col_masks, precision=precise)
     first_mom = ROT_ONE * block_m[:, :, 0] + (1 - ROT_ONE) * rotated
     second_mom = ROT_TWO * block_v[:, :, 0] + (1 - ROT_TWO) * rotated * rotated
     direction = adam_direction(first_mom, second_mom, ROT_ONE, ROT_TWO)
     turned_back = jnp.einsum("lkde,lec,kc->ldc", new_bases, direction, col_masks, precision=precise)
     master = block_w[:, :, 0]
     new_block_w = (master - LR_BLOCK * (turned_back + WEIGHT_DECAY * master))[:, :, None]
-    new_head_w, new_head_m, new_head_v = adamw(
-        head_w, clip_factor * head_g, head_m, head_v, LR_HEAD, WEIGHT_DECAY
-    )
-    new_proto_w, new_proto_m, new_proto_v = adamw(
-        proto_w, clip_factor * proto_g, proto_m, proto_v, LR_PROTO, WEIGHT_DECAY
-    )
     new_norm, new_norm_m, new_norm_v = adamw(
         norm_params, clip_factor * norm_total, norm_m, norm_v, LR_NORM, 0.0
     )
     new_teacher_block = TEACHER_MOM * teacher_block + (1 - TEACHER_MOM) * new_block_w
-    new_teacher_head = TEACHER_MOM * teacher_head + (1 - TEACHER_MOM) * new_head_w
-    new_teacher_proto = TEACHER_MOM * teacher_proto + (1 - TEACHER_MOM) * new_proto_w
     new_teacher_norm = TEACHER_MOM * teacher_norm + (1 - TEACHER_MOM) * new_norm
     new_center = CENTER_MOM * center + (1 - CENTER_MOM) * center_total / (2.0 * images)
     return (

time: 1050 us -> 810 us (0.77)
  waiting for transfers between devices: 413 us -> 242 us
  Pallas kernels: 290 us -> 172 us
  starting transfers between devices: 151 us -> 104 us
  other arithmetic: 44.4 us -> 86.4 us
  local copies, waits for them, and re-layouts: 68.8 us -> 97.7 us
  blocking collectives: 16.2 us -> 27 us
    reduce_scatter x3 -> x0, waiting for transfers between devices: 234 us -> none  [the longest x2 212 us: shards(): lax.psum_scatter(dwt.reshape(-1, D), ('mp', 'dp'), scatter_dimension=0, t...]
    pallas_call x2 -> x4, Pallas kernels: 219 us -> 101 us  [the longest x1 51.1 us: renew_bases(): pl.pallas_call(basis_kernel, in_specs=[pl.BlockSpec(memory_space=pltpu.VM...]
    ppermute x70 -> x51, starting transfers between devices: 126 us -> 74.8 us  [the longest x14 28.6 us: swap_over(): got = lax.ppermute(picks[step - 1], axis, shift_perm(count, step))]
    all_to_all x0 -> x6, waiting for transfers between devices: none -> 43.8 us  [the longest x4 40.9 us: gather_over(): lax.all_to_all(jnp.broadcast_to(array[None], (count, *array.shape)), axis...]
    ppermute x70 -> x51, waiting for transfers between devices: 57.6 us -> 91.1 us  [the longest x8 29.8 us: step(): self.left = lax.ppermute(self.send_left, 'dp', ring_perm(-1))]
    all_gather x5 -> x3, waiting for transfers between devices: 103 us -> 78.1 us  [the longest x1 56.1 us: shards(): lax.all_gather(jnp.concatenate([*own_t, *own_s], axis=1), ('mp', 'dp'), a...]
    add x0 -> x12, other arithmetic: none -> 25 us  [the longest x6 12.8 us: step(): right, left = (right + self.right, left + self.left)]
    all_to_all x0 -> x6, starting transfers between devices: none -> 22.9 us  [the longest x4 15.8 us: gather_over(): lax.all_to_all(jnp.broadcast_to(array[None], (count, *array.shape)), axis...]
  transfers between devices with their start and end apart: 90 -> 71, of which waited for: 33 -> 32; matrix products, arithmetic and copies ran while one was open for 9% -> 20% of each run, Pallas kernels for 5% -> 21%
where the time goes in v2:
time: 810 us; the launch traced here: 803 us
  waiting for transfers between devices  242 us (30%)
  Pallas kernels  172 us (21%)
  starting transfers between devices  104 us (13%)
  local copies, waits for them, and re-layouts  97.7 us (12%)
  other arithmetic  86.4 us (11%)
  matrix products  45.7 us (6%)
  between operations  28.4 us (4%)
  blocking collectives  27 us (3%)
    all_gather x1, waiting for transfers between devices, shards(): lax.all_gather(jnp.concatenate([*own_t, *own_s], axis=1), ('mp', 'dp'), a...  56.1 us
    pallas_call x1, Pallas kernels, renew_bases(): pl.pallas_call(basis_kernel, in_specs=[pl.BlockSpec(memory_space=pltpu.VM...  51.1 us
    all_to_all x4, waiting for transfers between devices, gather_over(): lax.all_to_all(jnp.broadcast_to(array[None], (count, *array.shape)), axis...  40.9 us
    pallas_call x2, Pallas kernels, block_fwd(): pl.pallas_call(block_fwd_kernel, grid=(rows // CHUNK,), in_specs=[s['row'...  36.4 us
    dot_general x18, matrix products, mm(): lax.dot_general(lhs, rhs, dims, precision=precision, preferred_element_ty...  30.8 us
    pallas_call x2, Pallas kernels, attention_bwd(): pl.pallas_call(functools.partial(attention_bwd_kernel, bool(last)), grid=...  30.5 us
    ppermute x8, waiting for transfers between devices, step(): self.left = lax.ppermute(self.send_left, 'dp', ring_perm(-1))  29.8 us
    ppermute x10, waiting for transfers between devices, sum_over(): array = array + lax.ppermute(array, axis, flip_perm(count, bit))  28.9 us
  transfers between devices with their start and end apart: 71, of which 32 were waited for; matrix products, arithmetic and copies ran while one was open for 20% of the time, Pallas kernels for 21%

profile of v2, /device:TPU:0, one launch (start us, length us, event | category | flops | bytes accessed | tf_op | source)
XLA Modules:
  0.0 803.0 jit_solution(13693075097840792248)
XLA Ops:
  13.8 3.0 collective-permute-start.1
  31.6 3.3 all-to-all-start
  44.0 32.2 %all-to-all-done = s32[8,1,4]{2,1,0:T(1,128)S(1)} async-done(((s32[8,1,4]{2,1,0:T(1,128)}), s32[8,1,4]{2,1,0:T(1,128)S(1)}, u32[]{:S(2)}, u32[]{:S(2)}) %all-to-all-start) | async-done | bytes 160 | tf_op jit(solution)/shard_map/all_to_all | solution.py:611
  77.4 4.6 collective-permute-start.6
  88.0 7.0 collective-permute-done.6
  98.7 56.1 %all-gather.6.cloned.1.call-done = bf16[5120,1536]{1,0:T(8,128)(2,1)} async-done(((bf16[160,1536]{1,0:T(8,128)(2,1)}), bf16[5120,1536]{1,0:T(8,128)(2,1)}) %all-gather.6.cloned.1.call-update) | async-done | bytes 15728656 | tf_op jit(solution)/shard_map/all_gather | solution.py:777
  160.2 12.9 %shard_map.663 = (f32[400,384]{1,0:T(8,128)}, bf16[400,384]{1,0:T(8,128)(2,1)}, bf16[4,400,384]{2,1,0:T(8,128)(2,1)}, bf16[4,400,128]{2,1,0:T(8,128)(2,1)}, f32[400,384]{1,0:T(8,128)}) custom-call(f32[400,384]{1,0:T(8,128)} %slice.266.x_ref, bf16[4,1280,1536]{2,1,0:T(8,128)(2,1)} %bitcast.491, f32[4,384]{1,0:T(4,128)} %get-tuple-element.358.gains_ref, ...), custom_call_target="tpu_custom_call" | custom-call | flops 12000000000 | bytes 8000000 | tf_op jit(solution)/shard_map/pallas_call | solution.py:242
  173.1 8.4 %shard_map.664 = (f32[16,384]{1,0:T(8,128)}, bf16[400,384]{1,0:T(8,128)(2,1)}, bf16[4,400,256]{2,1,0:T(8,128)(2,1)}, bf16[4,16,128]{2,1,0:T(8,128)(2,1)}, bf16[4...) custom-call(f32[400,384]{1,0:T(8,128)} %get-tuple-element.97.x_ref, bf16[4,1280,1536]{2,1,0:T(8,128)(2,1)} %bitcast.492, ...), custom_call_target="tpu_custom_call" | custom-call | flops 6000000000 | bytes 8000000 | tf_op jit(solution)/shard_map/pallas_call | solution.py:456
  182.2 23.5 %shard_map.661 = (f32[800,384]{1,0:T(8,128)}, bf16[800,384]{1,0:T(8,128)(2,1)}, bf16[4,800,384]{2,1,0:T(8,128)(2,1)}, bf16[4,800,128]{2,1,0:T(8,128)(2,1)}, f32[800,384]{1,0:T(8,128)}) custom-call(f32[800,384]{1,0:T(8,128)} %copy-done.37, bf16[4,1280,1536]{2,1,0:T(8,128)(2,1)} %bitcast.493, f32[4,384]{1,0:T(4,128)} %get-tuple-element.356.gains_ref, ...), custom_call_target="tpu_custom_call" | custom-call | flops 24000000000 | bytes 8000000 | tf_op jit(solution)/shard_map/pallas_call | solution.py:242
  205.7 10.0 %shard_map.662 = (f32[16,384]{1,0:T(8,128)}, bf16[800,384]{1,0:T(8,128)(2,1)}, bf16[4,800,256]{2,1,0:T(8,128)(2,1)}, bf16[4,16,128]{2,1,0:T(8,128)(2,1)}, bf16[4...) custom-call(f32[800,384]{1,0:T(8,128)} %get-tuple-element.94.x_ref, bf16[4,1280,1536]{2,1,0:T(8,128)(2,1)} %bitcast.494, ...), custom_call_target="tpu_custom_call" | custom-call | flops 12000000000 | bytes 8000000 | tf_op jit(solution)/shard_map/pallas_call | solution.py:456
  216.4 5.3 all-gather
  223.4 21.9 %all-gather.8.cloned.1.call-done = bf16[2688,1024]{1,0:T(8,128)(2,1)} async-done(((bf16[336,1024]{1,0:T(8,128)(2,1)}), bf16[2688,1024]{1,0:T(8,128)(2,1)}) %all-gather.8.cloned.1.call-update) | async-done | bytes 5505040 | tf_op jit(solution)/shard_map/all_gather | solution.py:818
  248.4 5.7 all_gather.25
  267.2 3.6 all-to-all-start.1
  272.3 6.5 all-to-all-done.1
  283.4 3.7 convolution_select_fusion
  291.4 3.3 all-to-all-start.2
  322.6 4.5 multiply_convert_fusion
  328.9 15.9 %all_to_all.40 = f32[8,48,256]{2,1,0:T(8,128)S(1)} all-to-all(f32[8,48,256]{2,1,0:T(8,128)S(1)} %fusion.247), channel_id=1, replica_groups=mesh['dp'=8,'mp'=4] {'dp'}, dimensions={0} | all-to-all | bytes 786432 | tf_op jit(solution)/shard_map/all_to_all | solution.py:905
  355.5 3.7 all-to-all-start.4
  369.1 3.4 all-to-all-start.5
  387.6 16.1 %shard_map.665 = (f32[4,1280,384]{2,1,0:T(8,128)}, f32[4,384]{1,0:T(4,128)}, f32[800,384]{1,0:T(8,128)}) custom-call(f32[800,384]{1,0:T(8,128)} %get-tuple-element.94.x_ref, bf16[4,1280,1536]{2,1,0:T(8,128)(2,1)} %bitcast.495, f32[4,384]{1,0:T(4,128)} %get-tuple-element.355.gains_ref, s32[32,1]{1,0:T(8,128)} %copy.218.seg_cls_ref, ...), custom_call_target="tpu_custom_call" | custom-call | flops 16000000000 | bytes 16000000 | tf_op jit(solution)/shard_map/pallas_call | solution.py:476
  403.7 4.3 dynamic-slice_bitcast_fusion.1
  422.4 19.1 %shard_map.666 = (f32[4,1280,384]{2,1,0:T(8,128)}, f32[2,384]{1,0:T(2,128)}, f32[800,384]{1,0:T(8,128)}) custom-call(bf16[4,1280,1536]{2,1,0:T(8,128)(2,1)} %bitcast.496, f32[4,384]{1,0:T(4,128)} %get-tuple-element.356.gains_ref, f32[800,384]{1,0:T(8,128)} %get-tuple-element.105.x2_ref, f32[800,384]{1,0:T(8,128)} %get-tuple-element.113.grad_ref), custom_call_target="tpu_custom_call" | custom-call | flops 19200000000 | bytes 16000000 | tf_op jit(solution)/shard_map/pallas_call | solution.py:264
  441.5 3.9 bitcast_add_fusion.1
  447.3 13.2 %collective-permute-start.15 = (f32[1,160,384]{2,1,0:T(8,128)S(1)}, f32[1,160,384]{2,1,0:T(8,128)S(1)}, u32[]{:S(2)}, u32[]{:S(2)}) collective-permute-start(f32[1,160,384]{2,1,0:T(8,128)S(1)} %get-tuple-element.308), channel_id=1, source_target_pairs={{0,8},{8,16},{16,24},{24,28},{28,20},{20,12},{12,4},{4,0},{1,9},{9... | collective-permute-start | bytes 737288 | tf_op jit(solution)/shard_map/ppermute | solution.py:697
  460.8 14.8 %shard_map.667 = (f32[4,1280,384]{2,1,0:T(8,128)}, f32[800,384]{1,0:T(8,128)}) custom-call(bf16[4,1280,1536]{2,1,0:T(8,128)(2,1)} %bitcast.497, f32[4,384]{1,0:T(4,128)} %get-tuple-element.356.gains_ref, s32[2,400,1]{2,1,0:T(8,128)} %add_select_fusion.4.seg_col_ref, s32[2,1,400]{2,1,0:T(1,128)} %and_select_fusion.seg_row_ref, ...), custom_call_target="tpu_custom_call", output_to_operand_aliasing={{0}: (9, {})} | custom-call | flops 15200000000 | bytes 8000000 | tf_op jit(solution)/shard_map/pallas_call | solution.py:296
  479.5 15.6 %shard_map.668 = (f32[4,1280,384]{2,1,0:T(8,128)}, f32[2,384]{1,0:T(2,128)}) custom-call(bf16[4,1280,1536]{2,1,0:T(8,128)(2,1)} %bitcast.498, f32[4,384]{1,0:T(4,128)} %get-tuple-element.356.gains_ref, s32[2,400,1]{2,1,0:T(8,128)} %add_select_fusion.4.seg_col_ref, s32[2,1,400]{2,1,0:T(1,128)} %and_select_fusion.seg_row_ref, ...), custom_call_target="tpu_custom_call", output_to_operand_aliasing={{0}: (11, {})} | custom-call | flops 15200000000 | bytes 8000000 | tf_op jit(solution)/shard_map/pallas_call | solution.py:296
  495.2 4.3 dynamic-slice_bitcast_fusion
  503.6 3.1 collective-permute-done.26
  506.8 3.7 bitcast_add_fusion
  526.1 15.4 %collective-permute-done.28 = f32[2,160,384]{2,1,0:T(8,128)S(1)} collective-permute-done((f32[2,160,384]{2,1,0:T(8,128)S(1)}, f32[2,160,384]{2,1,0:T(8,128)S(1)}, u32[]{:S(2)}, u32[]{:S(2)}) %collective-permute-start.28) | collective-permute-done | bytes 491552 | tf_op jit(solution)/shard_map/ppermute | solution.py:697
  560.6 6.7 collective-permute-done.38
  571.1 6.7 collective-permute-done.33
  579.8 8.6 %collective-permute-done.39 = f32[2,160,384]{2,1,0:T(8,128)S(1)} collective-permute-done((f32[2,160,384]{2,1,0:T(8,128)S(1)}, f32[2,160,384]{2,1,0:T(8,128)S(1)}, u32[]{:S(2)}, u32[]{:S(2)}) %collective-permute-start.39) | collective-permute-done | bytes 491552 | tf_op jit(solution)/shard_map/ppermute | solution.py:698
  591.3 6.9 collective-permute-done.34
  601.2 5.5 collective-permute-done.35
  621.6 5.6 all-to-all-start.6
  631.1 3.7 collective-permute-done.45
  638.6 4.6 collective-permute-done.47
  659.9 22.9 %collective-permute-done.52 = f32[1,128]{1,0:T(1,128)S(1)} collective-permute-done((f32[1,128]{1,0:T(1,128)S(1)}, f32[1,128]{1,0:T(1,128)S(1)}, u32[]{:S(2)}, u32[]{:S(2)}) %collective-permute-start.52) | collective-permute-done | bytes 544 | tf_op jit(solution)/shard_map/ppermute | solution.py:599
  684.9 4.9 fusion.41.stats_ref
  691.8 51.1 %shard_map.669 = f32[2,384,384]{2,1,0:T(8,128)} custom-call(f32[2,384,384]{2,1,0:T(8,128)} %fusion.41.stats_ref, f32[2,384,384]{2,1,0:T(8,128)} %dynamic-slice_bitcast_fusion.2.bases_ref), custom_call_target="tpu_custom_call" | custom-call | flops 60000002048 | bytes 6000000 | tf_op jit(solution)/shard_map/pallas_call | solution.py:556
  745.8 6.9 multiply_add_fusion.2
  757.7 5.3 multiply_add_fusion
  763.0 8.6 %collective-permute-done.58 = f32[2,384,384]{2,1,0:T(8,128)S(1)} collective-permute-done((f32[2,384,384]{2,1,0:T(8,128)S(1)}, f32[2,384,384]{2,1,0:T(8,128)S(1)}, u32[]{:S(2)}, u32[]{:S(2)}) %collective-permute-start.58) | collective-permute-done | bytes 1179680 | tf_op jit(solution)/shard_map/ppermute | solution.py:1037
  781.5 5.1 fusion.134
  786.6 4.9 fusion.37
  (559 shorter events, 264.5 us)
Async XLA Ops:
  7.2 147.6 %all-gather.6.cloned.1.call-start = ((), (), s32[]{:S(2)}) async-start(), calls=%async_computation.7 | async-start | bytes 16220160 | tf_op jit(solution)/shard_map/all_gather | solution.py:777
  13.8 63.6 %collective-permute-start.1 = (bf16[2,32,2048]{2,1,0:T(8,128)(2,1)}, bf16[2,32,2048]{2,1,0:T(8,128)(2,1)}, u32[]{:S(2)}, u32[]{:S(2)}) collective-permute-start(bf16[2,32,2048]{2,1,0:T(8,128)(2,1)} %pad_maximum_fusion.11), channel_id=1, source_target_pairs={{0,4},{4,8},{8,12},{12,16},{16,20},{20,24},{24,28},{28,0},{1,5},{5... | collective-permute-start | bytes 786440 | tf_op jit(solution)/shard_map/ppermute | solution.py:626
  17.6 65.4 %collective-permute-start.2 = (bf16[2,32,2048]{2,1,0:T(8,128)(2,1)}, bf16[2,32,2048]{2,1,0:T(8,128)(2,1)}, u32[]{:S(2)}, u32[]{:S(2)}) collective-permute-start(bf16[2,32,2048]{2,1,0:T(8,128)(2,1)} %pad_maximum_fusion.12), channel_id=1, source_target_pairs={{0,8},{4,12},{8,16},{12,20},{16,24},{20,28},{24,0},{28,4},{1,9},{5... | collective-permute-start | bytes 786440 | tf_op jit(solution)/shard_map/ppermute | solution.py:626
  19.8 65.1 %collective-permute-start.3 = (bf16[2,32,2048]{2,1,0:T(8,128)(2,1)}, bf16[2,32,2048]{2,1,0:T(8,128)(2,1)}, u32[]{:S(2)}, u32[]{:S(2)}) collective-permute-start(bf16[2,32,2048]{2,1,0:T(8,128)(2,1)} %pad_maximum_fusion.13), channel_id=1, source_target_pairs={{0,12},{4,16},{8,20},{12,24},{16,28},{20,0},{24,4},{28,8},{1,13},{... | collective-permute-start | bytes 786440 | tf_op jit(solution)/shard_map/ppermute | solution.py:626
  23.1 63.0 %collective-permute-start.4 = (bf16[2,32,2048]{2,1,0:T(8,128)(2,1)}, bf16[2,32,2048]{2,1,0:T(8,128)(2,1)}, u32[]{:S(2)}, u32[]{:S(2)}) collective-permute-start(bf16[2,32,2048]{2,1,0:T(8,128)(2,1)} %pad_maximum_fusion.14), channel_id=1, source_target_pairs={{0,16},{4,20},{8,24},{12,28},{16,0},{20,4},{24,8},{28,12},{1,17},{... | collective-permute-start | bytes 786440 | tf_op jit(solution)/shard_map/ppermute | solution.py:626
  25.1 62.0 %collective-permute-start.5 = (bf16[2,32,2048]{2,1,0:T(8,128)(2,1)}, bf16[2,32,2048]{2,1,0:T(8,128)(2,1)}, u32[]{:S(2)}, u32[]{:S(2)}) collective-permute-start(bf16[2,32,2048]{2,1,0:T(8,128)(2,1)} %pad_maximum_fusion.15), channel_id=1, source_target_pairs={{0,20},{4,24},{8,28},{12,0},{16,4},{20,8},{24,12},{28,16},{1,21},{... | collective-permute-start | bytes 786440 | tf_op jit(solution)/shard_map/ppermute | solution.py:626
  31.6 44.6 %all-to-all-start = ((s32[8,1,4]{2,1,0:T(1,128)}), s32[8,1,4]{2,1,0:T(1,128)S(1)}, u32[]{:S(2)}, u32[]{:S(2)}) async-start(s32[8,1,4]{2,1,0:T(1,128)} %broadcast_in_dim.304), calls=%async_computation | async-start | bytes 8192 | tf_op jit(solution)/shard_map/all_to_all | solution.py:611
  34.9 210.4 %all-gather.8.cloned.1.call-start = ((), (), s32[]{:S(2)}) async-start(), calls=%async_computation.8 | async-start | bytes 6193152 | tf_op jit(solution)/shard_map/all_gather | solution.py:818
  77.4 17.6 %collective-permute-start.6 = (bf16[2,32,2048]{2,1,0:T(8,128)(2,1)}, bf16[2,32,2048]{2,1,0:T(8,128)(2,1)S(1)}, u32[]{:S(2)}, u32[]{:S(2)}) collective-permute-start(bf16[2,32,2048]{2,1,0:T(8,128)(2,1)} %pad_maximum_fusion.16), channel_id=1, source_target_pairs={{0,24},{4,28},{8,0},{12,4},{16,8},{20,12},{24,16},{28,20},{1,25},{... | collective-permute-start | bytes 786440 | tf_op jit(solution)/shard_map/ppermute | solution.py:626
  83.0 14.7 %collective-permute-start.7 = (bf16[2,32,2048]{2,1,0:T(8,128)(2,1)}, bf16[2,32,2048]{2,1,0:T(8,128)(2,1)S(1)}, u32[]{:S(2)}, u32[]{:S(2)}) collective-permute-start(bf16[2,32,2048]{2,1,0:T(8,128)(2,1)} %pad_maximum_fusion.17), channel_id=1, source_target_pairs={{0,28},{4,0},{8,4},{12,8},{16,12},{20,16},{24,20},{28,24},{1,29},{... | collective-permute-start | bytes 786440 | tf_op jit(solution)/shard_map/ppermute | solution.py:626
  85.0 12.7 %collective-permute-start = (bf16[384,384]{1,0:T(8,128)(2,1)S(1)}, bf16[384,384]{1,0:T(8,128)(2,1)S(1)}, u32[]{:S(2)}, u32[]{:S(2)}) collective-permute-start(bf16[384,384]{1,0:T(8,128)(2,1)S(1)} %copy-done.38), channel_id=1, source_target_pairs={{0,1},{1,0},{2,3},{3,2},{4,5},{5,4},{6,7},{7,6},{8,9},{9,8},{10,11... | collective-permute-start | bytes 884744 | tf_op jit(solution)/shard_map/ppermute | solution.py:800
  267.2 11.6 %all-to-all-start.1 = ((bf16[8,56,256]{2,1,0:T(8,128)(2,1)}), bf16[8,56,256]{2,1,0:T(8,128)(2,1)S(1)}, u32[]{:S(2)}, u32[]{:S(2)}) async-start(bf16[8,56,256]{2,1,0:T(8,128)(2,1)} %broadcast_in_dim.315), calls=%async_computation.1 | async-start | bytes 458752 | tf_op jit(solution)/shard_map/all_to_all | solution.py:611
  291.4 12.7 %all-to-all-start.2 = ((f32[32,1,1664]{2,1,0:T(1,128)}), f32[32,1,1664]{2,1,0:T(1,128)S(1)}, u32[]{:S(2)}, u32[]{:S(2)}) async-start(f32[32,1,1664]{2,1,0:T(1,128)} %broadcast_in_dim.317), calls=%async_computation.2 | async-start | bytes 425984 | tf_op jit(solution)/shard_map/all_to_all | solution.py:611
  362.5 18.2 %collective-permute-start.19 = (f32[32,2048]{1,0:T(8,128)}, f32[32,2048]{1,0:T(8,128)S(1)}, u32[]{:S(2)}, u32[]{:S(2)}) collective-permute-start(f32[32,2048]{1,0:T(8,128)} %get-tuple-element.126), channel_id=1, source_target_pairs={{0,4},{4,8},{8,12},{12,16},{16,20},{20,24},{24,28},{28,0},{1,5},{5... | collective-permute-start | bytes 786440 | tf_op jit(solution)/shard_map/ppermute | solution.py:626
  369.1 130.4 %all-to-all-start.5 = ((bf16[8,48,336]{2,1,0:T(8,128)(2,1)}), bf16[8,48,336]{2,1,0:T(8,128)(2,1)S(1)}, u32[]{:S(2)}, u32[]{:S(2)}) async-start(bf16[8,48,336]{2,1,0:T(8,128)(2,1)} %bitcast.437), calls=%async_computation.5 | async-start | bytes 589824 | tf_op jit(solution)/shard_map/all_to_all | solution.py:930
  372.6 127.0 %all-gather.10.cloned.1.call-start = ((), (), s32[]{:S(2)}) async-start(), calls=%async_computation.9 | async-start | bytes 1327104 | tf_op jit(solution)/shard_map/all_gather | solution.py:931
  372.6 35.4 %collective-permute-start.20 = (f32[32,2048]{1,0:T(8,128)}, f32[32,2048]{1,0:T(8,128)S(1)}, u32[]{:S(2)}, u32[]{:S(2)}) collective-permute-start(f32[32,2048]{1,0:T(8,128)} %get-tuple-element.127), channel_id=1, source_target_pairs={{0,8},{4,12},{8,16},{12,20},{16,24},{20,28},{24,0},{28,4},{1,9},{5... | collective-permute-start | bytes 786440 | tf_op jit(solution)/shard_map/ppermute | solution.py:626
  374.5 34.2 %collective-permute-start.21 = (f32[32,2048]{1,0:T(8,128)}, f32[32,2048]{1,0:T(8,128)S(1)}, u32[]{:S(2)}, u32[]{:S(2)}) collective-permute-start(f32[32,2048]{1,0:T(8,128)} %get-tuple-element.128), channel_id=1, source_target_pairs={{0,12},{4,16},{8,20},{12,24},{16,28},{20,0},{24,4},{28,8},{1,13},{... | collective-permute-start | bytes 786440 | tf_op jit(solution)/shard_map/ppermute | solution.py:626
  376.9 34.6 %collective-permute-start.22 = (f32[32,2048]{1,0:T(8,128)}, f32[32,2048]{1,0:T(8,128)S(1)}, u32[]{:S(2)}, u32[]{:S(2)}) collective-permute-start(f32[32,2048]{1,0:T(8,128)} %get-tuple-element.129), channel_id=1, source_target_pairs={{0,16},{4,20},{8,24},{12,28},{16,0},{20,4},{24,8},{28,12},{1,17},{... | collective-permute-start | bytes 786440 | tf_op jit(solution)/shard_map/ppermute | solution.py:626
  378.3 33.9 %collective-permute-start.23 = (f32[32,2048]{1,0:T(8,128)}, f32[32,2048]{1,0:T(8,128)S(1)}, u32[]{:S(2)}, u32[]{:S(2)}) collective-permute-start(f32[32,2048]{1,0:T(8,128)} %get-tuple-element.130), channel_id=1, source_target_pairs={{0,20},{4,24},{8,28},{12,0},{16,4},{20,8},{24,12},{28,16},{1,21},{... | collective-permute-start | bytes 786440 | tf_op jit(solution)/shard_map/ppermute | solution.py:626
  385.2 27.8 %collective-permute-start.24 = (f32[32,2048]{1,0:T(8,128)S(1)}, f32[32,2048]{1,0:T(8,128)S(1)}, u32[]{:S(2)}, u32[]{:S(2)}) collective-permute-start(f32[32,2048]{1,0:T(8,128)S(1)} %get-tuple-element.131), channel_id=1, source_target_pairs={{0,24},{4,28},{8,0},{12,4},{16,8},{20,12},{24,16},{28,20},{1,25},{... | collective-permute-start | bytes 786440 | tf_op jit(solution)/shard_map/ppermute | solution.py:626
  408.0 33.5 %collective-permute-start.14 = (f32[2,8,160,384]{3,2,1,0:T(8,128)}, f32[2,8,160,384]{3,2,1,0:T(8,128)}, u32[]{:S(2)}, u32[]{:S(2)}) collective-permute-start(f32[2,8,160,384]{3,2,1,0:T(8,128)} %dynamic-slice_bitcast_fusion.1), channel_id=1, source_target_pairs={{0,1},{1,0},{2,3},{3,2},{4,5},{5,4},{6,7},{7,6},{8,9},{9,8},{10,11... | collective-permute-start | bytes 11796488 | tf_op jit(solution)/shard_map/ppermute | solution.py:938
  447.3 28.4 %collective-permute-start.15 = (f32[1,160,384]{2,1,0:T(8,128)S(1)}, f32[1,160,384]{2,1,0:T(8,128)S(1)}, u32[]{:S(2)}, u32[]{:S(2)}) collective-permute-start(f32[1,160,384]{2,1,0:T(8,128)S(1)} %get-tuple-element.308), channel_id=1, source_target_pairs={{0,8},{8,16},{16,24},{24,28},{28,20},{20,12},{12,4},{4,0},{1,9},{9... | collective-permute-start | bytes 737288 | tf_op jit(solution)/shard_map/ppermute | solution.py:697
  460.4 15.6 %collective-permute-start.16 = (f32[1,160,384]{2,1,0:T(8,128)S(1)}, f32[1,160,384]{2,1,0:T(8,128)S(1)}, u32[]{:S(2)}, u32[]{:S(2)}) collective-permute-start(f32[1,160,384]{2,1,0:T(8,128)S(1)} %get-tuple-element.310), channel_id=1, source_target_pairs={{0,4},{8,0},{16,8},{24,16},{28,24},{20,28},{12,20},{4,12},{1,5},{9... | collective-permute-start | bytes 737288 | tf_op jit(solution)/shard_map/ppermute | solution.py:698
  477.3 22.2 %collective-permute-start.18 = (f32[2,160,384]{2,1,0:T(8,128)S(1)}, f32[2,160,384]{2,1,0:T(8,128)S(1)}, u32[]{:S(2)}, u32[]{:S(2)}) collective-permute-start(f32[2,160,384]{2,1,0:T(8,128)S(1)} %pad_maximum_fusion.6), channel_id=1, source_target_pairs={{0,4},{8,0},{16,8},{24,16},{28,24},{20,28},{12,20},{4,12},{1,5},{9... | collective-permute-start | bytes 1474568 | tf_op jit(solution)/shard_map/ppermute | solution.py:698
  477.4 22.1 %collective-permute-start.17 = (f32[2,160,384]{2,1,0:T(8,128)S(1)}, f32[2,160,384]{2,1,0:T(8,128)S(1)}, u32[]{:S(2)}, u32[]{:S(2)}) collective-permute-start(f32[2,160,384]{2,1,0:T(8,128)S(1)} %pad_maximum_fusion.5), channel_id=1, source_target_pairs={{0,8},{8,16},{16,24},{24,28},{28,20},{20,12},{12,4},{4,0},{1,9},{9... | collective-permute-start | bytes 1474568 | tf_op jit(solution)/shard_map/ppermute | solution.py:697
  517.0 33.6 %collective-permute-start.36 = (f32[2,160,384]{2,1,0:T(8,128)}, f32[2,160,384]{2,1,0:T(8,128)S(1)}, u32[]{:S(2)}, u32[]{:S(2)}) collective-permute-start(f32[2,160,384]{2,1,0:T(8,128)} %bitcast_add_fusion.5), channel_id=1, source_target_pairs={{0,8},{8,16},{16,24},{24,28},{28,20},{20,12},{12,4},{4,0},{1,9},{9... | collective-permute-start | bytes 1474568 | tf_op jit(solution)/shard_map/ppermute | solution.py:697
  523.1 18.4 %collective-permute-start.28 = (f32[2,160,384]{2,1,0:T(8,128)S(1)}, f32[2,160,384]{2,1,0:T(8,128)S(1)}, u32[]{:S(2)}, u32[]{:S(2)}) collective-permute-start(f32[2,160,384]{2,1,0:T(8,128)S(1)} %pad_maximum_fusion.7), channel_id=1, source_target_pairs={{0,8},{8,16},{16,24},{24,28},{28,20},{20,12},{12,4},{4,0},{1,9},{9... | collective-permute-start | bytes 1474568 | tf_op jit(solution)/shard_map/ppermute | solution.py:697
  525.6 27.8 %collective-permute-start.32 = (f32[2,160,384]{2,1,0:T(8,128)S(1)}, f32[2,160,384]{2,1,0:T(8,128)S(1)}, u32[]{:S(2)}, u32[]{:S(2)}) collective-permute-start(f32[2,160,384]{2,1,0:T(8,128)S(1)} %pad_maximum_fusion.8), channel_id=1, source_target_pairs={{0,4},{8,0},{16,8},{24,16},{28,24},{20,28},{12,20},{4,12},{1,5},{9... | collective-permute-start | bytes 1474568 | tf_op jit(solution)/shard_map/ppermute | solution.py:698
  543.0 12.8 %collective-permute-start.29 = (f32[2,160,384]{2,1,0:T(8,128)}, f32[2,160,384]{2,1,0:T(8,128)}, u32[]{:S(2)}, u32[]{:S(2)}) collective-permute-start(f32[2,160,384]{2,1,0:T(8,128)} %bitcast_add_fusion.10), channel_id=1, source_target_pairs={{0,8},{8,16},{16,24},{24,28},{28,20},{20,12},{12,4},{4,0},{1,9},{9... | collective-permute-start | bytes 1474568 | tf_op jit(solution)/shard_map/ppermute | solution.py:697
  553.2 14.1 %collective-permute-start.38 = (f32[2,160,384]{2,1,0:T(8,128)S(1)}, f32[2,160,384]{2,1,0:T(8,128)S(1)}, u32[]{:S(2)}, u32[]{:S(2)}) collective-permute-start(f32[2,160,384]{2,1,0:T(8,128)S(1)} %get-tuple-element.306), channel_id=1, source_target_pairs={{0,4},{8,0},{16,8},{24,16},{28,24},{20,28},{12,20},{4,12},{1,5},{9... | collective-permute-start | bytes 1474568 | tf_op jit(solution)/shard_map/ppermute | solution.py:698
  558.5 19.4 %collective-permute-start.33 = (f32[2,160,384]{2,1,0:T(8,128)S(1)}, f32[2,160,384]{2,1,0:T(8,128)S(1)}, u32[]{:S(2)}, u32[]{:S(2)}) collective-permute-start(f32[2,160,384]{2,1,0:T(8,128)S(1)} %get-tuple-element.298), channel_id=1, source_target_pairs={{0,4},{8,0},{16,8},{24,16},{28,24},{20,28},{12,20},{4,12},{1,5},{9... | collective-permute-start | bytes 1474568 | tf_op jit(solution)/shard_map/ppermute | solution.py:698
  560.4 19.5 %collective-permute-start.37 = (f32[2,160,384]{2,1,0:T(8,128)S(1)}, f32[2,160,384]{2,1,0:T(8,128)S(1)}, u32[]{:S(2)}, u32[]{:S(2)}) collective-permute-start(f32[2,160,384]{2,1,0:T(8,128)S(1)} %get-tuple-element.305), channel_id=1, source_target_pairs={{0,8},{8,16},{16,24},{24,28},{28,20},{20,12},{12,4},{4,0},{1,9},{9... | collective-permute-start | bytes 1474568 | tf_op jit(solution)/shard_map/ppermute | solution.py:697
  569.1 19.3 %collective-permute-start.39 = (f32[2,160,384]{2,1,0:T(8,128)S(1)}, f32[2,160,384]{2,1,0:T(8,128)S(1)}, u32[]{:S(2)}, u32[]{:S(2)}) collective-permute-start(f32[2,160,384]{2,1,0:T(8,128)S(1)} %bitcast_add_fusion.4), channel_id=1, source_target_pairs={{0,4},{8,0},{16,8},{24,16},{28,24},{20,28},{12,20},{4,12},{1,5},{9... | collective-permute-start | bytes 1474568 | tf_op jit(solution)/shard_map/ppermute | solution.py:698
  569.3 22.0 %collective-permute-start.30 = (f32[2,160,384]{2,1,0:T(8,128)S(1)}, f32[2,160,384]{2,1,0:T(8,128)S(1)}, u32[]{:S(2)}, u32[]{:S(2)}) collective-permute-start(f32[2,160,384]{2,1,0:T(8,128)S(1)} %get-tuple-element.297), channel_id=1, source_target_pairs={{0,8},{8,16},{16,24},{24,28},{28,20},{20,12},{12,4},{4,0},{1,9},{9... | collective-permute-start | bytes 1474568 | tf_op jit(solution)/shard_map/ppermute | solution.py:697
  579.6 18.6 %collective-permute-start.34 = (f32[2,160,384]{2,1,0:T(8,128)S(1)}, f32[2,160,384]{2,1,0:T(8,128)S(1)}, u32[]{:S(2)}, u32[]{:S(2)}) collective-permute-start(f32[2,160,384]{2,1,0:T(8,128)S(1)} %bitcast_add_fusion.9), channel_id=1, source_target_pairs={{0,4},{8,0},{16,8},{24,16},{28,24},{20,28},{12,20},{4,12},{1,5},{9... | collective-permute-start | bytes 1474568 | tf_op jit(solution)/shard_map/ppermute | solution.py:698
  589.5 11.6 %collective-permute-start.40 = (f32[160,384]{1,0:T(8,128)S(1)}, f32[160,384]{1,0:T(8,128)S(1)}, u32[]{:S(2)}, u32[]{:S(2)}) collective-permute-start(f32[160,384]{1,0:T(8,128)S(1)} %dynamic-slice_bitcast_fusion.16), channel_id=1, source_target_pairs={{0,2},{1,3},{2,0},{3,1},{4,6},{5,7},{6,4},{7,5},{8,10},{9,11},{10,... | collective-permute-start | bytes 737288 | tf_op jit(solution)/shard_map/ppermute | solution.py:720
  607.5 20.1 %collective-permute-start.43 = (bf16[2,184,384]{2,1,0:T(8,128)(2,1)S(1)}, bf16[2,184,384]{2,1,0:T(8,128)(2,1)S(1)}, u32[]{:S(2)}, u32[]{:S(2)}) collective-permute-start(bf16[2,184,384]{2,1,0:T(8,128)(2,1)S(1)} %pad_maximum_fusion.10), channel_id=1, source_target_pairs={{0,8},{8,16},{16,24},{24,28},{28,20},{20,12},{12,4},{4,0},{1,9},{9... | collective-permute-start | bytes 847880 | tf_op jit(solution)/shard_map/ppermute | solution.py:662
  609.4 20.3 %collective-permute-start.44 = (bf16[2,184,384]{2,1,0:T(8,128)(2,1)S(1)}, bf16[2,184,384]{2,1,0:T(8,128)(2,1)S(1)}, u32[]{:S(2)}, u32[]{:S(2)}) collective-permute-start(bf16[2,184,384]{2,1,0:T(8,128)(2,1)S(1)} %pad_maximum_fusion.10), channel_id=1, source_target_pairs={{0,4},{8,0},{16,8},{24,16},{28,24},{20,28},{12,20},{4,12},{1,5},{9... | collective-permute-start | bytes 847880 | tf_op jit(solution)/shard_map/ppermute | solution.py:663
  621.6 150.1 %all-to-all-start.6 = ((f32[8,1,2048]{2,1,0:T(1,128)}), f32[8,1,2048]{2,1,0:T(1,128)S(1)}, u32[]{:S(2)}, u32[]{:S(2)}) async-start(f32[8,1,2048]{2,1,0:T(1,128)} %broadcast_in_dim.362), calls=%async_computation.6 | async-start | bytes 131072 | tf_op jit(solution)/shard_map/all_to_all | solution.py:611
  654.3 30.5 %collective-permute-start.53 = (bf16[2,384,384]{2,1,0:T(8,128)(2,1)S(1)}, bf16[2,384,384]{2,1,0:T(8,128)(2,1)}, u32[]{:S(2)}, u32[]{:S(2)}) collective-permute-start(bf16[2,384,384]{2,1,0:T(8,128)(2,1)S(1)} %get-tuple-element.341), channel_id=1, source_target_pairs={{0,1},{1,0},{2,3},{3,2},{4,5},{5,4},{6,7},{7,6},{8,9},{9,8},{10,11... | collective-permute-start | bytes 1769480 | tf_op jit(solution)/shard_map/ppermute | solution.py:1007
  654.9 30.0 %collective-permute-start.54 = (bf16[2,384,384]{2,1,0:T(8,128)(2,1)S(1)}, bf16[2,384,384]{2,1,0:T(8,128)(2,1)}, u32[]{:S(2)}, u32[]{:S(2)}) collective-permute-start(bf16[2,384,384]{2,1,0:T(8,128)(2,1)S(1)} %get-tuple-element.340), channel_id=1, source_target_pairs={{0,2},{1,3},{2,0},{3,1},{4,6},{5,7},{6,4},{7,5},{8,10},{9,11},{10,... | collective-permute-start | bytes 1769480 | tf_op jit(solution)/shard_map/ppermute | solution.py:1007
  656.6 28.3 %collective-permute-start.55 = (bf16[2,384,384]{2,1,0:T(8,128)(2,1)S(1)}, bf16[2,384,384]{2,1,0:T(8,128)(2,1)}, u32[]{:S(2)}, u32[]{:S(2)}) collective-permute-start(bf16[2,384,384]{2,1,0:T(8,128)(2,1)S(1)} %get-tuple-element.339), channel_id=1, source_target_pairs={{0,3},{1,2},{2,1},{3,0},{4,7},{5,6},{6,5},{7,4},{8,11},{9,10},{10,... | collective-permute-start | bytes 1769480 | tf_op jit(solution)/shard_map/ppermute | solution.py:1007
  657.3 25.5 %collective-permute-start.52 = (f32[1,128]{1,0:T(1,128)S(1)}, f32[1,128]{1,0:T(1,128)S(1)}, u32[]{:S(2)}, u32[]{:S(2)}) collective-permute-start(f32[1,128]{1,0:T(1,128)S(1)} %broadcast_add_fusion), channel_id=1, source_target_pairs={{0,2},{1,3},{2,0},{3,1},{4,6},{5,7},{6,4},{7,5},{8,10},{9,11},{10,... | collective-permute-start | bytes 1544 | tf_op jit(solution)/shard_map/ppermute | solution.py:599
  689.7 73.3 %collective-permute-start.57 = (f32[2,384,384]{2,1,0:T(8,128)}, f32[2,384,384]{2,1,0:T(8,128)}, u32[]{:S(2)}, u32[]{:S(2)}) collective-permute-start(f32[2,384,384]{2,1,0:T(8,128)} %fusion.41.stats_ref), channel_id=1, source_target_pairs={{0,2},{1,3},{2,0},{3,1},{4,6},{5,7},{6,4},{7,5},{8,10},{9,11},{10,... | collective-permute-start | bytes 3538952 | tf_op jit(solution)/shard_map/ppermute | solution.py:1017
  691.4 51.7 %collective-permute-start.56 = (f32[336,512]{1,0:T(8,128)S(1)}, f32[336,512]{1,0:T(8,128)S(1)}, u32[]{:S(2)}, u32[]{:S(2)}) collective-permute-start(f32[336,512]{1,0:T(8,128)S(1)} %get-tuple-element.142), channel_id=1, source_target_pairs={{0,2},{1,3},{2,0},{3,1},{4,6},{5,7},{6,4},{7,5},{8,10},{9,11},{10,... | collective-permute-start | bytes 2064392 | tf_op jit(solution)/shard_map/ppermute | solution.py:1019
  744.2 27.4 %collective-permute-start.58 = (f32[2,384,384]{2,1,0:T(8,128)S(1)}, f32[2,384,384]{2,1,0:T(8,128)S(1)}, u32[]{:S(2)}, u32[]{:S(2)}) collective-permute-start(f32[2,384,384]{2,1,0:T(8,128)S(1)} %copy-done.23), channel_id=1, source_target_pairs={{0,2},{1,3},{2,0},{3,1},{4,6},{5,7},{6,4},{7,5},{8,10},{9,11},{10,... | collective-permute-start | bytes 3538952 | tf_op jit(solution)/shard_map/ppermute | solution.py:1037
  775.8 16.7 %collective-permute-start.61 = (f32[2,2,384,384]{3,2,1,0:T(8,128)S(1)}, f32[2,2,384,384]{3,2,1,0:T(8,128)S(1)}, u32[]{:S(2)}, u32[]{:S(2)}) collective-permute-start(f32[2,2,384,384]{3,2,1,0:T(8,128)S(1)} %bitcast_dynamic-update-slice_fusion.5), channel_id=1, source_target_pairs={{0,1},{1,0},{2,3},{3,2},{4,5},{5,4},{6,7},{7,6},{8,9},{9,8},{10,11... | collective-permute-start | bytes 7077896 | tf_op jit(solution)/shard_map/ppermute | solution.py:725
  (109 other events, 1880.4 us)
Sparse Core Ops, SparseCore 0:
  11.5 143.2 all-gather.5
  157.6 87.6 all-gather.7
  422.5 56.5 all-gather.9

commit v3 on v2

--- a/solution.py
+++ b/solution.py
@@ -136,11 +136,17 @@
     out_ref[...] = x2 + lax.fori_loop(0, wt_ref.shape[0], units, jnp.zeros(x.shape, f32))
 
 
-def mlp_bwd_kernel(wt_ref, gains_ref, x2_ref, grad_ref, dwt_ref, dgains_ref, dx2_ref):
+def mlp_bwd_kernel(last, wt_ref, gains_ref, x2_ref, grad_ref, *refs):
+    if last:
+        partial_ref, _, dwt_ref, dx2_ref, dgains_ref = refs
+    else:
+        dwt_ref, dx2_ref = refs
+
     @pl.when(pl.program_id(0) == 0)
     def _():
         dwt_ref[...] = jnp.zeros_like(dwt_ref)
-        dgains_ref[...] = jnp.zeros_like(dgains_ref)
+        if last:
+            dgains_ref[...] = jnp.zeros_like(dgains_ref)
 
     grad = grad_ref[...]
     grad_low = grad.astype(bf16)
@@ -157,10 +163,14 @@
         dwt_ref[group, 896:1280] += mm(hidden, grad_low, TN)
         return total + mm(grad_up, wt_ref[group, 512:896])
 
-    grad_h2 = lax.fori_loop(0, wt_ref.shape[0], units, jnp.zeros(grad.shape, f32))
-    grad_x2, gain_two, bias_two = norm_back(x2, gains_ref[2:3], grad_h2)
-    dx2_ref[...] = grad + grad_x2
-    dgains_ref[...] += jnp.concatenate([gain_two, bias_two], axis=0)
+    start = partial_ref[...] if last else jnp.zeros(grad.shape, f32)
+    grad_h2 = lax.fori_loop(0, wt_ref.shape[0], units, start)
+    if last:
+        grad_x2, gain_two, bias_two = norm_back(x2, gains_ref[2:3], grad_h2)
+        dx2_ref[...] = grad + grad_x2
+        dgains_ref[...] += jnp.concatenate([gain_two, bias_two], axis=0)
+    else:
+        dx2_ref[...] = grad_h2
 
 
 def attention_bwd_kernel(
@@ -258,24 +268,29 @@
     )(x, weights, gains, seg_col, seg_row, slot)
 
 
-def mlp_bwd(weights, layer, gains, x2, grad):
-    rows, groups = x2.shape[0], weights.shape[0]
+def mlp_bwd(part, weights, layer, gains, x2, grad, last=()):
+    rows, groups = x2.shape[0], weights.shape[0] // 2
     s = block_specs(groups, layer)
+    half = pl.BlockSpec((groups, 1280, D), lambda c: (part, 0, layer))
+    any_spec = [pl.BlockSpec(memory_space=pl.ANY)] if last else []
+    args = (weights, gains, x2, grad, *last)
     return pl.pallas_call(
-        mlp_bwd_kernel,
+        functools.partial(mlp_bwd_kernel, bool(last)),
         grid=(rows // CHUNK,),
-        in_specs=[s["wt"], s["gains"], s["row"], s["row"]],
-        out_specs=[whole_spec((groups, 1280, D)), whole_spec((2, D)), s["row"]],
+        in_specs=[half, s["gains"], s["row"], s["row"]] + [s["row"]] * len(last[:1]) + any_spec,
+        out_specs=[pl.BlockSpec((groups, 1280, D), lambda c: (part, 0, 0)), s["row"]]
+        + [whole_spec((2, D))] * len(last[:1]),
         out_shape=[
-            jax.ShapeDtypeStruct((groups, 1280, D), f32),
-            jax.ShapeDtypeStruct((2, D), f32),
+            jax.ShapeDtypeStruct((2 * groups, 1280, D), f32),
             jax.ShapeDtypeStruct((rows, D), f32),
-        ],
+        ]
+        + [jax.ShapeDtypeStruct((2, D), f32)] * len(last[:1]),
+        input_output_aliases={len(args) - 1: 0} if last else {},
         compiler_params=pltpu.CompilerParams(vmem_limit_bytes=VMEM_LIMIT),
         cost_estimate=pl.CostEstimate(
-            flops=rows * 24_000_000, bytes_accessed=16_000_000, transcendentals=rows * 6000
+            flops=rows * 13_000_000, bytes_accessed=8_000_000, transcendentals=rows * 3000
         ),
-    )(weights, gains, x2, grad)
+    )(*args)
 
 
 def attention_bwd(part, weights, layer, gains, seg_col, seg_row, slot, saved, grad_x2, dwt, last=()):
@@ -566,6 +581,116 @@
     )(new_stats, bases)
 
 
+def crop_pairs(r_t, r_s):
+    rows = lax.broadcasted_iota(jnp.int32, (r_t, r_s), 0)
+    crops = lax.broadcasted_iota(jnp.int32, (r_t, r_s), 1)
+    first = (rows // 2) * CROPS
+    return (crops >= first) & (crops < first + CROPS), rows % 2 == 0
+
+
+def spread_pairs(values, same, even):
+    first = jnp.where(same & even, 1.0, 0.0)
+    second = jnp.where(same & ~even, 1.0, 0.0)
+    return mm(values, first, NN, precise), mm(values, second, NN, precise)
+
+
+def logits_kernel(
+    zs_ref, zt_ref, ps_ref, pt_ref, center_ref, exp_s_ref, exp_t_ref, stats_ref, part_ref
+):
+    scaled_s = mm(ps_ref[...], zs_ref[...], (((0,), (1,)), ((), ()))) / TAU_S
+    glob = mm(pt_ref[...], zt_ref[...], (((0,), (1,)), ((), ())))
+    part_ref[...] = jnp.sum(glob, axis=1, keepdims=True)
+    scaled_t = (glob - center_ref[...]) / TAU_T
+    max_s = jnp.max(scaled_s, axis=0, keepdims=True)
+    max_t = jnp.max(scaled_t, axis=0, keepdims=True)
+    exp_s = jnp.exp(scaled_s - max_s)
+    exp_t = jnp.exp(scaled_t - max_t)
+    exp_s_ref[...] = exp_s
+    exp_t_ref[...] = exp_t
+    same, even = crop_pairs(exp_t.shape[1], exp_s.shape[1])
+    cross = jnp.where(same, mm(exp_t, scaled_s, TN, precise), 0.0)
+    stats_ref[...] = jnp.concatenate(
+        [
+            max_s,
+            jnp.sum(exp_s, axis=0, keepdims=True),
+            *spread_pairs(max_t, same, even),
+            *spread_pairs(jnp.sum(exp_t, axis=0, keepdims=True), same, even),
+            jnp.sum(jnp.where(even, cross, 0.0), axis=0, keepdims=True),
+            jnp.sum(jnp.where(even, 0.0, cross), axis=0, keepdims=True),
+        ],
+        axis=0,
+    )
+
+
+def prototype_logits(z_s, z_t, proto_s, proto_t, center):
+    cols, r_s, r_t = proto_s.shape[1], z_s.shape[0], z_t.shape[0]
+    return pl.pallas_call(
+        logits_kernel,
+        in_specs=[pl.BlockSpec(memory_space=pltpu.VMEM)] * 5,
+        out_specs=[pl.BlockSpec(memory_space=pltpu.VMEM)] * 4,
+        out_shape=[
+            jax.ShapeDtypeStruct((cols, r_s), f32),
+            jax.ShapeDtypeStruct((cols, r_t), f32),
+            jax.ShapeDtypeStruct((8, r_s), f32),
+            jax.ShapeDtypeStruct((cols, 1), f32),
+        ],
+        compiler_params=pltpu.CompilerParams(vmem_limit_bytes=VMEM_LIMIT),
+        cost_estimate=pl.CostEstimate(
+            flops=8_000_000_000, bytes_accessed=8_000_000, transcendentals=1_000_000
+        ),
+    )(z_s, z_t, proto_s, proto_t, center)
+
+
+def join_stats(every):
+    tops = jnp.max(every, axis=0)
+
+    def add_up(row, shrink):
+        return jnp.sum(every[:, row : row + 1] * shrink, axis=0)
+
+    shrink = [jnp.exp(every[:, row : row + 1] - tops[row : row + 1][None]) for row in (0, 2, 3)]
+    sums = [add_up(4, shrink[1]), add_up(5, shrink[2]), add_up(6, shrink[1]), add_up(7, shrink[2])]
+    return jnp.concatenate([tops[0:1], add_up(1, shrink[0]), tops[2:4], *sums], axis=0)
+
+
+def loss_kernel(
+    all_ref, own_ref, weight_ref, exp_s_ref, exp_t_ref, zs_ref, ps_ref, dz_ref, dproto_ref, loss_ref
+):
+    every, own = all_ref[...], own_ref[...]
+    every = join_stats(every) if every.ndim == 3 else every
+    top_s, total_s, top_0, top_1 = every[0:1], every[1:2], every[2:3], every[3:4]
+    total_0, total_1, cross_0, cross_1 = every[4:5], every[5:6], every[6:7], every[7:8]
+    weight_0, weight_1 = weight_ref[0:1], weight_ref[1:2]
+    log_norm = jnp.log(total_s) + top_s
+    loss = weight_0 * (log_norm - cross_0 / total_0) + weight_1 * (log_norm - cross_1 / total_1)
+    loss_ref[...] = jnp.broadcast_to(jnp.sum(loss, axis=1, keepdims=True), loss_ref.shape)
+    coef_s = (weight_0 + weight_1) / total_s * jnp.exp(own[0:1] - top_s)
+    coef_0 = weight_0 / total_0 * jnp.exp(own[2:3] - top_0)
+    coef_1 = weight_1 / total_1 * jnp.exp(own[3:4] - top_1)
+    same, even = crop_pairs(exp_t_ref.shape[1], exp_s_ref.shape[1])
+    mix = jnp.where(same, jnp.where(even, coef_0, coef_1), 0.0)
+    target = mm(exp_t_ref[...], mix, NN, precise)
+    grad = ((coef_s * exp_s_ref[...] - target) / TAU_S).astype(bf16)
+    dz_ref[...] = mm(grad, ps_ref[...], (((0,), (1,)), ((), ())))
+    dproto_ref[...] = mm(zs_ref[...], grad, (((0,), (1,)), ((), ())))
+
+
+def loss_and_grads(every, own, weights, exp_s, exp_t, z_s, proto_s):
+    return pl.pallas_call(
+        loss_kernel,
+        in_specs=[pl.BlockSpec(memory_space=pltpu.VMEM)] * 7,
+        out_specs=[pl.BlockSpec(memory_space=pltpu.VMEM)] * 3,
+        out_shape=[
+            jax.ShapeDtypeStruct(z_s.shape, f32),
+            jax.ShapeDtypeStruct(proto_s.shape, f32),
+            jax.ShapeDtypeStruct((1, 128), f32),
+        ],
+        compiler_params=pltpu.CompilerParams(vmem_limit_bytes=VMEM_LIMIT),
+        cost_estimate=pl.CostEstimate(
+            flops=8_000_000_000, bytes_accessed=8_000_000, transcendentals=10_000
+        ),
+    )(every, own, weights, exp_s, exp_t, z_s, proto_s)
+
+
 def flip_perm(count, bit):
     return [(i, i ^ bit) for i in range(count)]
 
@@ -611,20 +736,27 @@
     return lax.all_to_all(jnp.broadcast_to(array[None], (count, *array.shape)), axis, 0, 0)
 
 
-def swap_over(pick, axis, after=None):
-    count = lax.axis_size(axis)
-    me = lax.axis_index(axis)
+def swap_pieces(pick, after=None):
+    count = lax.axis_size("dp")
+    me = lax.axis_index("dp")
     if count > 8:
-        return lax.all_to_all(jnp.stack([pick(i) for i in range(count)]), axis, 0, 0)
-    own = pick(me)
+        return [lax.all_to_all(jnp.stack([pick(i) for i in range(count)]), "dp", 0, 0)]
     picks = [pick(lax.rem(me + step, count)) for step in range(1, count)]
     if after is not None:
         picks, _ = lax.optimization_barrier((picks, after))
-    out = jnp.zeros((count, *own.shape), own.dtype)
-    out = put(out, own, me)
-    for step in range(1, count):
-        got = lax.ppermute(picks[step - 1], axis, shift_perm(count, step))
-        out = put(out, got, lax.rem(me + (count - step), count))
+    got = [
+        lax.ppermute(piece, "dp", shift_perm(count, step + 1)) for step, piece in enumerate(picks)
+    ]
+    return [pick(me), *got]
+
+
+def swap_joined(pieces):
+    if len(pieces) == 1:
+        return pieces[0]
+    count = lax.axis_size("dp")
+    out = jnp.zeros((count, *pieces[0].shape), pieces[0].dtype)
+    for step, piece in enumerate(pieces):
+        out = put(out, piece, lax.rem(lax.axis_index("dp") + (count - step), count))
     return out
 
 
@@ -811,9 +943,19 @@
     seg_cls = jnp.concatenate([segment[jnp.array(starts)], jnp.zeros((CLS - CROPS,), jnp.int32)])
     seg_cls = jnp.concatenate([seg_cls, seg_cls])[:, None]
     slot = jnp.repeat(slot_live.astype(f32).reshape(mp_count, SLOT_DEV), HD, axis=1)[:, None, :]
-    protos = swap_over(pick_cols, "dp")
-    x0, weights, heads, protos, counts, seg_col, seg_row, seg_cls, slot = lax.optimization_barrier(
-        (x0, weights, heads, protos, counts, seg_col, seg_row, seg_cls, slot)
+    protos = swap_joined(swap_pieces(pick_cols))
+    center_own = lax.dynamic_slice_in_dim(center, unsigned(dp_index * proto_cols), proto_cols)
+    center_own = center_own[:, None]
+    crop_ids = jnp.arange(CROPS)
+    pair_weight = (
+        (crop_ids[None, None, :] != jnp.arange(2)[:, None, None])
+        & (crop_ids[None, None, :] < 2 + counts[None, :, None])
+    ).astype(f32) / (2.0 * counts.astype(f32) + 2.0)[None, :, None]
+    pair_weight = pair_weight.reshape(2, -1)
+    x0, weights, heads, protos, seg_col, seg_row, seg_cls, slot, center_own, pair_weight = (
+        lax.optimization_barrier(
+            (x0, weights, heads, protos, seg_col, seg_row, seg_cls, slot, center_own, pair_weight)
+        )
     )
     heads = lax.all_gather(heads, "dp", axis=0, tiled=True)
     head_t, head_s = heads[:, :head_cols], heads[:, head_cols:]
@@ -850,58 +992,15 @@
     z_s = unit_all[:, :n_s].reshape(dp_count * n_s, -1)
     z_t = unit_all[:, n_s:].reshape(dp_count * n_t, -1)
     images = dp_count * mp_count
-    scaled_s = mm(z_s, proto_s) / TAU_S
-    glob = mm(z_t, proto_t)
-    center_own = lax.dynamic_slice_in_dim(center, dp_index * proto_cols, proto_cols)
-    scaled_t = (glob - center_own) / TAU_T
-    center_part = jnp.sum(glob, axis=0)
-    max_s = jnp.max(scaled_s, axis=-1, keepdims=True)
-    max_t = jnp.max(scaled_t, axis=-1, keepdims=True)
-    exp_s, exp_t = jnp.exp(scaled_s - max_s), jnp.exp(scaled_t - max_t)
-    cross = mm(exp_t, scaled_s, NT, precise)
-    same = jnp.arange(images * 2)[:, None] // 2 == jnp.arange(images * CROPS)[None, :] // CROPS
-    cross = jnp.sum(
-        jnp.where(same, cross, 0.0).reshape(images * 2, images, CROPS), axis=1
-    )
-    stats = jnp.concatenate(
-        [
-            max_s.reshape(-1),
-            jnp.sum(exp_s, axis=-1),
-            max_t.reshape(-1),
-            jnp.sum(exp_t, axis=-1),
-            cross.reshape(-1),
-        ]
-    )
-    stats = gather_over(stats, ("dp", "mp"))
-    r_s, r_t = images * CROPS, images * 2
-    maxes_s, sums_s = stats[:, :r_s], stats[:, r_s : 2 * r_s]
-    maxes_t, sums_t = stats[:, 2 * r_s : 2 * r_s + r_t], stats[:, 2 * r_s + r_t : 2 * (r_s + r_t)]
-    crosses = stats[:, 2 * (r_s + r_t) :].reshape(images, r_t, CROPS)
-    top_s, top_t = jnp.max(maxes_s, axis=0), jnp.max(maxes_t, axis=0)
-    total_s = jnp.sum(sums_s * jnp.exp(maxes_s - top_s), axis=0)
-    shrink_t = jnp.exp(maxes_t - top_t)
-    total_t = jnp.sum(sums_t * shrink_t, axis=0)
-    cross_total = jnp.sum(crosses * shrink_t[:, :, None], axis=0) / total_t[:, None]
-    log_norm = (jnp.log(total_s) + top_s).reshape(images, 1, CROPS)
-    crop_ids = jnp.arange(CROPS)
-    pairs = (
-        (crop_ids[None, None, :] != jnp.arange(2)[None, :, None])
-        & (crop_ids[None, None, :] < 2 + counts[:, None, None])
-    ).astype(f32)
-    image_weight = 1.0 / (2.0 * counts.astype(f32) + 2.0)
-    pair_weight = pairs * image_weight[:, None, None]
-    entropy = log_norm - cross_total.reshape(images, 2, CROPS)
-    loss_total = jnp.sum(entropy * pair_weight)
-    coef_s = jnp.sum(pair_weight, axis=1).reshape(-1, 1) / total_s[:, None]
-    coef_s = coef_s * jnp.exp(max_s - top_s[:, None])
-    coef_t = jnp.exp(max_t[:, 0] - top_t) / total_t
-    coef_t = pair_weight.reshape(r_t, CROPS) * coef_t[:, None]
-    mix = jnp.where(same, jnp.tile(coef_t, (1, images)), 0.0)
-    grad_scaled = (coef_s * exp_s - mm(mix, exp_t, TN, precise)) / TAU_S
-    grad_logits = grad_scaled.astype(bf16)
-    grad_unit_part = mm(grad_logits, proto_s, NT)
-    grad_proto = mm(z_s, grad_logits, TN)
-
+    exp_s, exp_t, own_stats, center_part = prototype_logits(z_s, z_t, proto_s, proto_t, center_own)
+    center_part = center_part.reshape(-1)
+    all_stats = gather_over(own_stats, ("dp", "mp"))
+    if dp_count > 8:
+        all_stats = join_stats(all_stats)
+    grad_unit_part, grad_proto, loss_total = loss_and_grads(
+        all_stats, own_stats, pair_weight, exp_s, exp_t, z_s, proto_s
+    )
+    loss_total = loss_total[0, 0]
     grad_unit = lax.all_to_all(grad_unit_part.reshape(dp_count, n_s, -1), "dp", 0, 0)
     grad_unit = sum_over(jnp.sum(grad_unit, axis=0), ("mp",))
     third_s, inv_s = third[:n_s], inv[:n_s]
@@ -921,8 +1020,7 @@
     def pick_proto(i):
         return lax.dynamic_slice_in_dim(grad_proto, unsigned(i * proto_rows), proto_rows, 0)
 
-    proto_g = swap_over(pick_proto, "dp", grad_unit)
-    proto_g = proto_g.transpose(1, 0, 2).reshape(proto_rows, -1)
+    proto_g = swap_pieces(pick_proto, grad_unit)
     rows_left = jnp.concatenate([feats_s, b1[:n_s], grad_third], axis=1)
     head_rows = head_w.shape[0]
 
@@ -936,14 +1034,18 @@
     send1, own1 = core_halves(dwt1, dp_count, core)
     grad_x1, send1 = lax.optimization_barrier((grad_x1, send1))
     got1 = lax.ppermute(send1, "mp", flip_perm(4, 1))
-    dwt0, dgains0b, grad_x2 = mlp_bwd(weights, 2, norm_params[0:4], saved0[3], grad_x1)
-    grad_x2, got1 = lax.optimization_barrier((grad_x2, got1))
+    mlp_args = (weights, 2, norm_params[0:4], saved0[3], grad_x1)
+    dwt0, grad_h2 = mlp_bwd(0, *mlp_args)
+    grad_h2, got1, proto_g[1:3] = lax.optimization_barrier((grad_h2, got1, proto_g[1:3]))
     ring1 = RingScatter(own1 + got1)
     ring1.step(0)
+    dwt0, grad_x2, dgains0b = mlp_bwd(1, *mlp_args, (grad_h2, dwt0))
+    grad_x2, proto_g[3:5] = lax.optimization_barrier((ring1.tie(grad_x2), proto_g[3:5]))
+    ring1.step(1)
     block_args = (weights, 2, norm_params[0:4], seg_col, seg_row, slot, saved0)
     dwt0, grad_h1 = attention_bwd(0, *block_args, grad_x2, dwt0)
-    grad_h1 = ring1.tie(grad_h1)
-    ring1.step(1)
+    grad_h1, proto_g[5:7] = lax.optimization_barrier((ring1.tie(grad_h1), proto_g[5:7]))
+    ring1.step(2)
     dwt0, dgains0a = attention_bwd(1, *block_args, grad_x2, dwt0, (x0, grad_h1))
     send0, own0 = core_halves(dwt0, dp_count, core)
     send0, proto_g, left, right = lax.optimization_barrier(
@@ -959,10 +1061,9 @@
         )
         for i in range(3)
     )
-    ring1.step(2)
+    ring1.step(3)
     ring0 = RingScatter(own0 + lax.ppermute(send0, "mp", flip_perm(4, 1)))
     ring0.step(0)
-    ring1.step(3)
     block_g1 = across_sum(ring1.total(), across)
     for index in range(1, RingScatter.steps):
         ring0.step(index)
@@ -989,30 +1090,35 @@
     columns = ring_gather(columns).transpose(1, 0, 2, 3)
     norm_sum = whole_of(columns[:, :, col_width:])
     norm_total = norm_sum[:10]
+    columns, proto_g = lax.optimization_barrier((columns, proto_g))
+    proto_g = swap_joined(proto_g).transpose(1, 0, 2).reshape(proto_rows, -1)
     columns = columns[:, :, :col_width].reshape(LAYERS, dp_count * col_width, D)
     wide = columns.astype(f32)
-    block_square = sum_over(jnp.full((1, 128), jnp.sum(wide * wide)), ("mp",))[0, 0]
-    grad_norm = jnp.sqrt(norm_sum[10, 0] + block_square + jnp.sum(norm_total * norm_total))
+    block_square = sum_over(jnp.full((1, 128), jnp.sum(wide * wide)), ("mp",))[:, :1]
+    norm_square = jnp.sum(norm_total * norm_total, axis=(0, 1), keepdims=True)
+    grad_norm = jnp.sqrt(norm_sum[10:11, :1] + block_square + norm_square)
     clip_factor = jnp.minimum(1.0, CLIP_NORM / (grad_norm + 1e-06))
     bounds = (0, 384, 512, 896, 1280)
     longest = 384
 
-    def kind_rows(kind):
-        start = jnp.array(bounds[:4])[kind]
+    own_kind = unsigned(mp_index)
+    starts = jnp.array([[bounds[kind ^ flip] for flip in range(4)] for kind in range(4)], jnp.uint32)
+
+    def kind_rows(flip):
+        start = lax.dynamic_slice(starts, (own_kind, jnp.uint32(flip)), (1, 1))[0, 0]
         rows = lax.dynamic_slice_in_dim(columns, start, longest, 1)
-        inside = start + jnp.arange(longest) < jnp.array(bounds[1:])[kind]
+        inside = (jnp.arange(longest) < 128) | (mp_index != 1 ^ flip)
         return jnp.where(inside[None, :, None], rows, 0).astype(bf16)
 
-    kinds = [kind_rows(mp_index)] + [
-        lax.ppermute(kind_rows(mp_index ^ flip), "mp", flip_perm(mp_count, flip))
-        for flip in (1, 2, 3)
+    kinds = [kind_rows(0)] + [
+        lax.ppermute(kind_rows(flip), "mp", flip_perm(mp_count, flip)) for flip in (1, 2, 3)
     ]
     kinds = jnp.concatenate(kinds, axis=1)
     stat = lax.dot_general(
         kinds, kinds, (((1,), (1,)), ((0,), (0,))), preferred_element_type=f32
     )
-    stats_own = lax.dynamic_index_in_dim(precond_stats, mp_index, 1, keepdims=False)
-    bases_own = lax.dynamic_index_in_dim(rotation_bases, mp_index, 1, keepdims=False)
+    stats_own = lax.dynamic_index_in_dim(precond_stats, own_kind, 1, keepdims=False)
+    bases_own = lax.dynamic_index_in_dim(rotation_bases, own_kind, 1, keepdims=False)
     stats_own = SHAMPOO_BETA * stats_own + (1 - SHAMPOO_BETA) * (clip_factor * clip_factor) * stat
     far_stats = lax.ppermute(stats_own, "mp", flip_perm(4, 2))
     stats_own, head_own = lax.optimization_barrier((stats_own, head_own))
@@ -1062,7 +1168,7 @@
     new_teacher_norm = TEACHER_MOM * teacher_norm + (1 - TEACHER_MOM) * new_norm
     new_center = CENTER_MOM * center + (1 - CENTER_MOM) * center_total / (2.0 * images)
     return (
-        loss_total, grad_norm, new_block_w, first_mom[:, :, None], second_mom[:, :, None],
+        loss_total, grad_norm[0, 0], new_block_w, first_mom[:, :, None], second_mom[:, :, None],
         new_bases, new_stats, new_head_w, new_head_m, new_head_v,
         new_proto_w, new_proto_m, new_proto_v, new_norm, new_norm_m, new_norm_v,
         new_teacher_block, new_teacher_head, new_teacher_proto, new_teacher_norm, new_center,

time: 810 us -> 817 us (level)
  Pallas kernels: 172 us -> 191 us
  waiting for transfers between devices: 242 us -> 225 us
  local copies, waits for them, and re-layouts: 97.7 us -> 112 us
  starting transfers between devices: 104 us -> 117 us
  matrix products: 45.7 us -> 33.2 us
  other arithmetic: 86.4 us -> 74.3 us
  blocking collectives: 27 us -> 37.8 us
    ppermute x17, starting transfers between devices: 30.9 us -> 60.6 us  [the longest x14 58.8 us: swap_pieces(): lax.ppermute(piece, 'dp', shift_perm(count, step + 1))]
    dynamic_update_slice x25 -> x24, local copies, waits for them, and re-layouts: 19.7 us -> 39.3 us  [put(): return lax.dynamic_update_index_in_dim(out, piece, unsigned(index), 0)]
    pallas_call x1 -> x4, Pallas kernels: 19.1 us -> 38.1 us  [the longest x2 22.3 us: mlp_bwd(): pl.pallas_call(functools.partial(mlp_bwd_kernel, bool(last)), grid=(rows...]
    ppermute x8, starting transfers between devices: 24 us -> 5.73 us  [step(): self.right = lax.ppermute(self.send_right, 'dp', ring_perm(1))]
    ppermute x10, waiting for transfers between devices: 28.9 us -> 11.3 us  [sum_over(): array = array + lax.ppermute(array, axis, flip_perm(count, bit))]
    dot_general x18 -> x12, matrix products: 30.8 us -> 18 us  [mm(): lax.dot_general(lhs, rhs, dims, precision=precision, preferred_element_ty...]
    broadcast_in_dim x1 -> x8, local copies, waits for them, and re-layouts: 0.27 us -> 11.8 us  [put(): return lax.dynamic_update_index_in_dim(out, piece, unsigned(index), 0)]
    all_to_all x1 -> x2, blocking collectives: 15.9 us -> 26.8 us  [the longest x1 16.4 us: gather_over(): lax.all_to_all(jnp.broadcast_to(array[None], (count, *array.shape)), axis...]
  transfers between devices with their start and end apart: 71 -> 70, of which waited for: 32 -> 29; matrix products, arithmetic and copies ran while one was open for 20% -> 22% of each run, Pallas kernels for 21% -> 20%
where the time goes in v3:
time: 817 us; the launch traced here: 809 us
  waiting for transfers between devices  225 us (28%)
  Pallas kernels  191 us (23%)
  starting transfers between devices  117 us (14%)
  local copies, waits for them, and re-layouts  112 us (14%)
  other arithmetic  74.3 us (9%)
  blocking collectives  37.8 us (5%)
  matrix products  33.2 us (4%)
  between operations  20.3 us (2%)
    ppermute x14, starting transfers between devices, swap_pieces(): lax.ppermute(piece, 'dp', shift_perm(count, step + 1))  58.8 us
    all_gather x1, waiting for transfers between devices, shards(): lax.all_gather(jnp.concatenate([*own_t, *own_s], axis=1), ('mp', 'dp'), a...  56.3 us
    pallas_call x1, Pallas kernels, renew_bases(): pl.pallas_call(basis_kernel, in_specs=[pl.BlockSpec(memory_space=pltpu.VM...  51 us
    dynamic_update_slice x24, local copies, waits for them, and re-layouts, put(): return lax.dynamic_update_index_in_dim(out, piece, unsigned(index), 0)  39.3 us
    all_to_all x3, waiting for transfers between devices, gather_over(): lax.all_to_all(jnp.broadcast_to(array[None], (count, *array.shape)), axis...  37.7 us
    pallas_call x2, Pallas kernels, block_fwd(): pl.pallas_call(block_fwd_kernel, grid=(rows // CHUNK,), in_specs=[s['row'...  36.6 us
    pallas_call x2, Pallas kernels, attention_bwd(): pl.pallas_call(functools.partial(attention_bwd_kernel, bool(last)), grid=...  30.5 us
    all_gather x1, waiting for transfers between devices, shards(): heads = lax.all_gather(heads, 'dp', axis=0, tiled=True)  23.6 us
  transfers between devices with their start and end apart: 70, of which 29 were waited for; matrix products, arithmetic and copies ran while one was open for 22% of the time, Pallas kernels for 20%

profile of v3, /device:TPU:0, one launch (start us, length us, event | category | flops | bytes accessed | tf_op | source)
XLA Modules:
  0.0 809.1 jit_solution(14246010402622779714)
XLA Ops:
  45.0 31.1 %all-to-all-done = s32[8,1,4]{2,1,0:T(1,128)S(1)} async-done(((s32[8,1,4]{2,1,0:T(1,128)}), s32[8,1,4]{2,1,0:T(1,128)S(1)}, u32[]{:S(2)}, u32[]{:S(2)}) %all-to-all-start) | async-done | bytes 160 | tf_op jit(solution)/shard_map/all_to_all | solution.py:736
  77.4 4.5 collective-permute-start.6
  87.6 7.4 collective-permute-done.6
  98.5 56.3 %all-gather.6.cloned.1.call-done = bf16[5120,1536]{1,0:T(8,128)(2,1)} async-done(((bf16[160,1536]{1,0:T(8,128)(2,1)}), bf16[5120,1536]{1,0:T(8,128)(2,1)}) %all-gather.6.cloned.1.call-update) | async-done | bytes 15728656 | tf_op jit(solution)/shard_map/all_gather | solution.py:909
  158.8 13.0 %shard_map.600 = (f32[400,384]{1,0:T(8,128)}, bf16[400,384]{1,0:T(8,128)(2,1)}, bf16[4,400,384]{2,1,0:T(8,128)(2,1)}, bf16[4,400,128]{2,1,0:T(8,128)(2,1)}, f32[400,384]{1,0:T(8,128)}) custom-call(f32[400,384]{1,0:T(8,128)} %slice.254.x_ref, bf16[4,1280,1536]{2,1,0:T(8,128)(2,1)} %bitcast.464, f32[4,384]{1,0:T(4,128)} %get-tuple-element.408.gains_ref, ...), custom_call_target="tpu_custom_call" | custom-call | flops 12000000000 | bytes 8000000 | tf_op jit(solution)/shard_map/pallas_call | solution.py:252
  171.8 8.5 %shard_map.601 = (f32[16,384]{1,0:T(8,128)}, bf16[400,384]{1,0:T(8,128)(2,1)}, bf16[4,400,256]{2,1,0:T(8,128)(2,1)}, bf16[4,16,128]{2,1,0:T(8,128)(2,1)}, bf16[4...) custom-call(f32[400,384]{1,0:T(8,128)} %get-tuple-element.134.x_ref, bf16[4,1280,1536]{2,1,0:T(8,128)(2,1)} %bitcast.465, ...), custom_call_target="tpu_custom_call" | custom-call | flops 6000000000 | bytes 8000000 | tf_op jit(solution)/shard_map/pallas_call | solution.py:471
  181.0 23.6 %shard_map.598 = (f32[800,384]{1,0:T(8,128)}, bf16[800,384]{1,0:T(8,128)(2,1)}, bf16[4,800,384]{2,1,0:T(8,128)(2,1)}, bf16[4,800,128]{2,1,0:T(8,128)(2,1)}, f32[800,384]{1,0:T(8,128)}) custom-call(f32[800,384]{1,0:T(8,128)} %copy-done.25, bf16[4,1280,1536]{2,1,0:T(8,128)(2,1)} %bitcast.466, f32[4,384]{1,0:T(4,128)} %get-tuple-element.406.gains_ref, ...), custom_call_target="tpu_custom_call" | custom-call | flops 24000000000 | bytes 8000000 | tf_op jit(solution)/shard_map/pallas_call | solution.py:252
  204.6 10.0 %shard_map.599 = (f32[16,384]{1,0:T(8,128)}, bf16[800,384]{1,0:T(8,128)(2,1)}, bf16[4,800,256]{2,1,0:T(8,128)(2,1)}, bf16[4,16,128]{2,1,0:T(8,128)(2,1)}, bf16[4...) custom-call(f32[800,384]{1,0:T(8,128)} %get-tuple-element.131.x_ref, bf16[4,1280,1536]{2,1,0:T(8,128)(2,1)} %bitcast.467, ...), custom_call_target="tpu_custom_call" | custom-call | flops 12000000000 | bytes 8000000 | tf_op jit(solution)/shard_map/pallas_call | solution.py:471
  215.3 5.3 all-gather
  221.6 23.6 %all-gather.8.cloned.1.call-done = bf16[2688,1024]{1,0:T(8,128)(2,1)} async-done(((bf16[336,1024]{1,0:T(8,128)(2,1)}), bf16[2688,1024]{1,0:T(8,128)(2,1)}) %all-gather.8.cloned.1.call-update) | async-done | bytes 5505040 | tf_op jit(solution)/shard_map/all_gather | solution.py:960
  247.7 5.7 all_gather.25
  270.3 6.5 all-to-all-done.1
  278.2 6.6 shard_map.602
  285.6 16.4 %all_to_all.36.all_ref = f32[32,8,384]{2,1,0:T(8,128)} all-to-all(f32[32,8,384]{2,1,0:T(8,128)S(1)} %broadcast_in_dim.308), channel_id=1, replica_groups=mesh['dp'=8,'mp'=4] {'dp','mp'}, dimensions={0} | all-to-all | bytes 786432 | tf_op jit(solution)/shard_map/all_to_all | solution.py:736
  302.0 9.2 %shard_map.603 = (f32[384,256]{1,0:T(8,128)}, f32[256,2048]{1,0:T(8,128)}, f32[1,128]{1,0:T(1,128)}) custom-call(f32[32,8,384]{2,1,0:T(8,128)} %all_to_all.36.all_ref, f32[8,384]{1,0:T(8,128)} %get-tuple-element.139.own_ref, f32[2,384]{1,0:T(2,128)} %fusion.189.weight_ref, f32[2048,384]{1,0:T(8,128)} %get-tuple-element.141.exp_s_ref, ...), custom_call_target="tpu_custom_call" | custom-call | flops 8000000000 | bytes 8000000 | tf_op jit(solution)/shard_map/pallas_call | solution.py:678
  314.6 11.6 %all-to-all-done.3 = f32[8,48,256]{2,1,0:T(8,128)S(1)} async-done(((f32[8,48,256]{2,1,0:T(8,128)}), f32[8,48,256]{2,1,0:T(8,128)S(1)}, u32[]{:S(2)}, u32[]{:S(2)}) %all-to-all-start.3) | async-done | bytes 393248 | tf_op jit(solution)/shard_map/all_to_all | solution.py:1004
  335.4 10.3 %all_to_all.37 = f32[4,48,512]{2,1,0:T(8,128)S(1)} all-to-all(f32[4,48,512]{2,1,0:T(8,128)S(1)} %bitcast.439), channel_id=1, replica_groups=mesh['dp'=8,'mp'=4] {'mp'}, dimensions={0} | all-to-all | bytes 786432 | tf_op jit(solution)/shard_map/all_to_all | solution.py:1011
  348.9 3.9 collective-permute-done.13
  353.8 16.0 %shard_map.604 = (f32[4,1280,384]{2,1,0:T(8,128)}, f32[4,384]{1,0:T(4,128)}, f32[800,384]{1,0:T(8,128)}) custom-call(f32[800,384]{1,0:T(8,128)} %get-tuple-element.131.x_ref, bf16[4,1280,1536]{2,1,0:T(8,128)(2,1)} %bitcast.468, f32[4,384]{1,0:T(4,128)} %get-tuple-element.405.gains_ref, s32[32,1]{1,0:T(8,128)} %copy.190.seg_cls_ref, ...), custom_call_target="tpu_custom_call" | custom-call | flops 16000000000 | bytes 16000000 | tf_op jit(solution)/shard_map/pallas_call | solution.py:491
  369.8 4.5 dynamic-slice_bitcast_fusion.1
  379.8 4.1 all-to-all-start.5
  391.8 10.8 %shard_map.605 = (f32[4,1280,384]{2,1,0:T(8,128)}, f32[800,384]{1,0:T(8,128)}) custom-call(bf16[4,1280,1536]{2,1,0:T(8,128)(2,1)} %bitcast.469, f32[4,384]{1,0:T(4,128)} %get-tuple-element.406.gains_ref, f32[800,384]{1,0:T(8,128)} %get-tuple-element.147.x2_ref, f32[800,384]{1,0:T(8,128)} %get-tuple-element.156.grad_ref), custom_call_target="tpu_custom_call" | custom-call | flops 10400000000 | bytes 8000000 | tf_op jit(solution)/shard_map/pallas_call | solution.py:277
  416.6 11.6 %shard_map.606 = (f32[4,1280,384]{2,1,0:T(8,128)}, f32[800,384]{1,0:T(8,128)}, f32[2,384]{1,0:T(2,128)}) custom-call(bf16[4,1280,1536]{2,1,0:T(8,128)(2,1)} %bitcast.470, f32[4,384]{1,0:T(4,128)} %get-tuple-element.406.gains_ref, f32[800,384]{1,0:T(8,128)} %get-tuple-element.147.x2_ref, ...), custom_call_target="tpu_custom_call", output_to_operand_aliasing={{0}: (5, {})} | custom-call | flops 10400000000 | bytes 8000000 | tf_op jit(solution)/shard_map/pallas_call | solution.py:277
  428.3 32.9 %collective-permute-start.27 = (f32[32,2048]{1,0:T(8,128)}, f32[32,2048]{1,0:T(8,128)}, u32[]{:S(2)}, u32[]{:S(2)}) collective-permute-start(f32[32,2048]{1,0:T(8,128)} %get-tuple-element.189), channel_id=1, source_target_pairs={{0,28},{4,0},{8,4},{12,8},{16,12},{20,16},{24,20},{28,24},{1,29},{... | collective-permute-start | bytes 786440 | tf_op jit(solution)/shard_map/ppermute | solution.py:748
  468.4 14.8 %shard_map.607 = (f32[4,1280,384]{2,1,0:T(8,128)}, f32[800,384]{1,0:T(8,128)}) custom-call(bf16[4,1280,1536]{2,1,0:T(8,128)(2,1)} %bitcast.471, f32[4,384]{1,0:T(4,128)} %get-tuple-element.406.gains_ref, s32[2,400,1]{2,1,0:T(8,128)} %add_select_fusion.4.seg_col_ref, s32[2,1,400]{2,1,0:T(1,128)} %and_select_fusion.seg_row_ref, ...), custom_call_target="tpu_custom_call", output_to_operand_aliasing={{0}: (9, {})} | custom-call | flops 15200000000 | bytes 8000000 | tf_op jit(solution)/shard_map/pallas_call | solution.py:311
  488.8 15.7 %shard_map.608 = (f32[4,1280,384]{2,1,0:T(8,128)}, f32[2,384]{1,0:T(2,128)}) custom-call(bf16[4,1280,1536]{2,1,0:T(8,128)(2,1)} %bitcast.472, f32[4,384]{1,0:T(4,128)} %get-tuple-element.406.gains_ref, s32[2,400,1]{2,1,0:T(8,128)} %add_select_fusion.4.seg_col_ref, s32[2,1,400]{2,1,0:T(1,128)} %and_select_fusion.seg_row_ref, ...), custom_call_target="tpu_custom_call", output_to_operand_aliasing={{0}: (11, {})} | custom-call | flops 15200000000 | bytes 8000000 | tf_op jit(solution)/shard_map/pallas_call | solution.py:311
  504.5 4.3 dynamic-slice_bitcast_fusion
  509.1 7.0 collective-permute-done.28
  525.1 4.8 collective-permute-done.29
  535.0 9.0 %collective-permute-done.30 = f32[2,160,384]{2,1,0:T(8,128)S(1)} collective-permute-done((f32[2,160,384]{2,1,0:T(8,128)S(1)}, f32[2,160,384]{2,1,0:T(8,128)S(1)}, u32[]{:S(2)}, u32[]{:S(2)}) %collective-permute-start.30) | collective-permute-done | bytes 491552 | tf_op jit(solution)/shard_map/ppermute | solution.py:829
  552.5 4.7 collective-permute-done.31
  566.7 7.4 collective-permute-done.35
  577.7 6.9 collective-permute-done.39
  586.2 5.4 collective-permute-done.36
  593.2 5.8 collective-permute-done.37
  605.8 4.4 all-to-all-start.6
  613.9 6.2 collective-permute-done.45
  636.7 4.5 dynamic-slice_select_fusion.3
  657.7 3.9 dynamic_update_slice.125
  661.6 3.9 dynamic_update_slice.126
  682.5 3.9 dynamic_update_slice.132
  688.5 5.2 fusion.40.stats_ref
  695.7 51.0 %shard_map.609 = f32[2,384,384]{2,1,0:T(8,128)} custom-call(f32[2,384,384]{2,1,0:T(8,128)} %fusion.40.stats_ref, f32[2,384,384]{2,1,0:T(8,128)} %dynamic-slice_bitcast_fusion.2.bases_ref), custom_call_target="tpu_custom_call" | custom-call | flops 60000002048 | bytes 6000000 | tf_op jit(solution)/shard_map/pallas_call | solution.py:571
  750.4 4.6 multiply_add_fusion.2
  761.7 5.2 multiply_add_fusion
  766.9 10.0 %collective-permute-done.58 = f32[2,384,384]{2,1,0:T(8,128)S(1)} collective-permute-done((f32[2,384,384]{2,1,0:T(8,128)}, f32[2,384,384]{2,1,0:T(8,128)S(1)}, u32[]{:S(2)}, u32[]{:S(2)}) %collective-permute-start.58) | collective-permute-done | bytes 1179680 | tf_op jit(solution)/shard_map/ppermute | solution.py:1143
  787.8 5.1 fusion.123
  792.9 4.9 fusion.36
  (475 shorter events, 256.8 us)
Async XLA Ops:
  7.2 147.6 %all-gather.6.cloned.1.call-start = ((), (), s32[]{:S(2)}) async-start(), calls=%async_computation.7 | async-start | bytes 16220160 | tf_op jit(solution)/shard_map/all_gather | solution.py:909
  13.8 63.5 %collective-permute-start.1 = (bf16[2,32,2048]{2,1,0:T(8,128)(2,1)}, bf16[2,32,2048]{2,1,0:T(8,128)(2,1)}, u32[]{:S(2)}, u32[]{:S(2)}) collective-permute-start(bf16[2,32,2048]{2,1,0:T(8,128)(2,1)} %pad_maximum_fusion.11), channel_id=1, source_target_pairs={{0,4},{4,8},{8,12},{12,16},{16,20},{20,24},{24,28},{28,0},{1,5},{5... | collective-permute-start | bytes 786440 | tf_op jit(solution)/shard_map/ppermute | solution.py:748
  17.6 65.3 %collective-permute-start.2 = (bf16[2,32,2048]{2,1,0:T(8,128)(2,1)}, bf16[2,32,2048]{2,1,0:T(8,128)(2,1)}, u32[]{:S(2)}, u32[]{:S(2)}) collective-permute-start(bf16[2,32,2048]{2,1,0:T(8,128)(2,1)} %pad_maximum_fusion.12), channel_id=1, source_target_pairs={{0,8},{4,12},{8,16},{12,20},{16,24},{20,28},{24,0},{28,4},{1,9},{5... | collective-permute-start | bytes 786440 | tf_op jit(solution)/shard_map/ppermute | solution.py:748
  19.8 64.7 %collective-permute-start.3 = (bf16[2,32,2048]{2,1,0:T(8,128)(2,1)}, bf16[2,32,2048]{2,1,0:T(8,128)(2,1)}, u32[]{:S(2)}, u32[]{:S(2)}) collective-permute-start(bf16[2,32,2048]{2,1,0:T(8,128)(2,1)} %pad_maximum_fusion.13), channel_id=1, source_target_pairs={{0,12},{4,16},{8,20},{12,24},{16,28},{20,0},{24,4},{28,8},{1,13},{... | collective-permute-start | bytes 786440 | tf_op jit(solution)/shard_map/ppermute | solution.py:748
  23.1 62.5 %collective-permute-start.4 = (bf16[2,32,2048]{2,1,0:T(8,128)(2,1)}, bf16[2,32,2048]{2,1,0:T(8,128)(2,1)}, u32[]{:S(2)}, u32[]{:S(2)}) collective-permute-start(bf16[2,32,2048]{2,1,0:T(8,128)(2,1)} %pad_maximum_fusion.14), channel_id=1, source_target_pairs={{0,16},{4,20},{8,24},{12,28},{16,0},{20,4},{24,8},{28,12},{1,17},{... | collective-permute-start | bytes 786440 | tf_op jit(solution)/shard_map/ppermute | solution.py:748
  25.1 61.6 %collective-permute-start.5 = (bf16[2,32,2048]{2,1,0:T(8,128)(2,1)}, bf16[2,32,2048]{2,1,0:T(8,128)(2,1)}, u32[]{:S(2)}, u32[]{:S(2)}) collective-permute-start(bf16[2,32,2048]{2,1,0:T(8,128)(2,1)} %pad_maximum_fusion.15), channel_id=1, source_target_pairs={{0,20},{4,24},{8,28},{12,0},{16,4},{20,8},{24,12},{28,16},{1,21},{... | collective-permute-start | bytes 786440 | tf_op jit(solution)/shard_map/ppermute | solution.py:748
  31.6 44.6 %all-to-all-start = ((s32[8,1,4]{2,1,0:T(1,128)}), s32[8,1,4]{2,1,0:T(1,128)S(1)}, u32[]{:S(2)}, u32[]{:S(2)}) async-start(s32[8,1,4]{2,1,0:T(1,128)} %broadcast_in_dim.303), calls=%async_computation | async-start | bytes 8192 | tf_op jit(solution)/shard_map/all_to_all | solution.py:736
  34.9 210.3 %all-gather.8.cloned.1.call-start = ((), (), s32[]{:S(2)}) async-start(), calls=%async_computation.8 | async-start | bytes 6193152 | tf_op jit(solution)/shard_map/all_gather | solution.py:960
  77.4 17.7 %collective-permute-start.6 = (bf16[2,32,2048]{2,1,0:T(8,128)(2,1)}, bf16[2,32,2048]{2,1,0:T(8,128)(2,1)S(1)}, u32[]{:S(2)}, u32[]{:S(2)}) collective-permute-start(bf16[2,32,2048]{2,1,0:T(8,128)(2,1)} %pad_maximum_fusion.16), channel_id=1, source_target_pairs={{0,24},{4,28},{8,0},{12,4},{16,8},{20,12},{24,16},{28,20},{1,25},{... | collective-permute-start | bytes 786440 | tf_op jit(solution)/shard_map/ppermute | solution.py:748
  82.9 14.7 %collective-permute-start.7 = (bf16[2,32,2048]{2,1,0:T(8,128)(2,1)}, bf16[2,32,2048]{2,1,0:T(8,128)(2,1)S(1)}, u32[]{:S(2)}, u32[]{:S(2)}) collective-permute-start(bf16[2,32,2048]{2,1,0:T(8,128)(2,1)} %pad_maximum_fusion.17), channel_id=1, source_target_pairs={{0,28},{4,0},{8,4},{12,8},{16,12},{20,16},{24,20},{28,24},{1,29},{... | collective-permute-start | bytes 786440 | tf_op jit(solution)/shard_map/ppermute | solution.py:748
  84.6 13.0 %collective-permute-start = (bf16[384,384]{1,0:T(8,128)(2,1)S(1)}, bf16[384,384]{1,0:T(8,128)(2,1)S(1)}, u32[]{:S(2)}, u32[]{:S(2)}) collective-permute-start(bf16[384,384]{1,0:T(8,128)(2,1)S(1)} %copy-done.26), channel_id=1, source_target_pairs={{0,1},{1,0},{2,3},{3,2},{4,5},{5,4},{6,7},{7,6},{8,9},{9,8},{10,11... | collective-permute-start | bytes 884744 | tf_op jit(solution)/shard_map/ppermute | solution.py:932
  265.3 11.6 %all-to-all-start.1 = ((bf16[8,56,256]{2,1,0:T(8,128)(2,1)}), bf16[8,56,256]{2,1,0:T(8,128)(2,1)S(1)}, u32[]{:S(2)}, u32[]{:S(2)}) async-start(bf16[8,56,256]{2,1,0:T(8,128)(2,1)} %broadcast_in_dim.307), calls=%async_computation.1 | async-start | bytes 458752 | tf_op jit(solution)/shard_map/all_to_all | solution.py:736
  311.2 15.0 %all-to-all-start.3 = ((f32[8,48,256]{2,1,0:T(8,128)}), f32[8,48,256]{2,1,0:T(8,128)S(1)}, u32[]{:S(2)}, u32[]{:S(2)}) async-start(f32[8,48,256]{2,1,0:T(8,128)} %bitcast.449), calls=%async_computation.3 | async-start | bytes 786432 | tf_op jit(solution)/shard_map/all_to_all | solution.py:1004
  374.3 30.7 %collective-permute-start.14 = (f32[2,8,160,384]{3,2,1,0:T(8,128)}, f32[2,8,160,384]{3,2,1,0:T(8,128)}, u32[]{:S(2)}, u32[]{:S(2)}) collective-permute-start(f32[2,8,160,384]{3,2,1,0:T(8,128)} %dynamic-slice_bitcast_fusion.1), channel_id=1, source_target_pairs={{0,1},{1,0},{2,3},{3,2},{4,5},{5,4},{6,7},{7,6},{8,9},{9,8},{10,11... | collective-permute-start | bytes 11796488 | tf_op jit(solution)/shard_map/ppermute | solution.py:1036
  379.8 129.0 %all-to-all-start.5 = ((bf16[8,48,336]{2,1,0:T(8,128)(2,1)}), bf16[8,48,336]{2,1,0:T(8,128)(2,1)}, u32[]{:S(2)}, u32[]{:S(2)}) async-start(bf16[8,48,336]{2,1,0:T(8,128)(2,1)} %bitcast.414), calls=%async_computation.5 | async-start | bytes 589824 | tf_op jit(solution)/shard_map/all_to_all | solution.py:1028
  383.9 125.0 %all-gather.10.cloned.1.call-start = ((), (), s32[]{:S(2)}) async-start(), calls=%async_computation.9 | async-start | bytes 1327104 | tf_op jit(solution)/shard_map/all_gather | solution.py:1029
  384.0 18.6 %collective-permute-start.15 = (f32[32,2048]{1,0:T(8,128)}, f32[32,2048]{1,0:T(8,128)S(1)}, u32[]{:S(2)}, u32[]{:S(2)}) collective-permute-start(f32[32,2048]{1,0:T(8,128)} %get-tuple-element.160), channel_id=1, source_target_pairs={{0,4},{4,8},{8,12},{12,16},{16,20},{20,24},{24,28},{28,0},{1,5},{5... | collective-permute-start | bytes 786440 | tf_op jit(solution)/shard_map/ppermute | solution.py:748
  385.8 19.2 %collective-permute-start.16 = (f32[32,2048]{1,0:T(8,128)S(1)}, f32[32,2048]{1,0:T(8,128)S(1)}, u32[]{:S(2)}, u32[]{:S(2)}) collective-permute-start(f32[32,2048]{1,0:T(8,128)S(1)} %get-tuple-element.161), channel_id=1, source_target_pairs={{0,8},{4,12},{8,16},{12,20},{16,24},{20,28},{24,0},{28,4},{1,9},{5... | collective-permute-start | bytes 786440 | tf_op jit(solution)/shard_map/ppermute | solution.py:748
  387.3 79.0 %collective-permute-start.19 = (f32[32,2048]{1,0:T(8,128)}, f32[32,2048]{1,0:T(8,128)}, u32[]{:S(2)}, u32[]{:S(2)}) collective-permute-start(f32[32,2048]{1,0:T(8,128)} %get-tuple-element.167), channel_id=1, source_target_pairs={{0,12},{4,16},{8,20},{12,24},{16,28},{20,0},{24,4},{28,8},{1,13},{... | collective-permute-start | bytes 786440 | tf_op jit(solution)/shard_map/ppermute | solution.py:748
  389.7 76.6 %collective-permute-start.20 = (f32[32,2048]{1,0:T(8,128)}, f32[32,2048]{1,0:T(8,128)}, u32[]{:S(2)}, u32[]{:S(2)}) collective-permute-start(f32[32,2048]{1,0:T(8,128)} %get-tuple-element.168), channel_id=1, source_target_pairs={{0,16},{4,20},{8,24},{12,28},{16,0},{20,4},{24,8},{28,12},{1,17},{... | collective-permute-start | bytes 786440 | tf_op jit(solution)/shard_map/ppermute | solution.py:748
  402.6 86.3 %collective-permute-start.23 = (f32[32,2048]{1,0:T(8,128)}, f32[32,2048]{1,0:T(8,128)}, u32[]{:S(2)}, u32[]{:S(2)}) collective-permute-start(f32[32,2048]{1,0:T(8,128)} %get-tuple-element.175), channel_id=1, source_target_pairs={{0,20},{4,24},{8,28},{12,0},{16,4},{20,8},{24,12},{28,16},{1,21},{... | collective-permute-start | bytes 786440 | tf_op jit(solution)/shard_map/ppermute | solution.py:748
  412.4 15.8 %collective-permute-start.17 = (f32[1,160,384]{2,1,0:T(8,128)}, f32[1,160,384]{2,1,0:T(8,128)}, u32[]{:S(2)}, u32[]{:S(2)}) collective-permute-start(f32[1,160,384]{2,1,0:T(8,128)} %get-tuple-element.357), channel_id=1, source_target_pairs={{0,8},{8,16},{16,24},{24,28},{28,20},{20,12},{12,4},{4,0},{1,9},{9... | collective-permute-start | bytes 737288 | tf_op jit(solution)/shard_map/ppermute | solution.py:829
  412.9 15.3 %collective-permute-start.18 = (f32[1,160,384]{2,1,0:T(8,128)}, f32[1,160,384]{2,1,0:T(8,128)}, u32[]{:S(2)}, u32[]{:S(2)}) collective-permute-start(f32[1,160,384]{2,1,0:T(8,128)} %get-tuple-element.359), channel_id=1, source_target_pairs={{0,4},{8,0},{16,8},{24,16},{28,24},{20,28},{12,20},{4,12},{1,5},{9... | collective-permute-start | bytes 737288 | tf_op jit(solution)/shard_map/ppermute | solution.py:830
  428.2 60.6 %collective-permute-start.24 = (f32[32,2048]{1,0:T(8,128)}, f32[32,2048]{1,0:T(8,128)}, u32[]{:S(2)}, u32[]{:S(2)}) collective-permute-start(f32[32,2048]{1,0:T(8,128)} %get-tuple-element.176), channel_id=1, source_target_pairs={{0,24},{4,28},{8,0},{12,4},{16,8},{20,12},{24,16},{28,20},{1,25},{... | collective-permute-start | bytes 786440 | tf_op jit(solution)/shard_map/ppermute | solution.py:748
  428.3 80.6 %collective-permute-start.27 = (f32[32,2048]{1,0:T(8,128)}, f32[32,2048]{1,0:T(8,128)}, u32[]{:S(2)}, u32[]{:S(2)}) collective-permute-start(f32[32,2048]{1,0:T(8,128)} %get-tuple-element.189), channel_id=1, source_target_pairs={{0,28},{4,0},{8,4},{12,8},{16,12},{20,16},{24,20},{28,24},{1,29},{... | collective-permute-start | bytes 786440 | tf_op jit(solution)/shard_map/ppermute | solution.py:748
  466.2 17.0 %collective-permute-start.22 = (f32[2,160,384]{2,1,0:T(8,128)}, f32[2,160,384]{2,1,0:T(8,128)}, u32[]{:S(2)}, u32[]{:S(2)}) collective-permute-start(f32[2,160,384]{2,1,0:T(8,128)} %pad_maximum_fusion.6), channel_id=1, source_target_pairs={{0,4},{8,0},{16,8},{24,16},{28,24},{20,28},{12,20},{4,12},{1,5},{9... | collective-permute-start | bytes 1474568 | tf_op jit(solution)/shard_map/ppermute | solution.py:830
  466.2 17.0 %collective-permute-start.21 = (f32[2,160,384]{2,1,0:T(8,128)}, f32[2,160,384]{2,1,0:T(8,128)}, u32[]{:S(2)}, u32[]{:S(2)}) collective-permute-start(f32[2,160,384]{2,1,0:T(8,128)} %pad_maximum_fusion.5), channel_id=1, source_target_pairs={{0,8},{8,16},{16,24},{24,28},{28,20},{20,12},{12,4},{4,0},{1,9},{9... | collective-permute-start | bytes 1474568 | tf_op jit(solution)/shard_map/ppermute | solution.py:829
  486.8 22.1 %collective-permute-start.25 = (f32[2,160,384]{2,1,0:T(8,128)}, f32[2,160,384]{2,1,0:T(8,128)S(1)}, u32[]{:S(2)}, u32[]{:S(2)}) collective-permute-start(f32[2,160,384]{2,1,0:T(8,128)} %get-tuple-element.355), channel_id=1, source_target_pairs={{0,8},{8,16},{16,24},{24,28},{28,20},{20,12},{12,4},{4,0},{1,9},{9... | collective-permute-start | bytes 1474568 | tf_op jit(solution)/shard_map/ppermute | solution.py:829
  486.8 22.0 %collective-permute-start.26 = (f32[2,160,384]{2,1,0:T(8,128)}, f32[2,160,384]{2,1,0:T(8,128)S(1)}, u32[]{:S(2)}, u32[]{:S(2)}) collective-permute-start(f32[2,160,384]{2,1,0:T(8,128)} %get-tuple-element.354), channel_id=1, source_target_pairs={{0,4},{8,0},{16,8},{24,16},{28,24},{20,28},{12,20},{4,12},{1,5},{9... | collective-permute-start | bytes 1474568 | tf_op jit(solution)/shard_map/ppermute | solution.py:830
  531.5 12.5 %collective-permute-start.30 = (f32[2,160,384]{2,1,0:T(8,128)S(1)}, f32[2,160,384]{2,1,0:T(8,128)S(1)}, u32[]{:S(2)}, u32[]{:S(2)}) collective-permute-start(f32[2,160,384]{2,1,0:T(8,128)S(1)} %pad_maximum_fusion.7), channel_id=1, source_target_pairs={{0,8},{8,16},{16,24},{24,28},{28,20},{20,12},{12,4},{4,0},{1,9},{9... | collective-permute-start | bytes 1474568 | tf_op jit(solution)/shard_map/ppermute | solution.py:829
  533.1 19.4 %collective-permute-start.34 = (f32[2,160,384]{2,1,0:T(8,128)S(1)}, f32[2,160,384]{2,1,0:T(8,128)S(1)}, u32[]{:S(2)}, u32[]{:S(2)}) collective-permute-start(f32[2,160,384]{2,1,0:T(8,128)S(1)} %pad_maximum_fusion.8), channel_id=1, source_target_pairs={{0,4},{8,0},{16,8},{24,16},{28,24},{20,28},{12,20},{4,12},{1,5},{9... | collective-permute-start | bytes 1474568 | tf_op jit(solution)/shard_map/ppermute | solution.py:830
  545.5 11.8 %collective-permute-start.31 = (f32[2,160,384]{2,1,0:T(8,128)}, f32[2,160,384]{2,1,0:T(8,128)S(1)}, u32[]{:S(2)}, u32[]{:S(2)}) collective-permute-start(f32[2,160,384]{2,1,0:T(8,128)} %bitcast_add_fusion.8), channel_id=1, source_target_pairs={{0,8},{8,16},{16,24},{24,28},{28,20},{20,12},{12,4},{4,0},{1,9},{9... | collective-permute-start | bytes 1474568 | tf_op jit(solution)/shard_map/ppermute | solution.py:829
  552.1 13.5 %collective-permute-start.42 = (f32[16,384]{1,0:T(8,128)S(1)}, f32[16,384]{1,0:T(8,128)S(1)}, u32[]{:S(2)}, u32[]{:S(2)}) collective-permute-start(f32[16,384]{1,0:T(8,128)S(1)} %add.804), channel_id=1, source_target_pairs={{0,2},{1,3},{2,0},{3,1},{4,6},{5,7},{6,4},{7,5},{8,10},{9,11},{10,... | collective-permute-start | bytes 73736 | tf_op jit(solution)/shard_map/ppermute | solution.py:724
  559.8 14.2 %collective-permute-start.35 = (f32[2,160,384]{2,1,0:T(8,128)S(1)}, f32[2,160,384]{2,1,0:T(8,128)S(1)}, u32[]{:S(2)}, u32[]{:S(2)}) collective-permute-start(f32[2,160,384]{2,1,0:T(8,128)S(1)} %get-tuple-element.345), channel_id=1, source_target_pairs={{0,4},{8,0},{16,8},{24,16},{28,24},{20,28},{12,20},{4,12},{1,5},{9... | collective-permute-start | bytes 1474568 | tf_op jit(solution)/shard_map/ppermute | solution.py:830
  563.5 14.2 %collective-permute-start.38 = (f32[2,160,384]{2,1,0:T(8,128)S(1)}, f32[2,160,384]{2,1,0:T(8,128)S(1)}, u32[]{:S(2)}, u32[]{:S(2)}) collective-permute-start(f32[2,160,384]{2,1,0:T(8,128)S(1)} %get-tuple-element.352), channel_id=1, source_target_pairs={{0,8},{8,16},{16,24},{24,28},{28,20},{20,12},{12,4},{4,0},{1,9},{9... | collective-permute-start | bytes 1474568 | tf_op jit(solution)/shard_map/ppermute | solution.py:829
  564.6 20.0 %collective-permute-start.39 = (f32[2,160,384]{2,1,0:T(8,128)S(1)}, f32[2,160,384]{2,1,0:T(8,128)S(1)}, u32[]{:S(2)}, u32[]{:S(2)}) collective-permute-start(f32[2,160,384]{2,1,0:T(8,128)S(1)} %get-tuple-element.353), channel_id=1, source_target_pairs={{0,4},{8,0},{16,8},{24,16},{28,24},{20,28},{12,20},{4,12},{1,5},{9... | collective-permute-start | bytes 1474568 | tf_op jit(solution)/shard_map/ppermute | solution.py:830
  565.6 20.6 %collective-permute-start.32 = (f32[2,160,384]{2,1,0:T(8,128)S(1)}, f32[2,160,384]{2,1,0:T(8,128)S(1)}, u32[]{:S(2)}, u32[]{:S(2)}) collective-permute-start(f32[2,160,384]{2,1,0:T(8,128)S(1)} %get-tuple-element.344), channel_id=1, source_target_pairs={{0,8},{8,16},{16,24},{24,28},{28,20},{20,12},{12,4},{4,0},{1,9},{9... | collective-permute-start | bytes 1474568 | tf_op jit(solution)/shard_map/ppermute | solution.py:829
  575.8 15.8 %collective-permute-start.36 = (f32[2,160,384]{2,1,0:T(8,128)S(1)}, f32[2,160,384]{2,1,0:T(8,128)S(1)}, u32[]{:S(2)}, u32[]{:S(2)}) collective-permute-start(f32[2,160,384]{2,1,0:T(8,128)S(1)} %bitcast_add_fusion.7), channel_id=1, source_target_pairs={{0,4},{8,0},{16,8},{24,16},{28,24},{20,28},{12,20},{4,12},{1,5},{9... | collective-permute-start | bytes 1474568 | tf_op jit(solution)/shard_map/ppermute | solution.py:830
  605.8 171.4 %all-to-all-start.6 = ((f32[8,1,2048]{2,1,0:T(1,128)}), f32[8,1,2048]{2,1,0:T(1,128)}, u32[]{:S(2)}, u32[]{:S(2)}) async-start(f32[8,1,2048]{2,1,0:T(1,128)} %broadcast_in_dim.355), calls=%async_computation.6 | async-start | bytes 131072 | tf_op jit(solution)/shard_map/all_to_all | solution.py:736
  636.4 17.8 %collective-permute-start.51 = (f32[1,128]{1,0:T(1,128)S(1)}, f32[1,128]{1,0:T(1,128)S(1)}, u32[]{:S(2)}, u32[]{:S(2)}) collective-permute-start(f32[1,128]{1,0:T(1,128)S(1)} %broadcast_in_dim.325), channel_id=1, source_target_pairs={{0,1},{1,0},{2,3},{3,2},{4,5},{5,4},{6,7},{7,6},{8,9},{9,8},{10,11... | collective-permute-start | bytes 1544 | tf_op jit(solution)/shard_map/ppermute | solution.py:724
  641.2 47.3 %collective-permute-start.53 = (bf16[2,384,384]{2,1,0:T(8,128)(2,1)}, bf16[2,384,384]{2,1,0:T(8,128)(2,1)}, u32[]{:S(2)}, u32[]{:S(2)}) collective-permute-start(bf16[2,384,384]{2,1,0:T(8,128)(2,1)} %get-tuple-element.391), channel_id=1, source_target_pairs={{0,1},{1,0},{2,3},{3,2},{4,5},{5,4},{6,7},{7,6},{8,9},{9,8},{10,11... | collective-permute-start | bytes 1769480 | tf_op jit(solution)/shard_map/ppermute | solution.py:1114
  641.7 46.8 %collective-permute-start.54 = (bf16[2,384,384]{2,1,0:T(8,128)(2,1)}, bf16[2,384,384]{2,1,0:T(8,128)(2,1)}, u32[]{:S(2)}, u32[]{:S(2)}) collective-permute-start(bf16[2,384,384]{2,1,0:T(8,128)(2,1)} %get-tuple-element.390), channel_id=1, source_target_pairs={{0,2},{1,3},{2,0},{3,1},{4,6},{5,7},{6,4},{7,5},{8,10},{9,11},{10,... | collective-permute-start | bytes 1769480 | tf_op jit(solution)/shard_map/ppermute | solution.py:1114
  642.1 46.4 %collective-permute-start.55 = (bf16[2,384,384]{2,1,0:T(8,128)(2,1)}, bf16[2,384,384]{2,1,0:T(8,128)(2,1)}, u32[]{:S(2)}, u32[]{:S(2)}) collective-permute-start(bf16[2,384,384]{2,1,0:T(8,128)(2,1)} %get-tuple-element.389), channel_id=1, source_target_pairs={{0,3},{1,2},{2,1},{3,0},{4,7},{5,6},{6,5},{7,4},{8,11},{9,10},{10,... | collective-permute-start | bytes 1769480 | tf_op jit(solution)/shard_map/ppermute | solution.py:1114
  654.8 31.6 %collective-permute-start.52 = (f32[1,128]{1,0:T(1,128)S(1)}, f32[1,128]{1,0:T(1,128)S(1)}, u32[]{:S(2)}, u32[]{:S(2)}) collective-permute-start(f32[1,128]{1,0:T(1,128)S(1)} %broadcast_add_fusion), channel_id=1, source_target_pairs={{0,2},{1,3},{2,0},{3,1},{4,6},{5,7},{6,4},{7,5},{8,10},{9,11},{10,... | collective-permute-start | bytes 1544 | tf_op jit(solution)/shard_map/ppermute | solution.py:724
  693.7 73.3 %collective-permute-start.57 = (f32[2,384,384]{2,1,0:T(8,128)}, f32[2,384,384]{2,1,0:T(8,128)}, u32[]{:S(2)}, u32[]{:S(2)}) collective-permute-start(f32[2,384,384]{2,1,0:T(8,128)} %fusion.40.stats_ref), channel_id=1, source_target_pairs={{0,2},{1,3},{2,0},{3,1},{4,6},{5,7},{6,4},{7,5},{8,10},{9,11},{10,... | collective-permute-start | bytes 3538952 | tf_op jit(solution)/shard_map/ppermute | solution.py:1123
  695.0 51.8 %collective-permute-start.56 = (f32[336,512]{1,0:T(8,128)S(1)}, f32[336,512]{1,0:T(8,128)S(1)}, u32[]{:S(2)}, u32[]{:S(2)}) collective-permute-start(f32[336,512]{1,0:T(8,128)S(1)} %get-tuple-element.208), channel_id=1, source_target_pairs={{0,2},{1,3},{2,0},{3,1},{4,6},{5,7},{6,4},{7,5},{8,10},{9,11},{10,... | collective-permute-start | bytes 2064392 | tf_op jit(solution)/shard_map/ppermute | solution.py:1125
  748.4 28.6 %collective-permute-start.58 = (f32[2,384,384]{2,1,0:T(8,128)}, f32[2,384,384]{2,1,0:T(8,128)S(1)}, u32[]{:S(2)}, u32[]{:S(2)}) collective-permute-start(f32[2,384,384]{2,1,0:T(8,128)} %shard_map.609), channel_id=1, source_target_pairs={{0,2},{1,3},{2,0},{3,1},{4,6},{5,7},{6,4},{7,5},{8,10},{9,11},{10,... | collective-permute-start | bytes 3538952 | tf_op jit(solution)/shard_map/ppermute | solution.py:1143
  782.0 16.8 %collective-permute-start.61 = (f32[2,2,384,384]{3,2,1,0:T(8,128)S(1)}, f32[2,2,384,384]{3,2,1,0:T(8,128)S(1)}, u32[]{:S(2)}, u32[]{:S(2)}) collective-permute-start(f32[2,2,384,384]{3,2,1,0:T(8,128)S(1)} %bitcast_dynamic-update-slice_fusion.5), channel_id=1, source_target_pairs={{0,1},{1,0},{2,3},{3,2},{4,5},{5,4},{6,7},{7,6},{8,9},{9,8},{10,11... | collective-permute-start | bytes 7077896 | tf_op jit(solution)/shard_map/ppermute | solution.py:857
  (77 other events, 786.8 us)
Sparse Core Ops, SparseCore 0:
  11.5 143.2 all-gather.5
  157.6 87.6 all-gather.7
  391.9 59.6 all-gather.9

commit v4 on v3

--- a/solution.py
+++ b/solution.py
@@ -1020,37 +1020,36 @@
     def pick_proto(i):
         return lax.dynamic_slice_in_dim(grad_proto, unsigned(i * proto_rows), proto_rows, 0)
 
-    proto_g = swap_pieces(pick_proto, grad_unit)
+    proto_g = swap_pieces(pick_proto)
     rows_left = jnp.concatenate([feats_s, b1[:n_s], grad_third], axis=1)
     head_rows = head_w.shape[0]
 
-    left = rows_left.reshape(n_s, dp_count, head_rows).transpose(1, 0, 2)
-    left = lax.all_to_all(left, "dp", 0, 0).reshape(dp_count * n_s, head_rows)
     right = lax.all_gather(jnp.concatenate([grad_a1, grad_a2, b2_s], axis=1), "dp", axis=0)
     right = right.reshape(dp_count * n_s, 3 * head_cols)
     dwt1, dgains1, grad_x1 = last_bwd(
         CROPS, x1, weights, 3, norm_params[4:8], seg_cls, segment[None], slot, saved1, grad_y
     )
     send1, own1 = core_halves(dwt1, dp_count, core)
-    grad_x1, send1 = lax.optimization_barrier((grad_x1, send1))
+    grad_x1, send1, proto_g = lax.optimization_barrier((grad_x1, send1, proto_g))
     got1 = lax.ppermute(send1, "mp", flip_perm(4, 1))
     mlp_args = (weights, 2, norm_params[0:4], saved0[3], grad_x1)
     dwt0, grad_h2 = mlp_bwd(0, *mlp_args)
-    grad_h2, got1, proto_g[1:3] = lax.optimization_barrier((grad_h2, got1, proto_g[1:3]))
+    grad_h2, got1 = lax.optimization_barrier((grad_h2, got1))
     ring1 = RingScatter(own1 + got1)
     ring1.step(0)
     dwt0, grad_x2, dgains0b = mlp_bwd(1, *mlp_args, (grad_h2, dwt0))
-    grad_x2, proto_g[3:5] = lax.optimization_barrier((ring1.tie(grad_x2), proto_g[3:5]))
+    grad_x2 = ring1.tie(grad_x2)
     ring1.step(1)
     block_args = (weights, 2, norm_params[0:4], seg_col, seg_row, slot, saved0)
+    grad_x2, rows_left = lax.optimization_barrier((grad_x2, rows_left))
+    left = rows_left.reshape(n_s, dp_count, head_rows).transpose(1, 0, 2)
+    left = lax.all_to_all(left, "dp", 0, 0).reshape(dp_count * n_s, head_rows)
     dwt0, grad_h1 = attention_bwd(0, *block_args, grad_x2, dwt0)
-    grad_h1, proto_g[5:7] = lax.optimization_barrier((ring1.tie(grad_h1), proto_g[5:7]))
+    grad_h1 = ring1.tie(grad_h1)
     ring1.step(2)
     dwt0, dgains0a = attention_bwd(1, *block_args, grad_x2, dwt0, (x0, grad_h1))
     send0, own0 = core_halves(dwt0, dp_count, core)
-    send0, proto_g, left, right = lax.optimization_barrier(
-        (ring1.tie(send0), proto_g, left, right)
-    )
+    send0, left, right = lax.optimization_barrier((ring1.tie(send0), left, right))
     stack_ids = dp_index * head_rows + jnp.arange(head_rows)[None, :]
     edges = (0, D, D + HID, D + HID + third.shape[1])
     head_own = sum(

time: 817 us -> 779 us (0.953)
  local copies, waits for them, and re-layouts: 112 us -> 75.6 us
  waiting for transfers between devices: 225 us -> 243 us
  starting transfers between devices: 117 us -> 102 us
    ppermute x14, starting transfers between devices: 58.8 us -> 28.5 us  [swap_pieces(): lax.ppermute(piece, 'dp', shift_perm(count, step + 1))]
    dynamic_update_slice x24 -> x25, local copies, waits for them, and re-layouts: 39.3 us -> 13.3 us  [put(): return lax.dynamic_update_index_in_dim(out, piece, unsigned(index), 0)]
    ppermute x10, waiting for transfers between devices: 11.3 us -> 26.9 us  [sum_over(): array = array + lax.ppermute(array, axis, flip_perm(count, bit))]
    ppermute x8, starting transfers between devices: 5.73 us -> 17.4 us  [step(): self.right = lax.ppermute(self.send_right, 'dp', ring_perm(1))]
    broadcast_in_dim x8 -> x1, local copies, waits for them, and re-layouts: 11.8 us -> 0.27 us  [put(): return lax.dynamic_update_index_in_dim(out, piece, unsigned(index), 0)]
  transfers between devices with their start and end apart: 70 -> 70, of which waited for: 29 -> 31; matrix products, arithmetic and copies ran while one was open for 22% -> 19% of each run, Pallas kernels for 20% -> 23%
where the time goes in v4:
time: 779 us; the launch traced here: 774 us
  waiting for transfers between devices  243 us (31%)
  Pallas kernels  191 us (25%)
  starting transfers between devices  102 us (13%)
  local copies, waits for them, and re-layouts  75.6 us (10%)
  other arithmetic  74.4 us (10%)
  blocking collectives  37.4 us (5%)
  matrix products  30.5 us (4%)
  between operations  20.4 us (3%)
    all_gather x1, waiting for transfers between devices, shards(): lax.all_gather(jnp.concatenate([*own_t, *own_s], axis=1), ('mp', 'dp'), a...  56.3 us
    pallas_call x1, Pallas kernels, renew_bases(): pl.pallas_call(basis_kernel, in_specs=[pl.BlockSpec(memory_space=pltpu.VM...  51.2 us
    all_to_all x3, waiting for transfers between devices, gather_over(): lax.all_to_all(jnp.broadcast_to(array[None], (count, *array.shape)), axis...  37.7 us
    pallas_call x2, Pallas kernels, block_fwd(): pl.pallas_call(block_fwd_kernel, grid=(rows // CHUNK,), in_specs=[s['row'...  36.5 us
    pallas_call x2, Pallas kernels, attention_bwd(): pl.pallas_call(functools.partial(attention_bwd_kernel, bool(last)), grid=...  30.5 us
    ppermute x14, starting transfers between devices, swap_pieces(): lax.ppermute(piece, 'dp', shift_perm(count, step + 1))  28.5 us
    ppermute x10, waiting for transfers between devices, sum_over(): array = array + lax.ppermute(array, axis, flip_perm(count, bit))  26.9 us
    all_gather x1, waiting for transfers between devices, shards(): heads = lax.all_gather(heads, 'dp', axis=0, tiled=True)  23.6 us
  transfers between devices with their start and end apart: 70, of which 31 were waited for; matrix products, arithmetic and copies ran while one was open for 19% of the time, Pallas kernels for 23%

profile of v4, /device:TPU:0, one launch (start us, length us, event | category | flops | bytes accessed | tf_op | source)
XLA Modules:
  0.0 773.6 jit_solution(15568412829425094819)
XLA Ops:
  45.0 31.1 %all-to-all-done = s32[8,1,4]{2,1,0:T(1,128)S(1)} async-done(((s32[8,1,4]{2,1,0:T(1,128)}), s32[8,1,4]{2,1,0:T(1,128)S(1)}, u32[]{:S(2)}, u32[]{:S(2)}) %all-to-all-start) | async-done | bytes 160 | tf_op jit(solution)/shard_map/all_to_all | solution.py:736
  77.4 4.5 collective-permute-start.6
  87.9 7.1 collective-permute-done.6
  98.5 56.3 %all-gather.6.cloned.1.call-done = bf16[5120,1536]{1,0:T(8,128)(2,1)} async-done(((bf16[160,1536]{1,0:T(8,128)(2,1)}), bf16[5120,1536]{1,0:T(8,128)(2,1)}) %all-gather.6.cloned.1.call-update) | async-done | bytes 15728656 | tf_op jit(solution)/shard_map/all_gather | solution.py:909
  158.8 12.9 %shard_map.600 = (f32[400,384]{1,0:T(8,128)}, bf16[400,384]{1,0:T(8,128)(2,1)}, bf16[4,400,384]{2,1,0:T(8,128)(2,1)}, bf16[4,400,128]{2,1,0:T(8,128)(2,1)}, f32[400,384]{1,0:T(8,128)}) custom-call(f32[400,384]{1,0:T(8,128)} %slice.254.x_ref, bf16[4,1280,1536]{2,1,0:T(8,128)(2,1)} %bitcast.472, f32[4,384]{1,0:T(4,128)} %get-tuple-element.380.gains_ref, ...), custom_call_target="tpu_custom_call" | custom-call | flops 12000000000 | bytes 8000000 | tf_op jit(solution)/shard_map/pallas_call | solution.py:252
  171.7 8.4 %shard_map.601 = (f32[16,384]{1,0:T(8,128)}, bf16[400,384]{1,0:T(8,128)(2,1)}, bf16[4,400,256]{2,1,0:T(8,128)(2,1)}, bf16[4,16,128]{2,1,0:T(8,128)(2,1)}, bf16[4...) custom-call(f32[400,384]{1,0:T(8,128)} %get-tuple-element.121.x_ref, bf16[4,1280,1536]{2,1,0:T(8,128)(2,1)} %bitcast.473, ...), custom_call_target="tpu_custom_call" | custom-call | flops 6000000000 | bytes 8000000 | tf_op jit(solution)/shard_map/pallas_call | solution.py:471
  180.9 23.6 %shard_map.598 = (f32[800,384]{1,0:T(8,128)}, bf16[800,384]{1,0:T(8,128)(2,1)}, bf16[4,800,384]{2,1,0:T(8,128)(2,1)}, bf16[4,800,128]{2,1,0:T(8,128)(2,1)}, f32[800,384]{1,0:T(8,128)}) custom-call(f32[800,384]{1,0:T(8,128)} %copy-done.29, bf16[4,1280,1536]{2,1,0:T(8,128)(2,1)} %bitcast.474, f32[4,384]{1,0:T(4,128)} %get-tuple-element.378.gains_ref, ...), custom_call_target="tpu_custom_call" | custom-call | flops 24000000000 | bytes 8000000 | tf_op jit(solution)/shard_map/pallas_call | solution.py:252
  204.5 10.0 %shard_map.599 = (f32[16,384]{1,0:T(8,128)}, bf16[800,384]{1,0:T(8,128)(2,1)}, bf16[4,800,256]{2,1,0:T(8,128)(2,1)}, bf16[4,16,128]{2,1,0:T(8,128)(2,1)}, bf16[4...) custom-call(f32[800,384]{1,0:T(8,128)} %get-tuple-element.118.x_ref, bf16[4,1280,1536]{2,1,0:T(8,128)(2,1)} %bitcast.475, ...), custom_call_target="tpu_custom_call" | custom-call | flops 12000000000 | bytes 8000000 | tf_op jit(solution)/shard_map/pallas_call | solution.py:471
  215.2 5.3 all-gather
  221.6 23.6 %all-gather.8.cloned.1.call-done = bf16[2688,1024]{1,0:T(8,128)(2,1)} async-done(((bf16[336,1024]{1,0:T(8,128)(2,1)}), bf16[2688,1024]{1,0:T(8,128)(2,1)}) %all-gather.8.cloned.1.call-update) | async-done | bytes 5505040 | tf_op jit(solution)/shard_map/all_gather | solution.py:960
  247.7 5.7 all_gather.25
  270.4 6.5 all-to-all-done.1
  278.2 6.6 shard_map.602
  285.6 16.4 %all_to_all.36.all_ref = f32[32,8,384]{2,1,0:T(8,128)} all-to-all(f32[32,8,384]{2,1,0:T(8,128)S(1)} %broadcast_in_dim.308), channel_id=1, replica_groups=mesh['dp'=8,'mp'=4] {'dp','mp'}, dimensions={0} | all-to-all | bytes 786432 | tf_op jit(solution)/shard_map/all_to_all | solution.py:736
  302.0 9.2 %shard_map.603 = (f32[384,256]{1,0:T(8,128)}, f32[256,2048]{1,0:T(8,128)}, f32[1,128]{1,0:T(1,128)}) custom-call(f32[32,8,384]{2,1,0:T(8,128)} %all_to_all.36.all_ref, f32[8,384]{1,0:T(8,128)} %get-tuple-element.126.own_ref, f32[2,384]{1,0:T(2,128)} %fusion.189.weight_ref, f32[2048,384]{1,0:T(8,128)} %get-tuple-element.128.exp_s_ref, ...), custom_call_target="tpu_custom_call" | custom-call | flops 8000000000 | bytes 8000000 | tf_op jit(solution)/shard_map/pallas_call | solution.py:678
  314.7 11.5 %all-to-all-done.3 = f32[8,48,256]{2,1,0:T(8,128)S(1)} async-done(((f32[8,48,256]{2,1,0:T(8,128)}), f32[8,48,256]{2,1,0:T(8,128)S(1)}, u32[]{:S(2)}, u32[]{:S(2)}) %all-to-all-start.3) | async-done | bytes 393248 | tf_op jit(solution)/shard_map/all_to_all | solution.py:1004
  335.6 10.0 %all_to_all.37 = f32[4,48,512]{2,1,0:T(8,128)S(1)} all-to-all(f32[4,48,512]{2,1,0:T(8,128)S(1)} %bitcast.449), channel_id=1, replica_groups=mesh['dp'=8,'mp'=4] {'mp'}, dimensions={0} | all-to-all | bytes 786432 | tf_op jit(solution)/shard_map/all_to_all | solution.py:1011
  357.9 3.8 collective-permute-done.14
  362.2 4.7 collective-permute-start.20
  367.0 16.0 %shard_map.604 = (f32[4,1280,384]{2,1,0:T(8,128)}, f32[4,384]{1,0:T(4,128)}, f32[800,384]{1,0:T(8,128)}) custom-call(f32[800,384]{1,0:T(8,128)} %get-tuple-element.118.x_ref, bf16[4,1280,1536]{2,1,0:T(8,128)(2,1)} %bitcast.476, f32[4,384]{1,0:T(4,128)} %get-tuple-element.377.gains_ref, s32[32,1]{1,0:T(8,128)} %copy.172.seg_cls_ref, ...), custom_call_target="tpu_custom_call" | custom-call | flops 16000000000 | bytes 16000000 | tf_op jit(solution)/shard_map/pallas_call | solution.py:491
  383.1 4.4 dynamic-slice_bitcast_fusion.1
  393.3 10.8 %shard_map.605 = (f32[4,1280,384]{2,1,0:T(8,128)}, f32[800,384]{1,0:T(8,128)}) custom-call(bf16[4,1280,1536]{2,1,0:T(8,128)(2,1)} %bitcast.477, f32[4,384]{1,0:T(4,128)} %get-tuple-element.378.gains_ref, f32[800,384]{1,0:T(8,128)} %get-tuple-element.134.x2_ref, f32[800,384]{1,0:T(8,128)} %get-tuple-element.144.grad_ref), custom_call_target="tpu_custom_call" | custom-call | flops 10400000000 | bytes 8000000 | tf_op jit(solution)/shard_map/pallas_call | solution.py:277
  410.7 8.1 %collective-permute-start.22 = (f32[1,160,384]{2,1,0:T(8,128)}, f32[1,160,384]{2,1,0:T(8,128)}, u32[]{:S(2)}, u32[]{:S(2)}) collective-permute-start(f32[1,160,384]{2,1,0:T(8,128)} %get-tuple-element.329), channel_id=1, source_target_pairs={{0,8},{8,16},{16,24},{24,28},{28,20},{20,12},{12,4},{4,0},{1,9},{9... | collective-permute-start | bytes 737288 | tf_op jit(solution)/shard_map/ppermute | solution.py:829
  418.9 11.6 %shard_map.606 = (f32[4,1280,384]{2,1,0:T(8,128)}, f32[800,384]{1,0:T(8,128)}, f32[2,384]{1,0:T(2,128)}) custom-call(bf16[4,1280,1536]{2,1,0:T(8,128)(2,1)} %bitcast.478, f32[4,384]{1,0:T(4,128)} %get-tuple-element.378.gains_ref, f32[800,384]{1,0:T(8,128)} %get-tuple-element.134.x2_ref, ...), custom_call_target="tpu_custom_call", output_to_operand_aliasing={{0}: (5, {})} | custom-call | flops 10400000000 | bytes 8000000 | tf_op jit(solution)/shard_map/pallas_call | solution.py:277
  434.6 5.8 collective-permute-start.25
  443.4 5.2 all-to-all-start.5
  448.6 14.9 %shard_map.607 = (f32[4,1280,384]{2,1,0:T(8,128)}, f32[800,384]{1,0:T(8,128)}) custom-call(bf16[4,1280,1536]{2,1,0:T(8,128)(2,1)} %bitcast.479, f32[4,384]{1,0:T(4,128)} %get-tuple-element.378.gains_ref, s32[2,400,1]{2,1,0:T(8,128)} %add_select_fusion.4.seg_col_ref, s32[2,1,400]{2,1,0:T(1,128)} %and_select_fusion.seg_row_ref, ...), custom_call_target="tpu_custom_call", output_to_operand_aliasing={{0}: (9, {})} | custom-call | flops 15200000000 | bytes 8000000 | tf_op jit(solution)/shard_map/pallas_call | solution.py:311
  468.4 15.7 %shard_map.608 = (f32[4,1280,384]{2,1,0:T(8,128)}, f32[2,384]{1,0:T(2,128)}) custom-call(bf16[4,1280,1536]{2,1,0:T(8,128)(2,1)} %bitcast.480, f32[4,384]{1,0:T(4,128)} %get-tuple-element.378.gains_ref, s32[2,400,1]{2,1,0:T(8,128)} %add_select_fusion.4.seg_col_ref, s32[2,1,400]{2,1,0:T(1,128)} %and_select_fusion.seg_row_ref, ...), custom_call_target="tpu_custom_call", output_to_operand_aliasing={{0}: (11, {})} | custom-call | flops 15200000000 | bytes 8000000 | tf_op jit(solution)/shard_map/pallas_call | solution.py:311
  484.0 4.3 dynamic-slice_bitcast_fusion
  488.6 7.0 collective-permute-done.28
  504.6 5.0 collective-permute-done.29
  515.0 9.6 %collective-permute-done.30 = f32[2,160,384]{2,1,0:T(8,128)S(1)} collective-permute-done((f32[2,160,384]{2,1,0:T(8,128)S(1)}, f32[2,160,384]{2,1,0:T(8,128)S(1)}, u32[]{:S(2)}, u32[]{:S(2)}) %collective-permute-start.30) | collective-permute-done | bytes 491552 | tf_op jit(solution)/shard_map/ppermute | solution.py:829
  533.5 4.2 collective-permute-done.31
  547.4 7.2 collective-permute-done.35
  558.4 6.7 collective-permute-done.39
  574.7 4.5 collective-permute-done.37
  586.0 4.9 all-to-all-start.6
  594.8 6.2 collective-permute-done.45
  604.4 3.8 collective-permute-done.47
  617.5 4.5 dynamic-slice_select_fusion.3
  631.1 19.6 %collective-permute-done.52 = f32[1,128]{1,0:T(1,128)S(1)} collective-permute-done((f32[1,128]{1,0:T(1,128)S(1)}, f32[1,128]{1,0:T(1,128)S(1)}, u32[]{:S(2)}, u32[]{:S(2)}) %collective-permute-start.52) | collective-permute-done | bytes 544 | tf_op jit(solution)/shard_map/ppermute | solution.py:724
  652.8 5.2 fusion.40.stats_ref
  660.0 51.2 %shard_map.609 = f32[2,384,384]{2,1,0:T(8,128)} custom-call(f32[2,384,384]{2,1,0:T(8,128)} %fusion.40.stats_ref, f32[2,384,384]{2,1,0:T(8,128)} %dynamic-slice_bitcast_fusion.2.bases_ref), custom_call_target="tpu_custom_call" | custom-call | flops 60000002048 | bytes 6000000 | tf_op jit(solution)/shard_map/pallas_call | solution.py:571
  714.9 4.6 multiply_add_fusion.2
  726.2 5.2 multiply_add_fusion
  731.4 10.1 %collective-permute-done.58 = f32[2,384,384]{2,1,0:T(8,128)S(1)} collective-permute-done((f32[2,384,384]{2,1,0:T(8,128)}, f32[2,384,384]{2,1,0:T(8,128)S(1)}, u32[]{:S(2)}, u32[]{:S(2)}) %collective-permute-start.58) | collective-permute-done | bytes 1179680 | tf_op jit(solution)/shard_map/ppermute | solution.py:1142
  752.3 5.1 fusion.123
  757.5 4.9 fusion.36
  (509 shorter events, 229.4 us)
Async XLA Ops:
  7.2 147.6 %all-gather.6.cloned.1.call-start = ((), (), s32[]{:S(2)}) async-start(), calls=%async_computation.7 | async-start | bytes 16220160 | tf_op jit(solution)/shard_map/all_gather | solution.py:909
  13.8 63.5 %collective-permute-start.1 = (bf16[2,32,2048]{2,1,0:T(8,128)(2,1)}, bf16[2,32,2048]{2,1,0:T(8,128)(2,1)}, u32[]{:S(2)}, u32[]{:S(2)}) collective-permute-start(bf16[2,32,2048]{2,1,0:T(8,128)(2,1)} %pad_maximum_fusion.11), channel_id=1, source_target_pairs={{0,4},{4,8},{8,12},{12,16},{16,20},{20,24},{24,28},{28,0},{1,5},{5... | collective-permute-start | bytes 786440 | tf_op jit(solution)/shard_map/ppermute | solution.py:748
  17.6 65.3 %collective-permute-start.2 = (bf16[2,32,2048]{2,1,0:T(8,128)(2,1)}, bf16[2,32,2048]{2,1,0:T(8,128)(2,1)}, u32[]{:S(2)}, u32[]{:S(2)}) collective-permute-start(bf16[2,32,2048]{2,1,0:T(8,128)(2,1)} %pad_maximum_fusion.12), channel_id=1, source_target_pairs={{0,8},{4,12},{8,16},{12,20},{16,24},{20,28},{24,0},{28,4},{1,9},{5... | collective-permute-start | bytes 786440 | tf_op jit(solution)/shard_map/ppermute | solution.py:748
  19.8 65.0 %collective-permute-start.3 = (bf16[2,32,2048]{2,1,0:T(8,128)(2,1)}, bf16[2,32,2048]{2,1,0:T(8,128)(2,1)}, u32[]{:S(2)}, u32[]{:S(2)}) collective-permute-start(bf16[2,32,2048]{2,1,0:T(8,128)(2,1)} %pad_maximum_fusion.13), channel_id=1, source_target_pairs={{0,12},{4,16},{8,20},{12,24},{16,28},{20,0},{24,4},{28,8},{1,13},{... | collective-permute-start | bytes 786440 | tf_op jit(solution)/shard_map/ppermute | solution.py:748
  23.1 62.8 %collective-permute-start.4 = (bf16[2,32,2048]{2,1,0:T(8,128)(2,1)}, bf16[2,32,2048]{2,1,0:T(8,128)(2,1)}, u32[]{:S(2)}, u32[]{:S(2)}) collective-permute-start(bf16[2,32,2048]{2,1,0:T(8,128)(2,1)} %pad_maximum_fusion.14), channel_id=1, source_target_pairs={{0,16},{4,20},{8,24},{12,28},{16,0},{20,4},{24,8},{28,12},{1,17},{... | collective-permute-start | bytes 786440 | tf_op jit(solution)/shard_map/ppermute | solution.py:748
  25.1 61.9 %collective-permute-start.5 = (bf16[2,32,2048]{2,1,0:T(8,128)(2,1)}, bf16[2,32,2048]{2,1,0:T(8,128)(2,1)}, u32[]{:S(2)}, u32[]{:S(2)}) collective-permute-start(bf16[2,32,2048]{2,1,0:T(8,128)(2,1)} %pad_maximum_fusion.15), channel_id=1, source_target_pairs={{0,20},{4,24},{8,28},{12,0},{16,4},{20,8},{24,12},{28,16},{1,21},{... | collective-permute-start | bytes 786440 | tf_op jit(solution)/shard_map/ppermute | solution.py:748
  31.6 44.6 %all-to-all-start = ((s32[8,1,4]{2,1,0:T(1,128)}), s32[8,1,4]{2,1,0:T(1,128)S(1)}, u32[]{:S(2)}, u32[]{:S(2)}) async-start(s32[8,1,4]{2,1,0:T(1,128)} %broadcast_in_dim.303), calls=%async_computation | async-start | bytes 8192 | tf_op jit(solution)/shard_map/all_to_all | solution.py:736
  34.9 210.4 %all-gather.8.cloned.1.call-start = ((), (), s32[]{:S(2)}) async-start(), calls=%async_computation.8 | async-start | bytes 6193152 | tf_op jit(solution)/shard_map/all_gather | solution.py:960
  77.4 17.7 %collective-permute-start.6 = (bf16[2,32,2048]{2,1,0:T(8,128)(2,1)}, bf16[2,32,2048]{2,1,0:T(8,128)(2,1)S(1)}, u32[]{:S(2)}, u32[]{:S(2)}) collective-permute-start(bf16[2,32,2048]{2,1,0:T(8,128)(2,1)} %pad_maximum_fusion.16), channel_id=1, source_target_pairs={{0,24},{4,28},{8,0},{12,4},{16,8},{20,12},{24,16},{28,20},{1,25},{... | collective-permute-start | bytes 786440 | tf_op jit(solution)/shard_map/ppermute | solution.py:748
  82.9 14.7 %collective-permute-start.7 = (bf16[2,32,2048]{2,1,0:T(8,128)(2,1)}, bf16[2,32,2048]{2,1,0:T(8,128)(2,1)S(1)}, u32[]{:S(2)}, u32[]{:S(2)}) collective-permute-start(bf16[2,32,2048]{2,1,0:T(8,128)(2,1)} %pad_maximum_fusion.17), channel_id=1, source_target_pairs={{0,28},{4,0},{8,4},{12,8},{16,12},{20,16},{24,20},{28,24},{1,29},{... | collective-permute-start | bytes 786440 | tf_op jit(solution)/shard_map/ppermute | solution.py:748
  84.9 12.7 %collective-permute-start = (bf16[384,384]{1,0:T(8,128)(2,1)S(1)}, bf16[384,384]{1,0:T(8,128)(2,1)S(1)}, u32[]{:S(2)}, u32[]{:S(2)}) collective-permute-start(bf16[384,384]{1,0:T(8,128)(2,1)S(1)} %copy-done.30), channel_id=1, source_target_pairs={{0,1},{1,0},{2,3},{3,2},{4,5},{5,4},{6,7},{7,6},{8,9},{9,8},{10,11... | collective-permute-start | bytes 884744 | tf_op jit(solution)/shard_map/ppermute | solution.py:932
  265.3 11.6 %all-to-all-start.1 = ((bf16[8,56,256]{2,1,0:T(8,128)(2,1)}), bf16[8,56,256]{2,1,0:T(8,128)(2,1)S(1)}, u32[]{:S(2)}, u32[]{:S(2)}) async-start(bf16[8,56,256]{2,1,0:T(8,128)(2,1)} %broadcast_in_dim.307), calls=%async_computation.1 | async-start | bytes 458752 | tf_op jit(solution)/shard_map/all_to_all | solution.py:736
  311.2 15.0 %all-to-all-start.3 = ((f32[8,48,256]{2,1,0:T(8,128)}), f32[8,48,256]{2,1,0:T(8,128)S(1)}, u32[]{:S(2)}, u32[]{:S(2)}) async-start(f32[8,48,256]{2,1,0:T(8,128)} %bitcast.458), calls=%async_computation.3 | async-start | bytes 786432 | tf_op jit(solution)/shard_map/all_to_all | solution.py:1004
  314.7 173.7 %all-gather.10.cloned.1.call-start = ((), (), s32[]{:S(2)}) async-start(), calls=%async_computation.9 | async-start | bytes 1327104 | tf_op jit(solution)/shard_map/all_gather | solution.py:1027
  349.6 12.1 %collective-permute-start.14 = (f32[32,2048]{1,0:T(8,128)S(1)}, f32[32,2048]{1,0:T(8,128)S(1)}, u32[]{:S(2)}, u32[]{:S(2)}) collective-permute-start(f32[32,2048]{1,0:T(8,128)S(1)} %get-tuple-element.340), channel_id=1, source_target_pairs={{0,4},{4,8},{8,12},{12,16},{16,20},{20,24},{24,28},{28,0},{1,5},{5... | collective-permute-start | bytes 786440 | tf_op jit(solution)/shard_map/ppermute | solution.py:748
  351.1 36.4 %collective-permute-start.16 = (f32[32,2048]{1,0:T(8,128)S(1)}, f32[32,2048]{1,0:T(8,128)S(1)}, u32[]{:S(2)}, u32[]{:S(2)}) collective-permute-start(f32[32,2048]{1,0:T(8,128)S(1)} %get-tuple-element.338), channel_id=1, source_target_pairs={{0,12},{4,16},{8,20},{12,24},{16,28},{20,0},{24,4},{28,8},{1,13},{... | collective-permute-start | bytes 786440 | tf_op jit(solution)/shard_map/ppermute | solution.py:748
  352.9 34.6 %collective-permute-start.17 = (f32[32,2048]{1,0:T(8,128)S(1)}, f32[32,2048]{1,0:T(8,128)S(1)}, u32[]{:S(2)}, u32[]{:S(2)}) collective-permute-start(f32[32,2048]{1,0:T(8,128)S(1)} %get-tuple-element.337), channel_id=1, source_target_pairs={{0,16},{4,20},{8,24},{12,28},{16,0},{20,4},{24,8},{28,12},{1,17},{... | collective-permute-start | bytes 786440 | tf_op jit(solution)/shard_map/ppermute | solution.py:748
  355.8 31.6 %collective-permute-start.18 = (f32[32,2048]{1,0:T(8,128)S(1)}, f32[32,2048]{1,0:T(8,128)S(1)}, u32[]{:S(2)}, u32[]{:S(2)}) collective-permute-start(f32[32,2048]{1,0:T(8,128)S(1)} %get-tuple-element.336), channel_id=1, source_target_pairs={{0,20},{4,24},{8,28},{12,0},{16,4},{20,8},{24,12},{28,16},{1,21},{... | collective-permute-start | bytes 786440 | tf_op jit(solution)/shard_map/ppermute | solution.py:748
  361.7 25.8 %collective-permute-start.19 = (f32[32,2048]{1,0:T(8,128)S(1)}, f32[32,2048]{1,0:T(8,128)S(1)}, u32[]{:S(2)}, u32[]{:S(2)}) collective-permute-start(f32[32,2048]{1,0:T(8,128)S(1)} %get-tuple-element.335), channel_id=1, source_target_pairs={{0,24},{4,28},{8,0},{12,4},{16,8},{20,12},{24,16},{28,20},{1,25},{... | collective-permute-start | bytes 786440 | tf_op jit(solution)/shard_map/ppermute | solution.py:748
  362.2 25.3 %collective-permute-start.20 = (f32[32,2048]{1,0:T(8,128)S(1)}, f32[32,2048]{1,0:T(8,128)S(1)}, u32[]{:S(2)}, u32[]{:S(2)}) collective-permute-start(f32[32,2048]{1,0:T(8,128)S(1)} %get-tuple-element.334), channel_id=1, source_target_pairs={{0,28},{4,0},{8,4},{12,8},{16,12},{20,16},{24,20},{28,24},{1,29},{... | collective-permute-start | bytes 786440 | tf_op jit(solution)/shard_map/ppermute | solution.py:748
  388.9 15.3 %collective-permute-start.21 = (f32[2,8,160,384]{3,2,1,0:T(8,128)}, f32[2,8,160,384]{3,2,1,0:T(8,128)}, u32[]{:S(2)}, u32[]{:S(2)}) collective-permute-start(f32[2,8,160,384]{3,2,1,0:T(8,128)} %dynamic-slice_bitcast_fusion.1), channel_id=1, source_target_pairs={{0,1},{1,0},{2,3},{3,2},{4,5},{5,4},{6,7},{7,6},{8,9},{9,8},{10,11... | collective-permute-start | bytes 11796488 | tf_op jit(solution)/shard_map/ppermute | solution.py:1034
  410.7 19.7 %collective-permute-start.22 = (f32[1,160,384]{2,1,0:T(8,128)}, f32[1,160,384]{2,1,0:T(8,128)}, u32[]{:S(2)}, u32[]{:S(2)}) collective-permute-start(f32[1,160,384]{2,1,0:T(8,128)} %get-tuple-element.329), channel_id=1, source_target_pairs={{0,8},{8,16},{16,24},{24,28},{28,20},{20,12},{12,4},{4,0},{1,9},{9... | collective-permute-start | bytes 737288 | tf_op jit(solution)/shard_map/ppermute | solution.py:829
  418.9 11.6 %collective-permute-start.23 = (f32[1,160,384]{2,1,0:T(8,128)}, f32[1,160,384]{2,1,0:T(8,128)}, u32[]{:S(2)}, u32[]{:S(2)}) collective-permute-start(f32[1,160,384]{2,1,0:T(8,128)} %get-tuple-element.331), channel_id=1, source_target_pairs={{0,4},{8,0},{16,8},{24,16},{28,24},{20,28},{12,20},{4,12},{1,5},{9... | collective-permute-start | bytes 737288 | tf_op jit(solution)/shard_map/ppermute | solution.py:830
  434.6 28.8 %collective-permute-start.25 = (f32[2,160,384]{2,1,0:T(8,128)}, f32[2,160,384]{2,1,0:T(8,128)S(1)}, u32[]{:S(2)}, u32[]{:S(2)}) collective-permute-start(f32[2,160,384]{2,1,0:T(8,128)} %pad_maximum_fusion.6), channel_id=1, source_target_pairs={{0,4},{8,0},{16,8},{24,16},{28,24},{20,28},{12,20},{4,12},{1,5},{9... | collective-permute-start | bytes 1474568 | tf_op jit(solution)/shard_map/ppermute | solution.py:830
  441.3 22.2 %collective-permute-start.24 = (f32[2,160,384]{2,1,0:T(8,128)}, f32[2,160,384]{2,1,0:T(8,128)}, u32[]{:S(2)}, u32[]{:S(2)}) collective-permute-start(f32[2,160,384]{2,1,0:T(8,128)} %pad_maximum_fusion.5), channel_id=1, source_target_pairs={{0,8},{8,16},{16,24},{24,28},{28,20},{20,12},{12,4},{4,0},{1,9},{9... | collective-permute-start | bytes 1474568 | tf_op jit(solution)/shard_map/ppermute | solution.py:829
  443.4 45.0 %all-to-all-start.5 = ((bf16[8,48,336]{2,1,0:T(8,128)(2,1)}), bf16[8,48,336]{2,1,0:T(8,128)(2,1)S(1)}, u32[]{:S(2)}, u32[]{:S(2)}) async-start(bf16[8,48,336]{2,1,0:T(8,128)(2,1)} %bitcast.421), calls=%async_computation.5 | async-start | bytes 589824 | tf_op jit(solution)/shard_map/all_to_all | solution.py:1046
  466.2 22.1 %collective-permute-start.26 = (f32[2,160,384]{2,1,0:T(8,128)S(1)}, f32[2,160,384]{2,1,0:T(8,128)S(1)}, u32[]{:S(2)}, u32[]{:S(2)}) collective-permute-start(f32[2,160,384]{2,1,0:T(8,128)S(1)} %get-tuple-element.327), channel_id=1, source_target_pairs={{0,8},{8,16},{16,24},{24,28},{28,20},{20,12},{12,4},{4,0},{1,9},{9... | collective-permute-start | bytes 1474568 | tf_op jit(solution)/shard_map/ppermute | solution.py:829
  468.3 20.1 %collective-permute-start.27 = (f32[2,160,384]{2,1,0:T(8,128)S(1)}, f32[2,160,384]{2,1,0:T(8,128)}, u32[]{:S(2)}, u32[]{:S(2)}) collective-permute-start(f32[2,160,384]{2,1,0:T(8,128)S(1)} %get-tuple-element.326), channel_id=1, source_target_pairs={{0,4},{8,0},{16,8},{24,16},{28,24},{20,28},{12,20},{4,12},{1,5},{9... | collective-permute-start | bytes 1474568 | tf_op jit(solution)/shard_map/ppermute | solution.py:830
  512.4 12.2 %collective-permute-start.30 = (f32[2,160,384]{2,1,0:T(8,128)S(1)}, f32[2,160,384]{2,1,0:T(8,128)S(1)}, u32[]{:S(2)}, u32[]{:S(2)}) collective-permute-start(f32[2,160,384]{2,1,0:T(8,128)S(1)} %pad_maximum_fusion.7), channel_id=1, source_target_pairs={{0,8},{8,16},{16,24},{24,28},{28,20},{20,12},{12,4},{4,0},{1,9},{9... | collective-permute-start | bytes 1474568 | tf_op jit(solution)/shard_map/ppermute | solution.py:829
  514.4 19.2 %collective-permute-start.34 = (f32[2,160,384]{2,1,0:T(8,128)S(1)}, f32[2,160,384]{2,1,0:T(8,128)S(1)}, u32[]{:S(2)}, u32[]{:S(2)}) collective-permute-start(f32[2,160,384]{2,1,0:T(8,128)S(1)} %pad_maximum_fusion.8), channel_id=1, source_target_pairs={{0,4},{8,0},{16,8},{24,16},{28,24},{20,28},{12,20},{4,12},{1,5},{9... | collective-permute-start | bytes 1474568 | tf_op jit(solution)/shard_map/ppermute | solution.py:830
  526.1 11.6 %collective-permute-start.31 = (f32[2,160,384]{2,1,0:T(8,128)}, f32[2,160,384]{2,1,0:T(8,128)}, u32[]{:S(2)}, u32[]{:S(2)}) collective-permute-start(f32[2,160,384]{2,1,0:T(8,128)} %bitcast_add_fusion.8), channel_id=1, source_target_pairs={{0,8},{8,16},{16,24},{24,28},{28,20},{20,12},{12,4},{4,0},{1,9},{9... | collective-permute-start | bytes 1474568 | tf_op jit(solution)/shard_map/ppermute | solution.py:829
  531.8 14.5 %collective-permute-start.42 = (f32[16,384]{1,0:T(8,128)S(1)}, f32[16,384]{1,0:T(8,128)S(1)}, u32[]{:S(2)}, u32[]{:S(2)}) collective-permute-start(f32[16,384]{1,0:T(8,128)S(1)} %add.804), channel_id=1, source_target_pairs={{0,2},{1,3},{2,0},{3,1},{4,6},{5,7},{6,4},{7,5},{8,10},{9,11},{10,... | collective-permute-start | bytes 73736 | tf_op jit(solution)/shard_map/ppermute | solution.py:724
  540.4 14.2 %collective-permute-start.35 = (f32[2,160,384]{2,1,0:T(8,128)S(1)}, f32[2,160,384]{2,1,0:T(8,128)S(1)}, u32[]{:S(2)}, u32[]{:S(2)}) collective-permute-start(f32[2,160,384]{2,1,0:T(8,128)S(1)} %get-tuple-element.317), channel_id=1, source_target_pairs={{0,4},{8,0},{16,8},{24,16},{28,24},{20,28},{12,20},{4,12},{1,5},{9... | collective-permute-start | bytes 1474568 | tf_op jit(solution)/shard_map/ppermute | solution.py:830
  544.2 14.2 %collective-permute-start.38 = (f32[2,160,384]{2,1,0:T(8,128)S(1)}, f32[2,160,384]{2,1,0:T(8,128)S(1)}, u32[]{:S(2)}, u32[]{:S(2)}) collective-permute-start(f32[2,160,384]{2,1,0:T(8,128)S(1)} %get-tuple-element.324), channel_id=1, source_target_pairs={{0,8},{8,16},{16,24},{24,28},{28,20},{20,12},{12,4},{4,0},{1,9},{9... | collective-permute-start | bytes 1474568 | tf_op jit(solution)/shard_map/ppermute | solution.py:829
  545.3 19.9 %collective-permute-start.39 = (f32[2,160,384]{2,1,0:T(8,128)S(1)}, f32[2,160,384]{2,1,0:T(8,128)S(1)}, u32[]{:S(2)}, u32[]{:S(2)}) collective-permute-start(f32[2,160,384]{2,1,0:T(8,128)S(1)} %get-tuple-element.325), channel_id=1, source_target_pairs={{0,4},{8,0},{16,8},{24,16},{28,24},{20,28},{12,20},{4,12},{1,5},{9... | collective-permute-start | bytes 1474568 | tf_op jit(solution)/shard_map/ppermute | solution.py:830
  546.3 21.7 %collective-permute-start.32 = (f32[2,160,384]{2,1,0:T(8,128)S(1)}, f32[2,160,384]{2,1,0:T(8,128)S(1)}, u32[]{:S(2)}, u32[]{:S(2)}) collective-permute-start(f32[2,160,384]{2,1,0:T(8,128)S(1)} %get-tuple-element.316), channel_id=1, source_target_pairs={{0,8},{8,16},{16,24},{24,28},{28,20},{20,12},{12,4},{4,0},{1,9},{9... | collective-permute-start | bytes 1474568 | tf_op jit(solution)/shard_map/ppermute | solution.py:829
  556.3 15.4 %collective-permute-start.36 = (f32[2,160,384]{2,1,0:T(8,128)S(1)}, f32[2,160,384]{2,1,0:T(8,128)S(1)}, u32[]{:S(2)}, u32[]{:S(2)}) collective-permute-start(f32[2,160,384]{2,1,0:T(8,128)S(1)} %bitcast_add_fusion.7), channel_id=1, source_target_pairs={{0,4},{8,0},{16,8},{24,16},{28,24},{20,28},{12,20},{4,12},{1,5},{9... | collective-permute-start | bytes 1474568 | tf_op jit(solution)/shard_map/ppermute | solution.py:830
  580.0 11.2 %collective-permute-start.43 = (bf16[2,184,384]{2,1,0:T(8,128)(2,1)}, bf16[2,184,384]{2,1,0:T(8,128)(2,1)S(1)}, u32[]{:S(2)}, u32[]{:S(2)}) collective-permute-start(bf16[2,184,384]{2,1,0:T(8,128)(2,1)} %pad_maximum_fusion.10), channel_id=1, source_target_pairs={{0,8},{8,16},{16,24},{24,28},{28,20},{20,12},{12,4},{4,0},{1,9},{9... | collective-permute-start | bytes 847880 | tf_op jit(solution)/shard_map/ppermute | solution.py:794
  581.5 11.8 %collective-permute-start.44 = (bf16[2,184,384]{2,1,0:T(8,128)(2,1)}, bf16[2,184,384]{2,1,0:T(8,128)(2,1)S(1)}, u32[]{:S(2)}, u32[]{:S(2)}) collective-permute-start(bf16[2,184,384]{2,1,0:T(8,128)(2,1)} %pad_maximum_fusion.10), channel_id=1, source_target_pairs={{0,4},{8,0},{16,8},{24,16},{28,24},{20,28},{12,20},{4,12},{1,5},{9... | collective-permute-start | bytes 847880 | tf_op jit(solution)/shard_map/ppermute | solution.py:795
  586.0 155.7 %all-to-all-start.6 = ((f32[8,1,2048]{2,1,0:T(1,128)}), f32[8,1,2048]{2,1,0:T(1,128)}, u32[]{:S(2)}, u32[]{:S(2)}) async-start(f32[8,1,2048]{2,1,0:T(1,128)} %broadcast_in_dim.355), calls=%async_computation.6 | async-start | bytes 131072 | tf_op jit(solution)/shard_map/all_to_all | solution.py:736
  622.0 30.7 %collective-permute-start.53 = (bf16[2,384,384]{2,1,0:T(8,128)(2,1)}, bf16[2,384,384]{2,1,0:T(8,128)(2,1)}, u32[]{:S(2)}, u32[]{:S(2)}) collective-permute-start(bf16[2,384,384]{2,1,0:T(8,128)(2,1)} %get-tuple-element.363), channel_id=1, source_target_pairs={{0,1},{1,0},{2,3},{3,2},{4,5},{5,4},{6,7},{7,6},{8,9},{9,8},{10,11... | collective-permute-start | bytes 1769480 | tf_op jit(solution)/shard_map/ppermute | solution.py:1113
  622.6 30.2 %collective-permute-start.54 = (bf16[2,384,384]{2,1,0:T(8,128)(2,1)}, bf16[2,384,384]{2,1,0:T(8,128)(2,1)}, u32[]{:S(2)}, u32[]{:S(2)}) collective-permute-start(bf16[2,384,384]{2,1,0:T(8,128)(2,1)} %get-tuple-element.362), channel_id=1, source_target_pairs={{0,2},{1,3},{2,0},{3,1},{4,6},{5,7},{6,4},{7,5},{8,10},{9,11},{10,... | collective-permute-start | bytes 1769480 | tf_op jit(solution)/shard_map/ppermute | solution.py:1113
  624.2 28.5 %collective-permute-start.55 = (bf16[2,384,384]{2,1,0:T(8,128)(2,1)}, bf16[2,384,384]{2,1,0:T(8,128)(2,1)}, u32[]{:S(2)}, u32[]{:S(2)}) collective-permute-start(bf16[2,384,384]{2,1,0:T(8,128)(2,1)} %get-tuple-element.361), channel_id=1, source_target_pairs={{0,3},{1,2},{2,1},{3,0},{4,7},{5,6},{6,5},{7,4},{8,11},{9,10},{10,... | collective-permute-start | bytes 1769480 | tf_op jit(solution)/shard_map/ppermute | solution.py:1113
  626.1 24.7 %collective-permute-start.52 = (f32[1,128]{1,0:T(1,128)S(1)}, f32[1,128]{1,0:T(1,128)S(1)}, u32[]{:S(2)}, u32[]{:S(2)}) collective-permute-start(f32[1,128]{1,0:T(1,128)S(1)} %broadcast_add_fusion), channel_id=1, source_target_pairs={{0,2},{1,3},{2,0},{3,1},{4,6},{5,7},{6,4},{7,5},{8,10},{9,11},{10,... | collective-permute-start | bytes 1544 | tf_op jit(solution)/shard_map/ppermute | solution.py:724
  658.0 73.5 %collective-permute-start.57 = (f32[2,384,384]{2,1,0:T(8,128)}, f32[2,384,384]{2,1,0:T(8,128)}, u32[]{:S(2)}, u32[]{:S(2)}) collective-permute-start(f32[2,384,384]{2,1,0:T(8,128)} %fusion.40.stats_ref), channel_id=1, source_target_pairs={{0,2},{1,3},{2,0},{3,1},{4,6},{5,7},{6,4},{7,5},{8,10},{9,11},{10,... | collective-permute-start | bytes 3538952 | tf_op jit(solution)/shard_map/ppermute | solution.py:1122
  659.6 51.7 %collective-permute-start.56 = (f32[336,512]{1,0:T(8,128)S(1)}, f32[336,512]{1,0:T(8,128)S(1)}, u32[]{:S(2)}, u32[]{:S(2)}) collective-permute-start(f32[336,512]{1,0:T(8,128)S(1)} %get-tuple-element.182), channel_id=1, source_target_pairs={{0,2},{1,3},{2,0},{3,1},{4,6},{5,7},{6,4},{7,5},{8,10},{9,11},{10,... | collective-permute-start | bytes 2064392 | tf_op jit(solution)/shard_map/ppermute | solution.py:1124
  712.9 28.6 %collective-permute-start.58 = (f32[2,384,384]{2,1,0:T(8,128)}, f32[2,384,384]{2,1,0:T(8,128)S(1)}, u32[]{:S(2)}, u32[]{:S(2)}) collective-permute-start(f32[2,384,384]{2,1,0:T(8,128)} %shard_map.609), channel_id=1, source_target_pairs={{0,2},{1,3},{2,0},{3,1},{4,6},{5,7},{6,4},{7,5},{8,10},{9,11},{10,... | collective-permute-start | bytes 3538952 | tf_op jit(solution)/shard_map/ppermute | solution.py:1142
  746.6 16.8 %collective-permute-start.61 = (f32[2,2,384,384]{3,2,1,0:T(8,128)S(1)}, f32[2,2,384,384]{3,2,1,0:T(8,128)S(1)}, u32[]{:S(2)}, u32[]{:S(2)}) collective-permute-start(f32[2,2,384,384]{3,2,1,0:T(8,128)S(1)} %bitcast_dynamic-update-slice_fusion.5), channel_id=1, source_target_pairs={{0,1},{1,0},{2,3},{3,2},{4,5},{5,4},{6,7},{7,6},{8,9},{9,8},{10,11... | collective-permute-start | bytes 7077896 | tf_op jit(solution)/shard_map/ppermute | solution.py:857
  (97 other events, 949.9 us)
Sparse Core Ops, SparseCore 0:
  11.5 143.2 all-gather.5
  157.6 87.6 all-gather.7
  393.5 52.8 all-gather.9

commit v5 on v4

--- a/solution.py
+++ b/solution.py
@@ -826,6 +826,9 @@
             else:
                 right, left = right + self.right, left + self.left
             self.send_right, self.send_left = right, left
+        if index < 2:
+            self.send_right = self.send_right.astype(bf16)
+            self.send_left = self.send_left.astype(bf16)
         self.right = lax.ppermute(self.send_right, "dp", ring_perm(1))
         self.left = lax.ppermute(self.send_left, "dp", ring_perm(-1))
 

time: 779 us -> 767 us (0.985)
  waiting for transfers between devices: 243 us -> 233 us
    ppermute x8, waiting for transfers between devices: 19.8 us -> 10.4 us  [step(): self.right = lax.ppermute(self.send_right, 'dp', ring_perm(1))]
  transfers between devices with their start and end apart: 70 -> 70, of which waited for: 31 -> 32; matrix products, arithmetic and copies ran while one was open for 19% -> 19% of each run, Pallas kernels for 23% -> 23%
where the time goes in v5:
time: 767 us; the launch traced here: 761 us
  waiting for transfers between devices  233 us (30%)
  Pallas kernels  191 us (25%)
  starting transfers between devices  101 us (13%)
  local copies, waits for them, and re-layouts  75.9 us (10%)
  other arithmetic  71.8 us (9%)
  blocking collectives  37.4 us (5%)
  matrix products  30.5 us (4%)
  between operations  20.5 us (3%)
    all_gather x1, waiting for transfers between devices, shards(): lax.all_gather(jnp.concatenate([*own_t, *own_s], axis=1), ('mp', 'dp'), a...  56.3 us
    pallas_call x1, Pallas kernels, renew_bases(): pl.pallas_call(basis_kernel, in_specs=[pl.BlockSpec(memory_space=pltpu.VM...  51.2 us
    all_to_all x3, waiting for transfers between devices, gather_over(): lax.all_to_all(jnp.broadcast_to(array[None], (count, *array.shape)), axis...  37.7 us
    pallas_call x2, Pallas kernels, block_fwd(): pl.pallas_call(block_fwd_kernel, grid=(rows // CHUNK,), in_specs=[s['row'...  36.4 us
    pallas_call x2, Pallas kernels, attention_bwd(): pl.pallas_call(functools.partial(attention_bwd_kernel, bool(last)), grid=...  30.5 us
    ppermute x14, starting transfers between devices, swap_pieces(): lax.ppermute(piece, 'dp', shift_perm(count, step + 1))  28.5 us
    ppermute x10, waiting for transfers between devices, sum_over(): array = array + lax.ppermute(array, axis, flip_perm(count, bit))  27 us
    all_gather x1, waiting for transfers between devices, shards(): heads = lax.all_gather(heads, 'dp', axis=0, tiled=True)  23.6 us
  transfers between devices with their start and end apart: 70, of which 32 were waited for; matrix products, arithmetic and copies ran while one was open for 19% of the time, Pallas kernels for 23%

profile of v5, /device:TPU:0, one launch (start us, length us, event | category | flops | bytes accessed | tf_op | source)
XLA Modules:
  0.0 761.3 jit_solution(3933121865028333581)
XLA Ops:
  45.0 31.1 %all-to-all-done = s32[8,1,4]{2,1,0:T(1,128)S(1)} async-done(((s32[8,1,4]{2,1,0:T(1,128)}), s32[8,1,4]{2,1,0:T(1,128)S(1)}, u32[]{:S(2)}, u32[]{:S(2)}) %all-to-all-start) | async-done | bytes 160 | tf_op jit(solution)/shard_map/all_to_all | solution.py:736
  77.4 4.5 collective-permute-start.6
  87.9 7.1 collective-permute-done.6
  98.5 56.3 %all-gather.6.cloned.1.call-done = bf16[5120,1536]{1,0:T(8,128)(2,1)} async-done(((bf16[160,1536]{1,0:T(8,128)(2,1)}), bf16[5120,1536]{1,0:T(8,128)(2,1)}) %all-gather.6.cloned.1.call-update) | async-done | bytes 15728656 | tf_op jit(solution)/shard_map/all_gather | solution.py:912
  158.8 12.9 %shard_map.600 = (f32[400,384]{1,0:T(8,128)}, bf16[400,384]{1,0:T(8,128)(2,1)}, bf16[4,400,384]{2,1,0:T(8,128)(2,1)}, bf16[4,400,128]{2,1,0:T(8,128)(2,1)}, f32[400,384]{1,0:T(8,128)}) custom-call(f32[400,384]{1,0:T(8,128)} %slice.254.x_ref, bf16[4,1280,1536]{2,1,0:T(8,128)(2,1)} %bitcast.480, f32[4,384]{1,0:T(4,128)} %get-tuple-element.380.gains_ref, ...), custom_call_target="tpu_custom_call" | custom-call | flops 12000000000 | bytes 8000000 | tf_op jit(solution)/shard_map/pallas_call | solution.py:252
  171.7 8.5 %shard_map.601 = (f32[16,384]{1,0:T(8,128)}, bf16[400,384]{1,0:T(8,128)(2,1)}, bf16[4,400,256]{2,1,0:T(8,128)(2,1)}, bf16[4,16,128]{2,1,0:T(8,128)(2,1)}, bf16[4...) custom-call(f32[400,384]{1,0:T(8,128)} %get-tuple-element.121.x_ref, bf16[4,1280,1536]{2,1,0:T(8,128)(2,1)} %bitcast.481, ...), custom_call_target="tpu_custom_call" | custom-call | flops 6000000000 | bytes 8000000 | tf_op jit(solution)/shard_map/pallas_call | solution.py:471
  181.0 23.5 %shard_map.598 = (f32[800,384]{1,0:T(8,128)}, bf16[800,384]{1,0:T(8,128)(2,1)}, bf16[4,800,384]{2,1,0:T(8,128)(2,1)}, bf16[4,800,128]{2,1,0:T(8,128)(2,1)}, f32[800,384]{1,0:T(8,128)}) custom-call(f32[800,384]{1,0:T(8,128)} %copy-done.28, bf16[4,1280,1536]{2,1,0:T(8,128)(2,1)} %bitcast.482, f32[4,384]{1,0:T(4,128)} %get-tuple-element.378.gains_ref, ...), custom_call_target="tpu_custom_call" | custom-call | flops 24000000000 | bytes 8000000 | tf_op jit(solution)/shard_map/pallas_call | solution.py:252
  204.5 10.0 %shard_map.599 = (f32[16,384]{1,0:T(8,128)}, bf16[800,384]{1,0:T(8,128)(2,1)}, bf16[4,800,256]{2,1,0:T(8,128)(2,1)}, bf16[4,16,128]{2,1,0:T(8,128)(2,1)}, bf16[4...) custom-call(f32[800,384]{1,0:T(8,128)} %get-tuple-element.118.x_ref, bf16[4,1280,1536]{2,1,0:T(8,128)(2,1)} %bitcast.483, ...), custom_call_target="tpu_custom_call" | custom-call | flops 12000000000 | bytes 8000000 | tf_op jit(solution)/shard_map/pallas_call | solution.py:471
  215.2 5.3 all-gather
  221.6 23.6 %all-gather.8.cloned.1.call-done = bf16[2688,1024]{1,0:T(8,128)(2,1)} async-done(((bf16[336,1024]{1,0:T(8,128)(2,1)}), bf16[2688,1024]{1,0:T(8,128)(2,1)}) %all-gather.8.cloned.1.call-update) | async-done | bytes 5505040 | tf_op jit(solution)/shard_map/all_gather | solution.py:963
  247.7 5.7 all_gather.25
  270.4 6.5 all-to-all-done.1
  278.2 6.6 shard_map.602
  285.6 16.4 %all_to_all.36.all_ref = f32[32,8,384]{2,1,0:T(8,128)} all-to-all(f32[32,8,384]{2,1,0:T(8,128)S(1)} %broadcast_in_dim.308), channel_id=1, replica_groups=mesh['dp'=8,'mp'=4] {'dp','mp'}, dimensions={0} | all-to-all | bytes 786432 | tf_op jit(solution)/shard_map/all_to_all | solution.py:736
  302.0 9.2 %shard_map.603 = (f32[384,256]{1,0:T(8,128)}, f32[256,2048]{1,0:T(8,128)}, f32[1,128]{1,0:T(1,128)}) custom-call(f32[32,8,384]{2,1,0:T(8,128)} %all_to_all.36.all_ref, f32[8,384]{1,0:T(8,128)} %get-tuple-element.126.own_ref, f32[2,384]{1,0:T(2,128)} %fusion.197.weight_ref, f32[2048,384]{1,0:T(8,128)} %get-tuple-element.128.exp_s_ref, ...), custom_call_target="tpu_custom_call" | custom-call | flops 8000000000 | bytes 8000000 | tf_op jit(solution)/shard_map/pallas_call | solution.py:678
  314.7 11.5 %all-to-all-done.3 = f32[8,48,256]{2,1,0:T(8,128)S(1)} async-done(((f32[8,48,256]{2,1,0:T(8,128)}), f32[8,48,256]{2,1,0:T(8,128)S(1)}, u32[]{:S(2)}, u32[]{:S(2)}) %all-to-all-start.3) | async-done | bytes 393248 | tf_op jit(solution)/shard_map/all_to_all | solution.py:1007
  335.6 10.0 %all_to_all.37 = f32[4,48,512]{2,1,0:T(8,128)S(1)} all-to-all(f32[4,48,512]{2,1,0:T(8,128)S(1)} %bitcast.457), channel_id=1, replica_groups=mesh['dp'=8,'mp'=4] {'mp'}, dimensions={0} | all-to-all | bytes 786432 | tf_op jit(solution)/shard_map/all_to_all | solution.py:1014
  357.9 3.8 collective-permute-done.14
  362.2 4.7 collective-permute-start.20
  367.0 16.0 %shard_map.604 = (f32[4,1280,384]{2,1,0:T(8,128)}, f32[4,384]{1,0:T(4,128)}, f32[800,384]{1,0:T(8,128)}) custom-call(f32[800,384]{1,0:T(8,128)} %get-tuple-element.118.x_ref, bf16[4,1280,1536]{2,1,0:T(8,128)(2,1)} %bitcast.484, f32[4,384]{1,0:T(4,128)} %get-tuple-element.377.gains_ref, s32[32,1]{1,0:T(8,128)} %copy.172.seg_cls_ref, ...), custom_call_target="tpu_custom_call" | custom-call | flops 16000000000 | bytes 16000000 | tf_op jit(solution)/shard_map/pallas_call | solution.py:491
  383.1 4.4 dynamic-slice_bitcast_fusion.1
  393.3 10.8 %shard_map.605 = (f32[4,1280,384]{2,1,0:T(8,128)}, f32[800,384]{1,0:T(8,128)}) custom-call(bf16[4,1280,1536]{2,1,0:T(8,128)(2,1)} %bitcast.485, f32[4,384]{1,0:T(4,128)} %get-tuple-element.378.gains_ref, f32[800,384]{1,0:T(8,128)} %get-tuple-element.134.x2_ref, f32[800,384]{1,0:T(8,128)} %get-tuple-element.144.grad_ref), custom_call_target="tpu_custom_call" | custom-call | flops 10400000000 | bytes 8000000 | tf_op jit(solution)/shard_map/pallas_call | solution.py:277
  404.2 3.7 bitcast_add_fusion.1
  409.8 8.1 %collective-permute-start.22 = (bf16[1,160,384]{2,1,0:T(8,128)(2,1)}, bf16[1,160,384]{2,1,0:T(8,128)(2,1)S(1)}, u32[]{:S(2)}, u32[]{:S(2)}) collective-permute-start(bf16[1,160,384]{2,1,0:T(8,128)(2,1)} %get-tuple-element.368), channel_id=1, source_target_pairs={{0,8},{8,16},{16,24},{24,28},{28,20},{20,12},{12,4},{4,0},{1,9},{9... | collective-permute-start | bytes 368648 | tf_op jit(solution)/shard_map/ppermute | solution.py:832
  417.9 11.6 %shard_map.606 = (f32[4,1280,384]{2,1,0:T(8,128)}, f32[800,384]{1,0:T(8,128)}, f32[2,384]{1,0:T(2,128)}) custom-call(bf16[4,1280,1536]{2,1,0:T(8,128)(2,1)} %bitcast.486, f32[4,384]{1,0:T(4,128)} %get-tuple-element.378.gains_ref, f32[800,384]{1,0:T(8,128)} %get-tuple-element.134.x2_ref, ...), custom_call_target="tpu_custom_call", output_to_operand_aliasing={{0}: (5, {})} | custom-call | flops 10400000000 | bytes 8000000 | tf_op jit(solution)/shard_map/pallas_call | solution.py:277
  433.1 5.9 collective-permute-start.25
  441.8 5.3 all-to-all-start.5
  447.1 14.8 %shard_map.607 = (f32[4,1280,384]{2,1,0:T(8,128)}, f32[800,384]{1,0:T(8,128)}) custom-call(bf16[4,1280,1536]{2,1,0:T(8,128)(2,1)} %bitcast.487, f32[4,384]{1,0:T(4,128)} %get-tuple-element.378.gains_ref, s32[2,400,1]{2,1,0:T(8,128)} %add_select_fusion.4.seg_col_ref, s32[2,1,400]{2,1,0:T(1,128)} %and_select_fusion.seg_row_ref, ...), custom_call_target="tpu_custom_call", output_to_operand_aliasing={{0}: (9, {})} | custom-call | flops 15200000000 | bytes 8000000 | tf_op jit(solution)/shard_map/pallas_call | solution.py:311
  466.6 15.7 %shard_map.608 = (f32[4,1280,384]{2,1,0:T(8,128)}, f32[2,384]{1,0:T(2,128)}) custom-call(bf16[4,1280,1536]{2,1,0:T(8,128)(2,1)} %bitcast.488, f32[4,384]{1,0:T(4,128)} %get-tuple-element.378.gains_ref, s32[2,400,1]{2,1,0:T(8,128)} %add_select_fusion.4.seg_col_ref, s32[2,1,400]{2,1,0:T(1,128)} %and_select_fusion.seg_row_ref, ...), custom_call_target="tpu_custom_call", output_to_operand_aliasing={{0}: (11, {})} | custom-call | flops 15200000000 | bytes 8000000 | tf_op jit(solution)/shard_map/pallas_call | solution.py:311
  482.3 4.3 dynamic-slice_bitcast_fusion
  488.0 5.8 collective-permute-done.28
  508.7 4.9 collective-permute-done.30
  535.1 7.2 collective-permute-done.35
  546.1 6.8 collective-permute-done.39
  555.7 3.9 collective-permute-done.36
  562.4 4.6 collective-permute-done.37
  573.8 4.8 all-to-all-start.6
  582.5 6.2 collective-permute-done.45
  592.1 3.9 collective-permute-done.47
  605.2 4.5 dynamic-slice_select_fusion.3
  618.8 19.7 %collective-permute-done.52 = f32[1,128]{1,0:T(1,128)S(1)} collective-permute-done((f32[1,128]{1,0:T(1,128)S(1)}, f32[1,128]{1,0:T(1,128)S(1)}, u32[]{:S(2)}, u32[]{:S(2)}) %collective-permute-start.52) | collective-permute-done | bytes 544 | tf_op jit(solution)/shard_map/ppermute | solution.py:724
  640.5 5.2 fusion.40.stats_ref
  647.7 51.2 %shard_map.609 = f32[2,384,384]{2,1,0:T(8,128)} custom-call(f32[2,384,384]{2,1,0:T(8,128)} %fusion.40.stats_ref, f32[2,384,384]{2,1,0:T(8,128)} %dynamic-slice_bitcast_fusion.2.bases_ref), custom_call_target="tpu_custom_call" | custom-call | flops 60000002048 | bytes 6000000 | tf_op jit(solution)/shard_map/pallas_call | solution.py:571
  702.6 4.6 multiply_add_fusion.2
  714.0 5.2 multiply_add_fusion
  719.2 10.1 %collective-permute-done.58 = f32[2,384,384]{2,1,0:T(8,128)S(1)} collective-permute-done((f32[2,384,384]{2,1,0:T(8,128)}, f32[2,384,384]{2,1,0:T(8,128)S(1)}, u32[]{:S(2)}, u32[]{:S(2)}) %collective-permute-start.58) | collective-permute-done | bytes 1179680 | tf_op jit(solution)/shard_map/ppermute | solution.py:1145
  740.1 5.1 fusion.127
  745.2 4.9 fusion.36
  (511 shorter events, 224.2 us)
Async XLA Ops:
  7.2 147.6 %all-gather.6.cloned.1.call-start = ((), (), s32[]{:S(2)}) async-start(), calls=%async_computation.7 | async-start | bytes 16220160 | tf_op jit(solution)/shard_map/all_gather | solution.py:912
  13.8 63.5 %collective-permute-start.1 = (bf16[2,32,2048]{2,1,0:T(8,128)(2,1)}, bf16[2,32,2048]{2,1,0:T(8,128)(2,1)}, u32[]{:S(2)}, u32[]{:S(2)}) collective-permute-start(bf16[2,32,2048]{2,1,0:T(8,128)(2,1)} %pad_maximum_fusion.7), channel_id=1, source_target_pairs={{0,4},{4,8},{8,12},{12,16},{16,20},{20,24},{24,28},{28,0},{1,5},{5... | collective-permute-start | bytes 786440 | tf_op jit(solution)/shard_map/ppermute | solution.py:748
  17.6 65.3 %collective-permute-start.2 = (bf16[2,32,2048]{2,1,0:T(8,128)(2,1)}, bf16[2,32,2048]{2,1,0:T(8,128)(2,1)}, u32[]{:S(2)}, u32[]{:S(2)}) collective-permute-start(bf16[2,32,2048]{2,1,0:T(8,128)(2,1)} %pad_maximum_fusion.8), channel_id=1, source_target_pairs={{0,8},{4,12},{8,16},{12,20},{16,24},{20,28},{24,0},{28,4},{1,9},{5... | collective-permute-start | bytes 786440 | tf_op jit(solution)/shard_map/ppermute | solution.py:748
  19.8 65.0 %collective-permute-start.3 = (bf16[2,32,2048]{2,1,0:T(8,128)(2,1)}, bf16[2,32,2048]{2,1,0:T(8,128)(2,1)}, u32[]{:S(2)}, u32[]{:S(2)}) collective-permute-start(bf16[2,32,2048]{2,1,0:T(8,128)(2,1)} %pad_maximum_fusion.9), channel_id=1, source_target_pairs={{0,12},{4,16},{8,20},{12,24},{16,28},{20,0},{24,4},{28,8},{1,13},{... | collective-permute-start | bytes 786440 | tf_op jit(solution)/shard_map/ppermute | solution.py:748
  23.1 62.8 %collective-permute-start.4 = (bf16[2,32,2048]{2,1,0:T(8,128)(2,1)}, bf16[2,32,2048]{2,1,0:T(8,128)(2,1)}, u32[]{:S(2)}, u32[]{:S(2)}) collective-permute-start(bf16[2,32,2048]{2,1,0:T(8,128)(2,1)} %pad_maximum_fusion.10), channel_id=1, source_target_pairs={{0,16},{4,20},{8,24},{12,28},{16,0},{20,4},{24,8},{28,12},{1,17},{... | collective-permute-start | bytes 786440 | tf_op jit(solution)/shard_map/ppermute | solution.py:748
  25.1 61.9 %collective-permute-start.5 = (bf16[2,32,2048]{2,1,0:T(8,128)(2,1)}, bf16[2,32,2048]{2,1,0:T(8,128)(2,1)}, u32[]{:S(2)}, u32[]{:S(2)}) collective-permute-start(bf16[2,32,2048]{2,1,0:T(8,128)(2,1)} %pad_maximum_fusion.11), channel_id=1, source_target_pairs={{0,20},{4,24},{8,28},{12,0},{16,4},{20,8},{24,12},{28,16},{1,21},{... | collective-permute-start | bytes 786440 | tf_op jit(solution)/shard_map/ppermute | solution.py:748
  31.6 44.6 %all-to-all-start = ((s32[8,1,4]{2,1,0:T(1,128)}), s32[8,1,4]{2,1,0:T(1,128)S(1)}, u32[]{:S(2)}, u32[]{:S(2)}) async-start(s32[8,1,4]{2,1,0:T(1,128)} %broadcast_in_dim.303), calls=%async_computation | async-start | bytes 8192 | tf_op jit(solution)/shard_map/all_to_all | solution.py:736
  34.9 210.4 %all-gather.8.cloned.1.call-start = ((), (), s32[]{:S(2)}) async-start(), calls=%async_computation.8 | async-start | bytes 6193152 | tf_op jit(solution)/shard_map/all_gather | solution.py:963
  77.4 17.7 %collective-permute-start.6 = (bf16[2,32,2048]{2,1,0:T(8,128)(2,1)}, bf16[2,32,2048]{2,1,0:T(8,128)(2,1)S(1)}, u32[]{:S(2)}, u32[]{:S(2)}) collective-permute-start(bf16[2,32,2048]{2,1,0:T(8,128)(2,1)} %pad_maximum_fusion.12), channel_id=1, source_target_pairs={{0,24},{4,28},{8,0},{12,4},{16,8},{20,12},{24,16},{28,20},{1,25},{... | collective-permute-start | bytes 786440 | tf_op jit(solution)/shard_map/ppermute | solution.py:748
  82.9 14.7 %collective-permute-start.7 = (bf16[2,32,2048]{2,1,0:T(8,128)(2,1)}, bf16[2,32,2048]{2,1,0:T(8,128)(2,1)S(1)}, u32[]{:S(2)}, u32[]{:S(2)}) collective-permute-start(bf16[2,32,2048]{2,1,0:T(8,128)(2,1)} %pad_maximum_fusion.13), channel_id=1, source_target_pairs={{0,28},{4,0},{8,4},{12,8},{16,12},{20,16},{24,20},{28,24},{1,29},{... | collective-permute-start | bytes 786440 | tf_op jit(solution)/shard_map/ppermute | solution.py:748
  84.9 12.7 %collective-permute-start = (bf16[384,384]{1,0:T(8,128)(2,1)S(1)}, bf16[384,384]{1,0:T(8,128)(2,1)S(1)}, u32[]{:S(2)}, u32[]{:S(2)}) collective-permute-start(bf16[384,384]{1,0:T(8,128)(2,1)S(1)} %copy-done.29), channel_id=1, source_target_pairs={{0,1},{1,0},{2,3},{3,2},{4,5},{5,4},{6,7},{7,6},{8,9},{9,8},{10,11... | collective-permute-start | bytes 884744 | tf_op jit(solution)/shard_map/ppermute | solution.py:935
  265.3 11.6 %all-to-all-start.1 = ((bf16[8,56,256]{2,1,0:T(8,128)(2,1)}), bf16[8,56,256]{2,1,0:T(8,128)(2,1)S(1)}, u32[]{:S(2)}, u32[]{:S(2)}) async-start(bf16[8,56,256]{2,1,0:T(8,128)(2,1)} %broadcast_in_dim.307), calls=%async_computation.1 | async-start | bytes 458752 | tf_op jit(solution)/shard_map/all_to_all | solution.py:736
  311.2 15.0 %all-to-all-start.3 = ((f32[8,48,256]{2,1,0:T(8,128)}), f32[8,48,256]{2,1,0:T(8,128)S(1)}, u32[]{:S(2)}, u32[]{:S(2)}) async-start(f32[8,48,256]{2,1,0:T(8,128)} %bitcast.466), calls=%async_computation.3 | async-start | bytes 786432 | tf_op jit(solution)/shard_map/all_to_all | solution.py:1007
  314.7 172.0 %all-gather.10.cloned.1.call-start = ((), (), s32[]{:S(2)}) async-start(), calls=%async_computation.9 | async-start | bytes 1327104 | tf_op jit(solution)/shard_map/all_gather | solution.py:1030
  349.6 12.1 %collective-permute-start.14 = (f32[32,2048]{1,0:T(8,128)S(1)}, f32[32,2048]{1,0:T(8,128)S(1)}, u32[]{:S(2)}, u32[]{:S(2)}) collective-permute-start(f32[32,2048]{1,0:T(8,128)S(1)} %get-tuple-element.336), channel_id=1, source_target_pairs={{0,4},{4,8},{8,12},{12,16},{16,20},{20,24},{24,28},{28,0},{1,5},{5... | collective-permute-start | bytes 786440 | tf_op jit(solution)/shard_map/ppermute | solution.py:748
  351.1 11.1 %collective-permute-start.15 = (f32[32,2048]{1,0:T(8,128)S(1)}, f32[32,2048]{1,0:T(8,128)S(1)}, u32[]{:S(2)}, u32[]{:S(2)}) collective-permute-start(f32[32,2048]{1,0:T(8,128)S(1)} %get-tuple-element.335), channel_id=1, source_target_pairs={{0,8},{4,12},{8,16},{12,20},{16,24},{20,28},{24,0},{28,4},{1,9},{5... | collective-permute-start | bytes 786440 | tf_op jit(solution)/shard_map/ppermute | solution.py:748
  351.1 36.4 %collective-permute-start.16 = (f32[32,2048]{1,0:T(8,128)S(1)}, f32[32,2048]{1,0:T(8,128)S(1)}, u32[]{:S(2)}, u32[]{:S(2)}) collective-permute-start(f32[32,2048]{1,0:T(8,128)S(1)} %get-tuple-element.334), channel_id=1, source_target_pairs={{0,12},{4,16},{8,20},{12,24},{16,28},{20,0},{24,4},{28,8},{1,13},{... | collective-permute-start | bytes 786440 | tf_op jit(solution)/shard_map/ppermute | solution.py:748
  352.9 34.6 %collective-permute-start.17 = (f32[32,2048]{1,0:T(8,128)S(1)}, f32[32,2048]{1,0:T(8,128)S(1)}, u32[]{:S(2)}, u32[]{:S(2)}) collective-permute-start(f32[32,2048]{1,0:T(8,128)S(1)} %get-tuple-element.333), channel_id=1, source_target_pairs={{0,16},{4,20},{8,24},{12,28},{16,0},{20,4},{24,8},{28,12},{1,17},{... | collective-permute-start | bytes 786440 | tf_op jit(solution)/shard_map/ppermute | solution.py:748
  355.8 31.6 %collective-permute-start.18 = (f32[32,2048]{1,0:T(8,128)S(1)}, f32[32,2048]{1,0:T(8,128)S(1)}, u32[]{:S(2)}, u32[]{:S(2)}) collective-permute-start(f32[32,2048]{1,0:T(8,128)S(1)} %get-tuple-element.332), channel_id=1, source_target_pairs={{0,20},{4,24},{8,28},{12,0},{16,4},{20,8},{24,12},{28,16},{1,21},{... | collective-permute-start | bytes 786440 | tf_op jit(solution)/shard_map/ppermute | solution.py:748
  361.7 25.8 %collective-permute-start.19 = (f32[32,2048]{1,0:T(8,128)S(1)}, f32[32,2048]{1,0:T(8,128)S(1)}, u32[]{:S(2)}, u32[]{:S(2)}) collective-permute-start(f32[32,2048]{1,0:T(8,128)S(1)} %get-tuple-element.331), channel_id=1, source_target_pairs={{0,24},{4,28},{8,0},{12,4},{16,8},{20,12},{24,16},{28,20},{1,25},{... | collective-permute-start | bytes 786440 | tf_op jit(solution)/shard_map/ppermute | solution.py:748
  362.2 25.3 %collective-permute-start.20 = (f32[32,2048]{1,0:T(8,128)S(1)}, f32[32,2048]{1,0:T(8,128)S(1)}, u32[]{:S(2)}, u32[]{:S(2)}) collective-permute-start(f32[32,2048]{1,0:T(8,128)S(1)} %get-tuple-element.330), channel_id=1, source_target_pairs={{0,28},{4,0},{8,4},{12,8},{16,12},{20,16},{24,20},{28,24},{1,29},{... | collective-permute-start | bytes 786440 | tf_op jit(solution)/shard_map/ppermute | solution.py:748
  388.9 15.3 %collective-permute-start.21 = (f32[2,8,160,384]{3,2,1,0:T(8,128)}, f32[2,8,160,384]{3,2,1,0:T(8,128)}, u32[]{:S(2)}, u32[]{:S(2)}) collective-permute-start(f32[2,8,160,384]{3,2,1,0:T(8,128)} %dynamic-slice_bitcast_fusion.1), channel_id=1, source_target_pairs={{0,1},{1,0},{2,3},{3,2},{4,5},{5,4},{6,7},{7,6},{8,9},{9,8},{10,11... | collective-permute-start | bytes 11796488 | tf_op jit(solution)/shard_map/ppermute | solution.py:1037
  409.8 21.0 %collective-permute-start.22 = (bf16[1,160,384]{2,1,0:T(8,128)(2,1)}, bf16[1,160,384]{2,1,0:T(8,128)(2,1)S(1)}, u32[]{:S(2)}, u32[]{:S(2)}) collective-permute-start(bf16[1,160,384]{2,1,0:T(8,128)(2,1)} %get-tuple-element.368), channel_id=1, source_target_pairs={{0,8},{8,16},{16,24},{24,28},{28,20},{20,12},{12,4},{4,0},{1,9},{9... | collective-permute-start | bytes 368648 | tf_op jit(solution)/shard_map/ppermute | solution.py:832
  417.9 12.9 %collective-permute-start.23 = (bf16[1,160,384]{2,1,0:T(8,128)(2,1)}, bf16[1,160,384]{2,1,0:T(8,128)(2,1)}, u32[]{:S(2)}, u32[]{:S(2)}) collective-permute-start(bf16[1,160,384]{2,1,0:T(8,128)(2,1)} %get-tuple-element.367), channel_id=1, source_target_pairs={{0,4},{8,0},{16,8},{24,16},{28,24},{20,28},{12,20},{4,12},{1,5},{9... | collective-permute-start | bytes 368648 | tf_op jit(solution)/shard_map/ppermute | solution.py:833
  433.1 28.8 %collective-permute-start.25 = (bf16[2,160,384]{2,1,0:T(8,128)(2,1)S(1)}, bf16[2,160,384]{2,1,0:T(8,128)(2,1)S(1)}, u32[]{:S(2)}, u32[]{:S(2)}) collective-permute-start(bf16[2,160,384]{2,1,0:T(8,128)(2,1)S(1)} %pad_maximum_fusion.16), channel_id=1, source_target_pairs={{0,4},{8,0},{16,8},{24,16},{28,24},{20,28},{12,20},{4,12},{1,5},{9... | collective-permute-start | bytes 737288 | tf_op jit(solution)/shard_map/ppermute | solution.py:833
  439.7 22.2 %collective-permute-start.24 = (bf16[2,160,384]{2,1,0:T(8,128)(2,1)}, bf16[2,160,384]{2,1,0:T(8,128)(2,1)S(1)}, u32[]{:S(2)}, u32[]{:S(2)}) collective-permute-start(bf16[2,160,384]{2,1,0:T(8,128)(2,1)} %pad_maximum_fusion.15), channel_id=1, source_target_pairs={{0,8},{8,16},{16,24},{24,28},{28,20},{20,12},{12,4},{4,0},{1,9},{9... | collective-permute-start | bytes 737288 | tf_op jit(solution)/shard_map/ppermute | solution.py:832
  441.8 44.8 %all-to-all-start.5 = ((bf16[8,48,336]{2,1,0:T(8,128)(2,1)}), bf16[8,48,336]{2,1,0:T(8,128)(2,1)S(1)}, u32[]{:S(2)}, u32[]{:S(2)}) async-start(bf16[8,48,336]{2,1,0:T(8,128)(2,1)} %bitcast.429), calls=%async_computation.5 | async-start | bytes 589824 | tf_op jit(solution)/shard_map/all_to_all | solution.py:1049
  464.5 22.1 %collective-permute-start.26 = (f32[2,160,384]{2,1,0:T(8,128)S(1)}, f32[2,160,384]{2,1,0:T(8,128)S(1)}, u32[]{:S(2)}, u32[]{:S(2)}) collective-permute-start(f32[2,160,384]{2,1,0:T(8,128)S(1)} %get-tuple-element.325), channel_id=1, source_target_pairs={{0,8},{8,16},{16,24},{24,28},{28,20},{20,12},{12,4},{4,0},{1,9},{9... | collective-permute-start | bytes 1474568 | tf_op jit(solution)/shard_map/ppermute | solution.py:832
  466.5 20.1 %collective-permute-start.27 = (f32[2,160,384]{2,1,0:T(8,128)S(1)}, f32[2,160,384]{2,1,0:T(8,128)}, u32[]{:S(2)}, u32[]{:S(2)}) collective-permute-start(f32[2,160,384]{2,1,0:T(8,128)S(1)} %get-tuple-element.324), channel_id=1, source_target_pairs={{0,4},{8,0},{16,8},{24,16},{28,24},{20,28},{12,20},{4,12},{1,5},{9... | collective-permute-start | bytes 1474568 | tf_op jit(solution)/shard_map/ppermute | solution.py:833
  514.4 11.2 %collective-permute-start.31 = (f32[2,160,384]{2,1,0:T(8,128)S(1)}, f32[2,160,384]{2,1,0:T(8,128)S(1)}, u32[]{:S(2)}, u32[]{:S(2)}) collective-permute-start(f32[2,160,384]{2,1,0:T(8,128)S(1)} %bitcast_add_fusion.8), channel_id=1, source_target_pairs={{0,8},{8,16},{16,24},{24,28},{28,20},{20,12},{12,4},{4,0},{1,9},{9... | collective-permute-start | bytes 1474568 | tf_op jit(solution)/shard_map/ppermute | solution.py:832
  521.0 13.0 %collective-permute-start.42 = (f32[16,384]{1,0:T(8,128)S(1)}, f32[16,384]{1,0:T(8,128)S(1)}, u32[]{:S(2)}, u32[]{:S(2)}) collective-permute-start(f32[16,384]{1,0:T(8,128)S(1)} %add.804), channel_id=1, source_target_pairs={{0,2},{1,3},{2,0},{3,1},{4,6},{5,7},{6,4},{7,5},{8,10},{9,11},{10,... | collective-permute-start | bytes 73736 | tf_op jit(solution)/shard_map/ppermute | solution.py:724
  528.1 14.2 %collective-permute-start.35 = (f32[2,160,384]{2,1,0:T(8,128)S(1)}, f32[2,160,384]{2,1,0:T(8,128)S(1)}, u32[]{:S(2)}, u32[]{:S(2)}) collective-permute-start(f32[2,160,384]{2,1,0:T(8,128)S(1)} %get-tuple-element.317), channel_id=1, source_target_pairs={{0,4},{8,0},{16,8},{24,16},{28,24},{20,28},{12,20},{4,12},{1,5},{9... | collective-permute-start | bytes 1474568 | tf_op jit(solution)/shard_map/ppermute | solution.py:833
  531.9 14.2 %collective-permute-start.38 = (f32[2,160,384]{2,1,0:T(8,128)S(1)}, f32[2,160,384]{2,1,0:T(8,128)S(1)}, u32[]{:S(2)}, u32[]{:S(2)}) collective-permute-start(f32[2,160,384]{2,1,0:T(8,128)S(1)} %get-tuple-element.322), channel_id=1, source_target_pairs={{0,8},{8,16},{16,24},{24,28},{28,20},{20,12},{12,4},{4,0},{1,9},{9... | collective-permute-start | bytes 1474568 | tf_op jit(solution)/shard_map/ppermute | solution.py:832
  533.0 19.9 %collective-permute-start.39 = (f32[2,160,384]{2,1,0:T(8,128)S(1)}, f32[2,160,384]{2,1,0:T(8,128)S(1)}, u32[]{:S(2)}, u32[]{:S(2)}) collective-permute-start(f32[2,160,384]{2,1,0:T(8,128)S(1)} %get-tuple-element.323), channel_id=1, source_target_pairs={{0,4},{8,0},{16,8},{24,16},{28,24},{20,28},{12,20},{4,12},{1,5},{9... | collective-permute-start | bytes 1474568 | tf_op jit(solution)/shard_map/ppermute | solution.py:833
  534.0 21.7 %collective-permute-start.32 = (f32[2,160,384]{2,1,0:T(8,128)S(1)}, f32[2,160,384]{2,1,0:T(8,128)S(1)}, u32[]{:S(2)}, u32[]{:S(2)}) collective-permute-start(f32[2,160,384]{2,1,0:T(8,128)S(1)} %get-tuple-element.316), channel_id=1, source_target_pairs={{0,8},{8,16},{16,24},{24,28},{28,20},{20,12},{12,4},{4,0},{1,9},{9... | collective-permute-start | bytes 1474568 | tf_op jit(solution)/shard_map/ppermute | solution.py:832
  544.1 15.5 %collective-permute-start.36 = (f32[2,160,384]{2,1,0:T(8,128)S(1)}, f32[2,160,384]{2,1,0:T(8,128)S(1)}, u32[]{:S(2)}, u32[]{:S(2)}) collective-permute-start(f32[2,160,384]{2,1,0:T(8,128)S(1)} %bitcast_add_fusion.7), channel_id=1, source_target_pairs={{0,4},{8,0},{16,8},{24,16},{28,24},{20,28},{12,20},{4,12},{1,5},{9... | collective-permute-start | bytes 1474568 | tf_op jit(solution)/shard_map/ppermute | solution.py:833
  567.8 11.1 %collective-permute-start.43 = (bf16[2,184,384]{2,1,0:T(8,128)(2,1)}, bf16[2,184,384]{2,1,0:T(8,128)(2,1)S(1)}, u32[]{:S(2)}, u32[]{:S(2)}) collective-permute-start(bf16[2,184,384]{2,1,0:T(8,128)(2,1)} %pad_maximum_fusion.6), channel_id=1, source_target_pairs={{0,8},{8,16},{16,24},{24,28},{28,20},{20,12},{12,4},{4,0},{1,9},{9... | collective-permute-start | bytes 847880 | tf_op jit(solution)/shard_map/ppermute | solution.py:794
  569.3 11.7 %collective-permute-start.44 = (bf16[2,184,384]{2,1,0:T(8,128)(2,1)}, bf16[2,184,384]{2,1,0:T(8,128)(2,1)S(1)}, u32[]{:S(2)}, u32[]{:S(2)}) collective-permute-start(bf16[2,184,384]{2,1,0:T(8,128)(2,1)} %pad_maximum_fusion.6), channel_id=1, source_target_pairs={{0,4},{8,0},{16,8},{24,16},{28,24},{20,28},{12,20},{4,12},{1,5},{9... | collective-permute-start | bytes 847880 | tf_op jit(solution)/shard_map/ppermute | solution.py:795
  573.8 155.6 %all-to-all-start.6 = ((f32[8,1,2048]{2,1,0:T(1,128)}), f32[8,1,2048]{2,1,0:T(1,128)}, u32[]{:S(2)}, u32[]{:S(2)}) async-start(f32[8,1,2048]{2,1,0:T(1,128)} %broadcast_in_dim.355), calls=%async_computation.6 | async-start | bytes 131072 | tf_op jit(solution)/shard_map/all_to_all | solution.py:736
  578.9 9.8 %collective-permute-start.45 = (bf16[2,184,384]{2,1,0:T(8,128)(2,1)S(1)}, bf16[2,184,384]{2,1,0:T(8,128)(2,1)S(1)}, u32[]{:S(2)}, u32[]{:S(2)}) collective-permute-start(bf16[2,184,384]{2,1,0:T(8,128)(2,1)S(1)} %collective-permute-done.43), channel_id=1, source_target_pairs={{0,8},{8,16},{16,24},{24,28},{28,20},{20,12},{12,4},{4,0},{1,9},{9... | collective-permute-start | bytes 847880 | tf_op jit(solution)/shard_map/ppermute | solution.py:794
  609.7 30.7 %collective-permute-start.53 = (bf16[2,384,384]{2,1,0:T(8,128)(2,1)}, bf16[2,384,384]{2,1,0:T(8,128)(2,1)}, u32[]{:S(2)}, u32[]{:S(2)}) collective-permute-start(bf16[2,384,384]{2,1,0:T(8,128)(2,1)} %get-tuple-element.359), channel_id=1, source_target_pairs={{0,1},{1,0},{2,3},{3,2},{4,5},{5,4},{6,7},{7,6},{8,9},{9,8},{10,11... | collective-permute-start | bytes 1769480 | tf_op jit(solution)/shard_map/ppermute | solution.py:1116
  610.3 30.2 %collective-permute-start.54 = (bf16[2,384,384]{2,1,0:T(8,128)(2,1)}, bf16[2,384,384]{2,1,0:T(8,128)(2,1)}, u32[]{:S(2)}, u32[]{:S(2)}) collective-permute-start(bf16[2,384,384]{2,1,0:T(8,128)(2,1)} %get-tuple-element.358), channel_id=1, source_target_pairs={{0,2},{1,3},{2,0},{3,1},{4,6},{5,7},{6,4},{7,5},{8,10},{9,11},{10,... | collective-permute-start | bytes 1769480 | tf_op jit(solution)/shard_map/ppermute | solution.py:1116
  611.9 28.6 %collective-permute-start.55 = (bf16[2,384,384]{2,1,0:T(8,128)(2,1)}, bf16[2,384,384]{2,1,0:T(8,128)(2,1)}, u32[]{:S(2)}, u32[]{:S(2)}) collective-permute-start(bf16[2,384,384]{2,1,0:T(8,128)(2,1)} %get-tuple-element.357), channel_id=1, source_target_pairs={{0,3},{1,2},{2,1},{3,0},{4,7},{5,6},{6,5},{7,4},{8,11},{9,10},{10,... | collective-permute-start | bytes 1769480 | tf_op jit(solution)/shard_map/ppermute | solution.py:1116
  613.7 24.7 %collective-permute-start.52 = (f32[1,128]{1,0:T(1,128)S(1)}, f32[1,128]{1,0:T(1,128)S(1)}, u32[]{:S(2)}, u32[]{:S(2)}) collective-permute-start(f32[1,128]{1,0:T(1,128)S(1)} %broadcast_add_fusion), channel_id=1, source_target_pairs={{0,2},{1,3},{2,0},{3,1},{4,6},{5,7},{6,4},{7,5},{8,10},{9,11},{10,... | collective-permute-start | bytes 1544 | tf_op jit(solution)/shard_map/ppermute | solution.py:724
  645.7 73.5 %collective-permute-start.57 = (f32[2,384,384]{2,1,0:T(8,128)}, f32[2,384,384]{2,1,0:T(8,128)}, u32[]{:S(2)}, u32[]{:S(2)}) collective-permute-start(f32[2,384,384]{2,1,0:T(8,128)} %fusion.40.stats_ref), channel_id=1, source_target_pairs={{0,2},{1,3},{2,0},{3,1},{4,6},{5,7},{6,4},{7,5},{8,10},{9,11},{10,... | collective-permute-start | bytes 3538952 | tf_op jit(solution)/shard_map/ppermute | solution.py:1125
  647.3 51.8 %collective-permute-start.56 = (f32[336,512]{1,0:T(8,128)S(1)}, f32[336,512]{1,0:T(8,128)S(1)}, u32[]{:S(2)}, u32[]{:S(2)}) collective-permute-start(f32[336,512]{1,0:T(8,128)S(1)} %get-tuple-element.182), channel_id=1, source_target_pairs={{0,2},{1,3},{2,0},{3,1},{4,6},{5,7},{6,4},{7,5},{8,10},{9,11},{10,... | collective-permute-start | bytes 2064392 | tf_op jit(solution)/shard_map/ppermute | solution.py:1127
  700.7 28.6 %collective-permute-start.58 = (f32[2,384,384]{2,1,0:T(8,128)}, f32[2,384,384]{2,1,0:T(8,128)S(1)}, u32[]{:S(2)}, u32[]{:S(2)}) collective-permute-start(f32[2,384,384]{2,1,0:T(8,128)} %shard_map.609), channel_id=1, source_target_pairs={{0,2},{1,3},{2,0},{3,1},{4,6},{5,7},{6,4},{7,5},{8,10},{9,11},{10,... | collective-permute-start | bytes 3538952 | tf_op jit(solution)/shard_map/ppermute | solution.py:1145
  734.3 16.8 %collective-permute-start.61 = (f32[2,2,384,384]{3,2,1,0:T(8,128)S(1)}, f32[2,2,384,384]{3,2,1,0:T(8,128)S(1)}, u32[]{:S(2)}, u32[]{:S(2)}) collective-permute-start(f32[2,2,384,384]{3,2,1,0:T(8,128)S(1)} %bitcast_dynamic-update-slice_fusion.5), channel_id=1, source_target_pairs={{0,1},{1,0},{2,3},{3,2},{4,5},{5,4},{6,7},{7,6},{8,9},{9,8},{10,11... | collective-permute-start | bytes 7077896 | tf_op jit(solution)/shard_map/ppermute | solution.py:860
  (96 other events, 955.4 us)
Sparse Core Ops, SparseCore 0:
  11.5 143.2 all-gather.5
  157.6 87.6 all-gather.7
  393.5 53.5 all-gather.9

commit v6 on v5

--- a/solution.py
+++ b/solution.py
@@ -826,7 +826,7 @@
             else:
                 right, left = right + self.right, left + self.left
             self.send_right, self.send_left = right, left
-        if index < 2:
+        if index < 3:
             self.send_right = self.send_right.astype(bf16)
             self.send_left = self.send_left.astype(bf16)
         self.right = lax.ppermute(self.send_right, "dp", ring_perm(1))

time: 767 us -> 753 us (0.982)
  waiting for transfers between devices: 233 us -> 222 us
  transfers between devices with their start and end apart: 70 -> 70, of which waited for: 32 -> 31; matrix products, arithmetic and copies ran while one was open for 19% -> 19% of each run, Pallas kernels for 23% -> 23%
where the time goes in v6:
time: 753 us; the launch traced here: 748 us
  waiting for transfers between devices  222 us (29%)
  Pallas kernels  191 us (25%)
  starting transfers between devices  100 us (13%)
  local copies, waits for them, and re-layouts  76.8 us (10%)
  other arithmetic  68.9 us (9%)
  blocking collectives  37.4 us (5%)
  matrix products  31.5 us (4%)
  between operations  20.6 us (3%)
    all_gather x1, waiting for transfers between devices, shards(): lax.all_gather(jnp.concatenate([*own_t, *own_s], axis=1), ('mp', 'dp'), a...  56.3 us
    pallas_call x1, Pallas kernels, renew_bases(): pl.pallas_call(basis_kernel, in_specs=[pl.BlockSpec(memory_space=pltpu.VM...  51.2 us
    all_to_all x3, waiting for transfers between devices, gather_over(): lax.all_to_all(jnp.broadcast_to(array[None], (count, *array.shape)), axis...  37.7 us
    pallas_call x2, Pallas kernels, block_fwd(): pl.pallas_call(block_fwd_kernel, grid=(rows // CHUNK,), in_specs=[s['row'...  36.4 us
    pallas_call x2, Pallas kernels, attention_bwd(): pl.pallas_call(functools.partial(attention_bwd_kernel, bool(last)), grid=...  30.5 us
    ppermute x14, starting transfers between devices, swap_pieces(): lax.ppermute(piece, 'dp', shift_perm(count, step + 1))  28.5 us
    ppermute x10, waiting for transfers between devices, sum_over(): array = array + lax.ppermute(array, axis, flip_perm(count, bit))  26.9 us
    all_gather x1, waiting for transfers between devices, shards(): heads = lax.all_gather(heads, 'dp', axis=0, tiled=True)  23.7 us
  transfers between devices with their start and end apart: 70, of which 31 were waited for; matrix products, arithmetic and copies ran while one was open for 19% of the time, Pallas kernels for 23%

profile of v6, /device:TPU:0, one launch (start us, length us, event | category | flops | bytes accessed | tf_op | source)
XLA Modules:
  0.0 747.7 jit_solution(109035401408492614)
XLA Ops:
  31.6 3.3 all-to-all-start
  45.1 31.1 %all-to-all-done = s32[8,1,4]{2,1,0:T(1,128)S(1)} async-done(((s32[8,1,4]{2,1,0:T(1,128)}), s32[8,1,4]{2,1,0:T(1,128)S(1)}, u32[]{:S(2)}, u32[]{:S(2)}) %all-to-all-start) | async-done | bytes 160 | tf_op jit(solution)/shard_map/all_to_all | solution.py:736
  77.4 4.5 collective-permute-start.6
  87.9 7.1 collective-permute-done.6
  98.5 56.3 %all-gather.6.cloned.1.call-done = bf16[5120,1536]{1,0:T(8,128)(2,1)} async-done(((bf16[160,1536]{1,0:T(8,128)(2,1)}), bf16[5120,1536]{1,0:T(8,128)(2,1)}) %all-gather.6.cloned.1.call-update) | async-done | bytes 15728656 | tf_op jit(solution)/shard_map/all_gather | solution.py:912
  158.8 12.9 %shard_map.600 = (f32[400,384]{1,0:T(8,128)}, bf16[400,384]{1,0:T(8,128)(2,1)}, bf16[4,400,384]{2,1,0:T(8,128)(2,1)}, bf16[4,400,128]{2,1,0:T(8,128)(2,1)}, f32[400,384]{1,0:T(8,128)}) custom-call(f32[400,384]{1,0:T(8,128)} %slice.254.x_ref, bf16[4,1280,1536]{2,1,0:T(8,128)(2,1)} %bitcast.488, f32[4,384]{1,0:T(4,128)} %get-tuple-element.380.gains_ref, ...), custom_call_target="tpu_custom_call" | custom-call | flops 12000000000 | bytes 8000000 | tf_op jit(solution)/shard_map/pallas_call | solution.py:252
  171.7 8.5 %shard_map.601 = (f32[16,384]{1,0:T(8,128)}, bf16[400,384]{1,0:T(8,128)(2,1)}, bf16[4,400,256]{2,1,0:T(8,128)(2,1)}, bf16[4,16,128]{2,1,0:T(8,128)(2,1)}, bf16[4...) custom-call(f32[400,384]{1,0:T(8,128)} %get-tuple-element.121.x_ref, bf16[4,1280,1536]{2,1,0:T(8,128)(2,1)} %bitcast.489, ...), custom_call_target="tpu_custom_call" | custom-call | flops 6000000000 | bytes 8000000 | tf_op jit(solution)/shard_map/pallas_call | solution.py:471
  181.0 23.5 %shard_map.598 = (f32[800,384]{1,0:T(8,128)}, bf16[800,384]{1,0:T(8,128)(2,1)}, bf16[4,800,384]{2,1,0:T(8,128)(2,1)}, bf16[4,800,128]{2,1,0:T(8,128)(2,1)}, f32[800,384]{1,0:T(8,128)}) custom-call(f32[800,384]{1,0:T(8,128)} %copy-done.27, bf16[4,1280,1536]{2,1,0:T(8,128)(2,1)} %bitcast.490, f32[4,384]{1,0:T(4,128)} %get-tuple-element.378.gains_ref, ...), custom_call_target="tpu_custom_call" | custom-call | flops 24000000000 | bytes 8000000 | tf_op jit(solution)/shard_map/pallas_call | solution.py:252
  204.5 10.0 %shard_map.599 = (f32[16,384]{1,0:T(8,128)}, bf16[800,384]{1,0:T(8,128)(2,1)}, bf16[4,800,256]{2,1,0:T(8,128)(2,1)}, bf16[4,16,128]{2,1,0:T(8,128)(2,1)}, bf16[4...) custom-call(f32[800,384]{1,0:T(8,128)} %get-tuple-element.118.x_ref, bf16[4,1280,1536]{2,1,0:T(8,128)(2,1)} %bitcast.491, ...), custom_call_target="tpu_custom_call" | custom-call | flops 12000000000 | bytes 8000000 | tf_op jit(solution)/shard_map/pallas_call | solution.py:471
  215.2 5.3 all-gather
  221.6 23.7 %all-gather.8.cloned.1.call-done = bf16[2688,1024]{1,0:T(8,128)(2,1)} async-done(((bf16[336,1024]{1,0:T(8,128)(2,1)}), bf16[2688,1024]{1,0:T(8,128)(2,1)}) %all-gather.8.cloned.1.call-update) | async-done | bytes 5505040 | tf_op jit(solution)/shard_map/all_gather | solution.py:963
  247.7 5.7 all_gather.25
  265.3 3.6 all-to-all-start.1
  270.4 6.5 all-to-all-done.1
  278.2 6.6 shard_map.602
  285.6 16.4 %all_to_all.36.all_ref = f32[32,8,384]{2,1,0:T(8,128)} all-to-all(f32[32,8,384]{2,1,0:T(8,128)S(1)} %broadcast_in_dim.308), channel_id=1, replica_groups=mesh['dp'=8,'mp'=4] {'dp','mp'}, dimensions={0} | all-to-all | bytes 786432 | tf_op jit(solution)/shard_map/all_to_all | solution.py:736
  302.0 9.2 %shard_map.603 = (f32[384,256]{1,0:T(8,128)}, f32[256,2048]{1,0:T(8,128)}, f32[1,128]{1,0:T(1,128)}) custom-call(f32[32,8,384]{2,1,0:T(8,128)} %all_to_all.36.all_ref, f32[8,384]{1,0:T(8,128)} %get-tuple-element.126.own_ref, f32[2,384]{1,0:T(2,128)} %fusion.201.weight_ref, f32[2048,384]{1,0:T(8,128)} %get-tuple-element.128.exp_s_ref, ...), custom_call_target="tpu_custom_call" | custom-call | flops 8000000000 | bytes 8000000 | tf_op jit(solution)/shard_map/pallas_call | solution.py:678
  311.2 3.5 all-to-all-start.3
  314.7 11.5 %all-to-all-done.3 = f32[8,48,256]{2,1,0:T(8,128)S(1)} async-done(((f32[8,48,256]{2,1,0:T(8,128)}), f32[8,48,256]{2,1,0:T(8,128)S(1)}, u32[]{:S(2)}, u32[]{:S(2)}) %all-to-all-start.3) | async-done | bytes 393248 | tf_op jit(solution)/shard_map/all_to_all | solution.py:1007
  335.6 10.0 %all_to_all.37 = f32[4,48,512]{2,1,0:T(8,128)S(1)} all-to-all(f32[4,48,512]{2,1,0:T(8,128)S(1)} %bitcast.465), channel_id=1, replica_groups=mesh['dp'=8,'mp'=4] {'mp'}, dimensions={0} | all-to-all | bytes 786432 | tf_op jit(solution)/shard_map/all_to_all | solution.py:1014
  357.9 3.8 collective-permute-done.14
  362.2 4.7 collective-permute-start.20
  366.9 16.0 %shard_map.604 = (f32[4,1280,384]{2,1,0:T(8,128)}, f32[4,384]{1,0:T(4,128)}, f32[800,384]{1,0:T(8,128)}) custom-call(f32[800,384]{1,0:T(8,128)} %get-tuple-element.118.x_ref, bf16[4,1280,1536]{2,1,0:T(8,128)(2,1)} %bitcast.492, f32[4,384]{1,0:T(4,128)} %get-tuple-element.377.gains_ref, s32[32,1]{1,0:T(8,128)} %copy.172.seg_cls_ref, ...), custom_call_target="tpu_custom_call" | custom-call | flops 16000000000 | bytes 16000000 | tf_op jit(solution)/shard_map/pallas_call | solution.py:491
  383.0 4.4 dynamic-slice_bitcast_fusion.1
  393.4 10.8 %shard_map.605 = (f32[4,1280,384]{2,1,0:T(8,128)}, f32[800,384]{1,0:T(8,128)}) custom-call(bf16[4,1280,1536]{2,1,0:T(8,128)(2,1)} %bitcast.493, f32[4,384]{1,0:T(4,128)} %get-tuple-element.378.gains_ref, f32[800,384]{1,0:T(8,128)} %get-tuple-element.134.x2_ref, f32[800,384]{1,0:T(8,128)} %get-tuple-element.144.grad_ref), custom_call_target="tpu_custom_call" | custom-call | flops 10400000000 | bytes 8000000 | tf_op jit(solution)/shard_map/pallas_call | solution.py:277
  404.1 3.7 bitcast_add_fusion.1
  409.8 8.2 %collective-permute-start.22 = (bf16[1,160,384]{2,1,0:T(8,128)(2,1)}, bf16[1,160,384]{2,1,0:T(8,128)(2,1)S(1)}, u32[]{:S(2)}, u32[]{:S(2)}) collective-permute-start(bf16[1,160,384]{2,1,0:T(8,128)(2,1)} %get-tuple-element.368), channel_id=1, source_target_pairs={{0,8},{8,16},{16,24},{24,28},{28,20},{20,12},{12,4},{4,0},{1,9},{9... | collective-permute-start | bytes 368648 | tf_op jit(solution)/shard_map/ppermute | solution.py:832
  417.9 11.6 %shard_map.606 = (f32[4,1280,384]{2,1,0:T(8,128)}, f32[800,384]{1,0:T(8,128)}, f32[2,384]{1,0:T(2,128)}) custom-call(bf16[4,1280,1536]{2,1,0:T(8,128)(2,1)} %bitcast.494, f32[4,384]{1,0:T(4,128)} %get-tuple-element.378.gains_ref, f32[800,384]{1,0:T(8,128)} %get-tuple-element.134.x2_ref, ...), custom_call_target="tpu_custom_call", output_to_operand_aliasing={{0}: (5, {})} | custom-call | flops 10400000000 | bytes 8000000 | tf_op jit(solution)/shard_map/pallas_call | solution.py:277
  433.1 5.9 collective-permute-start.25
  441.8 5.2 all-to-all-start.5
  447.1 14.8 %shard_map.607 = (f32[4,1280,384]{2,1,0:T(8,128)}, f32[800,384]{1,0:T(8,128)}) custom-call(bf16[4,1280,1536]{2,1,0:T(8,128)(2,1)} %bitcast.495, f32[4,384]{1,0:T(4,128)} %get-tuple-element.378.gains_ref, s32[2,400,1]{2,1,0:T(8,128)} %add_select_fusion.4.seg_col_ref, s32[2,1,400]{2,1,0:T(1,128)} %and_select_fusion.seg_row_ref, ...), custom_call_target="tpu_custom_call", output_to_operand_aliasing={{0}: (9, {})} | custom-call | flops 15200000000 | bytes 8000000 | tf_op jit(solution)/shard_map/pallas_call | solution.py:311
  467.4 15.7 %shard_map.608 = (f32[4,1280,384]{2,1,0:T(8,128)}, f32[2,384]{1,0:T(2,128)}) custom-call(bf16[4,1280,1536]{2,1,0:T(8,128)(2,1)} %bitcast.496, f32[4,384]{1,0:T(4,128)} %get-tuple-element.378.gains_ref, s32[2,400,1]{2,1,0:T(8,128)} %add_select_fusion.4.seg_col_ref, s32[2,1,400]{2,1,0:T(1,128)} %and_select_fusion.seg_row_ref, ...), custom_call_target="tpu_custom_call", output_to_operand_aliasing={{0}: (11, {})} | custom-call | flops 15200000000 | bytes 8000000 | tf_op jit(solution)/shard_map/pallas_call | solution.py:311
  483.1 4.3 dynamic-slice_bitcast_fusion
  494.7 3.7 bitcast_add_fusion
  527.9 9.9 %collective-permute-done.35 = bf16[2,160,384]{2,1,0:T(8,128)(2,1)S(1)} collective-permute-done((bf16[2,160,384]{2,1,0:T(8,128)(2,1)S(1)}, bf16[2,160,384]{2,1,0:T(8,128)(2,1)S(1)}, u32[]{:S(2)}, u32[]{:S(2)}) %collective-permute-start.35) | collective-permute-done | bytes 245792 | tf_op jit(solution)/shard_map/ppermute | solution.py:833
  543.6 4.7 collective-permute-done.36
  550.2 4.5 collective-permute-done.37
  561.5 4.1 all-to-all-start.6
  569.4 5.3 collective-permute-done.45
  591.5 4.5 dynamic-slice_select_fusion.3
  605.1 19.6 %collective-permute-done.52 = f32[1,128]{1,0:T(1,128)S(1)} collective-permute-done((f32[1,128]{1,0:T(1,128)S(1)}, f32[1,128]{1,0:T(1,128)S(1)}, u32[]{:S(2)}, u32[]{:S(2)}) %collective-permute-start.52) | collective-permute-done | bytes 544 | tf_op jit(solution)/shard_map/ppermute | solution.py:724
  626.8 5.3 fusion.40.stats_ref
  634.1 51.2 %shard_map.609 = f32[2,384,384]{2,1,0:T(8,128)} custom-call(f32[2,384,384]{2,1,0:T(8,128)} %fusion.40.stats_ref, f32[2,384,384]{2,1,0:T(8,128)} %dynamic-slice_bitcast_fusion.2.bases_ref), custom_call_target="tpu_custom_call" | custom-call | flops 60000002048 | bytes 6000000 | tf_op jit(solution)/shard_map/pallas_call | solution.py:571
  689.0 4.6 multiply_add_fusion.2
  700.3 5.2 multiply_add_fusion
  705.5 10.1 %collective-permute-done.58 = f32[2,384,384]{2,1,0:T(8,128)S(1)} collective-permute-done((f32[2,384,384]{2,1,0:T(8,128)}, f32[2,384,384]{2,1,0:T(8,128)S(1)}, u32[]{:S(2)}, u32[]{:S(2)}) %collective-permute-start.58) | collective-permute-done | bytes 1179680 | tf_op jit(solution)/shard_map/ppermute | solution.py:1145
  726.4 5.1 fusion.131
  731.6 4.9 fusion.36
  (519 shorter events, 216.0 us)
Async XLA Ops:
  7.2 147.6 %all-gather.6.cloned.1.call-start = ((), (), s32[]{:S(2)}) async-start(), calls=%async_computation.7 | async-start | bytes 16220160 | tf_op jit(solution)/shard_map/all_gather | solution.py:912
  13.8 63.5 %collective-permute-start.1 = (bf16[2,32,2048]{2,1,0:T(8,128)(2,1)}, bf16[2,32,2048]{2,1,0:T(8,128)(2,1)}, u32[]{:S(2)}, u32[]{:S(2)}) collective-permute-start(bf16[2,32,2048]{2,1,0:T(8,128)(2,1)} %pad_maximum_fusion.7), channel_id=1, source_target_pairs={{0,4},{4,8},{8,12},{12,16},{16,20},{20,24},{24,28},{28,0},{1,5},{5... | collective-permute-start | bytes 786440 | tf_op jit(solution)/shard_map/ppermute | solution.py:748
  17.6 65.3 %collective-permute-start.2 = (bf16[2,32,2048]{2,1,0:T(8,128)(2,1)}, bf16[2,32,2048]{2,1,0:T(8,128)(2,1)}, u32[]{:S(2)}, u32[]{:S(2)}) collective-permute-start(bf16[2,32,2048]{2,1,0:T(8,128)(2,1)} %pad_maximum_fusion.8), channel_id=1, source_target_pairs={{0,8},{4,12},{8,16},{12,20},{16,24},{20,28},{24,0},{28,4},{1,9},{5... | collective-permute-start | bytes 786440 | tf_op jit(solution)/shard_map/ppermute | solution.py:748
  19.8 65.0 %collective-permute-start.3 = (bf16[2,32,2048]{2,1,0:T(8,128)(2,1)}, bf16[2,32,2048]{2,1,0:T(8,128)(2,1)}, u32[]{:S(2)}, u32[]{:S(2)}) collective-permute-start(bf16[2,32,2048]{2,1,0:T(8,128)(2,1)} %pad_maximum_fusion.9), channel_id=1, source_target_pairs={{0,12},{4,16},{8,20},{12,24},{16,28},{20,0},{24,4},{28,8},{1,13},{... | collective-permute-start | bytes 786440 | tf_op jit(solution)/shard_map/ppermute | solution.py:748
  23.1 62.8 %collective-permute-start.4 = (bf16[2,32,2048]{2,1,0:T(8,128)(2,1)}, bf16[2,32,2048]{2,1,0:T(8,128)(2,1)}, u32[]{:S(2)}, u32[]{:S(2)}) collective-permute-start(bf16[2,32,2048]{2,1,0:T(8,128)(2,1)} %pad_maximum_fusion.10), channel_id=1, source_target_pairs={{0,16},{4,20},{8,24},{12,28},{16,0},{20,4},{24,8},{28,12},{1,17},{... | collective-permute-start | bytes 786440 | tf_op jit(solution)/shard_map/ppermute | solution.py:748
  25.1 61.9 %collective-permute-start.5 = (bf16[2,32,2048]{2,1,0:T(8,128)(2,1)}, bf16[2,32,2048]{2,1,0:T(8,128)(2,1)}, u32[]{:S(2)}, u32[]{:S(2)}) collective-permute-start(bf16[2,32,2048]{2,1,0:T(8,128)(2,1)} %pad_maximum_fusion.11), channel_id=1, source_target_pairs={{0,20},{4,24},{8,28},{12,0},{16,4},{20,8},{24,12},{28,16},{1,21},{... | collective-permute-start | bytes 786440 | tf_op jit(solution)/shard_map/ppermute | solution.py:748
  31.6 44.6 %all-to-all-start = ((s32[8,1,4]{2,1,0:T(1,128)}), s32[8,1,4]{2,1,0:T(1,128)S(1)}, u32[]{:S(2)}, u32[]{:S(2)}) async-start(s32[8,1,4]{2,1,0:T(1,128)} %broadcast_in_dim.303), calls=%async_computation | async-start | bytes 8192 | tf_op jit(solution)/shard_map/all_to_all | solution.py:736
  34.9 210.4 %all-gather.8.cloned.1.call-start = ((), (), s32[]{:S(2)}) async-start(), calls=%async_computation.8 | async-start | bytes 6193152 | tf_op jit(solution)/shard_map/all_gather | solution.py:963
  77.4 17.7 %collective-permute-start.6 = (bf16[2,32,2048]{2,1,0:T(8,128)(2,1)}, bf16[2,32,2048]{2,1,0:T(8,128)(2,1)S(1)}, u32[]{:S(2)}, u32[]{:S(2)}) collective-permute-start(bf16[2,32,2048]{2,1,0:T(8,128)(2,1)} %pad_maximum_fusion.12), channel_id=1, source_target_pairs={{0,24},{4,28},{8,0},{12,4},{16,8},{20,12},{24,16},{28,20},{1,25},{... | collective-permute-start | bytes 786440 | tf_op jit(solution)/shard_map/ppermute | solution.py:748
  82.9 14.7 %collective-permute-start.7 = (bf16[2,32,2048]{2,1,0:T(8,128)(2,1)}, bf16[2,32,2048]{2,1,0:T(8,128)(2,1)S(1)}, u32[]{:S(2)}, u32[]{:S(2)}) collective-permute-start(bf16[2,32,2048]{2,1,0:T(8,128)(2,1)} %pad_maximum_fusion.13), channel_id=1, source_target_pairs={{0,28},{4,0},{8,4},{12,8},{16,12},{20,16},{24,20},{28,24},{1,29},{... | collective-permute-start | bytes 786440 | tf_op jit(solution)/shard_map/ppermute | solution.py:748
  84.9 12.7 %collective-permute-start = (bf16[384,384]{1,0:T(8,128)(2,1)S(1)}, bf16[384,384]{1,0:T(8,128)(2,1)S(1)}, u32[]{:S(2)}, u32[]{:S(2)}) collective-permute-start(bf16[384,384]{1,0:T(8,128)(2,1)S(1)} %copy-done.28), channel_id=1, source_target_pairs={{0,1},{1,0},{2,3},{3,2},{4,5},{5,4},{6,7},{7,6},{8,9},{9,8},{10,11... | collective-permute-start | bytes 884744 | tf_op jit(solution)/shard_map/ppermute | solution.py:935
  265.3 11.6 %all-to-all-start.1 = ((bf16[8,56,256]{2,1,0:T(8,128)(2,1)}), bf16[8,56,256]{2,1,0:T(8,128)(2,1)S(1)}, u32[]{:S(2)}, u32[]{:S(2)}) async-start(bf16[8,56,256]{2,1,0:T(8,128)(2,1)} %broadcast_in_dim.307), calls=%async_computation.1 | async-start | bytes 458752 | tf_op jit(solution)/shard_map/all_to_all | solution.py:736
  311.2 15.0 %all-to-all-start.3 = ((f32[8,48,256]{2,1,0:T(8,128)}), f32[8,48,256]{2,1,0:T(8,128)S(1)}, u32[]{:S(2)}, u32[]{:S(2)}) async-start(f32[8,48,256]{2,1,0:T(8,128)} %bitcast.474), calls=%async_computation.3 | async-start | bytes 786432 | tf_op jit(solution)/shard_map/all_to_all | solution.py:1007
  314.6 172.8 %all-gather.10.cloned.1.call-start = ((), (), s32[]{:S(2)}) async-start(), calls=%async_computation.9 | async-start | bytes 1327104 | tf_op jit(solution)/shard_map/all_gather | solution.py:1030
  349.6 12.1 %collective-permute-start.14 = (f32[32,2048]{1,0:T(8,128)S(1)}, f32[32,2048]{1,0:T(8,128)S(1)}, u32[]{:S(2)}, u32[]{:S(2)}) collective-permute-start(f32[32,2048]{1,0:T(8,128)S(1)} %get-tuple-element.336), channel_id=1, source_target_pairs={{0,4},{4,8},{8,12},{12,16},{16,20},{20,24},{24,28},{28,0},{1,5},{5... | collective-permute-start | bytes 786440 | tf_op jit(solution)/shard_map/ppermute | solution.py:748
  351.1 11.1 %collective-permute-start.15 = (f32[32,2048]{1,0:T(8,128)S(1)}, f32[32,2048]{1,0:T(8,128)S(1)}, u32[]{:S(2)}, u32[]{:S(2)}) collective-permute-start(f32[32,2048]{1,0:T(8,128)S(1)} %get-tuple-element.335), channel_id=1, source_target_pairs={{0,8},{4,12},{8,16},{12,20},{16,24},{20,28},{24,0},{28,4},{1,9},{5... | collective-permute-start | bytes 786440 | tf_op jit(solution)/shard_map/ppermute | solution.py:748
  351.1 36.4 %collective-permute-start.16 = (f32[32,2048]{1,0:T(8,128)S(1)}, f32[32,2048]{1,0:T(8,128)S(1)}, u32[]{:S(2)}, u32[]{:S(2)}) collective-permute-start(f32[32,2048]{1,0:T(8,128)S(1)} %get-tuple-element.334), channel_id=1, source_target_pairs={{0,12},{4,16},{8,20},{12,24},{16,28},{20,0},{24,4},{28,8},{1,13},{... | collective-permute-start | bytes 786440 | tf_op jit(solution)/shard_map/ppermute | solution.py:748
  352.9 34.6 %collective-permute-start.17 = (f32[32,2048]{1,0:T(8,128)S(1)}, f32[32,2048]{1,0:T(8,128)S(1)}, u32[]{:S(2)}, u32[]{:S(2)}) collective-permute-start(f32[32,2048]{1,0:T(8,128)S(1)} %get-tuple-element.333), channel_id=1, source_target_pairs={{0,16},{4,20},{8,24},{12,28},{16,0},{20,4},{24,8},{28,12},{1,17},{... | collective-permute-start | bytes 786440 | tf_op jit(solution)/shard_map/ppermute | solution.py:748
  355.8 31.6 %collective-permute-start.18 = (f32[32,2048]{1,0:T(8,128)S(1)}, f32[32,2048]{1,0:T(8,128)S(1)}, u32[]{:S(2)}, u32[]{:S(2)}) collective-permute-start(f32[32,2048]{1,0:T(8,128)S(1)} %get-tuple-element.332), channel_id=1, source_target_pairs={{0,20},{4,24},{8,28},{12,0},{16,4},{20,8},{24,12},{28,16},{1,21},{... | collective-permute-start | bytes 786440 | tf_op jit(solution)/shard_map/ppermute | solution.py:748
  361.7 25.8 %collective-permute-start.19 = (f32[32,2048]{1,0:T(8,128)S(1)}, f32[32,2048]{1,0:T(8,128)S(1)}, u32[]{:S(2)}, u32[]{:S(2)}) collective-permute-start(f32[32,2048]{1,0:T(8,128)S(1)} %get-tuple-element.331), channel_id=1, source_target_pairs={{0,24},{4,28},{8,0},{12,4},{16,8},{20,12},{24,16},{28,20},{1,25},{... | collective-permute-start | bytes 786440 | tf_op jit(solution)/shard_map/ppermute | solution.py:748
  362.2 25.3 %collective-permute-start.20 = (f32[32,2048]{1,0:T(8,128)S(1)}, f32[32,2048]{1,0:T(8,128)S(1)}, u32[]{:S(2)}, u32[]{:S(2)}) collective-permute-start(f32[32,2048]{1,0:T(8,128)S(1)} %get-tuple-element.330), channel_id=1, source_target_pairs={{0,28},{4,0},{8,4},{12,8},{16,12},{20,16},{24,20},{28,24},{1,29},{... | collective-permute-start | bytes 786440 | tf_op jit(solution)/shard_map/ppermute | solution.py:748
  388.9 15.3 %collective-permute-start.21 = (f32[2,8,160,384]{3,2,1,0:T(8,128)}, f32[2,8,160,384]{3,2,1,0:T(8,128)}, u32[]{:S(2)}, u32[]{:S(2)}) collective-permute-start(f32[2,8,160,384]{3,2,1,0:T(8,128)} %dynamic-slice_bitcast_fusion.1), channel_id=1, source_target_pairs={{0,1},{1,0},{2,3},{3,2},{4,5},{5,4},{6,7},{7,6},{8,9},{9,8},{10,11... | collective-permute-start | bytes 11796488 | tf_op jit(solution)/shard_map/ppermute | solution.py:1037
  409.8 21.1 %collective-permute-start.22 = (bf16[1,160,384]{2,1,0:T(8,128)(2,1)}, bf16[1,160,384]{2,1,0:T(8,128)(2,1)S(1)}, u32[]{:S(2)}, u32[]{:S(2)}) collective-permute-start(bf16[1,160,384]{2,1,0:T(8,128)(2,1)} %get-tuple-element.368), channel_id=1, source_target_pairs={{0,8},{8,16},{16,24},{24,28},{28,20},{20,12},{12,4},{4,0},{1,9},{9... | collective-permute-start | bytes 368648 | tf_op jit(solution)/shard_map/ppermute | solution.py:832
  417.9 12.9 %collective-permute-start.23 = (bf16[1,160,384]{2,1,0:T(8,128)(2,1)}, bf16[1,160,384]{2,1,0:T(8,128)(2,1)}, u32[]{:S(2)}, u32[]{:S(2)}) collective-permute-start(bf16[1,160,384]{2,1,0:T(8,128)(2,1)} %get-tuple-element.367), channel_id=1, source_target_pairs={{0,4},{8,0},{16,8},{24,16},{28,24},{20,28},{12,20},{4,12},{1,5},{9... | collective-permute-start | bytes 368648 | tf_op jit(solution)/shard_map/ppermute | solution.py:833
  433.1 28.8 %collective-permute-start.25 = (bf16[2,160,384]{2,1,0:T(8,128)(2,1)S(1)}, bf16[2,160,384]{2,1,0:T(8,128)(2,1)S(1)}, u32[]{:S(2)}, u32[]{:S(2)}) collective-permute-start(bf16[2,160,384]{2,1,0:T(8,128)(2,1)S(1)} %pad_maximum_fusion.16), channel_id=1, source_target_pairs={{0,4},{8,0},{16,8},{24,16},{28,24},{20,28},{12,20},{4,12},{1,5},{9... | collective-permute-start | bytes 737288 | tf_op jit(solution)/shard_map/ppermute | solution.py:833
  439.7 22.2 %collective-permute-start.24 = (bf16[2,160,384]{2,1,0:T(8,128)(2,1)}, bf16[2,160,384]{2,1,0:T(8,128)(2,1)S(1)}, u32[]{:S(2)}, u32[]{:S(2)}) collective-permute-start(bf16[2,160,384]{2,1,0:T(8,128)(2,1)} %pad_maximum_fusion.15), channel_id=1, source_target_pairs={{0,8},{8,16},{16,24},{24,28},{28,20},{20,12},{12,4},{4,0},{1,9},{9... | collective-permute-start | bytes 737288 | tf_op jit(solution)/shard_map/ppermute | solution.py:832
  441.8 45.7 %all-to-all-start.5 = ((bf16[8,48,336]{2,1,0:T(8,128)(2,1)}), bf16[8,48,336]{2,1,0:T(8,128)(2,1)S(1)}, u32[]{:S(2)}, u32[]{:S(2)}) async-start(bf16[8,48,336]{2,1,0:T(8,128)(2,1)} %bitcast.437), calls=%async_computation.5 | async-start | bytes 589824 | tf_op jit(solution)/shard_map/all_to_all | solution.py:1049
  465.3 22.2 %collective-permute-start.26 = (bf16[2,160,384]{2,1,0:T(8,128)(2,1)S(1)}, bf16[2,160,384]{2,1,0:T(8,128)(2,1)S(1)}, u32[]{:S(2)}, u32[]{:S(2)}) collective-permute-start(bf16[2,160,384]{2,1,0:T(8,128)(2,1)S(1)} %get-tuple-element.325), channel_id=1, source_target_pairs={{0,8},{8,16},{16,24},{24,28},{28,20},{20,12},{12,4},{4,0},{1,9},{9... | collective-permute-start | bytes 737288 | tf_op jit(solution)/shard_map/ppermute | solution.py:832
  467.3 20.1 %collective-permute-start.27 = (bf16[2,160,384]{2,1,0:T(8,128)(2,1)S(1)}, bf16[2,160,384]{2,1,0:T(8,128)(2,1)S(1)}, u32[]{:S(2)}, u32[]{:S(2)}) collective-permute-start(bf16[2,160,384]{2,1,0:T(8,128)(2,1)S(1)} %get-tuple-element.324), channel_id=1, source_target_pairs={{0,4},{8,0},{16,8},{24,16},{28,24},{20,28},{12,20},{4,12},{1,5},{9... | collective-permute-start | bytes 737288 | tf_op jit(solution)/shard_map/ppermute | solution.py:833
  511.6 10.8 %collective-permute-start.41 = (f32[16,384]{1,0:T(8,128)S(1)}, f32[16,384]{1,0:T(8,128)S(1)}, u32[]{:S(2)}, u32[]{:S(2)}) collective-permute-start(f32[16,384]{1,0:T(8,128)S(1)} %concatenate.76), channel_id=1, source_target_pairs={{0,1},{1,0},{2,3},{3,2},{4,5},{5,4},{6,7},{7,6},{8,9},{9,8},{10,11... | collective-permute-start | bytes 73736 | tf_op jit(solution)/shard_map/ppermute | solution.py:724
  511.8 12.4 %collective-permute-start.34 = (bf16[2,160,384]{2,1,0:T(8,128)(2,1)S(1)}, bf16[2,160,384]{2,1,0:T(8,128)(2,1)S(1)}, u32[]{:S(2)}, u32[]{:S(2)}) collective-permute-start(bf16[2,160,384]{2,1,0:T(8,128)(2,1)S(1)} %pad_maximum_fusion.18), channel_id=1, source_target_pairs={{0,4},{8,0},{16,8},{24,16},{28,24},{20,28},{12,20},{4,12},{1,5},{9... | collective-permute-start | bytes 737288 | tf_op jit(solution)/shard_map/ppermute | solution.py:833
  520.3 18.7 %collective-permute-start.38 = (f32[2,160,384]{2,1,0:T(8,128)S(1)}, f32[2,160,384]{2,1,0:T(8,128)S(1)}, u32[]{:S(2)}, u32[]{:S(2)}) collective-permute-start(f32[2,160,384]{2,1,0:T(8,128)S(1)} %get-tuple-element.322), channel_id=1, source_target_pairs={{0,8},{8,16},{16,24},{24,28},{28,20},{20,12},{12,4},{4,0},{1,9},{9... | collective-permute-start | bytes 1474568 | tf_op jit(solution)/shard_map/ppermute | solution.py:832
  521.9 17.2 %collective-permute-start.39 = (f32[2,160,384]{2,1,0:T(8,128)S(1)}, f32[2,160,384]{2,1,0:T(8,128)S(1)}, u32[]{:S(2)}, u32[]{:S(2)}) collective-permute-start(f32[2,160,384]{2,1,0:T(8,128)S(1)} %get-tuple-element.323), channel_id=1, source_target_pairs={{0,4},{8,0},{16,8},{24,16},{28,24},{20,28},{12,20},{4,12},{1,5},{9... | collective-permute-start | bytes 1474568 | tf_op jit(solution)/shard_map/ppermute | solution.py:833
  525.7 12.1 %collective-permute-start.35 = (bf16[2,160,384]{2,1,0:T(8,128)(2,1)S(1)}, bf16[2,160,384]{2,1,0:T(8,128)(2,1)S(1)}, u32[]{:S(2)}, u32[]{:S(2)}) collective-permute-start(bf16[2,160,384]{2,1,0:T(8,128)(2,1)S(1)} %get-tuple-element.317), channel_id=1, source_target_pairs={{0,4},{8,0},{16,8},{24,16},{28,24},{20,28},{12,20},{4,12},{1,5},{9... | collective-permute-start | bytes 737288 | tf_op jit(solution)/shard_map/ppermute | solution.py:833
  526.6 17.0 %collective-permute-start.32 = (f32[2,160,384]{2,1,0:T(8,128)S(1)}, f32[2,160,384]{2,1,0:T(8,128)S(1)}, u32[]{:S(2)}, u32[]{:S(2)}) collective-permute-start(f32[2,160,384]{2,1,0:T(8,128)S(1)} %get-tuple-element.316), channel_id=1, source_target_pairs={{0,8},{8,16},{16,24},{24,28},{28,20},{20,12},{12,4},{4,0},{1,9},{9... | collective-permute-start | bytes 1474568 | tf_op jit(solution)/shard_map/ppermute | solution.py:832
  538.5 9.8 %collective-permute-start.36 = (f32[2,160,384]{2,1,0:T(8,128)S(1)}, f32[2,160,384]{2,1,0:T(8,128)S(1)}, u32[]{:S(2)}, u32[]{:S(2)}) collective-permute-start(f32[2,160,384]{2,1,0:T(8,128)S(1)} %bitcast_add_fusion.7), channel_id=1, source_target_pairs={{0,4},{8,0},{16,8},{24,16},{28,24},{20,28},{12,20},{4,12},{1,5},{9... | collective-permute-start | bytes 1474568 | tf_op jit(solution)/shard_map/ppermute | solution.py:833
  540.2 9.9 %collective-permute-start.40 = (f32[160,384]{1,0:T(8,128)S(1)}, f32[160,384]{1,0:T(8,128)S(1)}, u32[]{:S(2)}, u32[]{:S(2)}) collective-permute-start(f32[160,384]{1,0:T(8,128)S(1)} %dynamic-slice_bitcast_fusion.8), channel_id=1, source_target_pairs={{0,2},{1,3},{2,0},{3,1},{4,6},{5,7},{6,4},{7,5},{8,10},{9,11},{10,... | collective-permute-start | bytes 737288 | tf_op jit(solution)/shard_map/ppermute | solution.py:855
  555.5 10.4 %collective-permute-start.43 = (bf16[2,184,384]{2,1,0:T(8,128)(2,1)}, bf16[2,184,384]{2,1,0:T(8,128)(2,1)S(1)}, u32[]{:S(2)}, u32[]{:S(2)}) collective-permute-start(bf16[2,184,384]{2,1,0:T(8,128)(2,1)} %pad_maximum_fusion.6), channel_id=1, source_target_pairs={{0,8},{8,16},{16,24},{24,28},{28,20},{20,12},{12,4},{4,0},{1,9},{9... | collective-permute-start | bytes 847880 | tf_op jit(solution)/shard_map/ppermute | solution.py:794
  556.9 11.0 %collective-permute-start.44 = (bf16[2,184,384]{2,1,0:T(8,128)(2,1)}, bf16[2,184,384]{2,1,0:T(8,128)(2,1)S(1)}, u32[]{:S(2)}, u32[]{:S(2)}) collective-permute-start(bf16[2,184,384]{2,1,0:T(8,128)(2,1)} %pad_maximum_fusion.6), channel_id=1, source_target_pairs={{0,4},{8,0},{16,8},{24,16},{28,24},{20,28},{12,20},{4,12},{1,5},{9... | collective-permute-start | bytes 847880 | tf_op jit(solution)/shard_map/ppermute | solution.py:795
  561.5 154.3 %all-to-all-start.6 = ((f32[8,1,2048]{2,1,0:T(1,128)}), f32[8,1,2048]{2,1,0:T(1,128)}, u32[]{:S(2)}, u32[]{:S(2)}) async-start(f32[8,1,2048]{2,1,0:T(1,128)} %broadcast_in_dim.355), calls=%async_computation.6 | async-start | bytes 131072 | tf_op jit(solution)/shard_map/all_to_all | solution.py:736
  596.0 30.7 %collective-permute-start.53 = (bf16[2,384,384]{2,1,0:T(8,128)(2,1)}, bf16[2,384,384]{2,1,0:T(8,128)(2,1)}, u32[]{:S(2)}, u32[]{:S(2)}) collective-permute-start(bf16[2,384,384]{2,1,0:T(8,128)(2,1)} %get-tuple-element.359), channel_id=1, source_target_pairs={{0,1},{1,0},{2,3},{3,2},{4,5},{5,4},{6,7},{7,6},{8,9},{9,8},{10,11... | collective-permute-start | bytes 1769480 | tf_op jit(solution)/shard_map/ppermute | solution.py:1116
  596.6 30.2 %collective-permute-start.54 = (bf16[2,384,384]{2,1,0:T(8,128)(2,1)}, bf16[2,384,384]{2,1,0:T(8,128)(2,1)}, u32[]{:S(2)}, u32[]{:S(2)}) collective-permute-start(bf16[2,384,384]{2,1,0:T(8,128)(2,1)} %get-tuple-element.358), channel_id=1, source_target_pairs={{0,2},{1,3},{2,0},{3,1},{4,6},{5,7},{6,4},{7,5},{8,10},{9,11},{10,... | collective-permute-start | bytes 1769480 | tf_op jit(solution)/shard_map/ppermute | solution.py:1116
  598.2 28.5 %collective-permute-start.55 = (bf16[2,384,384]{2,1,0:T(8,128)(2,1)}, bf16[2,384,384]{2,1,0:T(8,128)(2,1)}, u32[]{:S(2)}, u32[]{:S(2)}) collective-permute-start(bf16[2,384,384]{2,1,0:T(8,128)(2,1)} %get-tuple-element.357), channel_id=1, source_target_pairs={{0,3},{1,2},{2,1},{3,0},{4,7},{5,6},{6,5},{7,4},{8,11},{9,10},{10,... | collective-permute-start | bytes 1769480 | tf_op jit(solution)/shard_map/ppermute | solution.py:1116
  600.1 24.7 %collective-permute-start.52 = (f32[1,128]{1,0:T(1,128)S(1)}, f32[1,128]{1,0:T(1,128)S(1)}, u32[]{:S(2)}, u32[]{:S(2)}) collective-permute-start(f32[1,128]{1,0:T(1,128)S(1)} %broadcast_add_fusion), channel_id=1, source_target_pairs={{0,2},{1,3},{2,0},{3,1},{4,6},{5,7},{6,4},{7,5},{8,10},{9,11},{10,... | collective-permute-start | bytes 1544 | tf_op jit(solution)/shard_map/ppermute | solution.py:724
  632.0 73.5 %collective-permute-start.57 = (f32[2,384,384]{2,1,0:T(8,128)}, f32[2,384,384]{2,1,0:T(8,128)}, u32[]{:S(2)}, u32[]{:S(2)}) collective-permute-start(f32[2,384,384]{2,1,0:T(8,128)} %fusion.40.stats_ref), channel_id=1, source_target_pairs={{0,2},{1,3},{2,0},{3,1},{4,6},{5,7},{6,4},{7,5},{8,10},{9,11},{10,... | collective-permute-start | bytes 3538952 | tf_op jit(solution)/shard_map/ppermute | solution.py:1125
  633.6 51.8 %collective-permute-start.56 = (f32[336,512]{1,0:T(8,128)S(1)}, f32[336,512]{1,0:T(8,128)S(1)}, u32[]{:S(2)}, u32[]{:S(2)}) collective-permute-start(f32[336,512]{1,0:T(8,128)S(1)} %get-tuple-element.182), channel_id=1, source_target_pairs={{0,2},{1,3},{2,0},{3,1},{4,6},{5,7},{6,4},{7,5},{8,10},{9,11},{10,... | collective-permute-start | bytes 2064392 | tf_op jit(solution)/shard_map/ppermute | solution.py:1127
  687.0 28.6 %collective-permute-start.58 = (f32[2,384,384]{2,1,0:T(8,128)}, f32[2,384,384]{2,1,0:T(8,128)S(1)}, u32[]{:S(2)}, u32[]{:S(2)}) collective-permute-start(f32[2,384,384]{2,1,0:T(8,128)} %shard_map.609), channel_id=1, source_target_pairs={{0,2},{1,3},{2,0},{3,1},{4,6},{5,7},{6,4},{7,5},{8,10},{9,11},{10,... | collective-permute-start | bytes 3538952 | tf_op jit(solution)/shard_map/ppermute | solution.py:1145
  720.7 16.8 %collective-permute-start.61 = (f32[2,2,384,384]{3,2,1,0:T(8,128)S(1)}, f32[2,2,384,384]{3,2,1,0:T(8,128)S(1)}, u32[]{:S(2)}, u32[]{:S(2)}) collective-permute-start(f32[2,2,384,384]{3,2,1,0:T(8,128)S(1)} %bitcast_dynamic-update-slice_fusion.5), channel_id=1, source_target_pairs={{0,1},{1,0},{2,3},{3,2},{4,5},{5,4},{6,7},{7,6},{8,9},{9,8},{10,11... | collective-permute-start | bytes 7077896 | tf_op jit(solution)/shard_map/ppermute | solution.py:860
  (100 other events, 967.2 us)
Sparse Core Ops, SparseCore 0:
  11.5 143.2 all-gather.5
  157.6 87.6 all-gather.7
  393.5 53.5 all-gather.9
